TPU v7x, 32 devices: a whole 2x2x4 slice. The times are simulated.
32 devices in a mesh: sec: 2 (over core), row: 4 (over y, x), col: 4 (over z).
Axes of the slice: x: 2, y: 2, z: 4, core: 2. Of those that a mesh axis runs over, the one named last changes fastest.
Arguments:
- leaf_rhs: bfloat16 [2, 4, 1, 4, 128, 256], P('sec', 'row', None, 'col'), may hold values from -6 to 6
- sep_rhs: bfloat16 [2, 4, 4, 128, 256], P('sec', 'row', 'col'), may hold values from -6 to 6
- top_rhs: bfloat16 [4, 4, 128, 256], P('row', 'col'), may hold values from -6 to 6
- leaf_inv: float32 [2, 4, 1, 4, 128, 128], P('sec', 'row', None, 'col'), may hold values from -1 to 3, as said below
- sep_inv: float32 [2, 4, 4, 128, 128], P('sec', 'row', 'col'), may hold values from -1 to 3, as said below
- top_inv: float32 [4, 4, 128, 128], P('row', 'col'), may hold values from -1 to 3, as said below
- sep_leaf: bfloat16 [2, 4, 4, 128, 4, 1, 4, 128], P('sec', 'row', None, None, None, None, 'col'), may hold values from -0.1875 to 0.1875
- top_leaf: bfloat16 [2, 4, 4, 128, 4, 1, 4, 128], P('sec', 'row', None, None, None, None, 'col'), may hold values from -0.125 to 0.125
- top_sep: bfloat16 [2, 4, 4, 128, 4, 4, 128], P('sec', 'row', None, None, None, 'col'), may hold values from -0.125 to 0.125
- sep_leaf_mask: int32 [2, 4, 4, 4, 1, 4], P('sec', 'row', None, None, None, 'col'), may hold values 0 or 1
- top_leaf_mask: int32 [2, 4, 4, 4, 1, 4], P('sec', 'row', None, None, None, 'col'), may hold values 0 or 1
- top_sep_mask: int32 [2, 4, 4, 4, 4], P('sec', 'row', None, None, 'col'), may hold values 0 or 1
Outputs:
- leaf_x: float32 [2, 4, 1, 4, 128, 256], P('sec', 'row', None, 'col')
- sep_x: float32 [2, 4, 4, 128, 256], P('sec', 'row', 'col')
- top_x: float32 [4, 4, 128, 256], P('row', 'col')
Inputs may be any that keep to these rules, and one draw needn't show every extreme that they name: `leaf_inv`: every 128 x 128 block is lower triangular with positive diagonal. `sep_inv`: every 128 x 128 block is lower triangular with positive diagonal. `top_inv`: every 128 x 128 block is lower triangular with positive diagonal.
All inputs are finite; a program needn't handle non-finite values. No bound on the sum of `sep_leaf_mask` or of `top_leaf_mask` or of `top_sep_mask` on one device may be relied on, other than what follows from the above.
Results may differ from a plain program's by a relative error of at most 0.0036.
Values may be sent and summed in bfloat16 or wider, within the bound.
No kernel may reach another device: no remote copies, remote signals or barrier semaphores. Data moves between devices by JAX's collectives and lax.ppermute only.
A program may use at most 128 MiB of HBM per device.

v0:
```python
import jax
import jax.numpy as jnp
from jax import lax
from jax.sharding import PartitionSpec as P


def lower_apply(inverse, right_side):
    return jnp.einsum("...ab,...bn->...an", inverse, right_side, precision=lax.Precision.HIGHEST)


def upper_apply(inverse, right_side):
    return jnp.einsum("...ba,...bn->...an", inverse, right_side, precision=lax.Precision.HIGHEST)


def mask_tiles(tile_set, pattern):
    return tile_set * pattern.astype(jnp.bfloat16)[:, None, :, :, None]


def spread_down(values, update, totals):
    return update(totals, lax.all_gather(values, "row", axis=0, tiled=True), jnp.int32(0))


def reduce_row(partial_value, rhs_cols):
    col_count = lax.axis_size("col")
    summed = lax.psum_scatter(
        partial_value.reshape(col_count, partial_value.shape[0] // col_count, rhs_cols),
        "col",
        scatter_dimension=0,
        tiled=True,
    )
    return summed.reshape(summed.shape[1], rhs_cols)


def add_sections(partial_value):
    return lax.psum(partial_value, "sec")


def spread_across(values):
    return lax.all_gather(values[None], "col", axis=0, tiled=True)


def collect_up(term_fn, row_span):
    return lax.psum_scatter(
        term_fn(jnp.int32(0), row_span * lax.axis_size("row")),
        "row",
        scatter_dimension=0,
        tiled=True,
    )


def body(
    leaf_rhs,
    sep_rhs,
    top_rhs,
    leaf_inv,
    sep_inv,
    top_inv,
    sep_leaf,
    top_leaf,
    top_sep,
    sep_leaf_mask,
    top_leaf_mask,
    top_sep_mask,
):
    leaf_count = leaf_rhs.shape[2]
    tile_width = leaf_rhs.shape[4]
    rhs_cols = leaf_rhs.shape[5]
    col_count = sep_leaf.shape[2]
    row_count = sep_leaf.shape[4]
    rows_out = col_count * tile_width
    leaf_span = leaf_count * tile_width
    contract = (((0,), (0,)), ((), ()))
    sep_tiles = mask_tiles(sep_leaf[0, 0, :, :, :, :, 0], sep_leaf_mask[0, 0, :, :, :, 0])
    top_tiles = mask_tiles(top_leaf[0, 0, :, :, :, :, 0], top_leaf_mask[0, 0, :, :, :, 0])
    cross_tiles = (
        top_sep[0, 0, :, :, :, 0]
        * top_sep_mask[0, 0, :, :, 0].astype(jnp.bfloat16)[:, None, :, None]
    )
    leaf_y = lower_apply(leaf_inv[0, 0, :, 0], leaf_rhs[0, 0, :, 0].astype(jnp.float32))
    leaf_send = leaf_y.astype(jnp.bfloat16)

    def leaf_update(totals, pieces, offset):
        how_many = pieces.shape[0]
        flat_values = pieces.reshape(how_many * leaf_span, rhs_cols)
        sep_block = sep_tiles.reshape(rows_out, how_many * leaf_span)
        top_block = top_tiles.reshape(rows_out, how_many * leaf_span)
        return (
            jnp.dot(sep_block, flat_values, preferred_element_type=jnp.float32),
            jnp.dot(top_block, flat_values, preferred_element_type=jnp.float32),
        )

    empty_sum = jnp.zeros((rows_out, rhs_cols), jnp.float32)
    sep_part, top_part = spread_down(leaf_send[None], leaf_update, (empty_sum, empty_sum))
    sep_total = reduce_row(sep_part, rhs_cols)
    sep_y = lower_apply(sep_inv[0, 0, 0], sep_rhs[0, 0, 0].astype(jnp.float32) - sep_total)
    sep_send = sep_y.astype(jnp.bfloat16)

    def sep_update(totals, pieces, offset):
        how_many = pieces.shape[0]
        tile_block = cross_tiles.reshape(rows_out, how_many * tile_width)
        return totals + jnp.dot(
            tile_block,
            pieces.reshape(how_many * tile_width, rhs_cols),
            preferred_element_type=jnp.float32,
        )

    top_part = spread_down(sep_send[None], sep_update, top_part)
    top_total = reduce_row(add_sections(top_part), rhs_cols)
    top_y = lower_apply(top_inv[0, 0], top_rhs[0, 0].astype(jnp.float32) - top_total)
    top_x = upper_apply(top_inv[0, 0], top_y)
    top_flat = spread_across(top_x.astype(jnp.bfloat16)).reshape(rows_out, rhs_cols)
    cross_flat = cross_tiles.reshape(rows_out, row_count * tile_width)
    sep_flat_tiles = sep_tiles.reshape(rows_out, row_count * leaf_span)
    top_flat_tiles = top_tiles.reshape(rows_out, row_count * leaf_span)

    def sep_terms(offset, how_many):
        return lax.dot_general(cross_flat, top_flat, contract, preferred_element_type=jnp.float32)

    sep_t = collect_up(sep_terms, tile_width)
    sep_x = upper_apply(sep_inv[0, 0, 0], sep_y - sep_t)
    sep_row = spread_across(sep_x.astype(jnp.bfloat16)).reshape(rows_out, rhs_cols)

    def both_terms(offset, how_many):
        return lax.dot_general(
            sep_flat_tiles, sep_row, contract, preferred_element_type=jnp.float32
        ) + lax.dot_general(top_flat_tiles, top_flat, contract, preferred_element_type=jnp.float32)

    leaf_t = collect_up(both_terms, leaf_span)
    leaf_x = upper_apply(
        leaf_inv[0, 0, :, 0], leaf_y - leaf_t.reshape(leaf_count, tile_width, rhs_cols)
    )
    return (leaf_x[None, None, :, None], sep_x[None, None, None], top_x[None, None])


def solution(mesh):
    in_specs = (
        P("sec", "row", None, "col", None, None),
        P("sec", "row", "col", None, None),
        P("row", "col", None, None),
        P("sec", "row", None, "col", None, None),
        P("sec", "row", "col", None, None),
        P("row", "col", None, None),
        P("sec", "row", None, None, None, None, "col", None),
        P("sec", "row", None, None, None, None, "col", None),
        P("sec", "row", None, None, None, "col", None),
        P("sec", "row", None, None, None, "col"),
        P("sec", "row", None, None, None, "col"),
        P("sec", "row", None, None, "col"),
    )
    out_specs = (
        P("sec", "row", None, "col", None, None),
        P("sec", "row", "col", None, None),
        P("row", "col", None, None),
    )
    return jax.shard_map(body, mesh=mesh, in_specs=in_specs, out_specs=out_specs, check_vma=False)
```

profile of v0, /device:TPU:0, one launch (start us, length us, event | category | flops | bytes accessed | tf_op | source)
XLA Modules:
  0.0 182.7 jit_solution(856589357141500560)
XLA Ops:
  7.2 0.7 convert_element_type.74
  7.9 1.3 broadcast_multiply_fusion.2
  10.3 10.4 %all-gather = bf16[512,256]{1,0:T(8,128)(2,1)S(1)} all-gather(bf16[128,256]{1,0:T(8,128)(2,1)S(1)} %get-tuple-element.6), channel_id=2, replica_groups=mesh['sec'=2,'row'=4,'col'=4] {'row'}, dimensions={0}, use_global_device_ids=true | all-gather | bytes 327680 | tf_op jit(solution)/shard_map/all_gather | solution.py:20
  20.8 1.1 fusion.13
  22.6 0.7 copy-done.9
  23.6 0.7 copy-done.2
  25.0 19.0 %reduce-scatter.5.cloned.1.call-done = f32[1,128,256]{2,1,0:T(8,128)} async-done(((f32[4,128,256]{2,1,0:T(8,128)}), f32[1,128,256]{2,1,0:T(8,128)}) %reduce-scatter.5.cloned.1.call-update) | async-done | bytes 131088 | tf_op jit(solution)/shard_map/reduce_scatter | solution.py:25
  44.0 1.3 fusion.35
  45.3 9.1 %all-gather.1 = bf16[512,256]{0,1:T(8,128)(2,1)S(1)} all-gather(bf16[128,256]{0,1:T(8,128)(2,1)S(1)} %get-tuple-element.8), channel_id=3, replica_groups=mesh['sec'=2,'row'=4,'col'=4] {'row'}, dimensions={0}, use_global_device_ids=true | all-gather | bytes 327680 | tf_op jit(solution)/shard_map/all_gather | solution.py:20
  54.4 1.1 convolution_add_fusion.1
  55.6 19.3 %reduce-scatter.11.cloned.1.call-done = f32[1,128,256]{2,1,0:T(8,128)} async-done(((f32[4,128,256]{2,1,0:T(8,128)}), f32[1,128,256]{2,1,0:T(8,128)}) %reduce-scatter.11.cloned.1.call-update) | async-done | bytes 131088 | tf_op jit(solution)/shard_map/reduce_scatter | solution.py:25
  75.0 18.4 %all-reduce.2.cloned.1.call-done = f32[1,128,256]{2,1,0:T(8,128)} async-done(((f32[1,128,256]{2,1,0:T(8,128)}), f32[1,128,256]{2,1,0:T(8,128)}) %all-reduce.2.cloned.1.call-update) | async-done | bytes 131088 | tf_op jit(solution)/shard_map/psum | solution.py:35
  93.4 1.3 fusion.16
  95.0 13.1 %all-gather.2 = bf16[512,256]{0,1:T(8,128)(2,1)S(1)} all-gather(bf16[128,256]{0,1:T(8,128)(2,1)S(1)} %get-tuple-element.10), channel_id=4, replica_groups=mesh['sec'=2,'row'=4,'col'=4] {'col'}, dimensions={0}, use_global_device_ids=true | all-gather | bytes 327680 | tf_op jit(solution)/shard_map/all_gather | solution.py:39
  108.1 1.1 fusion
  109.3 25.0 %reduce-scatter.7.cloned.1.call-done = f32[128,256]{0,1:T(8,128)} async-done(((f32[512,256]{0,1:T(8,128)}), f32[128,256]{0,1:T(8,128)}) %reduce-scatter.7.cloned.1.call-update) | async-done | bytes 131088 | tf_op jit(solution)/shard_map/reduce_scatter | solution.py:43
  134.3 1.2 bitcast_convert_fusion
  135.5 12.8 %all-gather.3 = bf16[512,256]{0,1:T(8,128)(2,1)S(1)} all-gather(bf16[128,256]{0,1:T(8,128)(2,1)S(1)} %get-tuple-element.12), channel_id=5, replica_groups=mesh['sec'=2,'row'=4,'col'=4] {'col'}, dimensions={0}, use_global_device_ids=true | all-gather | bytes 327680 | tf_op jit(solution)/shard_map/all_gather | solution.py:39
  148.7 1.1 convolution_add_fusion
  149.8 0.8 copy.17
  150.6 0.8 copy.16
  151.3 22.8 %reduce-scatter.9.cloned.1.call-done = f32[128,256]{1,0:T(8,128)} async-done(((f32[512,256]{1,0:T(8,128)}), f32[128,256]{1,0:T(8,128)}) %reduce-scatter.9.cloned.1.call-update) | async-done | bytes 131088 | tf_op jit(solution)/shard_map/reduce_scatter | solution.py:43
  174.1 1.3 convolution_bitcast_fusion
  175.4 0.8 copy.15
  (40 shorter events, 3.6 us)
Async XLA Ops:
  7.2 36.9 %copy-start = (f32[1,1,1,128,128]{4,3,2,1,0:T(8,128)S(1)}, f32[1,1,1,128,128]{4,3,2,1,0:T(8,128)}, u32[]{:S(2)}) copy-start(f32[1,1,1,128,128]{4,3,2,1,0:T(8,128)} %param.16) | copy-start | bytes 196612
  7.2 36.8 %reduce-scatter.5.cloned.1.call-start = ((), (), s32[]{:S(2)}) async-start(), calls=%async_computation.4 | async-start | bytes 655360 | tf_op jit(solution)/shard_map/reduce_scatter | solution.py:25
  9.3 0.8 copy-start.3
  9.3 0.9 copy-start.5
  21.9 1.4 copy-start.1
  21.9 0.7 copy-start.8
  21.9 53.0 %reduce-scatter.11.cloned.1.call-start = ((), (), s32[]{:S(2)}) async-start(), calls=%async_computation.7 | async-start | bytes 655360 | tf_op jit(solution)/shard_map/reduce_scatter | solution.py:25
  22.6 0.7 copy-start.9
  23.3 1.0 copy-start.2
  24.7 19.3 %copy-start.6 = (bf16[1,1,1,128,256]{4,3,2,1,0:T(8,128)(2,1)S(1)}, bf16[1,1,1,128,256]{4,3,2,1,0:T(8,128)(2,1)}, u32[]{:S(2)}) copy-start(bf16[1,1,1,128,256]{4,3,2,1,0:T(8,128)(2,1)} %param.13) | copy-start | bytes 196612
  55.6 37.8 %all-reduce.2.cloned.1.call-start = ((), (), s32[]{:S(2)}) async-start(), calls=%async_computation.8 | async-start | bytes 262144 | tf_op jit(solution)/shard_map/psum | solution.py:35
  74.9 18.5 %copy-start.4 = (f32[1,1,128,128]{3,2,1,0:T(8,128)S(1)}, f32[1,1,128,128]{3,2,1,0:T(8,128)}, u32[]{:S(2)}) copy-start(f32[1,1,128,128]{3,2,1,0:T(8,128)} %param.17) | copy-start | bytes 196612
  74.9 18.5 %copy-start.7 = (bf16[1,1,128,256]{3,2,1,0:T(8,128)(2,1)S(1)}, bf16[1,1,128,256]{3,2,1,0:T(8,128)(2,1)}, u32[]{:S(2)}) copy-start(bf16[1,1,128,256]{3,2,1,0:T(8,128)(2,1)} %param.14) | copy-start | bytes 196612
  74.9 59.4 %reduce-scatter.7.cloned.1.call-start = ((), (), s32[]{:S(2)}) async-start(), calls=%async_computation.5 | async-start | bytes 655360 | tf_op jit(solution)/shard_map/reduce_scatter | solution.py:43
  109.2 64.9 %reduce-scatter.9.cloned.1.call-start = ((), (), s32[]{:S(2)}) async-start(), calls=%async_computation.6 | async-start | bytes 655360 | tf_op jit(solution)/shard_map/reduce_scatter | solution.py:43
Sparse Core Ops, SparseCore 0:
  22.0 21.9 reduce-scatter.4
  55.7 19.1 reduce-scatter.10
  77.2 16.1 all-reduce.1
  109.3 24.9 reduce-scatter.6
  150.0 24.1 reduce-scatter.8
where the time goes:
time: 183 us
  waiting for transfers between devices  105 us (57%)
  blocking collectives  45.5 us (25%)
  between operations  13.9 us (8%)
  matrix products  10.6 us (6%)
  local copies, waits for them, and re-layouts  5.24 us (3%)
  other arithmetic  2.63 us (1%)
    reduce_scatter x2, waiting for transfers between devices, collect_up(): lax.psum_scatter(term_fn(jnp.int32(0), row_span * lax.axis_size('row')),...  47.8 us
    reduce_scatter x2, waiting for transfers between devices, reduce_row(): lax.psum_scatter(partial_value.reshape(col_count, partial_value.shape[0]...  38.3 us
    all_gather x2, blocking collectives, spread_across(): return lax.all_gather(values[None], 'col', axis=0, tiled=True)  26 us
    all_gather x2, blocking collectives, spread_down(): lax.all_gather(values, 'row', axis=0, tiled=True)  19.5 us
    psum x1, waiting for transfers between devices, add_sections(): return lax.psum(partial_value, 'sec')  18.4 us
    unnamed x26, local copies, waits for them, and re-layouts  5.04 us
  transfers between devices with their start and end apart: 5, of which 5 were waited for; matrix products, arithmetic and copies ran while one was open for 1% of the time, Pallas kernels for 0%

commit v1 on v0

v1 whole, which is shorter than its diff:
```python
import jax
import jax.numpy as jnp
from jax import lax
from jax.sharding import PartitionSpec as P

BF = jnp.bfloat16
F32 = jnp.float32
HI = lax.Precision.HIGHEST


def is_direct(n):
    return n in (1, 2, 4)


def swap(values, axis, n, step):
    return lax.ppermute(values, axis, [(i, i ^ step) for i in range(n)])


def partner_order(values, axis_name, n, dim):
    if not is_direct(n):
        return values
    me = lax.axis_index(axis_name)
    return jnp.concatenate(
        [lax.dynamic_slice_in_dim(values, me ^ d, 1, dim) for d in range(n)], axis=dim
    )


def gather(values, axis, n):
    if not is_direct(n):
        return lax.all_gather(values, axis, axis=0, tiled=True)
    return jnp.concatenate([values] + [swap(values, axis, n, d) for d in range(1, n)], axis=0)


def scatter_sum(block_fn, axis, n):
    if not is_direct(n):
        stacked = jnp.stack([block_fn(d) for d in range(n)])
        return lax.psum_scatter(stacked, axis, scatter_dimension=0, tiled=True)[0]
    got = [swap(block_fn(d).astype(BF), axis, n, d) for d in range(1, n)]
    total = block_fn(0)
    for piece in got:
        total = total + piece.astype(F32)
    return total


def dot(a, b):
    return jnp.dot(a, b, preferred_element_type=F32)


def dot_t(a, b):
    return lax.dot_general(a, b, (((0,), (0,)), ((), ())), preferred_element_type=F32)


def lower_apply(inverse, right_side):
    return jnp.einsum("...ab,...bn->...an", inverse, right_side, precision=HI)


def upper_apply(inverse, right_side):
    return jnp.einsum("...ba,...bn->...an", inverse, right_side, precision=HI)


def make_body(n_sec, n_row, n_col):
    def body(leaf_rhs, sep_rhs, top_rhs, leaf_inv, sep_inv, top_inv,
             sep_leaf, top_leaf, top_sep, sep_leaf_mask, top_leaf_mask, top_sep_mask):
        leaf_count, width, cols = leaf_rhs.shape[2], leaf_rhs.shape[4], leaf_rhs.shape[5]
        span = leaf_count * width
        half = cols // n_sec
        sec = lax.axis_index("sec")

        def tiles(values, mask):
            masked = values * mask.astype(BF)[:, None, :, :, None]
            masked = masked.reshape(n_col, width, n_row, -1)
            masked = partner_order(partner_order(masked, "col", n_col, 0), "row", n_row, 2)
            return masked.reshape(n_col, width, -1)

        sl = tiles(sep_leaf[0, 0, :, :, :, :, 0], sep_leaf_mask[0, 0, :, :, :, 0])
        tl = tiles(top_leaf[0, 0, :, :, :, :, 0], top_leaf_mask[0, 0, :, :, :, 0])
        ts = tiles(top_sep[0, 0, :, :, :, None, 0], top_sep_mask[0, 0, :, :, None, 0])

        leaf_y = lower_apply(leaf_inv[0, 0, :, 0], leaf_rhs[0, 0, :, 0].astype(F32))
        leaf_col = gather(leaf_y.astype(BF).reshape(span, cols), "row", n_row)
        sep_sum = scatter_sum(lambda d: dot(sl[d], leaf_col), "col", n_col)
        sep_y = lower_apply(sep_inv[0, 0, 0], sep_rhs[0, 0, 0].astype(F32) - sep_sum)
        sep_col = gather(sep_y.astype(BF), "row", n_row)

        top_part = dot(ts.reshape(n_col * width, -1), sep_col) + dot(tl.reshape(n_col * width, -1), leaf_col)
        if n_sec == 2:
            mine = lax.dynamic_slice_in_dim(top_part, sec * half, half, 1)
            other = lax.dynamic_slice_in_dim(top_part, (1 - sec) * half, half, 1).astype(BF)
            top_half = mine + swap(other, "sec", 2, 1).astype(F32)
        else:
            top_half = lax.psum_scatter(top_part, "sec", scatter_dimension=1, tiled=True)
        top_half = top_half.reshape(n_col, width, half)
        top_sum = scatter_sum(lambda d: top_half[d], "col", n_col)
        rhs_half = lax.dynamic_slice_in_dim(top_rhs[0, 0], sec * half, half, 1).astype(F32)
        top_y = lower_apply(top_inv[0, 0], rhs_half - top_sum)
        top_xh = upper_apply(top_inv[0, 0], top_y)
        top_xb = gather(top_xh.astype(BF), "col", n_col)
        if n_sec == 2:
            other = swap(top_xb, "sec", 2, 1)
            low = jnp.where(sec == 0, top_xb, other)
            high = jnp.where(sec == 0, other, top_xb)
            top_row = jnp.concatenate([low, high], axis=1)
            other = swap(top_xh, "sec", 2, 1)
            top_x = jnp.concatenate([jnp.where(sec == 0, top_xh, other), jnp.where(sec == 0, other, top_xh)], axis=1)
        else:
            top_row = lax.all_gather(top_xb, "sec", axis=1, tiled=True)
            top_x = lax.all_gather(top_xh, "sec", axis=1, tiled=True)

        ts_flat = ts.reshape(n_col * width, n_row, width)
        sl_flat = sl.reshape(n_col * width, n_row, span)
        tl_flat = tl.reshape(n_col * width, n_row, span)
        sep_t = scatter_sum(lambda d: dot_t(ts_flat[:, d], top_row), "row", n_row)
        sep_x = upper_apply(sep_inv[0, 0, 0], sep_y - sep_t)
        sep_row = gather(sep_x.astype(BF), "col", n_col)
        leaf_t = scatter_sum(
            lambda d: dot_t(sl_flat[:, d], sep_row) + dot_t(tl_flat[:, d], top_row), "row", n_row
        )
        leaf_x = upper_apply(leaf_inv[0, 0, :, 0], leaf_y - leaf_t.reshape(leaf_count, width, cols))
        return leaf_x[None, None, :, None], sep_x[None, None, None], top_x[None, None]

    return body


def solution(mesh):
    in_specs = (
        P("sec", "row", None, "col", None, None),
        P("sec", "row", "col", None, None),
        P("row", "col", None, None),
        P("sec", "row", None, "col", None, None),
        P("sec", "row", "col", None, None),
        P("row", "col", None, None),
        P("sec", "row", None, None, None, None, "col", None),
        P("sec", "row", None, None, None, None, "col", None),
        P("sec", "row", None, None, None, "col", None),
        P("sec", "row", None, None, None, "col"),
        P("sec", "row", None, None, None, "col"),
        P("sec", "row", None, None, "col"),
    )
    out_specs = (
        P("sec", "row", None, "col", None, None),
        P("sec", "row", "col", None, None),
        P("row", "col", None, None),
    )
    body = make_body(mesh.shape["sec"], mesh.shape["row"], mesh.shape["col"])
    return jax.shard_map(body, mesh=mesh, in_specs=in_specs, out_specs=out_specs, check_vma=False)
```

time: 183 us -> 80.2 us (0.44)
  waiting for transfers between devices: 105 us -> 23.9 us
  blocking collectives: 45.5 us -> 0 us
  starting transfers between devices: 0.2 us -> 33.5 us
  between operations: 13.9 us -> 1.2 us
  matrix products: 10.6 us -> 13.1 us
    reduce_scatter x4 -> x0, waiting for transfers between devices: 86.1 us -> none  [the longest x2 47.8 us: collect_up(): lax.psum_scatter(term_fn(jnp.int32(0), row_span * lax.axis_size('row')),...]
    all_gather x4 -> x0, blocking collectives: 45.5 us -> none  [the longest x2 26 us: spread_across(): return lax.all_gather(values[None], 'col', axis=0, tiled=True)]
    ppermute x0 -> x27, starting transfers between devices: none -> 33.5 us  [swap(): return lax.ppermute(values, axis, [(i, i ^ step) for i in range(n)])]
    ppermute x0 -> x27, waiting for transfers between devices: none -> 23.9 us  [swap(): return lax.ppermute(values, axis, [(i, i ^ step) for i in range(n)])]
    psum x1 -> x0, waiting for transfers between devices: 18.4 us -> none  [add_sections(): return lax.psum(partial_value, 'sec')]
    dot_general x12 -> x24, matrix products: 10.6 us -> 13.1 us  [the longest x6 7.12 us: dot(): return jnp.dot(a, b, preferred_element_type=F32)]
    unnamed x26 -> x25, local copies, waits for them, and re-layouts: 5.04 us -> 4.14 us
  transfers between devices with their start and end apart: 5 -> 27, of which waited for: 5 -> 21; matrix products, arithmetic and copies ran while one was open for 1% -> 12% of each run, Pallas kernels for 0% -> 0%
where the time goes in v1:
time: 80.2 us; the launch traced here: 79.7 us
  starting transfers between devices  33.5 us (42%)
  waiting for transfers between devices  23.9 us (30%)
  matrix products  13.1 us (16%)
  local copies, waits for them, and re-layouts  5.98 us (7%)
  other arithmetic  1.98 us (2%)
  between operations  1.2 us (1%)
    ppermute x27, starting transfers between devices, swap(): return lax.ppermute(values, axis, [(i, i ^ step) for i in range(n)])  33.5 us
    ppermute x27, waiting for transfers between devices, swap(): return lax.ppermute(values, axis, [(i, i ^ step) for i in range(n)])  23.9 us
    dot_general x6, matrix products, dot(): return jnp.dot(a, b, preferred_element_type=F32)  7.12 us
    unnamed x25, local copies, waits for them, and re-layouts  4.14 us
    dot_general x12, matrix products, dot_t(): lax.dot_general(a, b, (((0,), (0,)), ((), ())), preferred_element_type=F32)  2.73 us
    dot_general x3, matrix products, lower_apply(): return jnp.einsum('...ab,...bn->...an', inverse, right_side, precision=HI)  1.67 us
  transfers between devices with their start and end apart: 27, of which 21 were waited for; matrix products, arithmetic and copies ran while one was open for 12% of the time, Pallas kernels for 0%

profile of v1, /device:TPU:0, one launch (start us, length us, event | category | flops | bytes accessed | tf_op | source)
XLA Modules:
  0.0 79.7 jit_solution(8930121560100379874)
XLA Ops:
  1.8 4.0 %collective-permute-start.2 = (bf16[128,256]{1,0:T(8,128)(2,1)S(1)}, bf16[128,256]{1,0:T(8,128)(2,1)S(1)}, u32[]{:S(2)}, u32[]{:S(2)}) collective-permute-start(bf16[128,256]{1,0:T(8,128)(2,1)S(1)} %get-tuple-element.53), channel_id=1, source_target_pairs={{0,12},{4,8},{8,4},{12,0},{1,13},{5,9},{9,5},{13,1},{2,14},{6,10},... | collective-permute-start | bytes 196616 | tf_op jit(solution)/shard_map/ppermute | solution.py:16
  11.5 1.7 %convolution_convert_fusion.3 = bf16[128,256]{1,0:T(8,128)(2,1)} fusion(bf16[128,512]{0,1:T(8,128)(2,1)S(1)} %bitcast.167, bf16[128,256]{1,0:T(8,128)(2,1)S(1)} %collective-permute-done.2, bf16[128,256]{1,0:T(8,128)(2,1)} %collective-permute-done.1, bf16[128,256]{1,0:T(8,128)(2,1)} %collective-permute-done, bf16[128,256]{1,0:T(8,128)(2,1)S(1)} %get-tuple-element.53), kind=kOutput, calls=%fused_computation.25 | convolution fusion | flops 34635776 | bytes 458752 | tf_op jit(solution)/shard_map/dot_general | solution.py:46
  13.2 4.0 %collective-permute-start.5 = (bf16[128,256]{1,0:T(8,128)(2,1)}, bf16[128,256]{1,0:T(8,128)(2,1)S(1)}, u32[]{:S(2)}, u32[]{:S(2)}) collective-permute-start(bf16[128,256]{1,0:T(8,128)(2,1)} %convolution_convert_fusion.3), channel_id=1, source_target_pairs={{0,3},{1,2},{2,1},{3,0},{4,7},{5,6},{6,5},{7,4},{8,11},{9,10},{10,... | collective-permute-start | bytes 196616 | tf_op jit(solution)/shard_map/ppermute | solution.py:16
  17.2 1.7 %convolution_convert_fusion.4 = bf16[128,256]{1,0:T(8,128)(2,1)} fusion(bf16[128,512]{0,1:T(8,128)(2,1)S(1)} %bitcast.165, bf16[128,256]{1,0:T(8,128)(2,1)S(1)} %collective-permute-done.2, bf16[128,256]{1,0:T(8,128)(2,1)} %collective-permute-done.1, bf16[128,256]{1,0:T(8,128)(2,1)} %collective-permute-done, bf16[128,256]{1,0:T(8,128)(2,1)S(1)} %get-tuple-element.53), kind=kOutput, calls=%fused_computation.26 | convolution fusion | flops 34635776 | bytes 458752 | tf_op jit(solution)/shard_map/dot_general | solution.py:46
  21.3 3.1 %collective-permute-done.4 = bf16[128,256]{1,0:T(8,128)(2,1)S(1)} collective-permute-done((bf16[128,256]{1,0:T(8,128)(2,1)}, bf16[128,256]{1,0:T(8,128)(2,1)S(1)}, u32[]{:S(2)}, u32[]{:S(2)}) %collective-permute-start.4) | collective-permute-done | bytes 65568 | tf_op jit(solution)/shard_map/ppermute | solution.py:16
  26.4 2.5 %collective-permute-start.8 = (bf16[128,256]{1,0:T(8,128)(2,1)S(1)}, bf16[128,256]{1,0:T(8,128)(2,1)S(1)}, u32[]{:S(2)}, u32[]{:S(2)}) collective-permute-start(bf16[128,256]{1,0:T(8,128)(2,1)S(1)} %get-tuple-element.55), channel_id=1, source_target_pairs={{0,12},{4,8},{8,4},{12,0},{1,13},{5,9},{9,5},{13,1},{2,14},{6,10},... | collective-permute-start | bytes 196616 | tf_op jit(solution)/shard_map/ppermute | solution.py:16
  31.7 1.5 %collective-permute-done.7 = bf16[128,256]{1,0:T(8,128)(2,1)S(1)} collective-permute-done((bf16[128,256]{1,0:T(8,128)(2,1)S(1)}, bf16[128,256]{1,0:T(8,128)(2,1)S(1)}, u32[]{:S(2)}, u32[]{:S(2)}) %collective-permute-start.7) | collective-permute-done | bytes 65568 | tf_op jit(solution)/shard_map/ppermute | solution.py:16
  34.1 1.3 %collective-permute-done.9 = bf16[512,128]{1,0:T(8,128)(2,1)S(1)} collective-permute-done((bf16[512,128]{1,0:T(8,128)(2,1)S(1)}, bf16[512,128]{1,0:T(8,128)(2,1)S(1)}, u32[]{:S(2)}, u32[]{:S(2)}) %collective-permute-start.9) | collective-permute-done | bytes 131104 | tf_op jit(solution)/shard_map/ppermute | solution.py:16
  35.6 1.8 %collective-permute-start.12 = (bf16[128,128]{1,0:T(8,128)(2,1)S(1)}, bf16[128,128]{1,0:T(8,128)(2,1)S(1)}, u32[]{:S(2)}, u32[]{:S(2)}) collective-permute-start(bf16[128,128]{1,0:T(8,128)(2,1)S(1)} %get-tuple-element.50), channel_id=1, source_target_pairs={{0,3},{1,2},{2,1},{3,0},{4,7},{5,6},{6,5},{7,4},{8,11},{9,10},{10,... | collective-permute-start | bytes 98312 | tf_op jit(solution)/shard_map/ppermute | solution.py:16
  38.0 2.0 %collective-permute-start.10 = (bf16[128,128]{1,0:T(8,128)(2,1)S(1)}, bf16[128,128]{1,0:T(8,128)(2,1)S(1)}, u32[]{:S(2)}, u32[]{:S(2)}) collective-permute-start(bf16[128,128]{1,0:T(8,128)(2,1)S(1)} %get-tuple-element.49), channel_id=1, source_target_pairs={{0,1},{1,0},{2,3},{3,2},{4,5},{5,4},{6,7},{7,6},{8,9},{9,8},{10,11... | collective-permute-start | bytes 98312 | tf_op jit(solution)/shard_map/ppermute | solution.py:16
  40.0 1.5 %collective-permute-done.12 = bf16[128,128]{1,0:T(8,128)(2,1)S(1)} collective-permute-done((bf16[128,128]{1,0:T(8,128)(2,1)S(1)}, bf16[128,128]{1,0:T(8,128)(2,1)S(1)}, u32[]{:S(2)}, u32[]{:S(2)}) %collective-permute-start.12) | collective-permute-done | bytes 32800 | tf_op jit(solution)/shard_map/ppermute | solution.py:16
  44.1 2.6 %collective-permute-start.15 = (bf16[128,128]{0,1:T(8,128)(2,1)S(1)}, bf16[128,128]{0,1:T(8,128)(2,1)S(1)}, u32[]{:S(2)}, u32[]{:S(2)}) collective-permute-start(bf16[128,128]{0,1:T(8,128)(2,1)S(1)} %get-tuple-element.52), channel_id=1, source_target_pairs={{0,3},{1,2},{2,1},{3,0},{4,7},{5,6},{6,5},{7,4},{8,11},{9,10},{10,... | collective-permute-start | bytes 98312 | tf_op jit(solution)/shard_map/ppermute | solution.py:16
  47.3 1.3 %collective-permute-start.13 = (bf16[128,128]{0,1:T(8,128)(2,1)S(1)}, bf16[128,128]{0,1:T(8,128)(2,1)S(1)}, u32[]{:S(2)}, u32[]{:S(2)}) collective-permute-start(bf16[128,128]{0,1:T(8,128)(2,1)S(1)} %get-tuple-element.52), channel_id=1, source_target_pairs={{0,1},{1,0},{2,3},{3,2},{4,5},{5,4},{6,7},{7,6},{8,9},{9,8},{10,11... | collective-permute-start | bytes 98312 | tf_op jit(solution)/shard_map/ppermute | solution.py:16
  48.6 1.6 %collective-permute-done.15 = bf16[128,128]{0,1:T(8,128)(2,1)S(1)} collective-permute-done((bf16[128,128]{0,1:T(8,128)(2,1)S(1)}, bf16[128,128]{0,1:T(8,128)(2,1)S(1)}, u32[]{:S(2)}, u32[]{:S(2)}) %collective-permute-start.15) | collective-permute-done | bytes 32800 | tf_op jit(solution)/shard_map/ppermute | solution.py:16
  50.2 1.4 %collective-permute-done.14 = bf16[128,128]{0,1:T(8,128)(2,1)S(1)} collective-permute-done((bf16[128,128]{0,1:T(8,128)(2,1)S(1)}, bf16[128,128]{0,1:T(8,128)(2,1)S(1)}, u32[]{:S(2)}, u32[]{:S(2)}) %collective-permute-start.14) | collective-permute-done | bytes 32800 | tf_op jit(solution)/shard_map/ppermute | solution.py:16
  54.0 1.6 %collective-permute-start.19 = (bf16[128,256]{1,0:T(8,128)(2,1)S(1)}, bf16[128,256]{1,0:T(8,128)(2,1)S(1)}, u32[]{:S(2)}, u32[]{:S(2)}) collective-permute-start(bf16[128,256]{1,0:T(8,128)(2,1)S(1)} %convolution_convert_fusion), channel_id=1, source_target_pairs={{0,12},{4,8},{8,4},{12,0},{1,13},{5,9},{9,5},{13,1},{2,14},{6,10},... | collective-permute-start | bytes 196616 | tf_op jit(solution)/shard_map/ppermute | solution.py:16
  56.1 1.5 %collective-permute-start.17 = (bf16[128,256]{1,0:T(8,128)(2,1)S(1)}, bf16[128,256]{1,0:T(8,128)(2,1)S(1)}, u32[]{:S(2)}, u32[]{:S(2)}) collective-permute-start(bf16[128,256]{1,0:T(8,128)(2,1)S(1)} %convolution_convert_fusion.2), channel_id=1, source_target_pairs={{0,4},{4,0},{8,12},{12,8},{1,5},{5,1},{9,13},{13,9},{2,6},{6,2},{1... | collective-permute-start | bytes 196616 | tf_op jit(solution)/shard_map/ppermute | solution.py:16
  57.8 1.5 %collective-permute-done.19 = bf16[128,256]{1,0:T(8,128)(2,1)S(1)} collective-permute-done((bf16[128,256]{1,0:T(8,128)(2,1)S(1)}, bf16[128,256]{1,0:T(8,128)(2,1)S(1)}, u32[]{:S(2)}, u32[]{:S(2)}) %collective-permute-start.19) | collective-permute-done | bytes 65568 | tf_op jit(solution)/shard_map/ppermute | solution.py:16
  61.8 1.8 %collective-permute-start.22 = (bf16[128,256]{1,0:T(8,128)(2,1)S(1)}, bf16[128,256]{1,0:T(8,128)(2,1)S(1)}, u32[]{:S(2)}, u32[]{:S(2)}) collective-permute-start(bf16[128,256]{1,0:T(8,128)(2,1)S(1)} %get-tuple-element.57), channel_id=1, source_target_pairs={{0,3},{1,2},{2,1},{3,0},{4,7},{5,6},{6,5},{7,4},{8,11},{9,10},{10,... | collective-permute-start | bytes 196616 | tf_op jit(solution)/shard_map/ppermute | solution.py:16
  64.2 2.0 %collective-permute-start.20 = (bf16[128,256]{1,0:T(8,128)(2,1)S(1)}, bf16[128,256]{1,0:T(8,128)(2,1)S(1)}, u32[]{:S(2)}, u32[]{:S(2)}) collective-permute-start(bf16[128,256]{1,0:T(8,128)(2,1)S(1)} %get-tuple-element.57), channel_id=1, source_target_pairs={{0,1},{1,0},{2,3},{3,2},{4,5},{5,4},{6,7},{7,6},{8,9},{9,8},{10,11... | collective-permute-start | bytes 196616 | tf_op jit(solution)/shard_map/ppermute | solution.py:16
  66.4 2.1 %collective-permute-done.22 = bf16[128,256]{1,0:T(8,128)(2,1)S(1)} collective-permute-done((bf16[128,256]{1,0:T(8,128)(2,1)S(1)}, bf16[128,256]{1,0:T(8,128)(2,1)S(1)}, u32[]{:S(2)}, u32[]{:S(2)}) %collective-permute-start.22) | collective-permute-done | bytes 65568 | tf_op jit(solution)/shard_map/ppermute | solution.py:16
  68.6 2.1 %collective-permute-done.21 = bf16[128,256]{1,0:T(8,128)(2,1)S(1)} collective-permute-done((bf16[128,256]{1,0:T(8,128)(2,1)S(1)}, bf16[128,256]{1,0:T(8,128)(2,1)S(1)}, u32[]{:S(2)}, u32[]{:S(2)}) %collective-permute-start.21) | collective-permute-done | bytes 65568 | tf_op jit(solution)/shard_map/ppermute | solution.py:16
  70.9 1.9 %collective-permute-start.25 = (bf16[128,256]{1,0:T(8,128)(2,1)S(1)}, bf16[128,256]{1,0:T(8,128)(2,1)S(1)}, u32[]{:S(2)}, u32[]{:S(2)}) collective-permute-start(bf16[128,256]{1,0:T(8,128)(2,1)S(1)} %fusion.12), channel_id=1, source_target_pairs={{0,12},{4,8},{8,4},{12,0},{1,13},{5,9},{9,5},{13,1},{2,14},{6,10},... | collective-permute-start | bytes 196616 | tf_op jit(solution)/shard_map/ppermute | solution.py:16
  73.3 1.7 %collective-permute-start.23 = (bf16[128,256]{1,0:T(8,128)(2,1)S(1)}, bf16[128,256]{1,0:T(8,128)(2,1)S(1)}, u32[]{:S(2)}, u32[]{:S(2)}) collective-permute-start(bf16[128,256]{1,0:T(8,128)(2,1)S(1)} %fusion.10), channel_id=1, source_target_pairs={{0,4},{4,0},{8,12},{12,8},{1,5},{5,1},{9,13},{13,9},{2,6},{6,2},{1... | collective-permute-start | bytes 196616 | tf_op jit(solution)/shard_map/ppermute | solution.py:16
  (113 shorter events, 30.2 us)
Async XLA Ops:
  1.8 9.7 %collective-permute-start.2 = (bf16[128,256]{1,0:T(8,128)(2,1)S(1)}, bf16[128,256]{1,0:T(8,128)(2,1)S(1)}, u32[]{:S(2)}, u32[]{:S(2)}) collective-permute-start(bf16[128,256]{1,0:T(8,128)(2,1)S(1)} %get-tuple-element.53), channel_id=1, source_target_pairs={{0,12},{4,8},{8,4},{12,0},{1,13},{5,9},{9,5},{13,1},{2,14},{6,10},... | collective-permute-start | bytes 196616 | tf_op jit(solution)/shard_map/ppermute | solution.py:16
  5.7 5.8 %collective-permute-start.1 = (bf16[128,256]{1,0:T(8,128)(2,1)S(1)}, bf16[128,256]{1,0:T(8,128)(2,1)}, u32[]{:S(2)}, u32[]{:S(2)}) collective-permute-start(bf16[128,256]{1,0:T(8,128)(2,1)S(1)} %get-tuple-element.53), channel_id=1, source_target_pairs={{0,8},{4,12},{8,0},{12,4},{1,9},{5,13},{9,1},{13,5},{2,10},{6,14},... | collective-permute-start | bytes 196616 | tf_op jit(solution)/shard_map/ppermute | solution.py:16
  6.2 5.3 %collective-permute-start = (bf16[128,256]{1,0:T(8,128)(2,1)S(1)}, bf16[128,256]{1,0:T(8,128)(2,1)}, u32[]{:S(2)}, u32[]{:S(2)}) collective-permute-start(bf16[128,256]{1,0:T(8,128)(2,1)S(1)} %get-tuple-element.53), channel_id=1, source_target_pairs={{0,4},{4,0},{8,12},{12,8},{1,5},{5,1},{9,13},{13,9},{2,6},{6,2},{1... | collective-permute-start | bytes 196616 | tf_op jit(solution)/shard_map/ppermute | solution.py:16
  13.2 8.1 %collective-permute-start.5 = (bf16[128,256]{1,0:T(8,128)(2,1)}, bf16[128,256]{1,0:T(8,128)(2,1)S(1)}, u32[]{:S(2)}, u32[]{:S(2)}) collective-permute-start(bf16[128,256]{1,0:T(8,128)(2,1)} %convolution_convert_fusion.3), channel_id=1, source_target_pairs={{0,3},{1,2},{2,1},{3,0},{4,7},{5,6},{6,5},{7,4},{8,11},{9,10},{10,... | collective-permute-start | bytes 196616 | tf_op jit(solution)/shard_map/ppermute | solution.py:16
  19.0 5.4 %collective-permute-start.4 = (bf16[128,256]{1,0:T(8,128)(2,1)}, bf16[128,256]{1,0:T(8,128)(2,1)S(1)}, u32[]{:S(2)}, u32[]{:S(2)}) collective-permute-start(bf16[128,256]{1,0:T(8,128)(2,1)} %convolution_convert_fusion.4), channel_id=1, source_target_pairs={{0,2},{1,3},{2,0},{3,1},{4,6},{5,7},{6,4},{7,5},{8,10},{9,11},{10,... | collective-permute-start | bytes 196616 | tf_op jit(solution)/shard_map/ppermute | solution.py:16
  20.1 5.0 %collective-permute-start.3 = (bf16[128,256]{1,0:T(8,128)(2,1)S(1)}, bf16[128,256]{1,0:T(8,128)(2,1)S(1)}, u32[]{:S(2)}, u32[]{:S(2)}) collective-permute-start(bf16[128,256]{1,0:T(8,128)(2,1)S(1)} %convolution_convert_fusion.5), channel_id=1, source_target_pairs={{0,1},{1,0},{2,3},{3,2},{4,5},{5,4},{6,7},{7,6},{8,9},{9,8},{10,11... | collective-permute-start | bytes 196616 | tf_op jit(solution)/shard_map/ppermute | solution.py:16
  26.4 5.2 %collective-permute-start.8 = (bf16[128,256]{1,0:T(8,128)(2,1)S(1)}, bf16[128,256]{1,0:T(8,128)(2,1)S(1)}, u32[]{:S(2)}, u32[]{:S(2)}) collective-permute-start(bf16[128,256]{1,0:T(8,128)(2,1)S(1)} %get-tuple-element.55), channel_id=1, source_target_pairs={{0,12},{4,8},{8,4},{12,0},{1,13},{5,9},{9,5},{13,1},{2,14},{6,10},... | collective-permute-start | bytes 196616 | tf_op jit(solution)/shard_map/ppermute | solution.py:16
  28.9 4.3 %collective-permute-start.7 = (bf16[128,256]{1,0:T(8,128)(2,1)S(1)}, bf16[128,256]{1,0:T(8,128)(2,1)S(1)}, u32[]{:S(2)}, u32[]{:S(2)}) collective-permute-start(bf16[128,256]{1,0:T(8,128)(2,1)S(1)} %get-tuple-element.55), channel_id=1, source_target_pairs={{0,8},{4,12},{8,0},{12,4},{1,9},{5,13},{9,1},{13,5},{2,10},{6,14},... | collective-permute-start | bytes 196616 | tf_op jit(solution)/shard_map/ppermute | solution.py:16
  29.5 4.3 %collective-permute-start.6 = (bf16[128,256]{1,0:T(8,128)(2,1)S(1)}, bf16[128,256]{1,0:T(8,128)(2,1)S(1)}, u32[]{:S(2)}, u32[]{:S(2)}) collective-permute-start(bf16[128,256]{1,0:T(8,128)(2,1)S(1)} %get-tuple-element.55), channel_id=1, source_target_pairs={{0,4},{4,0},{8,12},{12,8},{1,5},{5,1},{9,13},{13,9},{2,6},{6,2},{1... | collective-permute-start | bytes 196616 | tf_op jit(solution)/shard_map/ppermute | solution.py:16
  35.6 5.9 %collective-permute-start.12 = (bf16[128,128]{1,0:T(8,128)(2,1)S(1)}, bf16[128,128]{1,0:T(8,128)(2,1)S(1)}, u32[]{:S(2)}, u32[]{:S(2)}) collective-permute-start(bf16[128,128]{1,0:T(8,128)(2,1)S(1)} %get-tuple-element.50), channel_id=1, source_target_pairs={{0,3},{1,2},{2,1},{3,0},{4,7},{5,6},{6,5},{7,4},{8,11},{9,10},{10,... | collective-permute-start | bytes 98312 | tf_op jit(solution)/shard_map/ppermute | solution.py:16
  37.4 4.9 %collective-permute-start.11 = (bf16[128,128]{1,0:T(8,128)(2,1)S(1)}, bf16[128,128]{1,0:T(8,128)(2,1)S(1)}, u32[]{:S(2)}, u32[]{:S(2)}) collective-permute-start(bf16[128,128]{1,0:T(8,128)(2,1)S(1)} %get-tuple-element.51), channel_id=1, source_target_pairs={{0,2},{1,3},{2,0},{3,1},{4,6},{5,7},{6,4},{7,5},{8,10},{9,11},{10,... | collective-permute-start | bytes 98312 | tf_op jit(solution)/shard_map/ppermute | solution.py:16
  38.0 4.3 %collective-permute-start.10 = (bf16[128,128]{1,0:T(8,128)(2,1)S(1)}, bf16[128,128]{1,0:T(8,128)(2,1)S(1)}, u32[]{:S(2)}, u32[]{:S(2)}) collective-permute-start(bf16[128,128]{1,0:T(8,128)(2,1)S(1)} %get-tuple-element.49), channel_id=1, source_target_pairs={{0,1},{1,0},{2,3},{3,2},{4,5},{5,4},{6,7},{7,6},{8,9},{9,8},{10,11... | collective-permute-start | bytes 98312 | tf_op jit(solution)/shard_map/ppermute | solution.py:16
  44.1 6.1 %collective-permute-start.15 = (bf16[128,128]{0,1:T(8,128)(2,1)S(1)}, bf16[128,128]{0,1:T(8,128)(2,1)S(1)}, u32[]{:S(2)}, u32[]{:S(2)}) collective-permute-start(bf16[128,128]{0,1:T(8,128)(2,1)S(1)} %get-tuple-element.52), channel_id=1, source_target_pairs={{0,3},{1,2},{2,1},{3,0},{4,7},{5,6},{6,5},{7,4},{8,11},{9,10},{10,... | collective-permute-start | bytes 98312 | tf_op jit(solution)/shard_map/ppermute | solution.py:16
  46.8 4.8 %collective-permute-start.14 = (bf16[128,128]{0,1:T(8,128)(2,1)S(1)}, bf16[128,128]{0,1:T(8,128)(2,1)S(1)}, u32[]{:S(2)}, u32[]{:S(2)}) collective-permute-start(bf16[128,128]{0,1:T(8,128)(2,1)S(1)} %get-tuple-element.52), channel_id=1, source_target_pairs={{0,2},{1,3},{2,0},{3,1},{4,6},{5,7},{6,4},{7,5},{8,10},{9,11},{10,... | collective-permute-start | bytes 98312 | tf_op jit(solution)/shard_map/ppermute | solution.py:16
  47.3 4.3 %collective-permute-start.13 = (bf16[128,128]{0,1:T(8,128)(2,1)S(1)}, bf16[128,128]{0,1:T(8,128)(2,1)S(1)}, u32[]{:S(2)}, u32[]{:S(2)}) collective-permute-start(bf16[128,128]{0,1:T(8,128)(2,1)S(1)} %get-tuple-element.52), channel_id=1, source_target_pairs={{0,1},{1,0},{2,3},{3,2},{4,5},{5,4},{6,7},{7,6},{8,9},{9,8},{10,11... | collective-permute-start | bytes 98312 | tf_op jit(solution)/shard_map/ppermute | solution.py:16
  54.0 5.3 %collective-permute-start.19 = (bf16[128,256]{1,0:T(8,128)(2,1)S(1)}, bf16[128,256]{1,0:T(8,128)(2,1)S(1)}, u32[]{:S(2)}, u32[]{:S(2)}) collective-permute-start(bf16[128,256]{1,0:T(8,128)(2,1)S(1)} %convolution_convert_fusion), channel_id=1, source_target_pairs={{0,12},{4,8},{8,4},{12,0},{1,13},{5,9},{9,5},{13,1},{2,14},{6,10},... | collective-permute-start | bytes 196616 | tf_op jit(solution)/shard_map/ppermute | solution.py:16
  55.6 5.0 %collective-permute-start.18 = (bf16[128,256]{1,0:T(8,128)(2,1)S(1)}, bf16[128,256]{1,0:T(8,128)(2,1)S(1)}, u32[]{:S(2)}, u32[]{:S(2)}) collective-permute-start(bf16[128,256]{1,0:T(8,128)(2,1)S(1)} %convolution_convert_fusion.1), channel_id=1, source_target_pairs={{0,8},{4,12},{8,0},{12,4},{1,9},{5,13},{9,1},{13,5},{2,10},{6,14},... | collective-permute-start | bytes 196616 | tf_op jit(solution)/shard_map/ppermute | solution.py:16
  56.1 4.5 %collective-permute-start.17 = (bf16[128,256]{1,0:T(8,128)(2,1)S(1)}, bf16[128,256]{1,0:T(8,128)(2,1)S(1)}, u32[]{:S(2)}, u32[]{:S(2)}) collective-permute-start(bf16[128,256]{1,0:T(8,128)(2,1)S(1)} %convolution_convert_fusion.2), channel_id=1, source_target_pairs={{0,4},{4,0},{8,12},{12,8},{1,5},{5,1},{9,13},{13,9},{2,6},{6,2},{1... | collective-permute-start | bytes 196616 | tf_op jit(solution)/shard_map/ppermute | solution.py:16
  61.8 6.8 %collective-permute-start.22 = (bf16[128,256]{1,0:T(8,128)(2,1)S(1)}, bf16[128,256]{1,0:T(8,128)(2,1)S(1)}, u32[]{:S(2)}, u32[]{:S(2)}) collective-permute-start(bf16[128,256]{1,0:T(8,128)(2,1)S(1)} %get-tuple-element.57), channel_id=1, source_target_pairs={{0,3},{1,2},{2,1},{3,0},{4,7},{5,6},{6,5},{7,4},{8,11},{9,10},{10,... | collective-permute-start | bytes 196616 | tf_op jit(solution)/shard_map/ppermute | solution.py:16
  63.6 7.0 %collective-permute-start.21 = (bf16[128,256]{1,0:T(8,128)(2,1)S(1)}, bf16[128,256]{1,0:T(8,128)(2,1)S(1)}, u32[]{:S(2)}, u32[]{:S(2)}) collective-permute-start(bf16[128,256]{1,0:T(8,128)(2,1)S(1)} %get-tuple-element.57), channel_id=1, source_target_pairs={{0,2},{1,3},{2,0},{3,1},{4,6},{5,7},{6,4},{7,5},{8,10},{9,11},{10,... | collective-permute-start | bytes 196616 | tf_op jit(solution)/shard_map/ppermute | solution.py:16
  64.2 6.5 %collective-permute-start.20 = (bf16[128,256]{1,0:T(8,128)(2,1)S(1)}, bf16[128,256]{1,0:T(8,128)(2,1)S(1)}, u32[]{:S(2)}, u32[]{:S(2)}) collective-permute-start(bf16[128,256]{1,0:T(8,128)(2,1)S(1)} %get-tuple-element.57), channel_id=1, source_target_pairs={{0,1},{1,0},{2,3},{3,2},{4,5},{5,4},{6,7},{7,6},{8,9},{9,8},{10,11... | collective-permute-start | bytes 196616 | tf_op jit(solution)/shard_map/ppermute | solution.py:16
  70.9 5.3 %collective-permute-start.25 = (bf16[128,256]{1,0:T(8,128)(2,1)S(1)}, bf16[128,256]{1,0:T(8,128)(2,1)S(1)}, u32[]{:S(2)}, u32[]{:S(2)}) collective-permute-start(bf16[128,256]{1,0:T(8,128)(2,1)S(1)} %fusion.12), channel_id=1, source_target_pairs={{0,12},{4,8},{8,4},{12,0},{1,13},{5,9},{9,5},{13,1},{2,14},{6,10},... | collective-permute-start | bytes 196616 | tf_op jit(solution)/shard_map/ppermute | solution.py:16
  73.0 4.3 %collective-permute-start.24 = (bf16[128,256]{1,0:T(8,128)(2,1)S(1)}, bf16[128,256]{1,0:T(8,128)(2,1)S(1)}, u32[]{:S(2)}, u32[]{:S(2)}) collective-permute-start(bf16[128,256]{1,0:T(8,128)(2,1)S(1)} %fusion.11), channel_id=1, source_target_pairs={{0,8},{4,12},{8,0},{12,4},{1,9},{5,13},{9,1},{13,5},{2,10},{6,14},... | collective-permute-start | bytes 196616 | tf_op jit(solution)/shard_map/ppermute | solution.py:16
  73.3 4.3 %collective-permute-start.23 = (bf16[128,256]{1,0:T(8,128)(2,1)S(1)}, bf16[128,256]{1,0:T(8,128)(2,1)S(1)}, u32[]{:S(2)}, u32[]{:S(2)}) collective-permute-start(bf16[128,256]{1,0:T(8,128)(2,1)S(1)} %fusion.10), channel_id=1, source_target_pairs={{0,4},{4,0},{8,12},{12,8},{1,5},{5,1},{9,13},{13,9},{2,6},{6,2},{1... | collective-permute-start | bytes 196616 | tf_op jit(solution)/shard_map/ppermute | solution.py:16
  (13 other events, 52.2 us)

commit v2 on v1

v2 whole, which is shorter than its diff:
```python
import jax
import jax.numpy as jnp
from jax import lax
from jax.experimental import pallas as pl
from jax.experimental.pallas import tpu as pltpu
from jax.sharding import PartitionSpec as P

BF = jnp.bfloat16
F32 = jnp.float32
HI = lax.Precision.HIGHEST
VMEM = pl.BlockSpec(memory_space=pltpu.VMEM)


def is_direct(n):
    return n in (1, 2, 4)


def swap(values, axis, n, step):
    return lax.ppermute(values, axis, [(i, i ^ step) for i in range(n)])


def gather(values, axis, n):
    if is_direct(n):
        return [values] + [swap(values, axis, n, d) for d in range(1, n)]
    return [lax.all_gather(values, axis, axis=0, tiled=True)]


def scatter_sum(blocks, axis, n):
    if is_direct(n):
        return [blocks[0]] + [swap(blocks[d], axis, n, d) for d in range(1, n)]
    return [lax.psum_scatter(blocks[0], axis, scatter_dimension=0, tiled=True)]


def nbytes(shape, dtype):
    size = jnp.dtype(dtype).itemsize
    for extent in shape:
        size *= extent
    return size


def call(kernel, outs, args, scratch=(), flops=0):
    total = sum(nbytes(s, t) for s, t in list(outs) + list(scratch)) + sum(nbytes(a.shape, a.dtype) for a in args)
    return pl.pallas_call(
        kernel,
        out_shape=tuple(jax.ShapeDtypeStruct(s, t) for s, t in outs),
        in_specs=[VMEM] * len(args),
        out_specs=(VMEM,) * len(outs),
        scratch_shapes=[pltpu.VMEM(s, t) for s, t in scratch],
        compiler_params=pltpu.CompilerParams(vmem_limit_bytes=total + (6 << 20)),
        cost_estimate=pl.CostEstimate(flops=flops, bytes_accessed=total, transcendentals=0),
    )(*args)


def place(n, axis):
    if not is_direct(n):
        return lambda d: d
    me = lax.axis_index(axis)
    return lambda d: me ^ d


def rows(index, size):
    return pl.ds(pl.multiple_of(index * size, size), size)


def dot(a, b):
    return jnp.dot(a, b, preferred_element_type=F32)


def dot_t(a, b):
    return lax.dot_general(a, b, (((0,), (0,)), ((), ())), preferred_element_type=F32)


def apply_lower(inverse, right_side):
    return jnp.dot(inverse, right_side, precision=HI, preferred_element_type=F32)


def apply_upper(inverse, right_side):
    return lax.dot_general(
        inverse, right_side, (((0,), (0,)), ((), ())), precision=HI, preferred_element_type=F32
    )


def total_of(refs):
    total = refs[0][...].astype(F32)
    for ref in refs[1:]:
        total = total + ref[...].astype(F32)
    return total


def lay_out(pieces, buf, n, axis):
    if not is_direct(n):
        buf[...] = pieces[0][...]
        return
    at = place(n, axis)
    size = pieces[0].shape[0]
    for d, piece in enumerate(pieces):
        buf[rows(at(d), size), :] = piece[...]


def block_outs(n, size, cols):
    if is_direct(n):
        return [((size, cols), F32)] + [((size, cols), BF)] * (n - 1)
    return [((n * size, cols), F32)]


def emit_blocks(term, outs, n, axis):
    at = place(n, axis)
    if is_direct(n):
        for d in list(range(1, n)) + [0]:
            outs[d][...] = term(at(d)).astype(outs[d].dtype)
    else:
        size = outs[0].shape[0] // n
        for d in range(n):
            outs[0][pl.ds(d * size, size), :] = term(d)


def leaf_first(leaf_inv, leaf_rhs):
    count, width, cols = leaf_rhs.shape

    def kernel(inv_ref, rhs_ref, y_ref, yb_ref):
        for m in range(count):
            y = apply_lower(inv_ref[m], rhs_ref[m].astype(F32))
            y_ref[pl.ds(m * width, width), :] = y
            yb_ref[pl.ds(m * width, width), :] = y.astype(BF)

    shape = (count * width, cols)
    return call(kernel, [(shape, F32), (shape, BF)], [leaf_inv, leaf_rhs])


def forward_blocks(tiles, pieces, n_row, n_col, width):
    cols = pieces[0].shape[1]
    depth = tiles.shape[1]
    count = len(pieces)

    def kernel(*refs):
        tile_ref, piece_refs, outs = refs[0], refs[1 : 1 + count], refs[1 + count : -1]
        buf = refs[-1]
        lay_out(piece_refs, buf, n_row, "row")
        emit_blocks(lambda i: dot(tile_ref[rows(i, width), :], buf[...]), outs, n_col, "col")

    outs = block_outs(n_col, width, cols) + [((depth, cols), BF)]
    got = call(kernel, outs, [tiles, *pieces], flops=2 * tiles.shape[0] * depth * cols)
    return got[:-1], got[-1]


def plain_product(tiles, values, transposed):
    cols = values.shape[1]
    product = dot_t if transposed else dot

    def kernel(tile_ref, value_ref, out_ref):
        out_ref[...] = product(tile_ref[...], value_ref[...])

    shape = (tiles.shape[1] if transposed else tiles.shape[0], cols)
    return call(kernel, [(shape, F32)], [tiles, values], flops=2 * tiles.shape[0] * tiles.shape[1] * cols)[0]


def solve_forward(sums, right_side, inverse):
    count = len(sums)

    def kernel(*refs):
        rhs_ref, inv_ref, y_ref, yb_ref = refs[count:]
        y = apply_lower(inv_ref[...], rhs_ref[...].astype(F32) - total_of(refs[:count]))
        y_ref[...] = y
        yb_ref[...] = y.astype(BF)

    shape = right_side.shape
    return call(kernel, [(shape, F32), (shape, BF)], [*sums, right_side, inverse])


def top_halves(tiles, pieces, leaf_part, n_row):
    cols = pieces[0].shape[1]
    half = cols // 2
    count = len(pieces)

    def kernel(*refs):
        tile_ref, piece_refs = refs[0], refs[1 : 1 + count]
        part_ref, mine_ref, other_ref, buf = refs[1 + count :]
        lay_out(piece_refs, buf, n_row, "row")
        sec = lax.axis_index("sec")
        for out_ref, which in ((other_ref, 1 - sec), (mine_ref, sec)):
            columns = rows(which, half)
            out = part_ref[:, columns] + dot(tile_ref[...], buf[:, columns])
            out_ref[...] = out.astype(out_ref.dtype)

    shape = (tiles.shape[0], half)
    return call(
        kernel,
        [(shape, F32), (shape, F32)],
        [tiles, *pieces, leaf_part],
        scratch=[((tiles.shape[1], cols), BF)],
        flops=2 * tiles.shape[0] * tiles.shape[1] * cols,
    )


def add_sections(mine, other, n_col, width):
    half = mine.shape[1]

    def kernel(mine_ref, other_ref, *outs):
        emit_blocks(lambda i: mine_ref[rows(i, width), :] + other_ref[rows(i, width), :], outs, n_col, "col")

    return call(kernel, block_outs(n_col, width, half), [mine, other])


def solve_top(sums, right_side, inverse):
    count = len(sums)
    half = right_side.shape[1] // 2

    def kernel(*refs):
        rhs_ref, inv_ref, x_ref, xb_ref = refs[count:]
        mine = rhs_ref[:, rows(lax.axis_index("sec"), half)].astype(F32)
        y = apply_lower(inv_ref[...], mine - total_of(refs[:count]))
        x = apply_upper(inv_ref[...], y)
        x_ref[...] = x
        xb_ref[...] = x.astype(BF)

    shape = (right_side.shape[0], half)
    return call(kernel, [(shape, F32), (shape, BF)], [*sums, right_side, inverse])


def stack_pieces(pieces, n, axis):
    if not is_direct(n):
        return pieces[0]

    def kernel(*refs):
        lay_out(refs[:-1], refs[-1], n, axis)

    shape = (n * pieces[0].shape[0], pieces[0].shape[1])
    return call(kernel, [(shape, BF)], list(pieces))[0]


def join_halves(mine, other):
    half = mine.shape[1]

    def kernel(mine_ref, other_ref, out_ref):
        sec = lax.axis_index("sec")
        out_ref[:, rows(sec, half)] = mine_ref[...]
        out_ref[:, rows(1 - sec, half)] = other_ref[...]

    return call(kernel, [((mine.shape[0], 2 * half), mine.dtype)], [mine, other])[0]


def top_back_blocks(tiles, mine, other, n_row, width):
    half = mine.shape[1]

    def kernel(tile_ref, mine_ref, other_ref, *outs):
        buf = outs[-1]
        sec = lax.axis_index("sec")
        buf[:, rows(sec, half)] = mine_ref[...]
        buf[:, rows(1 - sec, half)] = other_ref[...]
        emit_blocks(lambda i: dot_t(tile_ref[:, rows(i, width)], buf[...]), outs[:-1], n_row, "row")

    outs = block_outs(n_row, width, 2 * half) + [((mine.shape[0], 2 * half), BF)]
    got = call(kernel, outs, [tiles, mine, other], flops=4 * tiles.shape[0] * tiles.shape[1] * half)
    return got[:-1], got[-1]


def back_blocks(tiles, pieces, top_part, n_row, n_col, span):
    cols = pieces[0].shape[1]
    count = len(pieces)

    def kernel(*refs):
        tile_ref, piece_refs, part_ref = refs[0], refs[1 : 1 + count], refs[1 + count]
        outs, buf = refs[2 + count : -1], refs[-1]
        lay_out(piece_refs, buf, n_col, "col")
        emit_blocks(
            lambda i: part_ref[rows(i, span), :] + dot_t(tile_ref[:, rows(i, span)], buf[...]),
            outs, n_row, "row",
        )

    return call(
        kernel,
        block_outs(n_row, span, cols),
        [tiles, *pieces, top_part],
        scratch=[((tiles.shape[0], cols), BF)],
        flops=2 * tiles.shape[0] * tiles.shape[1] * cols,
    )


def solve_back(sums, right_side, inverse):
    count = len(sums)
    blocks, width = inverse.shape[:2]
    shape = right_side.shape

    def kernel(*refs):
        y_ref, inv_ref, x_ref, xb_ref = refs[count:]
        rest = y_ref[...] - total_of(refs[:count])
        for m in range(blocks):
            x = apply_upper(inv_ref[m], rest[m * width : (m + 1) * width])
            x_ref[pl.ds(m * width, width), :] = x
            xb_ref[pl.ds(m * width, width), :] = x.astype(BF)

    return call(kernel, [(shape, F32), (shape, BF)], [*sums, right_side, inverse])


def solve_last(sums, right_side, inverse):
    count = len(sums)
    blocks, width = inverse.shape[:2]

    def kernel(*refs):
        y_ref, inv_ref, x_ref = refs[count:]
        rest = y_ref[...] - total_of(refs[:count])
        for m in range(blocks):
            x_ref[pl.ds(m * width, width), :] = apply_upper(inv_ref[m], rest[m * width : (m + 1) * width])

    return call(kernel, [(right_side.shape, F32)], [*sums, right_side, inverse])[0]


def make_body(n_row, n_col):
    def body(leaf_rhs, sep_rhs, top_rhs, leaf_inv, sep_inv, top_inv,
             sep_leaf, top_leaf, top_sep, sep_leaf_mask, top_leaf_mask, top_sep_mask):
        leaf_count, width, cols = leaf_rhs.shape[2], leaf_rhs.shape[4], leaf_rhs.shape[5]
        span = leaf_count * width

        def tiles(values, mask):
            masked = values * mask.astype(BF)[:, None, :, :, None]
            return masked.reshape(n_col * width, -1)

        leaf_y, leaf_yb = leaf_first(leaf_inv[0, 0, :, 0], leaf_rhs[0, 0, :, 0])
        sl = tiles(sep_leaf[0, 0, :, :, :, :, 0], sep_leaf_mask[0, 0, :, :, :, 0])
        blocks, leaf_col = forward_blocks(sl, gather(leaf_yb, "row", n_row), n_row, n_col, width)
        sums = scatter_sum(blocks, "col", n_col)
        top_leaf, top_sep, top_leaf_mask, top_sep_mask, leaf_col = lax.optimization_barrier(
            (top_leaf, top_sep, top_leaf_mask, top_sep_mask, leaf_col)
        )
        tl = tiles(top_leaf[0, 0, :, :, :, :, 0], top_leaf_mask[0, 0, :, :, :, 0])
        ts = tiles(top_sep[0, 0, :, :, :, None, 0], top_sep_mask[0, 0, :, :, None, 0])
        leaf_part = plain_product(tl, leaf_col, False)
        sep_y, sep_yb = solve_forward(sums, sep_rhs[0, 0, 0], sep_inv[0, 0, 0])
        mine, other = top_halves(ts, gather(sep_yb, "row", n_row), leaf_part, n_row)
        blocks = add_sections(mine, swap(other, "sec", 2, 1), n_col, width)
        sums = scatter_sum(blocks, "col", n_col)
        top_xh, top_xhb = solve_top(sums, top_rhs[0, 0], top_inv[0, 0])
        top_stack = stack_pieces(gather(top_xhb, "col", n_col), n_col, "col")
        blocks, top_row = top_back_blocks(ts, top_stack, swap(top_stack, "sec", 2, 1), n_row, width)
        sums = scatter_sum(blocks, "row", n_row)
        top_part = plain_product(tl, top_row, True)
        top_x = join_halves(top_xh, swap(top_xh, "sec", 2, 1))
        sep_x, sep_xb = solve_back(sums, sep_y, sep_inv[0, 0])
        pieces = gather(sep_xb, "col", n_col)
        sums = scatter_sum(back_blocks(sl, pieces, top_part, n_row, n_col, span), "row", n_row)
        leaf_x = solve_last(sums, leaf_y, leaf_inv[0, 0, :, 0])
        return (
            leaf_x.reshape(1, 1, leaf_count, 1, width, cols),
            sep_x[None, None, None],
            top_x[None, None],
        )

    return body


def solution(mesh):
    in_specs = (
        P("sec", "row", None, "col", None, None),
        P("sec", "row", "col", None, None),
        P("row", "col", None, None),
        P("sec", "row", None, "col", None, None),
        P("sec", "row", "col", None, None),
        P("row", "col", None, None),
        P("sec", "row", None, None, None, None, "col", None),
        P("sec", "row", None, None, None, None, "col", None),
        P("sec", "row", None, None, None, "col", None),
        P("sec", "row", None, None, None, "col"),
        P("sec", "row", None, None, None, "col"),
        P("sec", "row", None, None, "col"),
    )
    out_specs = (
        P("sec", "row", None, "col", None, None),
        P("sec", "row", "col", None, None),
        P("row", "col", None, None),
    )
    body = make_body(mesh.shape["row"], mesh.shape["col"])
    return jax.shard_map(body, mesh=mesh, in_specs=in_specs, out_specs=out_specs, check_vma=False)
```

time: 80.2 us -> 73.5 us (0.916)
  matrix products: 13.1 us -> 0 us
  Pallas kernels: 0 us -> 5.89 us
  waiting for transfers between devices: 23.9 us -> 29.7 us
  local copies, waits for them, and re-layouts: 5.98 us -> 3.22 us
  other arithmetic: 1.98 us -> 0.38 us
    dot_general x24 -> x0, matrix products: 13.1 us -> none  [the longest x6 7.12 us: dot(): return jnp.dot(a, b, preferred_element_type=F32)]
    pallas_call x0 -> x14, Pallas kernels: none -> 5.89 us  [call(): pl.pallas_call(kernel, out_shape=tuple((jax.ShapeDtypeStruct(s, t) for s,...]
    ppermute x27, waiting for transfers between devices: 23.9 us -> 29.7 us  [swap(): return lax.ppermute(values, axis, [(i, i ^ step) for i in range(n)])]
    unnamed x25 -> x29, local copies, waits for them, and re-layouts: 4.14 us -> 2.6 us
    mul x3, other arithmetic: 1.42 us -> 0.37 us  [tiles(): masked = values * mask.astype(BF)[:, None, :, :, None]]
    concatenate x5 -> x0, local copies, waits for them, and re-layouts: 0.94 us -> none  [partner_order(): jnp.concatenate([lax.dynamic_slice_in_dim(values, me ^ d, 1, dim) for d i...]
  transfers between devices with their start and end apart: 27 -> 27, of which waited for: 21 -> 22; matrix products, arithmetic and copies ran while one was open for 12% -> 1% of each run, Pallas kernels for 0% -> 2%
where the time goes in v2:
time: 73.5 us; the launch traced here: 73.2 us
  starting transfers between devices  33.1 us (45%)
  waiting for transfers between devices  29.7 us (40%)
  Pallas kernels  5.89 us (8%)
  local copies, waits for them, and re-layouts  3.22 us (4%)
  between operations  0.88 us (1%)
    ppermute x27, starting transfers between devices, swap(): return lax.ppermute(values, axis, [(i, i ^ step) for i in range(n)])  33.1 us
    ppermute x27, waiting for transfers between devices, swap(): return lax.ppermute(values, axis, [(i, i ^ step) for i in range(n)])  29.7 us
    pallas_call x14, Pallas kernels, call(): pl.pallas_call(kernel, out_shape=tuple((jax.ShapeDtypeStruct(s, t) for s,...  5.89 us
    unnamed x29, local copies, waits for them, and re-layouts  2.6 us
  transfers between devices with their start and end apart: 27, of which 22 were waited for; matrix products, arithmetic and copies ran while one was open for 1% of the time, Pallas kernels for 2%

profile of v2, /device:TPU:0, one launch (start us, length us, event | category | flops | bytes accessed | tf_op | source)
XLA Modules:
  0.0 73.2 jit_solution(11151033508075448564)
XLA Ops:
  2.6 4.0 %collective-permute-start.2 = (bf16[128,256]{1,0:T(8,128)(2,1)S(1)}, bf16[128,256]{1,0:T(8,128)(2,1)S(1)}, u32[]{:S(2)}, u32[]{:S(2)}) collective-permute-start(bf16[128,256]{1,0:T(8,128)(2,1)S(1)} %get-tuple-element.36.refs_1_), channel_id=1, source_target_pairs={{0,12},{4,8},{8,4},{12,0},{1,13},{5,9},{9,5},{13,1},{2,14},{6,10},... | collective-permute-start | bytes 196616 | tf_op jit(solution)/shard_map/ppermute | solution.py:19
  8.8 2.0 %collective-permute-done.1.refs_3_ = bf16[128,256]{1,0:T(8,128)(2,1)S(1)} collective-permute-done((bf16[128,256]{1,0:T(8,128)(2,1)S(1)}, bf16[128,256]{1,0:T(8,128)(2,1)S(1)}, u32[]{:S(2)}, u32[]{:S(2)}) %collective-permute-start.1) | collective-permute-done | bytes 65568 | tf_op jit(solution)/shard_map/ppermute | solution.py:19
  12.0 1.6 %collective-permute-start.3 = (bf16[128,256]{1,0:T(8,128)(2,1)S(1)}, bf16[128,256]{1,0:T(8,128)(2,1)S(1)}, u32[]{:S(2)}, u32[]{:S(2)}) collective-permute-start(bf16[128,256]{1,0:T(8,128)(2,1)S(1)} %get-tuple-element.41), channel_id=1, source_target_pairs={{0,1},{1,0},{2,3},{3,2},{4,5},{5,4},{6,7},{7,6},{8,9},{9,8},{10,11... | collective-permute-start | bytes 196616 | tf_op jit(solution)/shard_map/ppermute | solution.py:19
  13.7 2.6 %collective-permute-start.4 = (bf16[128,256]{1,0:T(8,128)(2,1)S(1)}, bf16[128,256]{1,0:T(8,128)(2,1)S(1)}, u32[]{:S(2)}, u32[]{:S(2)}) collective-permute-start(bf16[128,256]{1,0:T(8,128)(2,1)S(1)} %get-tuple-element.42), channel_id=1, source_target_pairs={{0,2},{1,3},{2,0},{3,1},{4,6},{5,7},{6,4},{7,5},{8,10},{9,11},{10,... | collective-permute-start | bytes 196616 | tf_op jit(solution)/shard_map/ppermute | solution.py:19
  17.4 2.8 %collective-permute-done.4.refs_2_ = bf16[128,256]{1,0:T(8,128)(2,1)S(1)} collective-permute-done((bf16[128,256]{1,0:T(8,128)(2,1)S(1)}, bf16[128,256]{1,0:T(8,128)(2,1)S(1)}, u32[]{:S(2)}, u32[]{:S(2)}) %collective-permute-start.4) | collective-permute-done | bytes 65568 | tf_op jit(solution)/shard_map/ppermute | solution.py:19
  20.2 2.1 %collective-permute-done.5.refs_3_ = bf16[128,256]{1,0:T(8,128)(2,1)S(1)} collective-permute-done((bf16[128,256]{1,0:T(8,128)(2,1)S(1)}, bf16[128,256]{1,0:T(8,128)(2,1)S(1)}, u32[]{:S(2)}, u32[]{:S(2)}) %collective-permute-start.5) | collective-permute-done | bytes 65568 | tf_op jit(solution)/shard_map/ppermute | solution.py:19
  22.6 1.5 %collective-permute-start.8 = (bf16[128,256]{1,0:T(8,128)(2,1)S(1)}, bf16[128,256]{1,0:T(8,128)(2,1)S(1)}, u32[]{:S(2)}, u32[]{:S(2)}) collective-permute-start(bf16[128,256]{1,0:T(8,128)(2,1)S(1)} %get-tuple-element.44.refs_1_), channel_id=1, source_target_pairs={{0,12},{4,8},{8,4},{12,0},{1,13},{5,9},{9,5},{13,1},{2,14},{6,10},... | collective-permute-start | bytes 196616 | tf_op jit(solution)/shard_map/ppermute | solution.py:19
  24.7 1.5 %collective-permute-start.6 = (bf16[128,256]{1,0:T(8,128)(2,1)S(1)}, bf16[128,256]{1,0:T(8,128)(2,1)S(1)}, u32[]{:S(2)}, u32[]{:S(2)}) collective-permute-start(bf16[128,256]{1,0:T(8,128)(2,1)S(1)} %get-tuple-element.44.refs_1_), channel_id=1, source_target_pairs={{0,4},{4,0},{8,12},{12,8},{1,5},{5,1},{9,13},{13,9},{2,6},{6,2},{1... | collective-permute-start | bytes 196616 | tf_op jit(solution)/shard_map/ppermute | solution.py:19
  29.5 1.5 %collective-permute-done.9.other_ref = f32[512,128]{1,0:T(8,128)S(1)} collective-permute-done((f32[512,128]{1,0:T(8,128)S(1)}, f32[512,128]{1,0:T(8,128)S(1)}, u32[]{:S(2)}, u32[]{:S(2)}) %collective-permute-start.9) | collective-permute-done | bytes 262176 | tf_op jit(solution)/shard_map/ppermute | solution.py:19
  31.1 1.7 %collective-permute-start.11 = (bf16[128,128]{1,0:T(8,128)(2,1)S(1)}, bf16[128,128]{1,0:T(8,128)(2,1)S(1)}, u32[]{:S(2)}, u32[]{:S(2)}) collective-permute-start(bf16[128,128]{1,0:T(8,128)(2,1)S(1)} %get-tuple-element.52), channel_id=1, source_target_pairs={{0,2},{1,3},{2,0},{3,1},{4,6},{5,7},{6,4},{7,5},{8,10},{9,11},{10,... | collective-permute-start | bytes 98312 | tf_op jit(solution)/shard_map/ppermute | solution.py:19
  32.8 2.7 %collective-permute-start.12 = (bf16[128,128]{1,0:T(8,128)(2,1)S(1)}, bf16[128,128]{1,0:T(8,128)(2,1)S(1)}, u32[]{:S(2)}, u32[]{:S(2)}) collective-permute-start(bf16[128,128]{1,0:T(8,128)(2,1)S(1)} %get-tuple-element.53), channel_id=1, source_target_pairs={{0,3},{1,2},{2,1},{3,0},{4,7},{5,6},{6,5},{7,4},{8,11},{9,10},{10,... | collective-permute-start | bytes 98312 | tf_op jit(solution)/shard_map/ppermute | solution.py:19
  36.7 1.9 %collective-permute-done.12.refs_3_ = bf16[128,128]{1,0:T(8,128)(2,1)S(1)} collective-permute-done((bf16[128,128]{1,0:T(8,128)(2,1)S(1)}, bf16[128,128]{1,0:T(8,128)(2,1)S(1)}, u32[]{:S(2)}, u32[]{:S(2)}) %collective-permute-start.12) | collective-permute-done | bytes 32800 | tf_op jit(solution)/shard_map/ppermute | solution.py:19
  39.0 2.8 %collective-permute-start.15 = (bf16[128,128]{1,0:T(8,128)(2,1)S(1)}, bf16[128,128]{1,0:T(8,128)(2,1)S(1)}, u32[]{:S(2)}, u32[]{:S(2)}) collective-permute-start(bf16[128,128]{1,0:T(8,128)(2,1)S(1)} %get-tuple-element.54.refs_0_), channel_id=1, source_target_pairs={{0,3},{1,2},{2,1},{3,0},{4,7},{5,6},{6,5},{7,4},{8,11},{9,10},{10,... | collective-permute-start | bytes 98312 | tf_op jit(solution)/shard_map/ppermute | solution.py:19
  41.8 1.7 %collective-permute-start.13 = (bf16[128,128]{1,0:T(8,128)(2,1)S(1)}, bf16[128,128]{1,0:T(8,128)(2,1)S(1)}, u32[]{:S(2)}, u32[]{:S(2)}) collective-permute-start(bf16[128,128]{1,0:T(8,128)(2,1)S(1)} %get-tuple-element.54.refs_0_), channel_id=1, source_target_pairs={{0,1},{1,0},{2,3},{3,2},{4,5},{5,4},{6,7},{7,6},{8,9},{9,8},{10,11... | collective-permute-start | bytes 98312 | tf_op jit(solution)/shard_map/ppermute | solution.py:19
  43.5 1.5 %collective-permute-done.15.refs_3_ = bf16[128,128]{1,0:T(8,128)(2,1)S(1)} collective-permute-done((bf16[128,128]{1,0:T(8,128)(2,1)S(1)}, bf16[128,128]{1,0:T(8,128)(2,1)S(1)}, u32[]{:S(2)}, u32[]{:S(2)}) %collective-permute-start.15) | collective-permute-done | bytes 32800 | tf_op jit(solution)/shard_map/ppermute | solution.py:19
  45.0 1.6 %collective-permute-done.14.refs_2_ = bf16[128,128]{1,0:T(8,128)(2,1)S(1)} collective-permute-done((bf16[128,128]{1,0:T(8,128)(2,1)S(1)}, bf16[128,128]{1,0:T(8,128)(2,1)S(1)}, u32[]{:S(2)}, u32[]{:S(2)}) %collective-permute-start.14) | collective-permute-done | bytes 32800 | tf_op jit(solution)/shard_map/ppermute | solution.py:19
  48.5 1.5 %collective-permute-start.17 = (bf16[128,256]{1,0:T(8,128)(2,1)S(1)}, bf16[128,256]{1,0:T(8,128)(2,1)S(1)}, u32[]{:S(2)}, u32[]{:S(2)}) collective-permute-start(bf16[128,256]{1,0:T(8,128)(2,1)S(1)} %get-tuple-element.56), channel_id=1, source_target_pairs={{0,4},{4,0},{8,12},{12,8},{1,5},{5,1},{9,13},{13,9},{2,6},{6,2},{1... | collective-permute-start | bytes 196616 | tf_op jit(solution)/shard_map/ppermute | solution.py:19
  50.0 1.5 %collective-permute-start.18 = (bf16[128,256]{1,0:T(8,128)(2,1)S(1)}, bf16[128,256]{1,0:T(8,128)(2,1)S(1)}, u32[]{:S(2)}, u32[]{:S(2)}) collective-permute-start(bf16[128,256]{1,0:T(8,128)(2,1)S(1)} %get-tuple-element.57), channel_id=1, source_target_pairs={{0,8},{4,12},{8,0},{12,4},{1,9},{5,13},{9,1},{13,5},{2,10},{6,14},... | collective-permute-start | bytes 196616 | tf_op jit(solution)/shard_map/ppermute | solution.py:19
  54.3 2.4 %collective-permute-done.19.refs_3_ = bf16[128,256]{1,0:T(8,128)(2,1)S(1)} collective-permute-done((bf16[128,256]{1,0:T(8,128)(2,1)S(1)}, bf16[128,256]{1,0:T(8,128)(2,1)S(1)}, u32[]{:S(2)}, u32[]{:S(2)}) %collective-permute-start.19) | collective-permute-done | bytes 65568 | tf_op jit(solution)/shard_map/ppermute | solution.py:19
  57.7 1.6 %collective-permute-start.22 = (bf16[128,256]{1,0:T(8,128)(2,1)S(1)}, bf16[128,256]{1,0:T(8,128)(2,1)S(1)}, u32[]{:S(2)}, u32[]{:S(2)}) collective-permute-start(bf16[128,256]{1,0:T(8,128)(2,1)S(1)} %get-tuple-element.60.refs_1_), channel_id=1, source_target_pairs={{0,3},{1,2},{2,1},{3,0},{4,7},{5,6},{6,5},{7,4},{8,11},{9,10},{10,... | collective-permute-start | bytes 196616 | tf_op jit(solution)/shard_map/ppermute | solution.py:19
  59.7 2.4 %collective-permute-start.20 = (bf16[128,256]{1,0:T(8,128)(2,1)S(1)}, bf16[128,256]{1,0:T(8,128)(2,1)S(1)}, u32[]{:S(2)}, u32[]{:S(2)}) collective-permute-start(bf16[128,256]{1,0:T(8,128)(2,1)S(1)} %get-tuple-element.60.refs_1_), channel_id=1, source_target_pairs={{0,1},{1,0},{2,3},{3,2},{4,5},{5,4},{6,7},{7,6},{8,9},{9,8},{10,11... | collective-permute-start | bytes 196616 | tf_op jit(solution)/shard_map/ppermute | solution.py:19
  63.9 1.6 %collective-permute-done.21.refs_3_ = bf16[128,256]{1,0:T(8,128)(2,1)S(1)} collective-permute-done((bf16[128,256]{1,0:T(8,128)(2,1)S(1)}, bf16[128,256]{1,0:T(8,128)(2,1)S(1)}, u32[]{:S(2)}, u32[]{:S(2)}) %collective-permute-start.21) | collective-permute-done | bytes 65568 | tf_op jit(solution)/shard_map/ppermute | solution.py:19
  67.0 2.3 %collective-permute-start.25 = (bf16[128,256]{1,0:T(8,128)(2,1)S(1)}, bf16[128,256]{1,0:T(8,128)(2,1)S(1)}, u32[]{:S(2)}, u32[]{:S(2)}) collective-permute-start(bf16[128,256]{1,0:T(8,128)(2,1)S(1)} %get-tuple-element.65), channel_id=1, source_target_pairs={{0,12},{4,8},{8,4},{12,0},{1,13},{5,9},{9,5},{13,1},{2,14},{6,10},... | collective-permute-start | bytes 196616 | tf_op jit(solution)/shard_map/ppermute | solution.py:19
  70.7 1.5 %collective-permute-done.25.refs_3_ = bf16[128,256]{1,0:T(8,128)(2,1)S(1)} collective-permute-done((bf16[128,256]{1,0:T(8,128)(2,1)S(1)}, bf16[128,256]{1,0:T(8,128)(2,1)S(1)}, u32[]{:S(2)}, u32[]{:S(2)}) %collective-permute-start.25) | collective-permute-done | bytes 65568 | tf_op jit(solution)/shard_map/ppermute | solution.py:19
  (82 shorter events, 24.0 us)
Async XLA Ops:
  2.6 6.2 %collective-permute-start.2 = (bf16[128,256]{1,0:T(8,128)(2,1)S(1)}, bf16[128,256]{1,0:T(8,128)(2,1)S(1)}, u32[]{:S(2)}, u32[]{:S(2)}) collective-permute-start(bf16[128,256]{1,0:T(8,128)(2,1)S(1)} %get-tuple-element.36.refs_1_), channel_id=1, source_target_pairs={{0,12},{4,8},{8,4},{12,0},{1,13},{5,9},{9,5},{13,1},{2,14},{6,10},... | collective-permute-start | bytes 196616 | tf_op jit(solution)/shard_map/ppermute | solution.py:19
  6.5 4.3 %collective-permute-start.1 = (bf16[128,256]{1,0:T(8,128)(2,1)S(1)}, bf16[128,256]{1,0:T(8,128)(2,1)S(1)}, u32[]{:S(2)}, u32[]{:S(2)}) collective-permute-start(bf16[128,256]{1,0:T(8,128)(2,1)S(1)} %get-tuple-element.36.refs_1_), channel_id=1, source_target_pairs={{0,8},{4,12},{8,0},{12,4},{1,9},{5,13},{9,1},{13,5},{2,10},{6,14},... | collective-permute-start | bytes 196616 | tf_op jit(solution)/shard_map/ppermute | solution.py:19
  7.1 4.3 %collective-permute-start = (bf16[128,256]{1,0:T(8,128)(2,1)S(1)}, bf16[128,256]{1,0:T(8,128)(2,1)S(1)}, u32[]{:S(2)}, u32[]{:S(2)}) collective-permute-start(bf16[128,256]{1,0:T(8,128)(2,1)S(1)} %get-tuple-element.36.refs_1_), channel_id=1, source_target_pairs={{0,4},{4,0},{8,12},{12,8},{1,5},{5,1},{9,13},{13,9},{2,6},{6,2},{1... | collective-permute-start | bytes 196616 | tf_op jit(solution)/shard_map/ppermute | solution.py:19
  12.0 5.4 %collective-permute-start.3 = (bf16[128,256]{1,0:T(8,128)(2,1)S(1)}, bf16[128,256]{1,0:T(8,128)(2,1)S(1)}, u32[]{:S(2)}, u32[]{:S(2)}) collective-permute-start(bf16[128,256]{1,0:T(8,128)(2,1)S(1)} %get-tuple-element.41), channel_id=1, source_target_pairs={{0,1},{1,0},{2,3},{3,2},{4,5},{5,4},{6,7},{7,6},{8,9},{9,8},{10,11... | collective-permute-start | bytes 196616 | tf_op jit(solution)/shard_map/ppermute | solution.py:19
  13.7 6.6 %collective-permute-start.4 = (bf16[128,256]{1,0:T(8,128)(2,1)S(1)}, bf16[128,256]{1,0:T(8,128)(2,1)S(1)}, u32[]{:S(2)}, u32[]{:S(2)}) collective-permute-start(bf16[128,256]{1,0:T(8,128)(2,1)S(1)} %get-tuple-element.42), channel_id=1, source_target_pairs={{0,2},{1,3},{2,0},{3,1},{4,6},{5,7},{6,4},{7,5},{8,10},{9,11},{10,... | collective-permute-start | bytes 196616 | tf_op jit(solution)/shard_map/ppermute | solution.py:19
  16.3 6.1 %collective-permute-start.5 = (bf16[128,256]{1,0:T(8,128)(2,1)S(1)}, bf16[128,256]{1,0:T(8,128)(2,1)S(1)}, u32[]{:S(2)}, u32[]{:S(2)}) collective-permute-start(bf16[128,256]{1,0:T(8,128)(2,1)S(1)} %get-tuple-element.43), channel_id=1, source_target_pairs={{0,3},{1,2},{2,1},{3,0},{4,7},{5,6},{6,5},{7,4},{8,11},{9,10},{10,... | collective-permute-start | bytes 196616 | tf_op jit(solution)/shard_map/ppermute | solution.py:19
  22.6 5.2 %collective-permute-start.8 = (bf16[128,256]{1,0:T(8,128)(2,1)S(1)}, bf16[128,256]{1,0:T(8,128)(2,1)S(1)}, u32[]{:S(2)}, u32[]{:S(2)}) collective-permute-start(bf16[128,256]{1,0:T(8,128)(2,1)S(1)} %get-tuple-element.44.refs_1_), channel_id=1, source_target_pairs={{0,12},{4,8},{8,4},{12,0},{1,13},{5,9},{9,5},{13,1},{2,14},{6,10},... | collective-permute-start | bytes 196616 | tf_op jit(solution)/shard_map/ppermute | solution.py:19
  24.2 4.4 %collective-permute-start.7 = (bf16[128,256]{1,0:T(8,128)(2,1)S(1)}, bf16[128,256]{1,0:T(8,128)(2,1)S(1)}, u32[]{:S(2)}, u32[]{:S(2)}) collective-permute-start(bf16[128,256]{1,0:T(8,128)(2,1)S(1)} %get-tuple-element.44.refs_1_), channel_id=1, source_target_pairs={{0,8},{4,12},{8,0},{12,4},{1,9},{5,13},{9,1},{13,5},{2,10},{6,14},... | collective-permute-start | bytes 196616 | tf_op jit(solution)/shard_map/ppermute | solution.py:19
  24.7 4.3 %collective-permute-start.6 = (bf16[128,256]{1,0:T(8,128)(2,1)S(1)}, bf16[128,256]{1,0:T(8,128)(2,1)S(1)}, u32[]{:S(2)}, u32[]{:S(2)}) collective-permute-start(bf16[128,256]{1,0:T(8,128)(2,1)S(1)} %get-tuple-element.44.refs_1_), channel_id=1, source_target_pairs={{0,4},{4,0},{8,12},{12,8},{1,5},{5,1},{9,13},{13,9},{2,6},{6,2},{1... | collective-permute-start | bytes 196616 | tf_op jit(solution)/shard_map/ppermute | solution.py:19
  31.1 4.5 %collective-permute-start.10 = (bf16[128,128]{1,0:T(8,128)(2,1)S(1)}, bf16[128,128]{1,0:T(8,128)(2,1)S(1)}, u32[]{:S(2)}, u32[]{:S(2)}) collective-permute-start(bf16[128,128]{1,0:T(8,128)(2,1)S(1)} %get-tuple-element.51), channel_id=1, source_target_pairs={{0,1},{1,0},{2,3},{3,2},{4,5},{5,4},{6,7},{7,6},{8,9},{9,8},{10,11... | collective-permute-start | bytes 98312 | tf_op jit(solution)/shard_map/ppermute | solution.py:19
  31.1 5.5 %collective-permute-start.11 = (bf16[128,128]{1,0:T(8,128)(2,1)S(1)}, bf16[128,128]{1,0:T(8,128)(2,1)S(1)}, u32[]{:S(2)}, u32[]{:S(2)}) collective-permute-start(bf16[128,128]{1,0:T(8,128)(2,1)S(1)} %get-tuple-element.52), channel_id=1, source_target_pairs={{0,2},{1,3},{2,0},{3,1},{4,6},{5,7},{6,4},{7,5},{8,10},{9,11},{10,... | collective-permute-start | bytes 98312 | tf_op jit(solution)/shard_map/ppermute | solution.py:19
  32.8 5.7 %collective-permute-start.12 = (bf16[128,128]{1,0:T(8,128)(2,1)S(1)}, bf16[128,128]{1,0:T(8,128)(2,1)S(1)}, u32[]{:S(2)}, u32[]{:S(2)}) collective-permute-start(bf16[128,128]{1,0:T(8,128)(2,1)S(1)} %get-tuple-element.53), channel_id=1, source_target_pairs={{0,3},{1,2},{2,1},{3,0},{4,7},{5,6},{6,5},{7,4},{8,11},{9,10},{10,... | collective-permute-start | bytes 98312 | tf_op jit(solution)/shard_map/ppermute | solution.py:19
  39.0 6.0 %collective-permute-start.15 = (bf16[128,128]{1,0:T(8,128)(2,1)S(1)}, bf16[128,128]{1,0:T(8,128)(2,1)S(1)}, u32[]{:S(2)}, u32[]{:S(2)}) collective-permute-start(bf16[128,128]{1,0:T(8,128)(2,1)S(1)} %get-tuple-element.54.refs_0_), channel_id=1, source_target_pairs={{0,3},{1,2},{2,1},{3,0},{4,7},{5,6},{6,5},{7,4},{8,11},{9,10},{10,... | collective-permute-start | bytes 98312 | tf_op jit(solution)/shard_map/ppermute | solution.py:19
  41.8 4.8 %collective-permute-start.14 = (bf16[128,128]{1,0:T(8,128)(2,1)S(1)}, bf16[128,128]{1,0:T(8,128)(2,1)S(1)}, u32[]{:S(2)}, u32[]{:S(2)}) collective-permute-start(bf16[128,128]{1,0:T(8,128)(2,1)S(1)} %get-tuple-element.54.refs_0_), channel_id=1, source_target_pairs={{0,2},{1,3},{2,0},{3,1},{4,6},{5,7},{6,4},{7,5},{8,10},{9,11},{10,... | collective-permute-start | bytes 98312 | tf_op jit(solution)/shard_map/ppermute | solution.py:19
  41.8 4.8 %collective-permute-start.13 = (bf16[128,128]{1,0:T(8,128)(2,1)S(1)}, bf16[128,128]{1,0:T(8,128)(2,1)S(1)}, u32[]{:S(2)}, u32[]{:S(2)}) collective-permute-start(bf16[128,128]{1,0:T(8,128)(2,1)S(1)} %get-tuple-element.54.refs_0_), channel_id=1, source_target_pairs={{0,1},{1,0},{2,3},{3,2},{4,5},{5,4},{6,7},{7,6},{8,9},{9,8},{10,11... | collective-permute-start | bytes 98312 | tf_op jit(solution)/shard_map/ppermute | solution.py:19
  48.5 4.3 %collective-permute-start.17 = (bf16[128,256]{1,0:T(8,128)(2,1)S(1)}, bf16[128,256]{1,0:T(8,128)(2,1)S(1)}, u32[]{:S(2)}, u32[]{:S(2)}) collective-permute-start(bf16[128,256]{1,0:T(8,128)(2,1)S(1)} %get-tuple-element.56), channel_id=1, source_target_pairs={{0,4},{4,0},{8,12},{12,8},{1,5},{5,1},{9,13},{13,9},{2,6},{6,2},{1... | collective-permute-start | bytes 196616 | tf_op jit(solution)/shard_map/ppermute | solution.py:19
  50.0 4.3 %collective-permute-start.18 = (bf16[128,256]{1,0:T(8,128)(2,1)S(1)}, bf16[128,256]{1,0:T(8,128)(2,1)S(1)}, u32[]{:S(2)}, u32[]{:S(2)}) collective-permute-start(bf16[128,256]{1,0:T(8,128)(2,1)S(1)} %get-tuple-element.57), channel_id=1, source_target_pairs={{0,8},{4,12},{8,0},{12,4},{1,9},{5,13},{9,1},{13,5},{2,10},{6,14},... | collective-permute-start | bytes 196616 | tf_op jit(solution)/shard_map/ppermute | solution.py:19
  51.5 5.2 %collective-permute-start.19 = (bf16[128,256]{1,0:T(8,128)(2,1)S(1)}, bf16[128,256]{1,0:T(8,128)(2,1)S(1)}, u32[]{:S(2)}, u32[]{:S(2)}) collective-permute-start(bf16[128,256]{1,0:T(8,128)(2,1)S(1)} %get-tuple-element.58), channel_id=1, source_target_pairs={{0,12},{4,8},{8,4},{12,0},{1,13},{5,9},{9,5},{13,1},{2,14},{6,10},... | collective-permute-start | bytes 196616 | tf_op jit(solution)/shard_map/ppermute | solution.py:19
  57.7 6.2 %collective-permute-start.22 = (bf16[128,256]{1,0:T(8,128)(2,1)S(1)}, bf16[128,256]{1,0:T(8,128)(2,1)S(1)}, u32[]{:S(2)}, u32[]{:S(2)}) collective-permute-start(bf16[128,256]{1,0:T(8,128)(2,1)S(1)} %get-tuple-element.60.refs_1_), channel_id=1, source_target_pairs={{0,3},{1,2},{2,1},{3,0},{4,7},{5,6},{6,5},{7,4},{8,11},{9,10},{10,... | collective-permute-start | bytes 196616 | tf_op jit(solution)/shard_map/ppermute | solution.py:19
  59.3 6.1 %collective-permute-start.21 = (bf16[128,256]{1,0:T(8,128)(2,1)S(1)}, bf16[128,256]{1,0:T(8,128)(2,1)S(1)}, u32[]{:S(2)}, u32[]{:S(2)}) collective-permute-start(bf16[128,256]{1,0:T(8,128)(2,1)S(1)} %get-tuple-element.60.refs_1_), channel_id=1, source_target_pairs={{0,2},{1,3},{2,0},{3,1},{4,6},{5,7},{6,4},{7,5},{8,10},{9,11},{10,... | collective-permute-start | bytes 196616 | tf_op jit(solution)/shard_map/ppermute | solution.py:19
  59.7 5.7 %collective-permute-start.20 = (bf16[128,256]{1,0:T(8,128)(2,1)S(1)}, bf16[128,256]{1,0:T(8,128)(2,1)S(1)}, u32[]{:S(2)}, u32[]{:S(2)}) collective-permute-start(bf16[128,256]{1,0:T(8,128)(2,1)S(1)} %get-tuple-element.60.refs_1_), channel_id=1, source_target_pairs={{0,1},{1,0},{2,3},{3,2},{4,5},{5,4},{6,7},{7,6},{8,9},{9,8},{10,11... | collective-permute-start | bytes 196616 | tf_op jit(solution)/shard_map/ppermute | solution.py:19
  62.1 7.3 %collective-permute-start.26 = (f32[128,128]{1,0:T(8,128)S(1)}, f32[128,128]{1,0:T(8,128)S(1)}, u32[]{:S(2)}, u32[]{:S(2)}) collective-permute-start(f32[128,128]{1,0:T(8,128)S(1)} %get-tuple-element.68.mine_ref), channel_id=1, source_target_pairs={{0,16},{16,0},{1,17},{17,1},{2,18},{18,2},{3,19},{19,3},{4,20},{20... | collective-permute-start | bytes 196616 | tf_op jit(solution)/shard_map/ppermute | solution.py:19
  65.8 4.3 %collective-permute-start.23 = (bf16[128,256]{1,0:T(8,128)(2,1)S(1)}, bf16[128,256]{1,0:T(8,128)(2,1)S(1)}, u32[]{:S(2)}, u32[]{:S(2)}) collective-permute-start(bf16[128,256]{1,0:T(8,128)(2,1)S(1)} %get-tuple-element.63), channel_id=1, source_target_pairs={{0,4},{4,0},{8,12},{12,8},{1,5},{5,1},{9,13},{13,9},{2,6},{6,2},{1... | collective-permute-start | bytes 196616 | tf_op jit(solution)/shard_map/ppermute | solution.py:19
  67.0 5.2 %collective-permute-start.25 = (bf16[128,256]{1,0:T(8,128)(2,1)S(1)}, bf16[128,256]{1,0:T(8,128)(2,1)S(1)}, u32[]{:S(2)}, u32[]{:S(2)}) collective-permute-start(bf16[128,256]{1,0:T(8,128)(2,1)S(1)} %get-tuple-element.65), channel_id=1, source_target_pairs={{0,12},{4,8},{8,4},{12,0},{1,13},{5,9},{9,5},{13,1},{2,14},{6,10},... | collective-permute-start | bytes 196616 | tf_op jit(solution)/shard_map/ppermute | solution.py:19
  (16 other events, 71.6 us)

commit v3 on v2

--- a/solution.py
+++ b/solution.py
@@ -7,27 +7,33 @@
 
 BF = jnp.bfloat16
 F32 = jnp.float32
-HI = lax.Precision.HIGHEST
 VMEM = pl.BlockSpec(memory_space=pltpu.VMEM)
+HBM = pl.BlockSpec(memory_space=pltpu.HBM)
 
 
 def is_direct(n):
     return n in (1, 2, 4)
 
 
+def swap_all(blocks, axis, n):
+    steps = (2, 1, 3) if axis == "col" and n == 4 else range(1, n)
+    got = {d: swap(blocks[d], axis, n, d) for d in steps}
+    return [got[d] for d in range(1, n)]
+
+
 def swap(values, axis, n, step):
     return lax.ppermute(values, axis, [(i, i ^ step) for i in range(n)])
 
 
 def gather(values, axis, n):
     if is_direct(n):
-        return [values] + [swap(values, axis, n, d) for d in range(1, n)]
+        return [values] + swap_all([values] * n, axis, n)
     return [lax.all_gather(values, axis, axis=0, tiled=True)]
 
 
 def scatter_sum(blocks, axis, n):
     if is_direct(n):
-        return [blocks[0]] + [swap(blocks[d], axis, n, d) for d in range(1, n)]
+        return [blocks[0]] + swap_all(blocks, axis, n)
     return [lax.psum_scatter(blocks[0], axis, scatter_dimension=0, tiled=True)]
 
 
@@ -38,14 +44,14 @@
     return size
 
 
-def call(kernel, outs, args, scratch=(), flops=0):
+def call(kernel, outs, args, scratch=(), flops=0, in_specs=None, sems=0):
     total = sum(nbytes(s, t) for s, t in list(outs) + list(scratch)) + sum(nbytes(a.shape, a.dtype) for a in args)
     return pl.pallas_call(
         kernel,
         out_shape=tuple(jax.ShapeDtypeStruct(s, t) for s, t in outs),
-        in_specs=[VMEM] * len(args),
+        in_specs=in_specs or [VMEM] * len(args),
         out_specs=(VMEM,) * len(outs),
-        scratch_shapes=[pltpu.VMEM(s, t) for s, t in scratch],
+        scratch_shapes=[pltpu.VMEM(s, t) for s, t in scratch] + ([pltpu.SemaphoreType.DMA((sems,))] if sems else []),
         compiler_params=pltpu.CompilerParams(vmem_limit_bytes=total + (6 << 20)),
         cost_estimate=pl.CostEstimate(flops=flops, bytes_accessed=total, transcendentals=0),
     )(*args)
@@ -70,14 +76,14 @@
     return lax.dot_general(a, b, (((0,), (0,)), ((), ())), preferred_element_type=F32)
 
 
-def apply_lower(inverse, right_side):
-    return jnp.dot(inverse, right_side, precision=HI, preferred_element_type=F32)
-
-
-def apply_upper(inverse, right_side):
-    return lax.dot_general(
-        inverse, right_side, (((0,), (0,)), ((), ())), precision=HI, preferred_element_type=F32
-    )
+def split(values):
+    high = values.astype(BF)
+    return high, (values - high.astype(F32)).astype(BF)
+
+
+def apply_split(parts, right_side):
+    high, low = split(right_side)
+    return dot(parts, jnp.concatenate([high, high, low], axis=0))
 
 
 def total_of(refs):
@@ -117,14 +123,82 @@
 def leaf_first(leaf_inv, leaf_rhs):
     count, width, cols = leaf_rhs.shape
 
-    def kernel(inv_ref, rhs_ref, y_ref, yb_ref):
+    def kernel(inv_hbm, rhs_hbm, y_ref, yb_ref, inv_ref, rhs_ref, sems):
+        copies = [
+            pltpu.make_async_copy(inv_hbm, inv_ref, sems.at[0]),
+            pltpu.make_async_copy(rhs_hbm, rhs_ref, sems.at[1]),
+        ]
+        for copy in copies:
+            copy.start()
+        for copy in copies:
+            copy.wait()
         for m in range(count):
-            y = apply_lower(inv_ref[m], rhs_ref[m].astype(F32))
+            high, low = split(inv_ref[m])
+            rhs = rhs_ref[m]
+            y = dot(jnp.concatenate([high, low], axis=1), jnp.concatenate([rhs, rhs], axis=0))
             y_ref[pl.ds(m * width, width), :] = y
             yb_ref[pl.ds(m * width, width), :] = y.astype(BF)
 
     shape = (count * width, cols)
-    return call(kernel, [(shape, F32), (shape, BF)], [leaf_inv, leaf_rhs])
+    return call(
+        kernel,
+        [(shape, F32), (shape, BF)],
+        [leaf_inv, leaf_rhs],
+        scratch=[(leaf_inv.shape, F32), (leaf_rhs.shape, BF)],
+        in_specs=[HBM] * 2,
+        sems=2,
+    )
+
+
+def mask_tiles(tile_sets, masks, width):
+    count = len(masks)
+    n_col = masks[0].shape[0]
+
+    def kernel(*refs):
+        masks_hbm, tile_refs, outs = refs[:count], refs[count : 2 * count], refs[2 * count : 3 * count]
+        mask_refs, sems = refs[3 * count : 4 * count], refs[4 * count]
+        copies = [pltpu.make_async_copy(masks_hbm[i], mask_refs[i], sems.at[i]) for i in range(count)]
+        for copy in copies:
+            copy.start()
+        for copy in copies:
+            copy.wait()
+        for i in range(count):
+            for k in range(masks[i].shape[2]):
+                weight = jnp.broadcast_to(mask_refs[i][:, :, k : k + 1].astype(F32), (n_col, 1, width)).astype(BF)
+                lanes = pl.ds(k * width, width)
+                outs[i][:, :, lanes] = tile_refs[i][:, :, lanes] * weight
+
+    return call(
+        kernel,
+        [(t.shape, BF) for t in tile_sets],
+        [*masks, *tile_sets],
+        scratch=[(m.shape, m.dtype) for m in masks],
+        in_specs=[HBM] * count + [VMEM] * count,
+        sems=count,
+    )
+
+
+def split_inverse(inverse):
+    blocks, width = inverse.shape[:2]
+
+    def kernel(inv_ref, low_ref, up_ref):
+        for m in range(blocks):
+            value = inv_ref[m]
+            for out_ref, part in ((low_ref, value), (up_ref, value.T)):
+                high, low = split(part)
+                out_ref[m, :, pl.ds(0, width)] = high
+                out_ref[m, :, pl.ds(width, width)] = low
+                out_ref[m, :, pl.ds(2 * width, width)] = high
+
+    shape = (blocks, width, 3 * width)
+    return call(kernel, [(shape, BF), (shape, BF)], [inverse])
+
+
+def keep(values):
+    def kernel(in_ref, out_ref):
+        out_ref[...] = in_ref[...]
+
+    return call(kernel, [(values.shape, values.dtype)], [values])[0]
 
 
 def forward_blocks(tiles, pieces, n_row, n_col, width):
@@ -159,7 +233,7 @@
 
     def kernel(*refs):
         rhs_ref, inv_ref, y_ref, yb_ref = refs[count:]
-        y = apply_lower(inv_ref[...], rhs_ref[...].astype(F32) - total_of(refs[:count]))
+        y = apply_split(inv_ref[0], rhs_ref[...].astype(F32) - total_of(refs[:count]))
         y_ref[...] = y
         yb_ref[...] = y.astype(BF)
 
@@ -201,20 +275,20 @@
     return call(kernel, block_outs(n_col, width, half), [mine, other])
 
 
-def solve_top(sums, right_side, inverse):
+def solve_top(sums, right_side, lower, upper):
     count = len(sums)
     half = right_side.shape[1] // 2
 
     def kernel(*refs):
-        rhs_ref, inv_ref, x_ref, xb_ref = refs[count:]
+        rhs_ref, low_ref, up_ref, x_ref, xb_ref = refs[count:]
         mine = rhs_ref[:, rows(lax.axis_index("sec"), half)].astype(F32)
-        y = apply_lower(inv_ref[...], mine - total_of(refs[:count]))
-        x = apply_upper(inv_ref[...], y)
+        y = apply_split(low_ref[0], mine - total_of(refs[:count]))
+        x = apply_split(up_ref[0], y)
         x_ref[...] = x
         xb_ref[...] = x.astype(BF)
 
     shape = (right_side.shape[0], half)
-    return call(kernel, [(shape, F32), (shape, BF)], [*sums, right_side, inverse])
+    return call(kernel, [(shape, F32), (shape, BF)], [*sums, right_side, lower, upper])
 
 
 def stack_pieces(pieces, n, axis):
@@ -285,7 +359,7 @@
         y_ref, inv_ref, x_ref, xb_ref = refs[count:]
         rest = y_ref[...] - total_of(refs[:count])
         for m in range(blocks):
-            x = apply_upper(inv_ref[m], rest[m * width : (m + 1) * width])
+            x = apply_split(inv_ref[m], rest[m * width : (m + 1) * width])
             x_ref[pl.ds(m * width, width), :] = x
             xb_ref[pl.ds(m * width, width), :] = x.astype(BF)
 
@@ -300,48 +374,48 @@
         y_ref, inv_ref, x_ref = refs[count:]
         rest = y_ref[...] - total_of(refs[:count])
         for m in range(blocks):
-            x_ref[pl.ds(m * width, width), :] = apply_upper(inv_ref[m], rest[m * width : (m + 1) * width])
+            x_ref[pl.ds(m * width, width), :] = apply_split(inv_ref[m], rest[m * width : (m + 1) * width])
 
     return call(kernel, [(right_side.shape, F32)], [*sums, right_side, inverse])[0]
 
 
 def make_body(n_row, n_col):
     def body(leaf_rhs, sep_rhs, top_rhs, leaf_inv, sep_inv, top_inv,
-             sep_leaf, top_leaf, top_sep, sep_leaf_mask, top_leaf_mask, top_sep_mask):
+             sep_leaf, top_leaf, top_sep, *masks):
         leaf_count, width, cols = leaf_rhs.shape[2], leaf_rhs.shape[4], leaf_rhs.shape[5]
         span = leaf_count * width
 
-        def tiles(values, mask):
-            masked = values * mask.astype(BF)[:, None, :, :, None]
-            return masked.reshape(n_col * width, -1)
-
         leaf_y, leaf_yb = leaf_first(leaf_inv[0, 0, :, 0], leaf_rhs[0, 0, :, 0])
-        sl = tiles(sep_leaf[0, 0, :, :, :, :, 0], sep_leaf_mask[0, 0, :, :, :, 0])
-        blocks, leaf_col = forward_blocks(sl, gather(leaf_yb, "row", n_row), n_row, n_col, width)
+        leaf_pieces = gather(leaf_yb, "row", n_row)
+        masked = mask_tiles(
+            [values.reshape(n_col, width, -1) for values in (sep_leaf, top_leaf, top_sep)],
+            [mask.reshape(n_col, 1, -1) for mask in masks],
+            width,
+        )
+        sl, tl, ts = [values.reshape(n_col * width, -1) for values in masked]
+        leaf_low, leaf_up = split_inverse(leaf_inv[0, 0, :, 0])
+        sep_low, sep_up = split_inverse(sep_inv[0, 0])
+        top_low, top_up = split_inverse(top_inv[0])
+        blocks, leaf_col = forward_blocks(sl, leaf_pieces, n_row, n_col, width)
         sums = scatter_sum(blocks, "col", n_col)
-        top_leaf, top_sep, top_leaf_mask, top_sep_mask, leaf_col = lax.optimization_barrier(
-            (top_leaf, top_sep, top_leaf_mask, top_sep_mask, leaf_col)
-        )
-        tl = tiles(top_leaf[0, 0, :, :, :, :, 0], top_leaf_mask[0, 0, :, :, :, 0])
-        ts = tiles(top_sep[0, 0, :, :, :, None, 0], top_sep_mask[0, 0, :, :, None, 0])
         leaf_part = plain_product(tl, leaf_col, False)
-        sep_y, sep_yb = solve_forward(sums, sep_rhs[0, 0, 0], sep_inv[0, 0, 0])
+        sep_y, sep_yb = solve_forward(sums, sep_rhs[0, 0, 0], sep_low)
         mine, other = top_halves(ts, gather(sep_yb, "row", n_row), leaf_part, n_row)
         blocks = add_sections(mine, swap(other, "sec", 2, 1), n_col, width)
         sums = scatter_sum(blocks, "col", n_col)
-        top_xh, top_xhb = solve_top(sums, top_rhs[0, 0], top_inv[0, 0])
+        top_xh, top_xhb = solve_top(sums, top_rhs[0, 0], top_low, top_up)
         top_stack = stack_pieces(gather(top_xhb, "col", n_col), n_col, "col")
         blocks, top_row = top_back_blocks(ts, top_stack, swap(top_stack, "sec", 2, 1), n_row, width)
         sums = scatter_sum(blocks, "row", n_row)
         top_part = plain_product(tl, top_row, True)
         top_x = join_halves(top_xh, swap(top_xh, "sec", 2, 1))
-        sep_x, sep_xb = solve_back(sums, sep_y, sep_inv[0, 0])
+        sep_x, sep_xb = solve_back(sums, sep_y, sep_up)
         pieces = gather(sep_xb, "col", n_col)
         sums = scatter_sum(back_blocks(sl, pieces, top_part, n_row, n_col, span), "row", n_row)
-        leaf_x = solve_last(sums, leaf_y, leaf_inv[0, 0, :, 0])
+        leaf_x = solve_last(sums, leaf_y, leaf_up)
         return (
             leaf_x.reshape(1, 1, leaf_count, 1, width, cols),
-            sep_x[None, None, None],
+            keep(sep_x)[None, None, None],
             top_x[None, None],
         )
 

time: 73.5 us -> 75.3 us (1.024)
  local copies, waits for them, and re-layouts: 3.22 us -> 4.86 us
  Pallas kernels: 5.89 us -> 6.8 us
    reshape x0 -> x3, local copies, waits for them, and re-layouts: none -> 1.64 us  [body(): values.reshape(n_col, width, -1)]
    pallas_call x14 -> x19, Pallas kernels: 5.89 us -> 6.8 us  [call(): pl.pallas_call(kernel, out_shape=tuple((jax.ShapeDtypeStruct(s, t) for s,...]
    unnamed x29 -> x24, local copies, waits for them, and re-layouts: 2.6 us -> 3.22 us
  transfers between devices with their start and end apart: 27 -> 27, of which waited for: 22 -> 18; matrix products, arithmetic and copies ran while one was open for 1% -> 2% of each run, Pallas kernels for 2% -> 5%
where the time goes in v3:
time: 75.3 us; the launch traced here: 74.9 us
  starting transfers between devices  33.1 us (44%)
  waiting for transfers between devices  29.2 us (39%)
  Pallas kernels  6.8 us (9%)
  local copies, waits for them, and re-layouts  4.86 us (6%)
  between operations  0.92 us (1%)
    ppermute x27, starting transfers between devices, swap(): return lax.ppermute(values, axis, [(i, i ^ step) for i in range(n)])  33.1 us
    ppermute x27, waiting for transfers between devices, swap(): return lax.ppermute(values, axis, [(i, i ^ step) for i in range(n)])  29.2 us
    pallas_call x19, Pallas kernels, call(): pl.pallas_call(kernel, out_shape=tuple((jax.ShapeDtypeStruct(s, t) for s,...  6.8 us
    unnamed x24, local copies, waits for them, and re-layouts  3.22 us
    reshape x3, local copies, waits for them, and re-layouts, body(): values.reshape(n_col, width, -1)  1.64 us
  transfers between devices with their start and end apart: 27, of which 18 were waited for; matrix products, arithmetic and copies ran while one was open for 2% of the time, Pallas kernels for 5%

profile of v3, /device:TPU:0, one launch (start us, length us, event | category | flops | bytes accessed | tf_op | source)
XLA Modules:
  0.0 74.9 jit_solution(8110468594574273806)
XLA Ops:
  2.6 3.0 %collective-permute-start = (bf16[128,256]{1,0:T(8,128)(2,1)S(1)}, bf16[128,256]{1,0:T(8,128)(2,1)S(1)}, u32[]{:S(2)}, u32[]{:S(2)}) collective-permute-start(bf16[128,256]{1,0:T(8,128)(2,1)S(1)} %get-tuple-element.41.refs_1_), channel_id=1, source_target_pairs={{0,4},{4,0},{8,12},{12,8},{1,5},{5,1},{9,13},{13,9},{2,6},{6,2},{1... | collective-permute-start | bytes 196616 | tf_op jit(solution)/shard_map/ppermute | solution.py:25
  5.7 1.5 %collective-permute-start.1 = (bf16[128,256]{1,0:T(8,128)(2,1)S(1)}, bf16[128,256]{1,0:T(8,128)(2,1)S(1)}, u32[]{:S(2)}, u32[]{:S(2)}) collective-permute-start(bf16[128,256]{1,0:T(8,128)(2,1)S(1)} %get-tuple-element.41.refs_1_), channel_id=1, source_target_pairs={{0,8},{4,12},{8,0},{12,4},{1,9},{5,13},{9,1},{13,5},{2,10},{6,14},... | collective-permute-start | bytes 196616 | tf_op jit(solution)/shard_map/ppermute | solution.py:25
  10.8 1.5 %collective-permute-done.2.refs_4_ = bf16[128,256]{1,0:T(8,128)(2,1)S(1)} collective-permute-done((bf16[128,256]{1,0:T(8,128)(2,1)S(1)}, bf16[128,256]{1,0:T(8,128)(2,1)S(1)}, u32[]{:S(2)}, u32[]{:S(2)}) %collective-permute-start.2) | collective-permute-done | bytes 65568 | tf_op jit(solution)/shard_map/ppermute | solution.py:25
  12.7 1.6 %collective-permute-start.3 = (bf16[128,256]{1,0:T(8,128)(2,1)S(1)}, bf16[128,256]{1,0:T(8,128)(2,1)S(1)}, u32[]{:S(2)}, u32[]{:S(2)}) collective-permute-start(bf16[128,256]{1,0:T(8,128)(2,1)S(1)} %get-tuple-element.43), channel_id=1, source_target_pairs={{0,1},{1,0},{2,3},{3,2},{4,5},{5,4},{6,7},{7,6},{8,9},{9,8},{10,11... | collective-permute-start | bytes 196616 | tf_op jit(solution)/shard_map/ppermute | solution.py:25
  14.3 2.6 %collective-permute-start.4 = (bf16[128,256]{1,0:T(8,128)(2,1)S(1)}, bf16[128,256]{1,0:T(8,128)(2,1)S(1)}, u32[]{:S(2)}, u32[]{:S(2)}) collective-permute-start(bf16[128,256]{1,0:T(8,128)(2,1)S(1)} %get-tuple-element.44), channel_id=1, source_target_pairs={{0,2},{1,3},{2,0},{3,1},{4,6},{5,7},{6,4},{7,5},{8,10},{9,11},{10,... | collective-permute-start | bytes 196616 | tf_op jit(solution)/shard_map/ppermute | solution.py:25
  17.3 3.6 %collective-permute-done.4.refs_2_ = bf16[128,256]{1,0:T(8,128)(2,1)S(1)} collective-permute-done((bf16[128,256]{1,0:T(8,128)(2,1)S(1)}, bf16[128,256]{1,0:T(8,128)(2,1)S(1)}, u32[]{:S(2)}, u32[]{:S(2)}) %collective-permute-start.4) | collective-permute-done | bytes 65568 | tf_op jit(solution)/shard_map/ppermute | solution.py:25
  20.9 2.1 %collective-permute-done.5.refs_3_ = bf16[128,256]{1,0:T(8,128)(2,1)S(1)} collective-permute-done((bf16[128,256]{1,0:T(8,128)(2,1)S(1)}, bf16[128,256]{1,0:T(8,128)(2,1)S(1)}, u32[]{:S(2)}, u32[]{:S(2)}) %collective-permute-start.5) | collective-permute-done | bytes 65568 | tf_op jit(solution)/shard_map/ppermute | solution.py:25
  23.8 1.4 %collective-permute-start.7 = (bf16[128,256]{1,0:T(8,128)(2,1)S(1)}, bf16[128,256]{1,0:T(8,128)(2,1)S(1)}, u32[]{:S(2)}, u32[]{:S(2)}) collective-permute-start(bf16[128,256]{1,0:T(8,128)(2,1)S(1)} %get-tuple-element.47.refs_1_), channel_id=1, source_target_pairs={{0,8},{4,12},{8,0},{12,4},{1,9},{5,13},{9,1},{13,5},{2,10},{6,14},... | collective-permute-start | bytes 196616 | tf_op jit(solution)/shard_map/ppermute | solution.py:25
  25.2 1.5 %collective-permute-start.8 = (bf16[128,256]{1,0:T(8,128)(2,1)S(1)}, bf16[128,256]{1,0:T(8,128)(2,1)S(1)}, u32[]{:S(2)}, u32[]{:S(2)}) collective-permute-start(bf16[128,256]{1,0:T(8,128)(2,1)S(1)} %get-tuple-element.47.refs_1_), channel_id=1, source_target_pairs={{0,12},{4,8},{8,4},{12,0},{1,13},{5,9},{9,5},{13,1},{2,14},{6,10},... | collective-permute-start | bytes 196616 | tf_op jit(solution)/shard_map/ppermute | solution.py:25
  28.1 2.3 %collective-permute-done.8.refs_4_ = bf16[128,256]{1,0:T(8,128)(2,1)S(1)} collective-permute-done((bf16[128,256]{1,0:T(8,128)(2,1)S(1)}, bf16[128,256]{1,0:T(8,128)(2,1)S(1)}, u32[]{:S(2)}, u32[]{:S(2)}) %collective-permute-start.8) | collective-permute-done | bytes 65568 | tf_op jit(solution)/shard_map/ppermute | solution.py:25
  31.0 1.5 %collective-permute-done.9.other_ref = f32[512,128]{1,0:T(8,128)S(1)} collective-permute-done((f32[512,128]{1,0:T(8,128)S(1)}, f32[512,128]{1,0:T(8,128)S(1)}, u32[]{:S(2)}, u32[]{:S(2)}) %collective-permute-start.9) | collective-permute-done | bytes 262176 | tf_op jit(solution)/shard_map/ppermute | solution.py:25
  32.6 1.5 %collective-permute-start.11 = (bf16[128,128]{1,0:T(8,128)(2,1)S(1)}, bf16[128,128]{1,0:T(8,128)(2,1)S(1)}, u32[]{:S(2)}, u32[]{:S(2)}) collective-permute-start(bf16[128,128]{1,0:T(8,128)(2,1)S(1)} %get-tuple-element.54), channel_id=1, source_target_pairs={{0,2},{1,3},{2,0},{3,1},{4,6},{5,7},{6,4},{7,5},{8,10},{9,11},{10,... | collective-permute-start | bytes 98312 | tf_op jit(solution)/shard_map/ppermute | solution.py:25
  34.1 2.9 %collective-permute-start.12 = (bf16[128,128]{1,0:T(8,128)(2,1)S(1)}, bf16[128,128]{1,0:T(8,128)(2,1)S(1)}, u32[]{:S(2)}, u32[]{:S(2)}) collective-permute-start(bf16[128,128]{1,0:T(8,128)(2,1)S(1)} %get-tuple-element.55), channel_id=1, source_target_pairs={{0,3},{1,2},{2,1},{3,0},{4,7},{5,6},{6,5},{7,4},{8,11},{9,10},{10,... | collective-permute-start | bytes 98312 | tf_op jit(solution)/shard_map/ppermute | solution.py:25
  38.0 1.8 %collective-permute-done.12.refs_3_ = bf16[128,128]{1,0:T(8,128)(2,1)S(1)} collective-permute-done((bf16[128,128]{1,0:T(8,128)(2,1)S(1)}, bf16[128,128]{1,0:T(8,128)(2,1)S(1)}, u32[]{:S(2)}, u32[]{:S(2)}) %collective-permute-start.12) | collective-permute-done | bytes 32800 | tf_op jit(solution)/shard_map/ppermute | solution.py:25
  40.3 3.4 %collective-permute-start.14 = (bf16[128,128]{1,0:T(8,128)(2,1)S(1)}, bf16[128,128]{1,0:T(8,128)(2,1)S(1)}, u32[]{:S(2)}, u32[]{:S(2)}) collective-permute-start(bf16[128,128]{1,0:T(8,128)(2,1)S(1)} %get-tuple-element.58.refs_0_), channel_id=1, source_target_pairs={{0,2},{1,3},{2,0},{3,1},{4,6},{5,7},{6,4},{7,5},{8,10},{9,11},{10,... | collective-permute-start | bytes 98312 | tf_op jit(solution)/shard_map/ppermute | solution.py:25
  45.6 3.8 %collective-permute-done.15.refs_3_ = bf16[128,128]{1,0:T(8,128)(2,1)S(1)} collective-permute-done((bf16[128,128]{1,0:T(8,128)(2,1)S(1)}, bf16[128,128]{1,0:T(8,128)(2,1)S(1)}, u32[]{:S(2)}, u32[]{:S(2)}) %collective-permute-start.15) | collective-permute-done | bytes 32800 | tf_op jit(solution)/shard_map/ppermute | solution.py:25
  51.9 1.5 %collective-permute-start.18 = (bf16[128,256]{1,0:T(8,128)(2,1)S(1)}, bf16[128,256]{1,0:T(8,128)(2,1)S(1)}, u32[]{:S(2)}, u32[]{:S(2)}) collective-permute-start(bf16[128,256]{1,0:T(8,128)(2,1)S(1)} %get-tuple-element.61), channel_id=1, source_target_pairs={{0,8},{4,12},{8,0},{12,4},{1,9},{5,13},{9,1},{13,5},{2,10},{6,14},... | collective-permute-start | bytes 196616 | tf_op jit(solution)/shard_map/ppermute | solution.py:25
  53.4 1.4 %collective-permute-start.19 = (bf16[128,256]{1,0:T(8,128)(2,1)S(1)}, bf16[128,256]{1,0:T(8,128)(2,1)S(1)}, u32[]{:S(2)}, u32[]{:S(2)}) collective-permute-start(bf16[128,256]{1,0:T(8,128)(2,1)S(1)} %get-tuple-element.62), channel_id=1, source_target_pairs={{0,12},{4,8},{8,4},{12,0},{1,13},{5,9},{9,5},{13,1},{2,14},{6,10},... | collective-permute-start | bytes 196616 | tf_op jit(solution)/shard_map/ppermute | solution.py:25
  56.2 2.4 %collective-permute-done.19.refs_3_ = bf16[128,256]{1,0:T(8,128)(2,1)S(1)} collective-permute-done((bf16[128,256]{1,0:T(8,128)(2,1)S(1)}, bf16[128,256]{1,0:T(8,128)(2,1)S(1)}, u32[]{:S(2)}, u32[]{:S(2)}) %collective-permute-start.19) | collective-permute-done | bytes 65568 | tf_op jit(solution)/shard_map/ppermute | solution.py:25
  60.2 3.0 %collective-permute-start.22 = (bf16[128,256]{1,0:T(8,128)(2,1)S(1)}, bf16[128,256]{1,0:T(8,128)(2,1)S(1)}, u32[]{:S(2)}, u32[]{:S(2)}) collective-permute-start(bf16[128,256]{1,0:T(8,128)(2,1)S(1)} %get-tuple-element.65.refs_1_), channel_id=1, source_target_pairs={{0,3},{1,2},{2,1},{3,0},{4,7},{5,6},{6,5},{7,4},{8,11},{9,10},{10,... | collective-permute-start | bytes 196616 | tf_op jit(solution)/shard_map/ppermute | solution.py:25
  64.6 1.8 %collective-permute-done.22.refs_4_ = bf16[128,256]{1,0:T(8,128)(2,1)S(1)} collective-permute-done((bf16[128,256]{1,0:T(8,128)(2,1)S(1)}, bf16[128,256]{1,0:T(8,128)(2,1)S(1)}, u32[]{:S(2)}, u32[]{:S(2)}) %collective-permute-start.22) | collective-permute-done | bytes 65568 | tf_op jit(solution)/shard_map/ppermute | solution.py:25
  67.4 1.5 %collective-permute-start.24 = (bf16[128,256]{1,0:T(8,128)(2,1)S(1)}, bf16[128,256]{1,0:T(8,128)(2,1)S(1)}, u32[]{:S(2)}, u32[]{:S(2)}) collective-permute-start(bf16[128,256]{1,0:T(8,128)(2,1)S(1)} %get-tuple-element.69), channel_id=1, source_target_pairs={{0,8},{4,12},{8,0},{12,4},{1,9},{5,13},{9,1},{13,5},{2,10},{6,14},... | collective-permute-start | bytes 196616 | tf_op jit(solution)/shard_map/ppermute | solution.py:25
  68.9 1.4 %collective-permute-start.25 = (bf16[128,256]{1,0:T(8,128)(2,1)S(1)}, bf16[128,256]{1,0:T(8,128)(2,1)S(1)}, u32[]{:S(2)}, u32[]{:S(2)}) collective-permute-start(bf16[128,256]{1,0:T(8,128)(2,1)S(1)} %get-tuple-element.70), channel_id=1, source_target_pairs={{0,12},{4,8},{8,4},{12,0},{1,13},{5,9},{9,5},{13,1},{2,14},{6,10},... | collective-permute-start | bytes 196616 | tf_op jit(solution)/shard_map/ppermute | solution.py:25
  72.3 1.8 %collective-permute-done.25.refs_3_ = bf16[128,256]{1,0:T(8,128)(2,1)S(1)} collective-permute-done((bf16[128,256]{1,0:T(8,128)(2,1)S(1)}, bf16[128,256]{1,0:T(8,128)(2,1)S(1)}, u32[]{:S(2)}, u32[]{:S(2)}) %collective-permute-start.25) | collective-permute-done | bytes 65568 | tf_op jit(solution)/shard_map/ppermute | solution.py:25
  (76 shorter events, 23.0 us)
Async XLA Ops:
  2.6 8.2 %collective-permute-start = (bf16[128,256]{1,0:T(8,128)(2,1)S(1)}, bf16[128,256]{1,0:T(8,128)(2,1)S(1)}, u32[]{:S(2)}, u32[]{:S(2)}) collective-permute-start(bf16[128,256]{1,0:T(8,128)(2,1)S(1)} %get-tuple-element.41.refs_1_), channel_id=1, source_target_pairs={{0,4},{4,0},{8,12},{12,8},{1,5},{5,1},{9,13},{13,9},{2,6},{6,2},{1... | collective-permute-start | bytes 196616 | tf_op jit(solution)/shard_map/ppermute | solution.py:25
  5.7 5.2 %collective-permute-start.1 = (bf16[128,256]{1,0:T(8,128)(2,1)S(1)}, bf16[128,256]{1,0:T(8,128)(2,1)S(1)}, u32[]{:S(2)}, u32[]{:S(2)}) collective-permute-start(bf16[128,256]{1,0:T(8,128)(2,1)S(1)} %get-tuple-element.41.refs_1_), channel_id=1, source_target_pairs={{0,8},{4,12},{8,0},{12,4},{1,9},{5,13},{9,1},{13,5},{2,10},{6,14},... | collective-permute-start | bytes 196616 | tf_op jit(solution)/shard_map/ppermute | solution.py:25
  7.2 5.2 %collective-permute-start.2 = (bf16[128,256]{1,0:T(8,128)(2,1)S(1)}, bf16[128,256]{1,0:T(8,128)(2,1)S(1)}, u32[]{:S(2)}, u32[]{:S(2)}) collective-permute-start(bf16[128,256]{1,0:T(8,128)(2,1)S(1)} %get-tuple-element.41.refs_1_), channel_id=1, source_target_pairs={{0,12},{4,8},{8,4},{12,0},{1,13},{5,9},{9,5},{13,1},{2,14},{6,10},... | collective-permute-start | bytes 196616 | tf_op jit(solution)/shard_map/ppermute | solution.py:25
  12.7 4.6 %collective-permute-start.3 = (bf16[128,256]{1,0:T(8,128)(2,1)S(1)}, bf16[128,256]{1,0:T(8,128)(2,1)S(1)}, u32[]{:S(2)}, u32[]{:S(2)}) collective-permute-start(bf16[128,256]{1,0:T(8,128)(2,1)S(1)} %get-tuple-element.43), channel_id=1, source_target_pairs={{0,1},{1,0},{2,3},{3,2},{4,5},{5,4},{6,7},{7,6},{8,9},{9,8},{10,11... | collective-permute-start | bytes 196616 | tf_op jit(solution)/shard_map/ppermute | solution.py:25
  14.3 6.6 %collective-permute-start.4 = (bf16[128,256]{1,0:T(8,128)(2,1)S(1)}, bf16[128,256]{1,0:T(8,128)(2,1)S(1)}, u32[]{:S(2)}, u32[]{:S(2)}) collective-permute-start(bf16[128,256]{1,0:T(8,128)(2,1)S(1)} %get-tuple-element.44), channel_id=1, source_target_pairs={{0,2},{1,3},{2,0},{3,1},{4,6},{5,7},{6,4},{7,5},{8,10},{9,11},{10,... | collective-permute-start | bytes 196616 | tf_op jit(solution)/shard_map/ppermute | solution.py:25
  16.9 6.1 %collective-permute-start.5 = (bf16[128,256]{1,0:T(8,128)(2,1)S(1)}, bf16[128,256]{1,0:T(8,128)(2,1)S(1)}, u32[]{:S(2)}, u32[]{:S(2)}) collective-permute-start(bf16[128,256]{1,0:T(8,128)(2,1)S(1)} %get-tuple-element.45), channel_id=1, source_target_pairs={{0,3},{1,2},{2,1},{3,0},{4,7},{5,6},{6,5},{7,4},{8,11},{9,10},{10,... | collective-permute-start | bytes 196616 | tf_op jit(solution)/shard_map/ppermute | solution.py:25
  23.2 4.3 %collective-permute-start.6 = (bf16[128,256]{1,0:T(8,128)(2,1)S(1)}, bf16[128,256]{1,0:T(8,128)(2,1)S(1)}, u32[]{:S(2)}, u32[]{:S(2)}) collective-permute-start(bf16[128,256]{1,0:T(8,128)(2,1)S(1)} %get-tuple-element.47.refs_1_), channel_id=1, source_target_pairs={{0,4},{4,0},{8,12},{12,8},{1,5},{5,1},{9,13},{13,9},{2,6},{6,2},{1... | collective-permute-start | bytes 196616 | tf_op jit(solution)/shard_map/ppermute | solution.py:25
  23.8 4.3 %collective-permute-start.7 = (bf16[128,256]{1,0:T(8,128)(2,1)S(1)}, bf16[128,256]{1,0:T(8,128)(2,1)S(1)}, u32[]{:S(2)}, u32[]{:S(2)}) collective-permute-start(bf16[128,256]{1,0:T(8,128)(2,1)S(1)} %get-tuple-element.47.refs_1_), channel_id=1, source_target_pairs={{0,8},{4,12},{8,0},{12,4},{1,9},{5,13},{9,1},{13,5},{2,10},{6,14},... | collective-permute-start | bytes 196616 | tf_op jit(solution)/shard_map/ppermute | solution.py:25
  25.2 5.2 %collective-permute-start.8 = (bf16[128,256]{1,0:T(8,128)(2,1)S(1)}, bf16[128,256]{1,0:T(8,128)(2,1)S(1)}, u32[]{:S(2)}, u32[]{:S(2)}) collective-permute-start(bf16[128,256]{1,0:T(8,128)(2,1)S(1)} %get-tuple-element.47.refs_1_), channel_id=1, source_target_pairs={{0,12},{4,8},{8,4},{12,0},{1,13},{5,9},{9,5},{13,1},{2,14},{6,10},... | collective-permute-start | bytes 196616 | tf_op jit(solution)/shard_map/ppermute | solution.py:25
  32.5 4.6 %collective-permute-start.10 = (bf16[128,128]{1,0:T(8,128)(2,1)S(1)}, bf16[128,128]{1,0:T(8,128)(2,1)S(1)}, u32[]{:S(2)}, u32[]{:S(2)}) collective-permute-start(bf16[128,128]{1,0:T(8,128)(2,1)S(1)} %get-tuple-element.53), channel_id=1, source_target_pairs={{0,1},{1,0},{2,3},{3,2},{4,5},{5,4},{6,7},{7,6},{8,9},{9,8},{10,11... | collective-permute-start | bytes 98312 | tf_op jit(solution)/shard_map/ppermute | solution.py:25
  32.6 5.4 %collective-permute-start.11 = (bf16[128,128]{1,0:T(8,128)(2,1)S(1)}, bf16[128,128]{1,0:T(8,128)(2,1)S(1)}, u32[]{:S(2)}, u32[]{:S(2)}) collective-permute-start(bf16[128,128]{1,0:T(8,128)(2,1)S(1)} %get-tuple-element.54), channel_id=1, source_target_pairs={{0,2},{1,3},{2,0},{3,1},{4,6},{5,7},{6,4},{7,5},{8,10},{9,11},{10,... | collective-permute-start | bytes 98312 | tf_op jit(solution)/shard_map/ppermute | solution.py:25
  34.1 5.7 %collective-permute-start.12 = (bf16[128,128]{1,0:T(8,128)(2,1)S(1)}, bf16[128,128]{1,0:T(8,128)(2,1)S(1)}, u32[]{:S(2)}, u32[]{:S(2)}) collective-permute-start(bf16[128,128]{1,0:T(8,128)(2,1)S(1)} %get-tuple-element.55), channel_id=1, source_target_pairs={{0,3},{1,2},{2,1},{3,0},{4,7},{5,6},{6,5},{7,4},{8,11},{9,10},{10,... | collective-permute-start | bytes 98312 | tf_op jit(solution)/shard_map/ppermute | solution.py:25
  40.2 4.5 %collective-permute-start.13 = (bf16[128,128]{1,0:T(8,128)(2,1)S(1)}, bf16[128,128]{1,0:T(8,128)(2,1)S(1)}, u32[]{:S(2)}, u32[]{:S(2)}) collective-permute-start(bf16[128,128]{1,0:T(8,128)(2,1)S(1)} %get-tuple-element.58.refs_0_), channel_id=1, source_target_pairs={{0,1},{1,0},{2,3},{3,2},{4,5},{5,4},{6,7},{7,6},{8,9},{9,8},{10,11... | collective-permute-start | bytes 98312 | tf_op jit(solution)/shard_map/ppermute | solution.py:25
  40.3 5.3 %collective-permute-start.14 = (bf16[128,128]{1,0:T(8,128)(2,1)S(1)}, bf16[128,128]{1,0:T(8,128)(2,1)S(1)}, u32[]{:S(2)}, u32[]{:S(2)}) collective-permute-start(bf16[128,128]{1,0:T(8,128)(2,1)S(1)} %get-tuple-element.58.refs_0_), channel_id=1, source_target_pairs={{0,2},{1,3},{2,0},{3,1},{4,6},{5,7},{6,4},{7,5},{8,10},{9,11},{10,... | collective-permute-start | bytes 98312 | tf_op jit(solution)/shard_map/ppermute | solution.py:25
  43.7 5.7 %collective-permute-start.15 = (bf16[128,128]{1,0:T(8,128)(2,1)S(1)}, bf16[128,128]{1,0:T(8,128)(2,1)S(1)}, u32[]{:S(2)}, u32[]{:S(2)}) collective-permute-start(bf16[128,128]{1,0:T(8,128)(2,1)S(1)} %get-tuple-element.58.refs_0_), channel_id=1, source_target_pairs={{0,3},{1,2},{2,1},{3,0},{4,7},{5,6},{6,5},{7,4},{8,11},{9,10},{10,... | collective-permute-start | bytes 98312 | tf_op jit(solution)/shard_map/ppermute | solution.py:25
  51.3 4.4 %collective-permute-start.17 = (bf16[128,256]{1,0:T(8,128)(2,1)S(1)}, bf16[128,256]{1,0:T(8,128)(2,1)S(1)}, u32[]{:S(2)}, u32[]{:S(2)}) collective-permute-start(bf16[128,256]{1,0:T(8,128)(2,1)S(1)} %get-tuple-element.60), channel_id=1, source_target_pairs={{0,4},{4,0},{8,12},{12,8},{1,5},{5,1},{9,13},{13,9},{2,6},{6,2},{1... | collective-permute-start | bytes 196616 | tf_op jit(solution)/shard_map/ppermute | solution.py:25
  53.4 5.2 %collective-permute-start.19 = (bf16[128,256]{1,0:T(8,128)(2,1)S(1)}, bf16[128,256]{1,0:T(8,128)(2,1)S(1)}, u32[]{:S(2)}, u32[]{:S(2)}) collective-permute-start(bf16[128,256]{1,0:T(8,128)(2,1)S(1)} %get-tuple-element.62), channel_id=1, source_target_pairs={{0,12},{4,8},{8,4},{12,0},{1,13},{5,9},{9,5},{13,1},{2,14},{6,10},... | collective-permute-start | bytes 196616 | tf_op jit(solution)/shard_map/ppermute | solution.py:25
  58.8 5.7 %collective-permute-start.20 = (bf16[128,256]{1,0:T(8,128)(2,1)S(1)}, bf16[128,256]{1,0:T(8,128)(2,1)S(1)}, u32[]{:S(2)}, u32[]{:S(2)}) collective-permute-start(bf16[128,256]{1,0:T(8,128)(2,1)S(1)} %get-tuple-element.65.refs_1_), channel_id=1, source_target_pairs={{0,1},{1,0},{2,3},{3,2},{4,5},{5,4},{6,7},{7,6},{8,9},{9,8},{10,11... | collective-permute-start | bytes 196616 | tf_op jit(solution)/shard_map/ppermute | solution.py:25
  58.9 5.7 %collective-permute-start.21 = (bf16[128,256]{1,0:T(8,128)(2,1)S(1)}, bf16[128,256]{1,0:T(8,128)(2,1)S(1)}, u32[]{:S(2)}, u32[]{:S(2)}) collective-permute-start(bf16[128,256]{1,0:T(8,128)(2,1)S(1)} %get-tuple-element.65.refs_1_), channel_id=1, source_target_pairs={{0,2},{1,3},{2,0},{3,1},{4,6},{5,7},{6,4},{7,5},{8,10},{9,11},{10,... | collective-permute-start | bytes 196616 | tf_op jit(solution)/shard_map/ppermute | solution.py:25
  60.2 6.1 %collective-permute-start.22 = (bf16[128,256]{1,0:T(8,128)(2,1)S(1)}, bf16[128,256]{1,0:T(8,128)(2,1)S(1)}, u32[]{:S(2)}, u32[]{:S(2)}) collective-permute-start(bf16[128,256]{1,0:T(8,128)(2,1)S(1)} %get-tuple-element.65.refs_1_), channel_id=1, source_target_pairs={{0,3},{1,2},{2,1},{3,0},{4,7},{5,6},{6,5},{7,4},{8,11},{9,10},{10,... | collective-permute-start | bytes 196616 | tf_op jit(solution)/shard_map/ppermute | solution.py:25
  63.3 7.7 %collective-permute-start.26 = (f32[128,128]{1,0:T(8,128)S(1)}, f32[128,128]{1,0:T(8,128)S(1)}, u32[]{:S(2)}, u32[]{:S(2)}) collective-permute-start(f32[128,128]{1,0:T(8,128)S(1)} %get-tuple-element.74.mine_ref), channel_id=1, source_target_pairs={{0,16},{16,0},{1,17},{17,1},{2,18},{18,2},{3,19},{19,3},{4,20},{20... | collective-permute-start | bytes 196616 | tf_op jit(solution)/shard_map/ppermute | solution.py:25
  66.7 5.6 %collective-permute-start.23 = (bf16[128,256]{1,0:T(8,128)(2,1)S(1)}, bf16[128,256]{1,0:T(8,128)(2,1)S(1)}, u32[]{:S(2)}, u32[]{:S(2)}) collective-permute-start(bf16[128,256]{1,0:T(8,128)(2,1)S(1)} %get-tuple-element.68), channel_id=1, source_target_pairs={{0,4},{4,0},{8,12},{12,8},{1,5},{5,1},{9,13},{13,9},{2,6},{6,2},{1... | collective-permute-start | bytes 196616 | tf_op jit(solution)/shard_map/ppermute | solution.py:25
  67.4 4.9 %collective-permute-start.24 = (bf16[128,256]{1,0:T(8,128)(2,1)S(1)}, bf16[128,256]{1,0:T(8,128)(2,1)S(1)}, u32[]{:S(2)}, u32[]{:S(2)}) collective-permute-start(bf16[128,256]{1,0:T(8,128)(2,1)S(1)} %get-tuple-element.69), channel_id=1, source_target_pairs={{0,8},{4,12},{8,0},{12,4},{1,9},{5,13},{9,1},{13,5},{2,10},{6,14},... | collective-permute-start | bytes 196616 | tf_op jit(solution)/shard_map/ppermute | solution.py:25
  68.9 5.2 %collective-permute-start.25 = (bf16[128,256]{1,0:T(8,128)(2,1)S(1)}, bf16[128,256]{1,0:T(8,128)(2,1)S(1)}, u32[]{:S(2)}, u32[]{:S(2)}) collective-permute-start(bf16[128,256]{1,0:T(8,128)(2,1)S(1)} %get-tuple-element.70), channel_id=1, source_target_pairs={{0,12},{4,8},{8,4},{12,0},{1,13},{5,9},{9,5},{13,1},{2,14},{6,10},... | collective-permute-start | bytes 196616 | tf_op jit(solution)/shard_map/ppermute | solution.py:25
  (15 other events, 51.5 us)

commit v4 on v3

--- a/solution.py
+++ b/solution.py
@@ -8,33 +8,36 @@
 BF = jnp.bfloat16
 F32 = jnp.float32
 VMEM = pl.BlockSpec(memory_space=pltpu.VMEM)
-HBM = pl.BlockSpec(memory_space=pltpu.HBM)
 
 
 def is_direct(n):
     return n in (1, 2, 4)
 
 
-def swap_all(blocks, axis, n):
-    steps = (2, 1, 3) if axis == "col" and n == 4 else range(1, n)
-    got = {d: swap(blocks[d], axis, n, d) for d in steps}
-    return [got[d] for d in range(1, n)]
-
-
 def swap(values, axis, n, step):
     return lax.ppermute(values, axis, [(i, i ^ step) for i in range(n)])
 
 
-def gather(values, axis, n):
+def swap_cross(values, axis, n, step):
+    pairs = [(s * n + i, (1 - s) * n + (i ^ step)) for s in range(2) for i in range(n)]
+    return lax.ppermute(values, ("sec", axis), pairs)
+
+
+def gather(values, axis, n, step_to=swap):
     if is_direct(n):
-        return [values] + swap_all([values] * n, axis, n)
+        return [values] + [step_to(values, axis, n, d) for d in range(1, n)]
     return [lax.all_gather(values, axis, axis=0, tiled=True)]
 
 
-def scatter_sum(blocks, axis, n):
+def scatter_sum(blocks, axis, n, step_to=swap):
     if is_direct(n):
-        return [blocks[0]] + swap_all(blocks, axis, n)
+        return [blocks[0]] + [step_to(blocks[d], axis, n, d) for d in range(1, n)]
     return [lax.psum_scatter(blocks[0], axis, scatter_dimension=0, tiled=True)]
+
+
+def own_half(n_col):
+    sec = lax.axis_index("sec")
+    return 1 - sec if is_direct(n_col) else sec
 
 
 def nbytes(shape, dtype):
@@ -44,14 +47,14 @@
     return size
 
 
-def call(kernel, outs, args, scratch=(), flops=0, in_specs=None, sems=0):
+def call(kernel, outs, args, scratch=(), flops=0):
     total = sum(nbytes(s, t) for s, t in list(outs) + list(scratch)) + sum(nbytes(a.shape, a.dtype) for a in args)
     return pl.pallas_call(
         kernel,
         out_shape=tuple(jax.ShapeDtypeStruct(s, t) for s, t in outs),
-        in_specs=in_specs or [VMEM] * len(args),
+        in_specs=[VMEM] * len(args),
         out_specs=(VMEM,) * len(outs),
-        scratch_shapes=[pltpu.VMEM(s, t) for s, t in scratch] + ([pltpu.SemaphoreType.DMA((sems,))] if sems else []),
+        scratch_shapes=[pltpu.VMEM(s, t) for s, t in scratch],
         compiler_params=pltpu.CompilerParams(vmem_limit_bytes=total + (6 << 20)),
         cost_estimate=pl.CostEstimate(flops=flops, bytes_accessed=total, transcendentals=0),
     )(*args)
@@ -121,33 +124,9 @@
 
 
 def leaf_first(leaf_inv, leaf_rhs):
-    count, width, cols = leaf_rhs.shape
-
-    def kernel(inv_hbm, rhs_hbm, y_ref, yb_ref, inv_ref, rhs_ref, sems):
-        copies = [
-            pltpu.make_async_copy(inv_hbm, inv_ref, sems.at[0]),
-            pltpu.make_async_copy(rhs_hbm, rhs_ref, sems.at[1]),
-        ]
-        for copy in copies:
-            copy.start()
-        for copy in copies:
-            copy.wait()
-        for m in range(count):
-            high, low = split(inv_ref[m])
-            rhs = rhs_ref[m]
-            y = dot(jnp.concatenate([high, low], axis=1), jnp.concatenate([rhs, rhs], axis=0))
-            y_ref[pl.ds(m * width, width), :] = y
-            yb_ref[pl.ds(m * width, width), :] = y.astype(BF)
-
-    shape = (count * width, cols)
-    return call(
-        kernel,
-        [(shape, F32), (shape, BF)],
-        [leaf_inv, leaf_rhs],
-        scratch=[(leaf_inv.shape, F32), (leaf_rhs.shape, BF)],
-        in_specs=[HBM] * 2,
-        sems=2,
-    )
+    y = jnp.einsum("mab,mbn->man", leaf_inv, leaf_rhs.astype(F32), precision=lax.Precision.HIGHEST)
+    y = y.reshape(-1, leaf_rhs.shape[2])
+    return y, y.astype(BF)
 
 
 def mask_tiles(tile_sets, masks, width):
@@ -155,43 +134,26 @@
     n_col = masks[0].shape[0]
 
     def kernel(*refs):
-        masks_hbm, tile_refs, outs = refs[:count], refs[count : 2 * count], refs[2 * count : 3 * count]
-        mask_refs, sems = refs[3 * count : 4 * count], refs[4 * count]
-        copies = [pltpu.make_async_copy(masks_hbm[i], mask_refs[i], sems.at[i]) for i in range(count)]
-        for copy in copies:
-            copy.start()
-        for copy in copies:
-            copy.wait()
+        mask_refs, tile_refs, outs = refs[:count], refs[count : 2 * count], refs[2 * count :]
         for i in range(count):
             for k in range(masks[i].shape[2]):
                 weight = jnp.broadcast_to(mask_refs[i][:, :, k : k + 1].astype(F32), (n_col, 1, width)).astype(BF)
                 lanes = pl.ds(k * width, width)
                 outs[i][:, :, lanes] = tile_refs[i][:, :, lanes] * weight
 
-    return call(
-        kernel,
-        [(t.shape, BF) for t in tile_sets],
-        [*masks, *tile_sets],
-        scratch=[(m.shape, m.dtype) for m in masks],
-        in_specs=[HBM] * count + [VMEM] * count,
-        sems=count,
-    )
-
-
-def split_inverse(inverse):
+    return call(kernel, [(t.shape, BF) for t in tile_sets], [*masks, *tile_sets])
+
+
+def split_inverse(inverse, transposed):
     blocks, width = inverse.shape[:2]
 
-    def kernel(inv_ref, low_ref, up_ref):
+    def kernel(inv_ref, out_ref):
         for m in range(blocks):
-            value = inv_ref[m]
-            for out_ref, part in ((low_ref, value), (up_ref, value.T)):
-                high, low = split(part)
-                out_ref[m, :, pl.ds(0, width)] = high
-                out_ref[m, :, pl.ds(width, width)] = low
-                out_ref[m, :, pl.ds(2 * width, width)] = high
-
-    shape = (blocks, width, 3 * width)
-    return call(kernel, [(shape, BF), (shape, BF)], [inverse])
+            high, low = split(inv_ref[m].T if transposed else inv_ref[m])
+            for k, part in enumerate((high, low, high)):
+                out_ref[m, :, pl.ds(k * width, width)] = part
+
+    return call(kernel, [((blocks, width, 3 * width), BF)], [inverse])[0]
 
 
 def keep(values):
@@ -241,29 +203,30 @@
     return call(kernel, [(shape, F32), (shape, BF)], [*sums, right_side, inverse])
 
 
-def top_halves(tiles, pieces, leaf_part, n_row):
+def top_half(tiles, pieces, leaf_part, n_row, n_col, width, passed):
     cols = pieces[0].shape[1]
     half = cols // 2
     count = len(pieces)
 
     def kernel(*refs):
         tile_ref, piece_refs = refs[0], refs[1 : 1 + count]
-        part_ref, mine_ref, other_ref, buf = refs[1 + count :]
+        part_ref, out_ref, buf = refs[1 + count :]
         lay_out(piece_refs, buf, n_row, "row")
         sec = lax.axis_index("sec")
-        for out_ref, which in ((other_ref, 1 - sec), (mine_ref, sec)):
-            columns = rows(which, half)
-            out = part_ref[:, columns] + dot(tile_ref[...], buf[:, columns])
-            out_ref[...] = out.astype(out_ref.dtype)
-
-    shape = (tiles.shape[0], half)
+        columns = rows(1 - sec if passed else sec, half)
+        out_ref[...] = part_ref[:, columns] + dot(tile_ref[...], buf[:, columns])
+        if is_direct(n_col):
+            own = rows(lax.axis_index("col"), width)
+            columns = rows(sec if passed else 1 - sec, half)
+            out_ref[own, :] = part_ref[own, columns] + dot(tile_ref[own, :], buf[:, columns])
+
     return call(
         kernel,
-        [(shape, F32), (shape, F32)],
+        [((tiles.shape[0], half), F32)],
         [tiles, *pieces, leaf_part],
         scratch=[((tiles.shape[1], cols), BF)],
-        flops=2 * tiles.shape[0] * tiles.shape[1] * cols,
-    )
+        flops=tiles.shape[0] * tiles.shape[1] * cols,
+    )[0]
 
 
 def add_sections(mine, other, n_col, width):
@@ -275,13 +238,13 @@
     return call(kernel, block_outs(n_col, width, half), [mine, other])
 
 
-def solve_top(sums, right_side, lower, upper):
+def solve_top(sums, right_side, lower, upper, n_col):
     count = len(sums)
     half = right_side.shape[1] // 2
 
     def kernel(*refs):
         rhs_ref, low_ref, up_ref, x_ref, xb_ref = refs[count:]
-        mine = rhs_ref[:, rows(lax.axis_index("sec"), half)].astype(F32)
+        mine = rhs_ref[:, rows(own_half(n_col), half)].astype(F32)
         y = apply_split(low_ref[0], mine - total_of(refs[:count]))
         x = apply_split(up_ref[0], y)
         x_ref[...] = x
@@ -302,18 +265,18 @@
     return call(kernel, [(shape, BF)], list(pieces))[0]
 
 
-def join_halves(mine, other):
+def join_halves(mine, other, n_col):
     half = mine.shape[1]
 
     def kernel(mine_ref, other_ref, out_ref):
-        sec = lax.axis_index("sec")
-        out_ref[:, rows(sec, half)] = mine_ref[...]
-        out_ref[:, rows(1 - sec, half)] = other_ref[...]
+        own = own_half(n_col)
+        out_ref[:, rows(own, half)] = mine_ref[...]
+        out_ref[:, rows(1 - own, half)] = other_ref[...]
 
     return call(kernel, [((mine.shape[0], 2 * half), mine.dtype)], [mine, other])[0]
 
 
-def top_back_blocks(tiles, mine, other, n_row, width):
+def top_back_blocks(tiles, mine, other, n_row, n_col, width):
     half = mine.shape[1]
 
     def kernel(tile_ref, mine_ref, other_ref, *outs):
@@ -321,6 +284,10 @@
         sec = lax.axis_index("sec")
         buf[:, rows(sec, half)] = mine_ref[...]
         buf[:, rows(1 - sec, half)] = other_ref[...]
+        if is_direct(n_col):
+            own = rows(lax.axis_index("col"), width)
+            buf[own, rows(1 - sec, half)] = mine_ref[own, :]
+            buf[own, rows(sec, half)] = other_ref[own, :]
         emit_blocks(lambda i: dot_t(tile_ref[:, rows(i, width)], buf[...]), outs[:-1], n_row, "row")
 
     outs = block_outs(n_row, width, 2 * half) + [((mine.shape[0], 2 * half), BF)]
@@ -393,26 +360,26 @@
             width,
         )
         sl, tl, ts = [values.reshape(n_col * width, -1) for values in masked]
-        leaf_low, leaf_up = split_inverse(leaf_inv[0, 0, :, 0])
-        sep_low, sep_up = split_inverse(sep_inv[0, 0])
-        top_low, top_up = split_inverse(top_inv[0])
         blocks, leaf_col = forward_blocks(sl, leaf_pieces, n_row, n_col, width)
         sums = scatter_sum(blocks, "col", n_col)
         leaf_part = plain_product(tl, leaf_col, False)
-        sep_y, sep_yb = solve_forward(sums, sep_rhs[0, 0, 0], sep_low)
-        mine, other = top_halves(ts, gather(sep_yb, "row", n_row), leaf_part, n_row)
-        blocks = add_sections(mine, swap(other, "sec", 2, 1), n_col, width)
-        sums = scatter_sum(blocks, "col", n_col)
-        top_xh, top_xhb = solve_top(sums, top_rhs[0, 0], top_low, top_up)
-        top_stack = stack_pieces(gather(top_xhb, "col", n_col), n_col, "col")
-        blocks, top_row = top_back_blocks(ts, top_stack, swap(top_stack, "sec", 2, 1), n_row, width)
+        sep_y, sep_yb = solve_forward(sums, sep_rhs[0, 0, 0], split_inverse(sep_inv[0, 0], False))
+        pieces = gather(sep_yb, "row", n_row)
+        passed = swap(top_half(ts, pieces, leaf_part, n_row, n_col, width, True), "sec", 2, 1)
+        kept = top_half(ts, pieces, leaf_part, n_row, n_col, width, False)
+        blocks = add_sections(kept, passed, n_col, width)
+        sums = scatter_sum(blocks, "col", n_col, swap_cross)
+        lower, upper = split_inverse(top_inv[0], False), split_inverse(top_inv[0], True)
+        top_xh, top_xhb = solve_top(sums, top_rhs[0, 0], lower, upper, n_col)
+        top_stack = stack_pieces(gather(top_xhb, "col", n_col, swap_cross), n_col, "col")
+        blocks, top_row = top_back_blocks(ts, top_stack, swap(top_stack, "sec", 2, 1), n_row, n_col, width)
         sums = scatter_sum(blocks, "row", n_row)
         top_part = plain_product(tl, top_row, True)
-        top_x = join_halves(top_xh, swap(top_xh, "sec", 2, 1))
-        sep_x, sep_xb = solve_back(sums, sep_y, sep_up)
+        top_x = join_halves(top_xh, swap(top_xh, "sec", 2, 1), n_col)
+        sep_x, sep_xb = solve_back(sums, sep_y, split_inverse(sep_inv[0, 0], True))
         pieces = gather(sep_xb, "col", n_col)
         sums = scatter_sum(back_blocks(sl, pieces, top_part, n_row, n_col, span), "row", n_row)
-        leaf_x = solve_last(sums, leaf_y, leaf_up)
+        leaf_x = solve_last(sums, leaf_y, split_inverse(leaf_inv[0, 0, :, 0], True))
         return (
             leaf_x.reshape(1, 1, leaf_count, 1, width, cols),
             keep(sep_x)[None, None, None],

time: 75.3 us -> 73.2 us (0.972)
  matrix products: 0 us -> 1.04 us
  local copies, waits for them, and re-layouts: 4.86 us -> 4.02 us
  starting transfers between devices: 33.1 us -> 32.3 us
    ppermute x27 -> x21, starting transfers between devices: 33.1 us -> 24.4 us  [swap(): return lax.ppermute(values, axis, [(i, i ^ step) for i in range(n)])]
    ppermute x0 -> x6, starting transfers between devices: none -> 7.86 us  [swap_cross(): return lax.ppermute(values, ('sec', axis), pairs)]
    ppermute x27 -> x21, waiting for transfers between devices: 29.2 us -> 21.7 us  [swap(): return lax.ppermute(values, axis, [(i, i ^ step) for i in range(n)])]
    ppermute x0 -> x6, waiting for transfers between devices: none -> 6.81 us  [swap_cross(): return lax.ppermute(values, ('sec', axis), pairs)]
    dot_general x0 -> x1, matrix products: none -> 1.04 us  [leaf_first(): jnp.einsum('mab,mbn->man', leaf_inv, leaf_rhs.astype(F32), precision=lax....]
    unnamed x24 -> x22, local copies, waits for them, and re-layouts: 3.22 us -> 2.39 us
    pallas_call x19 -> x21, Pallas kernels: 6.8 us -> 6.12 us  [call(): pl.pallas_call(kernel, out_shape=tuple((jax.ShapeDtypeStruct(s, t) for s,...]
where the time goes in v4:
time: 73.2 us; the launch traced here: 72.9 us
  starting transfers between devices  32.3 us (44%)
  waiting for transfers between devices  28.5 us (39%)
  Pallas kernels  6.12 us (8%)
  local copies, waits for them, and re-layouts  4.02 us (5%)
  matrix products  1.04 us (1%)
  between operations  0.93 us (1%)
    ppermute x21, starting transfers between devices, swap(): return lax.ppermute(values, axis, [(i, i ^ step) for i in range(n)])  24.4 us
    ppermute x21, waiting for transfers between devices, swap(): return lax.ppermute(values, axis, [(i, i ^ step) for i in range(n)])  21.7 us
    ppermute x6, starting transfers between devices, swap_cross(): return lax.ppermute(values, ('sec', axis), pairs)  7.86 us
    ppermute x6, waiting for transfers between devices, swap_cross(): return lax.ppermute(values, ('sec', axis), pairs)  6.81 us
    pallas_call x21, Pallas kernels, call(): pl.pallas_call(kernel, out_shape=tuple((jax.ShapeDtypeStruct(s, t) for s,...  6.12 us
    unnamed x22, local copies, waits for them, and re-layouts  2.39 us
    reshape x3, local copies, waits for them, and re-layouts, body(): values.reshape(n_col, width, -1)  1.64 us
  transfers between devices with their start and end apart: 27, of which 18 were waited for; matrix products, arithmetic and copies ran while one was open for 2% of the time, Pallas kernels for 5%

profile of v4, /device:TPU:0, one launch (start us, length us, event | category | flops | bytes accessed | tf_op | source)
XLA Modules:
  0.0 72.9 jit_solution(5881853844018811873)
XLA Ops:
  2.5 3.0 %collective-permute-start = (bf16[128,256]{1,0:T(8,128)(2,1)S(1)}, bf16[128,256]{1,0:T(8,128)(2,1)S(1)}, u32[]{:S(2)}, u32[]{:S(2)}) collective-permute-start(bf16[128,256]{1,0:T(8,128)(2,1)S(1)} %get-tuple-element.57.refs_1_), channel_id=1, source_target_pairs={{0,4},{4,0},{8,12},{12,8},{1,5},{5,1},{9,13},{13,9},{2,6},{6,2},{1... | collective-permute-start | bytes 196616 | tf_op jit(solution)/shard_map/ppermute | solution.py:18
  5.5 1.5 %collective-permute-start.1 = (bf16[128,256]{1,0:T(8,128)(2,1)S(1)}, bf16[128,256]{1,0:T(8,128)(2,1)S(1)}, u32[]{:S(2)}, u32[]{:S(2)}) collective-permute-start(bf16[128,256]{1,0:T(8,128)(2,1)S(1)} %get-tuple-element.57.refs_1_), channel_id=1, source_target_pairs={{0,8},{4,12},{8,0},{12,4},{1,9},{5,13},{9,1},{13,5},{2,10},{6,14},... | collective-permute-start | bytes 196616 | tf_op jit(solution)/shard_map/ppermute | solution.py:18
  7.1 1.2 %reshape.50.refs_3_ = bf16[4,128,512]{2,1,0:T(8,128)(2,1)S(1)} reshape(bf16[1,1,4,128,4,1,1,128]{7,4,6,5,3,2,1,0:T(4,128)(2,1)} %param.18) | data formatting | bytes 1048576 | tf_op jit(solution)/shard_map/reshape | solution.py:358
  10.7 1.6 %collective-permute-done.2.refs_4_ = bf16[128,256]{1,0:T(8,128)(2,1)S(1)} collective-permute-done((bf16[128,256]{1,0:T(8,128)(2,1)S(1)}, bf16[128,256]{1,0:T(8,128)(2,1)S(1)}, u32[]{:S(2)}, u32[]{:S(2)}) %collective-permute-start.2) | collective-permute-done | bytes 65568 | tf_op jit(solution)/shard_map/ppermute | solution.py:18
  12.6 1.6 %collective-permute-start.3 = (bf16[128,256]{1,0:T(8,128)(2,1)S(1)}, bf16[128,256]{1,0:T(8,128)(2,1)S(1)}, u32[]{:S(2)}, u32[]{:S(2)}) collective-permute-start(bf16[128,256]{1,0:T(8,128)(2,1)S(1)} %get-tuple-element.33), channel_id=1, source_target_pairs={{0,1},{1,0},{2,3},{3,2},{4,5},{5,4},{6,7},{7,6},{8,9},{9,8},{10,11... | collective-permute-start | bytes 196616 | tf_op jit(solution)/shard_map/ppermute | solution.py:18
  14.2 2.6 %collective-permute-start.4 = (bf16[128,256]{1,0:T(8,128)(2,1)S(1)}, bf16[128,256]{1,0:T(8,128)(2,1)S(1)}, u32[]{:S(2)}, u32[]{:S(2)}) collective-permute-start(bf16[128,256]{1,0:T(8,128)(2,1)S(1)} %get-tuple-element.34), channel_id=1, source_target_pairs={{0,2},{1,3},{2,0},{3,1},{4,6},{5,7},{6,4},{7,5},{8,10},{9,11},{10,... | collective-permute-start | bytes 196616 | tf_op jit(solution)/shard_map/ppermute | solution.py:18
  17.0 3.7 %collective-permute-done.4.refs_2_ = bf16[128,256]{1,0:T(8,128)(2,1)S(1)} collective-permute-done((bf16[128,256]{1,0:T(8,128)(2,1)S(1)}, bf16[128,256]{1,0:T(8,128)(2,1)S(1)}, u32[]{:S(2)}, u32[]{:S(2)}) %collective-permute-start.4) | collective-permute-done | bytes 65568 | tf_op jit(solution)/shard_map/ppermute | solution.py:18
  20.8 2.1 %collective-permute-done.5.refs_3_ = bf16[128,256]{1,0:T(8,128)(2,1)S(1)} collective-permute-done((bf16[128,256]{1,0:T(8,128)(2,1)S(1)}, bf16[128,256]{1,0:T(8,128)(2,1)S(1)}, u32[]{:S(2)}, u32[]{:S(2)}) %collective-permute-start.5) | collective-permute-done | bytes 65568 | tf_op jit(solution)/shard_map/ppermute | solution.py:18
  23.7 1.4 %collective-permute-start.7 = (bf16[128,256]{1,0:T(8,128)(2,1)S(1)}, bf16[128,256]{1,0:T(8,128)(2,1)S(1)}, u32[]{:S(2)}, u32[]{:S(2)}) collective-permute-start(bf16[128,256]{1,0:T(8,128)(2,1)S(1)} %get-tuple-element.36.refs_1_), channel_id=1, source_target_pairs={{0,8},{4,12},{8,0},{12,4},{1,9},{5,13},{9,1},{13,5},{2,10},{6,14},... | collective-permute-start | bytes 196616 | tf_op jit(solution)/shard_map/ppermute | solution.py:18
  25.1 1.6 %collective-permute-start.8 = (bf16[128,256]{1,0:T(8,128)(2,1)S(1)}, bf16[128,256]{1,0:T(8,128)(2,1)S(1)}, u32[]{:S(2)}, u32[]{:S(2)}) collective-permute-start(bf16[128,256]{1,0:T(8,128)(2,1)S(1)} %get-tuple-element.36.refs_1_), channel_id=1, source_target_pairs={{0,12},{4,8},{8,4},{12,0},{1,13},{5,9},{9,5},{13,1},{2,14},{6,10},... | collective-permute-start | bytes 196616 | tf_op jit(solution)/shard_map/ppermute | solution.py:18
  27.9 2.3 %collective-permute-done.8.refs_4_ = bf16[128,256]{1,0:T(8,128)(2,1)S(1)} collective-permute-done((bf16[128,256]{1,0:T(8,128)(2,1)S(1)}, bf16[128,256]{1,0:T(8,128)(2,1)S(1)}, u32[]{:S(2)}, u32[]{:S(2)}) %collective-permute-start.8) | collective-permute-done | bytes 65568 | tf_op jit(solution)/shard_map/ppermute | solution.py:18
  33.5 2.6 %collective-permute-start.12 = (bf16[128,128]{1,0:T(8,128)(2,1)S(1)}, bf16[128,128]{1,0:T(8,128)(2,1)S(1)}, u32[]{:S(2)}, u32[]{:S(2)}) collective-permute-start(bf16[128,128]{1,0:T(8,128)(2,1)S(1)} %get-tuple-element.42), channel_id=1, source_target_pairs={{0,19},{1,18},{2,17},{3,16},{16,3},{17,2},{18,1},{19,0},{4,23},{5,... | collective-permute-start | bytes 98312 | tf_op jit(solution)/shard_map/ppermute | solution.py:23
  36.7 2.1 %collective-permute-done.12.refs_3_ = bf16[128,128]{1,0:T(8,128)(2,1)S(1)} collective-permute-done((bf16[128,128]{1,0:T(8,128)(2,1)S(1)}, bf16[128,128]{1,0:T(8,128)(2,1)S(1)}, u32[]{:S(2)}, u32[]{:S(2)}) %collective-permute-start.12) | collective-permute-done | bytes 32800 | tf_op jit(solution)/shard_map/ppermute | solution.py:23
  39.7 2.5 %collective-permute-start.14 = (bf16[128,128]{1,0:T(8,128)(2,1)S(1)}, bf16[128,128]{1,0:T(8,128)(2,1)S(1)}, u32[]{:S(2)}, u32[]{:S(2)}) collective-permute-start(bf16[128,128]{1,0:T(8,128)(2,1)S(1)} %get-tuple-element.43.refs_0_), channel_id=1, source_target_pairs={{0,18},{1,19},{2,16},{3,17},{16,2},{17,3},{18,0},{19,1},{4,22},{5,... | collective-permute-start | bytes 98312 | tf_op jit(solution)/shard_map/ppermute | solution.py:23
  44.1 3.3 %collective-permute-done.15.refs_3_ = bf16[128,128]{1,0:T(8,128)(2,1)S(1)} collective-permute-done((bf16[128,128]{1,0:T(8,128)(2,1)S(1)}, bf16[128,128]{1,0:T(8,128)(2,1)S(1)}, u32[]{:S(2)}, u32[]{:S(2)}) %collective-permute-start.15) | collective-permute-done | bytes 32800 | tf_op jit(solution)/shard_map/ppermute | solution.py:23
  49.9 1.5 %collective-permute-start.18 = (bf16[128,256]{1,0:T(8,128)(2,1)S(1)}, bf16[128,256]{1,0:T(8,128)(2,1)S(1)}, u32[]{:S(2)}, u32[]{:S(2)}) collective-permute-start(bf16[128,256]{1,0:T(8,128)(2,1)S(1)} %get-tuple-element.46), channel_id=1, source_target_pairs={{0,8},{4,12},{8,0},{12,4},{1,9},{5,13},{9,1},{13,5},{2,10},{6,14},... | collective-permute-start | bytes 196616 | tf_op jit(solution)/shard_map/ppermute | solution.py:18
  51.5 1.3 %collective-permute-start.19 = (bf16[128,256]{1,0:T(8,128)(2,1)S(1)}, bf16[128,256]{1,0:T(8,128)(2,1)S(1)}, u32[]{:S(2)}, u32[]{:S(2)}) collective-permute-start(bf16[128,256]{1,0:T(8,128)(2,1)S(1)} %get-tuple-element.47), channel_id=1, source_target_pairs={{0,12},{4,8},{8,4},{12,0},{1,13},{5,9},{9,5},{13,1},{2,14},{6,10},... | collective-permute-start | bytes 196616 | tf_op jit(solution)/shard_map/ppermute | solution.py:18
  54.2 2.4 %collective-permute-done.19.refs_3_ = bf16[128,256]{1,0:T(8,128)(2,1)S(1)} collective-permute-done((bf16[128,256]{1,0:T(8,128)(2,1)S(1)}, bf16[128,256]{1,0:T(8,128)(2,1)S(1)}, u32[]{:S(2)}, u32[]{:S(2)}) %collective-permute-start.19) | collective-permute-done | bytes 65568 | tf_op jit(solution)/shard_map/ppermute | solution.py:18
  56.9 1.7 %collective-permute-start.21 = (bf16[128,256]{1,0:T(8,128)(2,1)S(1)}, bf16[128,256]{1,0:T(8,128)(2,1)S(1)}, u32[]{:S(2)}, u32[]{:S(2)}) collective-permute-start(bf16[128,256]{1,0:T(8,128)(2,1)S(1)} %get-tuple-element.49.refs_1_), channel_id=1, source_target_pairs={{0,2},{1,3},{2,0},{3,1},{4,6},{5,7},{6,4},{7,5},{8,10},{9,11},{10,... | collective-permute-start | bytes 196616 | tf_op jit(solution)/shard_map/ppermute | solution.py:18
  58.6 2.6 %collective-permute-start.22 = (bf16[128,256]{1,0:T(8,128)(2,1)S(1)}, bf16[128,256]{1,0:T(8,128)(2,1)S(1)}, u32[]{:S(2)}, u32[]{:S(2)}) collective-permute-start(bf16[128,256]{1,0:T(8,128)(2,1)S(1)} %get-tuple-element.49.refs_1_), channel_id=1, source_target_pairs={{0,3},{1,2},{2,1},{3,0},{4,7},{5,6},{6,5},{7,4},{8,11},{9,10},{10,... | collective-permute-start | bytes 196616 | tf_op jit(solution)/shard_map/ppermute | solution.py:18
  62.6 2.1 %collective-permute-done.22.refs_4_ = bf16[128,256]{1,0:T(8,128)(2,1)S(1)} collective-permute-done((bf16[128,256]{1,0:T(8,128)(2,1)S(1)}, bf16[128,256]{1,0:T(8,128)(2,1)S(1)}, u32[]{:S(2)}, u32[]{:S(2)}) %collective-permute-start.22) | collective-permute-done | bytes 65568 | tf_op jit(solution)/shard_map/ppermute | solution.py:18
  65.5 1.4 %collective-permute-start.24 = (bf16[128,256]{1,0:T(8,128)(2,1)S(1)}, bf16[128,256]{1,0:T(8,128)(2,1)S(1)}, u32[]{:S(2)}, u32[]{:S(2)}) collective-permute-start(bf16[128,256]{1,0:T(8,128)(2,1)S(1)} %get-tuple-element.53), channel_id=1, source_target_pairs={{0,8},{4,12},{8,0},{12,4},{1,9},{5,13},{9,1},{13,5},{2,10},{6,14},... | collective-permute-start | bytes 196616 | tf_op jit(solution)/shard_map/ppermute | solution.py:18
  66.9 1.7 %collective-permute-start.25 = (bf16[128,256]{1,0:T(8,128)(2,1)S(1)}, bf16[128,256]{1,0:T(8,128)(2,1)S(1)}, u32[]{:S(2)}, u32[]{:S(2)}) collective-permute-start(bf16[128,256]{1,0:T(8,128)(2,1)S(1)} %get-tuple-element.54), channel_id=1, source_target_pairs={{0,12},{4,8},{8,4},{12,0},{1,13},{5,9},{9,5},{13,1},{2,14},{6,10},... | collective-permute-start | bytes 196616 | tf_op jit(solution)/shard_map/ppermute | solution.py:18
  70.1 2.0 %collective-permute-done.25.refs_3_ = bf16[128,256]{1,0:T(8,128)(2,1)S(1)} collective-permute-done((bf16[128,256]{1,0:T(8,128)(2,1)S(1)}, bf16[128,256]{1,0:T(8,128)(2,1)S(1)}, u32[]{:S(2)}, u32[]{:S(2)}) %collective-permute-start.25) | collective-permute-done | bytes 65568 | tf_op jit(solution)/shard_map/ppermute | solution.py:18
  (77 shorter events, 21.9 us)
Async XLA Ops:
  2.5 8.1 %collective-permute-start = (bf16[128,256]{1,0:T(8,128)(2,1)S(1)}, bf16[128,256]{1,0:T(8,128)(2,1)S(1)}, u32[]{:S(2)}, u32[]{:S(2)}) collective-permute-start(bf16[128,256]{1,0:T(8,128)(2,1)S(1)} %get-tuple-element.57.refs_1_), channel_id=1, source_target_pairs={{0,4},{4,0},{8,12},{12,8},{1,5},{5,1},{9,13},{13,9},{2,6},{6,2},{1... | collective-permute-start | bytes 196616 | tf_op jit(solution)/shard_map/ppermute | solution.py:18
  5.5 5.1 %collective-permute-start.1 = (bf16[128,256]{1,0:T(8,128)(2,1)S(1)}, bf16[128,256]{1,0:T(8,128)(2,1)S(1)}, u32[]{:S(2)}, u32[]{:S(2)}) collective-permute-start(bf16[128,256]{1,0:T(8,128)(2,1)S(1)} %get-tuple-element.57.refs_1_), channel_id=1, source_target_pairs={{0,8},{4,12},{8,0},{12,4},{1,9},{5,13},{9,1},{13,5},{2,10},{6,14},... | collective-permute-start | bytes 196616 | tf_op jit(solution)/shard_map/ppermute | solution.py:18
  7.1 5.2 %collective-permute-start.2 = (bf16[128,256]{1,0:T(8,128)(2,1)S(1)}, bf16[128,256]{1,0:T(8,128)(2,1)S(1)}, u32[]{:S(2)}, u32[]{:S(2)}) collective-permute-start(bf16[128,256]{1,0:T(8,128)(2,1)S(1)} %get-tuple-element.57.refs_1_), channel_id=1, source_target_pairs={{0,12},{4,8},{8,4},{12,0},{1,13},{5,9},{9,5},{13,1},{2,14},{6,10},... | collective-permute-start | bytes 196616 | tf_op jit(solution)/shard_map/ppermute | solution.py:18
  12.6 4.5 %collective-permute-start.3 = (bf16[128,256]{1,0:T(8,128)(2,1)S(1)}, bf16[128,256]{1,0:T(8,128)(2,1)S(1)}, u32[]{:S(2)}, u32[]{:S(2)}) collective-permute-start(bf16[128,256]{1,0:T(8,128)(2,1)S(1)} %get-tuple-element.33), channel_id=1, source_target_pairs={{0,1},{1,0},{2,3},{3,2},{4,5},{5,4},{6,7},{7,6},{8,9},{9,8},{10,11... | collective-permute-start | bytes 196616 | tf_op jit(solution)/shard_map/ppermute | solution.py:18
  14.2 6.6 %collective-permute-start.4 = (bf16[128,256]{1,0:T(8,128)(2,1)S(1)}, bf16[128,256]{1,0:T(8,128)(2,1)S(1)}, u32[]{:S(2)}, u32[]{:S(2)}) collective-permute-start(bf16[128,256]{1,0:T(8,128)(2,1)S(1)} %get-tuple-element.34), channel_id=1, source_target_pairs={{0,2},{1,3},{2,0},{3,1},{4,6},{5,7},{6,4},{7,5},{8,10},{9,11},{10,... | collective-permute-start | bytes 196616 | tf_op jit(solution)/shard_map/ppermute | solution.py:18
  16.8 6.1 %collective-permute-start.5 = (bf16[128,256]{1,0:T(8,128)(2,1)S(1)}, bf16[128,256]{1,0:T(8,128)(2,1)S(1)}, u32[]{:S(2)}, u32[]{:S(2)}) collective-permute-start(bf16[128,256]{1,0:T(8,128)(2,1)S(1)} %get-tuple-element.35), channel_id=1, source_target_pairs={{0,3},{1,2},{2,1},{3,0},{4,7},{5,6},{6,5},{7,4},{8,11},{9,10},{10,... | collective-permute-start | bytes 196616 | tf_op jit(solution)/shard_map/ppermute | solution.py:18
  23.1 4.3 %collective-permute-start.6 = (bf16[128,256]{1,0:T(8,128)(2,1)S(1)}, bf16[128,256]{1,0:T(8,128)(2,1)S(1)}, u32[]{:S(2)}, u32[]{:S(2)}) collective-permute-start(bf16[128,256]{1,0:T(8,128)(2,1)S(1)} %get-tuple-element.36.refs_1_), channel_id=1, source_target_pairs={{0,4},{4,0},{8,12},{12,8},{1,5},{5,1},{9,13},{13,9},{2,6},{6,2},{1... | collective-permute-start | bytes 196616 | tf_op jit(solution)/shard_map/ppermute | solution.py:18
  23.7 4.3 %collective-permute-start.7 = (bf16[128,256]{1,0:T(8,128)(2,1)S(1)}, bf16[128,256]{1,0:T(8,128)(2,1)S(1)}, u32[]{:S(2)}, u32[]{:S(2)}) collective-permute-start(bf16[128,256]{1,0:T(8,128)(2,1)S(1)} %get-tuple-element.36.refs_1_), channel_id=1, source_target_pairs={{0,8},{4,12},{8,0},{12,4},{1,9},{5,13},{9,1},{13,5},{2,10},{6,14},... | collective-permute-start | bytes 196616 | tf_op jit(solution)/shard_map/ppermute | solution.py:18
  25.1 5.2 %collective-permute-start.8 = (bf16[128,256]{1,0:T(8,128)(2,1)S(1)}, bf16[128,256]{1,0:T(8,128)(2,1)S(1)}, u32[]{:S(2)}, u32[]{:S(2)}) collective-permute-start(bf16[128,256]{1,0:T(8,128)(2,1)S(1)} %get-tuple-element.36.refs_1_), channel_id=1, source_target_pairs={{0,12},{4,8},{8,4},{12,0},{1,13},{5,9},{9,5},{13,1},{2,14},{6,10},... | collective-permute-start | bytes 196616 | tf_op jit(solution)/shard_map/ppermute | solution.py:18
  32.2 4.1 %collective-permute-start.10 = (bf16[128,128]{1,0:T(8,128)(2,1)S(1)}, bf16[128,128]{1,0:T(8,128)(2,1)S(1)}, u32[]{:S(2)}, u32[]{:S(2)}) collective-permute-start(bf16[128,128]{1,0:T(8,128)(2,1)S(1)} %get-tuple-element.40), channel_id=1, source_target_pairs={{0,17},{1,16},{2,19},{3,18},{16,1},{17,0},{18,3},{19,2},{4,21},{5,... | collective-permute-start | bytes 98312 | tf_op jit(solution)/shard_map/ppermute | solution.py:23
  32.3 4.3 %collective-permute-start.11 = (bf16[128,128]{1,0:T(8,128)(2,1)S(1)}, bf16[128,128]{1,0:T(8,128)(2,1)S(1)}, u32[]{:S(2)}, u32[]{:S(2)}) collective-permute-start(bf16[128,128]{1,0:T(8,128)(2,1)S(1)} %get-tuple-element.41), channel_id=1, source_target_pairs={{0,18},{1,19},{2,16},{3,17},{16,2},{17,3},{18,0},{19,1},{4,22},{5,... | collective-permute-start | bytes 98312 | tf_op jit(solution)/shard_map/ppermute | solution.py:23
  33.5 5.2 %collective-permute-start.12 = (bf16[128,128]{1,0:T(8,128)(2,1)S(1)}, bf16[128,128]{1,0:T(8,128)(2,1)S(1)}, u32[]{:S(2)}, u32[]{:S(2)}) collective-permute-start(bf16[128,128]{1,0:T(8,128)(2,1)S(1)} %get-tuple-element.42), channel_id=1, source_target_pairs={{0,19},{1,18},{2,17},{3,16},{16,3},{17,2},{18,1},{19,0},{4,23},{5,... | collective-permute-start | bytes 98312 | tf_op jit(solution)/shard_map/ppermute | solution.py:23
  39.7 4.4 %collective-permute-start.14 = (bf16[128,128]{1,0:T(8,128)(2,1)S(1)}, bf16[128,128]{1,0:T(8,128)(2,1)S(1)}, u32[]{:S(2)}, u32[]{:S(2)}) collective-permute-start(bf16[128,128]{1,0:T(8,128)(2,1)S(1)} %get-tuple-element.43.refs_0_), channel_id=1, source_target_pairs={{0,18},{1,19},{2,16},{3,17},{16,2},{17,3},{18,0},{19,1},{4,22},{5,... | collective-permute-start | bytes 98312 | tf_op jit(solution)/shard_map/ppermute | solution.py:23
  42.3 5.1 %collective-permute-start.15 = (bf16[128,128]{1,0:T(8,128)(2,1)S(1)}, bf16[128,128]{1,0:T(8,128)(2,1)S(1)}, u32[]{:S(2)}, u32[]{:S(2)}) collective-permute-start(bf16[128,128]{1,0:T(8,128)(2,1)S(1)} %get-tuple-element.43.refs_0_), channel_id=1, source_target_pairs={{0,19},{1,18},{2,17},{3,16},{16,3},{17,2},{18,1},{19,0},{4,23},{5,... | collective-permute-start | bytes 98312 | tf_op jit(solution)/shard_map/ppermute | solution.py:23
  49.2 4.3 %collective-permute-start.17 = (bf16[128,256]{1,0:T(8,128)(2,1)S(1)}, bf16[128,256]{1,0:T(8,128)(2,1)S(1)}, u32[]{:S(2)}, u32[]{:S(2)}) collective-permute-start(bf16[128,256]{1,0:T(8,128)(2,1)S(1)} %get-tuple-element.45), channel_id=1, source_target_pairs={{0,4},{4,0},{8,12},{12,8},{1,5},{5,1},{9,13},{13,9},{2,6},{6,2},{1... | collective-permute-start | bytes 196616 | tf_op jit(solution)/shard_map/ppermute | solution.py:18
  49.9 4.3 %collective-permute-start.18 = (bf16[128,256]{1,0:T(8,128)(2,1)S(1)}, bf16[128,256]{1,0:T(8,128)(2,1)S(1)}, u32[]{:S(2)}, u32[]{:S(2)}) collective-permute-start(bf16[128,256]{1,0:T(8,128)(2,1)S(1)} %get-tuple-element.46), channel_id=1, source_target_pairs={{0,8},{4,12},{8,0},{12,4},{1,9},{5,13},{9,1},{13,5},{2,10},{6,14},... | collective-permute-start | bytes 196616 | tf_op jit(solution)/shard_map/ppermute | solution.py:18
  51.5 5.2 %collective-permute-start.19 = (bf16[128,256]{1,0:T(8,128)(2,1)S(1)}, bf16[128,256]{1,0:T(8,128)(2,1)S(1)}, u32[]{:S(2)}, u32[]{:S(2)}) collective-permute-start(bf16[128,256]{1,0:T(8,128)(2,1)S(1)} %get-tuple-element.47), channel_id=1, source_target_pairs={{0,12},{4,8},{8,4},{12,0},{1,13},{5,9},{9,5},{13,1},{2,14},{6,10},... | collective-permute-start | bytes 196616 | tf_op jit(solution)/shard_map/ppermute | solution.py:18
  56.8 5.7 %collective-permute-start.20 = (bf16[128,256]{1,0:T(8,128)(2,1)S(1)}, bf16[128,256]{1,0:T(8,128)(2,1)S(1)}, u32[]{:S(2)}, u32[]{:S(2)}) collective-permute-start(bf16[128,256]{1,0:T(8,128)(2,1)S(1)} %get-tuple-element.49.refs_1_), channel_id=1, source_target_pairs={{0,1},{1,0},{2,3},{3,2},{4,5},{5,4},{6,7},{7,6},{8,9},{9,8},{10,11... | collective-permute-start | bytes 196616 | tf_op jit(solution)/shard_map/ppermute | solution.py:18
  56.9 5.7 %collective-permute-start.21 = (bf16[128,256]{1,0:T(8,128)(2,1)S(1)}, bf16[128,256]{1,0:T(8,128)(2,1)S(1)}, u32[]{:S(2)}, u32[]{:S(2)}) collective-permute-start(bf16[128,256]{1,0:T(8,128)(2,1)S(1)} %get-tuple-element.49.refs_1_), channel_id=1, source_target_pairs={{0,2},{1,3},{2,0},{3,1},{4,6},{5,7},{6,4},{7,5},{8,10},{9,11},{10,... | collective-permute-start | bytes 196616 | tf_op jit(solution)/shard_map/ppermute | solution.py:18
  58.6 6.1 %collective-permute-start.22 = (bf16[128,256]{1,0:T(8,128)(2,1)S(1)}, bf16[128,256]{1,0:T(8,128)(2,1)S(1)}, u32[]{:S(2)}, u32[]{:S(2)}) collective-permute-start(bf16[128,256]{1,0:T(8,128)(2,1)S(1)} %get-tuple-element.49.refs_1_), channel_id=1, source_target_pairs={{0,3},{1,2},{2,1},{3,0},{4,7},{5,6},{6,5},{7,4},{8,11},{9,10},{10,... | collective-permute-start | bytes 196616 | tf_op jit(solution)/shard_map/ppermute | solution.py:18
  61.3 7.4 %collective-permute-start.26 = (f32[128,128]{1,0:T(8,128)S(1)}, f32[128,128]{1,0:T(8,128)S(1)}, u32[]{:S(2)}, u32[]{:S(2)}) collective-permute-start(f32[128,128]{1,0:T(8,128)S(1)} %get-tuple-element.56.mine_ref), channel_id=1, source_target_pairs={{0,16},{16,0},{1,17},{17,1},{2,18},{18,2},{3,19},{19,3},{4,20},{20... | collective-permute-start | bytes 196616 | tf_op jit(solution)/shard_map/ppermute | solution.py:18
  65.1 5.0 %collective-permute-start.23 = (bf16[128,256]{1,0:T(8,128)(2,1)S(1)}, bf16[128,256]{1,0:T(8,128)(2,1)S(1)}, u32[]{:S(2)}, u32[]{:S(2)}) collective-permute-start(bf16[128,256]{1,0:T(8,128)(2,1)S(1)} %get-tuple-element.52), channel_id=1, source_target_pairs={{0,4},{4,0},{8,12},{12,8},{1,5},{5,1},{9,13},{13,9},{2,6},{6,2},{1... | collective-permute-start | bytes 196616 | tf_op jit(solution)/shard_map/ppermute | solution.py:18
  65.5 4.6 %collective-permute-start.24 = (bf16[128,256]{1,0:T(8,128)(2,1)S(1)}, bf16[128,256]{1,0:T(8,128)(2,1)S(1)}, u32[]{:S(2)}, u32[]{:S(2)}) collective-permute-start(bf16[128,256]{1,0:T(8,128)(2,1)S(1)} %get-tuple-element.53), channel_id=1, source_target_pairs={{0,8},{4,12},{8,0},{12,4},{1,9},{5,13},{9,1},{13,5},{2,10},{6,14},... | collective-permute-start | bytes 196616 | tf_op jit(solution)/shard_map/ppermute | solution.py:18
  66.9 5.2 %collective-permute-start.25 = (bf16[128,256]{1,0:T(8,128)(2,1)S(1)}, bf16[128,256]{1,0:T(8,128)(2,1)S(1)}, u32[]{:S(2)}, u32[]{:S(2)}) collective-permute-start(bf16[128,256]{1,0:T(8,128)(2,1)S(1)} %get-tuple-element.54), channel_id=1, source_target_pairs={{0,12},{4,8},{8,4},{12,0},{1,13},{5,9},{9,5},{13,1},{2,14},{6,10},... | collective-permute-start | bytes 196616 | tf_op jit(solution)/shard_map/ppermute | solution.py:18
  (14 other events, 42.0 us)

commit v5 on v4

--- a/solution.py
+++ b/solution.py
@@ -106,17 +106,17 @@
         buf[rows(at(d), size), :] = piece[...]
 
 
-def block_outs(n, size, cols):
+def block_outs(n, size, cols, own=True):
     if is_direct(n):
-        return [((size, cols), F32)] + [((size, cols), BF)] * (n - 1)
+        return [((size, cols), F32)] * own + [((size, cols), BF)] * (n - 1)
     return [((n * size, cols), F32)]
 
 
 def emit_blocks(term, outs, n, axis):
     at = place(n, axis)
     if is_direct(n):
-        for d in list(range(1, n)) + [0]:
-            outs[d][...] = term(at(d)).astype(outs[d].dtype)
+        for d, out_ref in zip(reversed(range(n)), reversed(outs)):
+            out_ref[...] = term(at(d)).astype(out_ref.dtype)
     else:
         size = outs[0].shape[0] // n
         for d in range(n):
@@ -174,9 +174,31 @@
         lay_out(piece_refs, buf, n_row, "row")
         emit_blocks(lambda i: dot(tile_ref[rows(i, width), :], buf[...]), outs, n_col, "col")
 
-    outs = block_outs(n_col, width, cols) + [((depth, cols), BF)]
+    outs = block_outs(n_col, width, cols, False) + [((depth, cols), BF)]
     got = call(kernel, outs, [tiles, *pieces], flops=2 * tiles.shape[0] * depth * cols)
-    return got[:-1], got[-1]
+    return blocks_of(got, n_col)
+
+
+def blocks_of(got, n):
+    return ([None] if is_direct(n) else []) + list(got[:-1]), got[-1]
+
+
+def own_forward(tiles, values, width):
+    def kernel(tile_ref, value_ref, out_ref):
+        out_ref[...] = dot(tile_ref[rows(lax.axis_index("col"), width), :], value_ref[...])
+
+    return call(kernel, [((width, values.shape[1]), F32)], [tiles, values], flops=2 * width * values.size)[0]
+
+
+def own_back(tiles, values, span, part=None):
+    args = [tiles, values] + ([] if part is None else [part])
+
+    def kernel(tile_ref, value_ref, *refs):
+        own = rows(lax.axis_index("row"), span)
+        out = dot_t(tile_ref[:, own], value_ref[...])
+        refs[-1][...] = out if part is None else out + refs[0][own, :]
+
+    return call(kernel, [((span, values.shape[1]), F32)], args, flops=2 * span * values.size)[0]
 
 
 def plain_product(tiles, values, transposed):
@@ -191,16 +213,11 @@
 
 
 def solve_forward(sums, right_side, inverse):
-    count = len(sums)
-
-    def kernel(*refs):
-        rhs_ref, inv_ref, y_ref, yb_ref = refs[count:]
-        y = apply_split(inv_ref[0], rhs_ref[...].astype(F32) - total_of(refs[:count]))
-        y_ref[...] = y
-        yb_ref[...] = y.astype(BF)
-
-    shape = right_side.shape
-    return call(kernel, [(shape, F32), (shape, BF)], [*sums, right_side, inverse])
+    total = sums[0].astype(F32)
+    for piece in sums[1:]:
+        total = total + piece.astype(F32)
+    y = jnp.dot(inverse, right_side.astype(F32) - total, precision=lax.Precision.HIGHEST)
+    return y, y.astype(BF)
 
 
 def top_half(tiles, pieces, leaf_part, n_row, n_col, width, passed):
@@ -290,9 +307,9 @@
             buf[own, rows(sec, half)] = other_ref[own, :]
         emit_blocks(lambda i: dot_t(tile_ref[:, rows(i, width)], buf[...]), outs[:-1], n_row, "row")
 
-    outs = block_outs(n_row, width, 2 * half) + [((mine.shape[0], 2 * half), BF)]
+    outs = block_outs(n_row, width, 2 * half, False) + [((mine.shape[0], 2 * half), BF)]
     got = call(kernel, outs, [tiles, mine, other], flops=4 * tiles.shape[0] * tiles.shape[1] * half)
-    return got[:-1], got[-1]
+    return blocks_of(got, n_row)
 
 
 def back_blocks(tiles, pieces, top_part, n_row, n_col, span):
@@ -308,29 +325,17 @@
             outs, n_row, "row",
         )
 
-    return call(
-        kernel,
-        block_outs(n_row, span, cols),
-        [tiles, *pieces, top_part],
-        scratch=[((tiles.shape[0], cols), BF)],
-        flops=2 * tiles.shape[0] * tiles.shape[1] * cols,
-    )
+    outs = block_outs(n_row, span, cols, False) + [((tiles.shape[0], cols), BF)]
+    got = call(kernel, outs, [tiles, *pieces, top_part], flops=2 * tiles.shape[0] * tiles.shape[1] * cols)
+    return blocks_of(got, n_row)
 
 
 def solve_back(sums, right_side, inverse):
-    count = len(sums)
-    blocks, width = inverse.shape[:2]
-    shape = right_side.shape
-
-    def kernel(*refs):
-        y_ref, inv_ref, x_ref, xb_ref = refs[count:]
-        rest = y_ref[...] - total_of(refs[:count])
-        for m in range(blocks):
-            x = apply_split(inv_ref[m], rest[m * width : (m + 1) * width])
-            x_ref[pl.ds(m * width, width), :] = x
-            xb_ref[pl.ds(m * width, width), :] = x.astype(BF)
-
-    return call(kernel, [(shape, F32), (shape, BF)], [*sums, right_side, inverse])
+    total = sums[0].astype(F32)
+    for piece in sums[1:]:
+        total = total + piece.astype(F32)
+    x = jnp.einsum("ba,bn->an", inverse, right_side - total, precision=lax.Precision.HIGHEST)
+    return x, x.astype(BF)
 
 
 def solve_last(sums, right_side, inverse):
@@ -354,16 +359,18 @@
 
         leaf_y, leaf_yb = leaf_first(leaf_inv[0, 0, :, 0], leaf_rhs[0, 0, :, 0])
         leaf_pieces = gather(leaf_yb, "row", n_row)
-        masked = mask_tiles(
-            [values.reshape(n_col, width, -1) for values in (sep_leaf, top_leaf, top_sep)],
-            [mask.reshape(n_col, 1, -1) for mask in masks],
-            width,
-        )
-        sl, tl, ts = [values.reshape(n_col * width, -1) for values in masked]
+        shaped = [mask.reshape(n_col, 1, -1) for mask in masks]
+        sl = mask_tiles([sep_leaf.reshape(n_col, width, -1)], shaped[:1], width)[0].reshape(n_col * width, -1)
         blocks, leaf_col = forward_blocks(sl, leaf_pieces, n_row, n_col, width)
+        top_leaf, top_sep, leaf_col = lax.optimization_barrier((top_leaf, top_sep, leaf_col))
         sums = scatter_sum(blocks, "col", n_col)
+        tops = [values.reshape(n_col, width, -1) for values in (top_leaf, top_sep)]
+        tl, ts = [values.reshape(n_col * width, -1) for values in mask_tiles(tops, shaped[1:], width)]
+        if is_direct(n_col):
+            sums[0] = own_forward(sl, leaf_col, width)
         leaf_part = plain_product(tl, leaf_col, False)
-        sep_y, sep_yb = solve_forward(sums, sep_rhs[0, 0, 0], split_inverse(sep_inv[0, 0], False))
+        sums[0], ts, leaf_part = lax.optimization_barrier((sums[0], ts, leaf_part))
+        sep_y, sep_yb = solve_forward(sums, sep_rhs[0, 0, 0], sep_inv[0, 0, 0])
         pieces = gather(sep_yb, "row", n_row)
         passed = swap(top_half(ts, pieces, leaf_part, n_row, n_col, width, True), "sec", 2, 1)
         kept = top_half(ts, pieces, leaf_part, n_row, n_col, width, False)
@@ -374,11 +381,16 @@
         top_stack = stack_pieces(gather(top_xhb, "col", n_col, swap_cross), n_col, "col")
         blocks, top_row = top_back_blocks(ts, top_stack, swap(top_stack, "sec", 2, 1), n_row, n_col, width)
         sums = scatter_sum(blocks, "row", n_row)
+        if is_direct(n_row):
+            sums[0] = own_back(ts, top_row, width)
         top_part = plain_product(tl, top_row, True)
         top_x = join_halves(top_xh, swap(top_xh, "sec", 2, 1), n_col)
-        sep_x, sep_xb = solve_back(sums, sep_y, split_inverse(sep_inv[0, 0], True))
+        sep_x, sep_xb = solve_back(sums, sep_y, sep_inv[0, 0, 0])
         pieces = gather(sep_xb, "col", n_col)
-        sums = scatter_sum(back_blocks(sl, pieces, top_part, n_row, n_col, span), "row", n_row)
+        blocks, sep_row = back_blocks(sl, pieces, top_part, n_row, n_col, span)
+        sums = scatter_sum(blocks, "row", n_row)
+        if is_direct(n_row):
+            sums[0] = own_back(sl, sep_row, span, top_part)
         leaf_x = solve_last(sums, leaf_y, split_inverse(leaf_inv[0, 0, :, 0], True))
         return (
             leaf_x.reshape(1, 1, leaf_count, 1, width, cols),

time: 73.2 us -> 71.7 us (0.980)
  waiting for transfers between devices: 28.5 us -> 27 us
  local copies, waits for them, and re-layouts: 4.02 us -> 3.21 us
    ppermute x21, waiting for transfers between devices: 21.7 us -> 20.2 us  [swap(): return lax.ppermute(values, axis, [(i, i ^ step) for i in range(n)])]
    unnamed x22 -> x20, local copies, waits for them, and re-layouts: 2.39 us -> 1.56 us
  transfers between devices with their start and end apart: 27 -> 27, of which waited for: 18 -> 19; matrix products, arithmetic and copies ran while one was open for 2% -> 2% of each run, Pallas kernels for 5% -> 6%
where the time goes in v5:
time: 71.7 us; the launch traced here: 71.4 us
  starting transfers between devices  32.3 us (45%)
  waiting for transfers between devices  27 us (38%)
  Pallas kernels  6.24 us (9%)
  local copies, waits for them, and re-layouts  3.21 us (4%)
  matrix products  1.73 us (2%)
  between operations  0.95 us (1%)
    ppermute x21, starting transfers between devices, swap(): return lax.ppermute(values, axis, [(i, i ^ step) for i in range(n)])  24.4 us
    ppermute x21, waiting for transfers between devices, swap(): return lax.ppermute(values, axis, [(i, i ^ step) for i in range(n)])  20.2 us
    ppermute x6, starting transfers between devices, swap_cross(): return lax.ppermute(values, ('sec', axis), pairs)  7.87 us
    ppermute x6, waiting for transfers between devices, swap_cross(): return lax.ppermute(values, ('sec', axis), pairs)  6.8 us
    pallas_call x21, Pallas kernels, call(): pl.pallas_call(kernel, out_shape=tuple((jax.ShapeDtypeStruct(s, t) for s,...  6.24 us
    unnamed x20, local copies, waits for them, and re-layouts  1.56 us
  transfers between devices with their start and end apart: 27, of which 19 were waited for; matrix products, arithmetic and copies ran while one was open for 2% of the time, Pallas kernels for 6%

profile of v5, /device:TPU:0, one launch (start us, length us, event | category | flops | bytes accessed | tf_op | source)
XLA Modules:
  0.0 71.4 jit_solution(16198809217010383665)
XLA Ops:
  1.8 3.0 %collective-permute-start = (bf16[128,256]{1,0:T(8,128)(2,1)S(1)}, bf16[128,256]{1,0:T(8,128)(2,1)S(1)}, u32[]{:S(2)}, u32[]{:S(2)}) collective-permute-start(bf16[128,256]{1,0:T(8,128)(2,1)S(1)} %get-tuple-element.55.refs_1_), channel_id=1, source_target_pairs={{0,4},{4,0},{8,12},{12,8},{1,5},{5,1},{9,13},{13,9},{2,6},{6,2},{1... | collective-permute-start | bytes 196616 | tf_op jit(solution)/shard_map/ppermute | solution.py:18
  4.8 1.5 %collective-permute-start.1 = (bf16[128,256]{1,0:T(8,128)(2,1)S(1)}, bf16[128,256]{1,0:T(8,128)(2,1)S(1)}, u32[]{:S(2)}, u32[]{:S(2)}) collective-permute-start(bf16[128,256]{1,0:T(8,128)(2,1)S(1)} %get-tuple-element.55.refs_1_), channel_id=1, source_target_pairs={{0,8},{4,12},{8,0},{12,4},{1,9},{5,13},{9,1},{13,5},{2,10},{6,14},... | collective-permute-start | bytes 196616 | tf_op jit(solution)/shard_map/ppermute | solution.py:18
  6.3 1.3 %reshape.50.refs_1_ = bf16[4,128,512]{2,1,0:T(8,128)(2,1)S(1)} reshape(bf16[1,1,4,128,4,1,1,128]{7,4,6,5,3,2,1,0:T(4,128)(2,1)} %param.18) | data formatting | bytes 1048576 | tf_op jit(solution)/shard_map/reshape | solution.py:363
  7.8 1.3 %collective-permute-done.1.refs_3_ = bf16[128,256]{1,0:T(8,128)(2,1)S(1)} collective-permute-done((bf16[128,256]{1,0:T(8,128)(2,1)S(1)}, bf16[128,256]{1,0:T(8,128)(2,1)S(1)}, u32[]{:S(2)}, u32[]{:S(2)}) %collective-permute-start.1) | collective-permute-done | bytes 65568 | tf_op jit(solution)/shard_map/ppermute | solution.py:18
  9.0 2.4 %collective-permute-done.2.refs_4_ = bf16[128,256]{1,0:T(8,128)(2,1)S(1)} collective-permute-done((bf16[128,256]{1,0:T(8,128)(2,1)S(1)}, bf16[128,256]{1,0:T(8,128)(2,1)S(1)}, u32[]{:S(2)}, u32[]{:S(2)}) %collective-permute-start.2) | collective-permute-done | bytes 65568 | tf_op jit(solution)/shard_map/ppermute | solution.py:18
  11.8 1.6 %collective-permute-start.3 = (bf16[128,256]{1,0:T(8,128)(2,1)S(1)}, bf16[128,256]{1,0:T(8,128)(2,1)S(1)}, u32[]{:S(2)}, u32[]{:S(2)}) collective-permute-start(bf16[128,256]{1,0:T(8,128)(2,1)S(1)} %get-tuple-element.36), channel_id=1, source_target_pairs={{0,1},{1,0},{2,3},{3,2},{4,5},{5,4},{6,7},{7,6},{8,9},{9,8},{10,11... | collective-permute-start | bytes 196616 | tf_op jit(solution)/shard_map/ppermute | solution.py:18
  13.4 2.6 %collective-permute-start.4 = (bf16[128,256]{1,0:T(8,128)(2,1)S(1)}, bf16[128,256]{1,0:T(8,128)(2,1)S(1)}, u32[]{:S(2)}, u32[]{:S(2)}) collective-permute-start(bf16[128,256]{1,0:T(8,128)(2,1)S(1)} %get-tuple-element.37), channel_id=1, source_target_pairs={{0,2},{1,3},{2,0},{3,1},{4,6},{5,7},{6,4},{7,5},{8,10},{9,11},{10,... | collective-permute-start | bytes 196616 | tf_op jit(solution)/shard_map/ppermute | solution.py:18
  20.0 2.1 %collective-permute-done.5 = bf16[128,256]{1,0:T(8,128)(2,1)S(1)} collective-permute-done((bf16[128,256]{1,0:T(8,128)(2,1)S(1)}, bf16[128,256]{1,0:T(8,128)(2,1)S(1)}, u32[]{:S(2)}, u32[]{:S(2)}) %collective-permute-start.5) | collective-permute-done | bytes 65568 | tf_op jit(solution)/shard_map/ppermute | solution.py:18
  23.5 2.4 %collective-permute-start.8 = (bf16[128,256]{1,0:T(8,128)(2,1)S(1)}, bf16[128,256]{1,0:T(8,128)(2,1)S(1)}, u32[]{:S(2)}, u32[]{:S(2)}) collective-permute-start(bf16[128,256]{1,0:T(8,128)(2,1)S(1)} %get-tuple-element.57.refs_1_), channel_id=1, source_target_pairs={{0,12},{4,8},{8,4},{12,0},{1,13},{5,9},{9,5},{13,1},{2,14},{6,10},... | collective-permute-start | bytes 196616 | tf_op jit(solution)/shard_map/ppermute | solution.py:18
  27.2 1.4 %collective-permute-done.8.refs_4_ = bf16[128,256]{1,0:T(8,128)(2,1)S(1)} collective-permute-done((bf16[128,256]{1,0:T(8,128)(2,1)S(1)}, bf16[128,256]{1,0:T(8,128)(2,1)S(1)}, u32[]{:S(2)}, u32[]{:S(2)}) %collective-permute-start.8) | collective-permute-done | bytes 65568 | tf_op jit(solution)/shard_map/ppermute | solution.py:18
  30.7 1.3 %collective-permute-start.11 = (bf16[128,128]{1,0:T(8,128)(2,1)S(1)}, bf16[128,128]{1,0:T(8,128)(2,1)S(1)}, u32[]{:S(2)}, u32[]{:S(2)}) collective-permute-start(bf16[128,128]{1,0:T(8,128)(2,1)S(1)} %get-tuple-element.43), channel_id=1, source_target_pairs={{0,18},{1,19},{2,16},{3,17},{16,2},{17,3},{18,0},{19,1},{4,22},{5,... | collective-permute-start | bytes 98312 | tf_op jit(solution)/shard_map/ppermute | solution.py:23
  32.0 2.6 %collective-permute-start.12 = (bf16[128,128]{1,0:T(8,128)(2,1)S(1)}, bf16[128,128]{1,0:T(8,128)(2,1)S(1)}, u32[]{:S(2)}, u32[]{:S(2)}) collective-permute-start(bf16[128,128]{1,0:T(8,128)(2,1)S(1)} %get-tuple-element.44), channel_id=1, source_target_pairs={{0,19},{1,18},{2,17},{3,16},{16,3},{17,2},{18,1},{19,0},{4,23},{5,... | collective-permute-start | bytes 98312 | tf_op jit(solution)/shard_map/ppermute | solution.py:23
  35.1 2.1 %collective-permute-done.12.refs_3_ = bf16[128,128]{1,0:T(8,128)(2,1)S(1)} collective-permute-done((bf16[128,128]{1,0:T(8,128)(2,1)S(1)}, bf16[128,128]{1,0:T(8,128)(2,1)S(1)}, u32[]{:S(2)}, u32[]{:S(2)}) %collective-permute-start.12) | collective-permute-done | bytes 32800 | tf_op jit(solution)/shard_map/ppermute | solution.py:23
  38.1 2.6 %collective-permute-start.14 = (bf16[128,128]{1,0:T(8,128)(2,1)S(1)}, bf16[128,128]{1,0:T(8,128)(2,1)S(1)}, u32[]{:S(2)}, u32[]{:S(2)}) collective-permute-start(bf16[128,128]{1,0:T(8,128)(2,1)S(1)} %get-tuple-element.45.refs_0_), channel_id=1, source_target_pairs={{0,18},{1,19},{2,16},{3,17},{16,2},{17,3},{18,0},{19,1},{4,22},{5,... | collective-permute-start | bytes 98312 | tf_op jit(solution)/shard_map/ppermute | solution.py:23
  42.4 3.4 %collective-permute-done.15.refs_3_ = bf16[128,128]{1,0:T(8,128)(2,1)S(1)} collective-permute-done((bf16[128,128]{1,0:T(8,128)(2,1)S(1)}, bf16[128,128]{1,0:T(8,128)(2,1)S(1)}, u32[]{:S(2)}, u32[]{:S(2)}) %collective-permute-start.15) | collective-permute-done | bytes 32800 | tf_op jit(solution)/shard_map/ppermute | solution.py:23
  46.1 1.2 %collective-permute-done.16.other_ref = bf16[512,128]{1,0:T(8,128)(2,1)S(1)} collective-permute-done((bf16[512,128]{1,0:T(8,128)(2,1)S(1)}, bf16[512,128]{1,0:T(8,128)(2,1)S(1)}, u32[]{:S(2)}, u32[]{:S(2)}) %collective-permute-start.16) | collective-permute-done | bytes 131104 | tf_op jit(solution)/shard_map/ppermute | solution.py:18
  47.6 1.6 %collective-permute-start.17 = (bf16[128,256]{1,0:T(8,128)(2,1)S(1)}, bf16[128,256]{1,0:T(8,128)(2,1)S(1)}, u32[]{:S(2)}, u32[]{:S(2)}) collective-permute-start(bf16[128,256]{1,0:T(8,128)(2,1)S(1)} %get-tuple-element.47), channel_id=1, source_target_pairs={{0,4},{4,0},{8,12},{12,8},{1,5},{5,1},{9,13},{13,9},{2,6},{6,2},{1... | collective-permute-start | bytes 196616 | tf_op jit(solution)/shard_map/ppermute | solution.py:18
  49.2 1.5 %collective-permute-start.18 = (bf16[128,256]{1,0:T(8,128)(2,1)S(1)}, bf16[128,256]{1,0:T(8,128)(2,1)S(1)}, u32[]{:S(2)}, u32[]{:S(2)}) collective-permute-start(bf16[128,256]{1,0:T(8,128)(2,1)S(1)} %get-tuple-element.48), channel_id=1, source_target_pairs={{0,8},{4,12},{8,0},{12,4},{1,9},{5,13},{9,1},{13,5},{2,10},{6,14},... | collective-permute-start | bytes 196616 | tf_op jit(solution)/shard_map/ppermute | solution.py:18
  52.0 1.5 %collective-permute-done.18 = bf16[128,256]{1,0:T(8,128)(2,1)S(1)} collective-permute-done((bf16[128,256]{1,0:T(8,128)(2,1)S(1)}, bf16[128,256]{1,0:T(8,128)(2,1)S(1)}, u32[]{:S(2)}, u32[]{:S(2)}) %collective-permute-start.18) | collective-permute-done | bytes 65568 | tf_op jit(solution)/shard_map/ppermute | solution.py:18
  53.5 2.4 %collective-permute-done.19 = bf16[128,256]{1,0:T(8,128)(2,1)S(1)} collective-permute-done((bf16[128,256]{1,0:T(8,128)(2,1)S(1)}, bf16[128,256]{1,0:T(8,128)(2,1)S(1)}, u32[]{:S(2)}, u32[]{:S(2)}) %collective-permute-start.19) | collective-permute-done | bytes 65568 | tf_op jit(solution)/shard_map/ppermute | solution.py:18
  56.3 1.6 %collective-permute-start.21 = (bf16[128,256]{1,0:T(8,128)(2,1)S(1)}, bf16[128,256]{1,0:T(8,128)(2,1)S(1)}, u32[]{:S(2)}, u32[]{:S(2)}) collective-permute-start(bf16[128,256]{1,0:T(8,128)(2,1)S(1)} %get-tuple-element.59.refs_1_), channel_id=1, source_target_pairs={{0,2},{1,3},{2,0},{3,1},{4,6},{5,7},{6,4},{7,5},{8,10},{9,11},{10,... | collective-permute-start | bytes 196616 | tf_op jit(solution)/shard_map/ppermute | solution.py:18
  57.8 2.8 %collective-permute-start.22 = (bf16[128,256]{1,0:T(8,128)(2,1)S(1)}, bf16[128,256]{1,0:T(8,128)(2,1)S(1)}, u32[]{:S(2)}, u32[]{:S(2)}) collective-permute-start(bf16[128,256]{1,0:T(8,128)(2,1)S(1)} %get-tuple-element.59.refs_1_), channel_id=1, source_target_pairs={{0,3},{1,2},{2,1},{3,0},{4,7},{5,6},{6,5},{7,4},{8,11},{9,10},{10,... | collective-permute-start | bytes 196616 | tf_op jit(solution)/shard_map/ppermute | solution.py:18
  61.9 2.0 %collective-permute-done.22.refs_4_ = bf16[128,256]{1,0:T(8,128)(2,1)S(1)} collective-permute-done((bf16[128,256]{1,0:T(8,128)(2,1)S(1)}, bf16[128,256]{1,0:T(8,128)(2,1)S(1)}, u32[]{:S(2)}, u32[]{:S(2)}) %collective-permute-start.22) | collective-permute-done | bytes 65568 | tf_op jit(solution)/shard_map/ppermute | solution.py:18
  65.4 2.4 %collective-permute-start.25 = (bf16[128,256]{1,0:T(8,128)(2,1)S(1)}, bf16[128,256]{1,0:T(8,128)(2,1)S(1)}, u32[]{:S(2)}, u32[]{:S(2)}) collective-permute-start(bf16[128,256]{1,0:T(8,128)(2,1)S(1)} %get-tuple-element.53), channel_id=1, source_target_pairs={{0,12},{4,8},{8,4},{12,0},{1,13},{5,9},{9,5},{13,1},{2,14},{6,10},... | collective-permute-start | bytes 196616 | tf_op jit(solution)/shard_map/ppermute | solution.py:18
  (77 shorter events, 22.0 us)
Async XLA Ops:
  1.8 6.0 %collective-permute-start = (bf16[128,256]{1,0:T(8,128)(2,1)S(1)}, bf16[128,256]{1,0:T(8,128)(2,1)S(1)}, u32[]{:S(2)}, u32[]{:S(2)}) collective-permute-start(bf16[128,256]{1,0:T(8,128)(2,1)S(1)} %get-tuple-element.55.refs_1_), channel_id=1, source_target_pairs={{0,4},{4,0},{8,12},{12,8},{1,5},{5,1},{9,13},{13,9},{2,6},{6,2},{1... | collective-permute-start | bytes 196616 | tf_op jit(solution)/shard_map/ppermute | solution.py:18
  4.8 4.3 %collective-permute-start.1 = (bf16[128,256]{1,0:T(8,128)(2,1)S(1)}, bf16[128,256]{1,0:T(8,128)(2,1)S(1)}, u32[]{:S(2)}, u32[]{:S(2)}) collective-permute-start(bf16[128,256]{1,0:T(8,128)(2,1)S(1)} %get-tuple-element.55.refs_1_), channel_id=1, source_target_pairs={{0,8},{4,12},{8,0},{12,4},{1,9},{5,13},{9,1},{13,5},{2,10},{6,14},... | collective-permute-start | bytes 196616 | tf_op jit(solution)/shard_map/ppermute | solution.py:18
  6.3 5.2 %collective-permute-start.2 = (bf16[128,256]{1,0:T(8,128)(2,1)S(1)}, bf16[128,256]{1,0:T(8,128)(2,1)S(1)}, u32[]{:S(2)}, u32[]{:S(2)}) collective-permute-start(bf16[128,256]{1,0:T(8,128)(2,1)S(1)} %get-tuple-element.55.refs_1_), channel_id=1, source_target_pairs={{0,12},{4,8},{8,4},{12,0},{1,13},{5,9},{9,5},{13,1},{2,14},{6,10},... | collective-permute-start | bytes 196616 | tf_op jit(solution)/shard_map/ppermute | solution.py:18
  11.8 7.2 %collective-permute-start.3 = (bf16[128,256]{1,0:T(8,128)(2,1)S(1)}, bf16[128,256]{1,0:T(8,128)(2,1)S(1)}, u32[]{:S(2)}, u32[]{:S(2)}) collective-permute-start(bf16[128,256]{1,0:T(8,128)(2,1)S(1)} %get-tuple-element.36), channel_id=1, source_target_pairs={{0,1},{1,0},{2,3},{3,2},{4,5},{5,4},{6,7},{7,6},{8,9},{9,8},{10,11... | collective-permute-start | bytes 196616 | tf_op jit(solution)/shard_map/ppermute | solution.py:18
  13.4 6.6 %collective-permute-start.4 = (bf16[128,256]{1,0:T(8,128)(2,1)S(1)}, bf16[128,256]{1,0:T(8,128)(2,1)S(1)}, u32[]{:S(2)}, u32[]{:S(2)}) collective-permute-start(bf16[128,256]{1,0:T(8,128)(2,1)S(1)} %get-tuple-element.37), channel_id=1, source_target_pairs={{0,2},{1,3},{2,0},{3,1},{4,6},{5,7},{6,4},{7,5},{8,10},{9,11},{10,... | collective-permute-start | bytes 196616 | tf_op jit(solution)/shard_map/ppermute | solution.py:18
  16.0 6.1 %collective-permute-start.5 = (bf16[128,256]{1,0:T(8,128)(2,1)S(1)}, bf16[128,256]{1,0:T(8,128)(2,1)S(1)}, u32[]{:S(2)}, u32[]{:S(2)}) collective-permute-start(bf16[128,256]{1,0:T(8,128)(2,1)S(1)} %get-tuple-element.38), channel_id=1, source_target_pairs={{0,3},{1,2},{2,1},{3,0},{4,7},{5,6},{6,5},{7,4},{8,11},{9,10},{10,... | collective-permute-start | bytes 196616 | tf_op jit(solution)/shard_map/ppermute | solution.py:18
  22.4 4.3 %collective-permute-start.6 = (bf16[128,256]{1,0:T(8,128)(2,1)S(1)}, bf16[128,256]{1,0:T(8,128)(2,1)S(1)}, u32[]{:S(2)}, u32[]{:S(2)}) collective-permute-start(bf16[128,256]{1,0:T(8,128)(2,1)S(1)} %get-tuple-element.57.refs_1_), channel_id=1, source_target_pairs={{0,4},{4,0},{8,12},{12,8},{1,5},{5,1},{9,13},{13,9},{2,6},{6,2},{1... | collective-permute-start | bytes 196616 | tf_op jit(solution)/shard_map/ppermute | solution.py:18
  23.0 4.3 %collective-permute-start.7 = (bf16[128,256]{1,0:T(8,128)(2,1)S(1)}, bf16[128,256]{1,0:T(8,128)(2,1)S(1)}, u32[]{:S(2)}, u32[]{:S(2)}) collective-permute-start(bf16[128,256]{1,0:T(8,128)(2,1)S(1)} %get-tuple-element.57.refs_1_), channel_id=1, source_target_pairs={{0,8},{4,12},{8,0},{12,4},{1,9},{5,13},{9,1},{13,5},{2,10},{6,14},... | collective-permute-start | bytes 196616 | tf_op jit(solution)/shard_map/ppermute | solution.py:18
  23.5 5.2 %collective-permute-start.8 = (bf16[128,256]{1,0:T(8,128)(2,1)S(1)}, bf16[128,256]{1,0:T(8,128)(2,1)S(1)}, u32[]{:S(2)}, u32[]{:S(2)}) collective-permute-start(bf16[128,256]{1,0:T(8,128)(2,1)S(1)} %get-tuple-element.57.refs_1_), channel_id=1, source_target_pairs={{0,12},{4,8},{8,4},{12,0},{1,13},{5,9},{9,5},{13,1},{2,14},{6,10},... | collective-permute-start | bytes 196616 | tf_op jit(solution)/shard_map/ppermute | solution.py:18
  30.6 4.1 %collective-permute-start.10 = (bf16[128,128]{1,0:T(8,128)(2,1)S(1)}, bf16[128,128]{1,0:T(8,128)(2,1)S(1)}, u32[]{:S(2)}, u32[]{:S(2)}) collective-permute-start(bf16[128,128]{1,0:T(8,128)(2,1)S(1)} %get-tuple-element.42), channel_id=1, source_target_pairs={{0,17},{1,16},{2,19},{3,18},{16,1},{17,0},{18,3},{19,2},{4,21},{5,... | collective-permute-start | bytes 98312 | tf_op jit(solution)/shard_map/ppermute | solution.py:23
  30.7 4.3 %collective-permute-start.11 = (bf16[128,128]{1,0:T(8,128)(2,1)S(1)}, bf16[128,128]{1,0:T(8,128)(2,1)S(1)}, u32[]{:S(2)}, u32[]{:S(2)}) collective-permute-start(bf16[128,128]{1,0:T(8,128)(2,1)S(1)} %get-tuple-element.43), channel_id=1, source_target_pairs={{0,18},{1,19},{2,16},{3,17},{16,2},{17,3},{18,0},{19,1},{4,22},{5,... | collective-permute-start | bytes 98312 | tf_op jit(solution)/shard_map/ppermute | solution.py:23
  32.0 5.2 %collective-permute-start.12 = (bf16[128,128]{1,0:T(8,128)(2,1)S(1)}, bf16[128,128]{1,0:T(8,128)(2,1)S(1)}, u32[]{:S(2)}, u32[]{:S(2)}) collective-permute-start(bf16[128,128]{1,0:T(8,128)(2,1)S(1)} %get-tuple-element.44), channel_id=1, source_target_pairs={{0,19},{1,18},{2,17},{3,16},{16,3},{17,2},{18,1},{19,0},{4,23},{5,... | collective-permute-start | bytes 98312 | tf_op jit(solution)/shard_map/ppermute | solution.py:23
  38.1 4.3 %collective-permute-start.14 = (bf16[128,128]{1,0:T(8,128)(2,1)S(1)}, bf16[128,128]{1,0:T(8,128)(2,1)S(1)}, u32[]{:S(2)}, u32[]{:S(2)}) collective-permute-start(bf16[128,128]{1,0:T(8,128)(2,1)S(1)} %get-tuple-element.45.refs_0_), channel_id=1, source_target_pairs={{0,18},{1,19},{2,16},{3,17},{16,2},{17,3},{18,0},{19,1},{4,22},{5,... | collective-permute-start | bytes 98312 | tf_op jit(solution)/shard_map/ppermute | solution.py:23
  40.7 5.1 %collective-permute-start.15 = (bf16[128,128]{1,0:T(8,128)(2,1)S(1)}, bf16[128,128]{1,0:T(8,128)(2,1)S(1)}, u32[]{:S(2)}, u32[]{:S(2)}) collective-permute-start(bf16[128,128]{1,0:T(8,128)(2,1)S(1)} %get-tuple-element.45.refs_0_), channel_id=1, source_target_pairs={{0,19},{1,18},{2,17},{3,16},{16,3},{17,2},{18,1},{19,0},{4,23},{5,... | collective-permute-start | bytes 98312 | tf_op jit(solution)/shard_map/ppermute | solution.py:23
  47.6 4.3 %collective-permute-start.17 = (bf16[128,256]{1,0:T(8,128)(2,1)S(1)}, bf16[128,256]{1,0:T(8,128)(2,1)S(1)}, u32[]{:S(2)}, u32[]{:S(2)}) collective-permute-start(bf16[128,256]{1,0:T(8,128)(2,1)S(1)} %get-tuple-element.47), channel_id=1, source_target_pairs={{0,4},{4,0},{8,12},{12,8},{1,5},{5,1},{9,13},{13,9},{2,6},{6,2},{1... | collective-permute-start | bytes 196616 | tf_op jit(solution)/shard_map/ppermute | solution.py:18
  49.2 4.3 %collective-permute-start.18 = (bf16[128,256]{1,0:T(8,128)(2,1)S(1)}, bf16[128,256]{1,0:T(8,128)(2,1)S(1)}, u32[]{:S(2)}, u32[]{:S(2)}) collective-permute-start(bf16[128,256]{1,0:T(8,128)(2,1)S(1)} %get-tuple-element.48), channel_id=1, source_target_pairs={{0,8},{4,12},{8,0},{12,4},{1,9},{5,13},{9,1},{13,5},{2,10},{6,14},... | collective-permute-start | bytes 196616 | tf_op jit(solution)/shard_map/ppermute | solution.py:18
  50.7 5.2 %collective-permute-start.19 = (bf16[128,256]{1,0:T(8,128)(2,1)S(1)}, bf16[128,256]{1,0:T(8,128)(2,1)S(1)}, u32[]{:S(2)}, u32[]{:S(2)}) collective-permute-start(bf16[128,256]{1,0:T(8,128)(2,1)S(1)} %get-tuple-element.49), channel_id=1, source_target_pairs={{0,12},{4,8},{8,4},{12,0},{1,13},{5,9},{9,5},{13,1},{2,14},{6,10},... | collective-permute-start | bytes 196616 | tf_op jit(solution)/shard_map/ppermute | solution.py:18
  56.2 5.7 %collective-permute-start.20 = (bf16[128,256]{1,0:T(8,128)(2,1)S(1)}, bf16[128,256]{1,0:T(8,128)(2,1)S(1)}, u32[]{:S(2)}, u32[]{:S(2)}) collective-permute-start(bf16[128,256]{1,0:T(8,128)(2,1)S(1)} %get-tuple-element.59.refs_1_), channel_id=1, source_target_pairs={{0,1},{1,0},{2,3},{3,2},{4,5},{5,4},{6,7},{7,6},{8,9},{9,8},{10,11... | collective-permute-start | bytes 196616 | tf_op jit(solution)/shard_map/ppermute | solution.py:18
  56.3 5.7 %collective-permute-start.21 = (bf16[128,256]{1,0:T(8,128)(2,1)S(1)}, bf16[128,256]{1,0:T(8,128)(2,1)S(1)}, u32[]{:S(2)}, u32[]{:S(2)}) collective-permute-start(bf16[128,256]{1,0:T(8,128)(2,1)S(1)} %get-tuple-element.59.refs_1_), channel_id=1, source_target_pairs={{0,2},{1,3},{2,0},{3,1},{4,6},{5,7},{6,4},{7,5},{8,10},{9,11},{10,... | collective-permute-start | bytes 196616 | tf_op jit(solution)/shard_map/ppermute | solution.py:18
  57.8 6.1 %collective-permute-start.22 = (bf16[128,256]{1,0:T(8,128)(2,1)S(1)}, bf16[128,256]{1,0:T(8,128)(2,1)S(1)}, u32[]{:S(2)}, u32[]{:S(2)}) collective-permute-start(bf16[128,256]{1,0:T(8,128)(2,1)S(1)} %get-tuple-element.59.refs_1_), channel_id=1, source_target_pairs={{0,3},{1,2},{2,1},{3,0},{4,7},{5,6},{6,5},{7,4},{8,11},{9,10},{10,... | collective-permute-start | bytes 196616 | tf_op jit(solution)/shard_map/ppermute | solution.py:18
  60.6 7.3 %collective-permute-start.26 = (f32[128,128]{1,0:T(8,128)S(1)}, f32[128,128]{1,0:T(8,128)S(1)}, u32[]{:S(2)}, u32[]{:S(2)}) collective-permute-start(f32[128,128]{1,0:T(8,128)S(1)} %get-tuple-element.54.mine_ref), channel_id=1, source_target_pairs={{0,16},{16,0},{1,17},{17,1},{2,18},{18,2},{3,19},{19,3},{4,20},{20... | collective-permute-start | bytes 196616 | tf_op jit(solution)/shard_map/ppermute | solution.py:18
  64.2 5.3 %collective-permute-start.23 = (bf16[128,256]{1,0:T(8,128)(2,1)S(1)}, bf16[128,256]{1,0:T(8,128)(2,1)S(1)}, u32[]{:S(2)}, u32[]{:S(2)}) collective-permute-start(bf16[128,256]{1,0:T(8,128)(2,1)S(1)} %get-tuple-element.51), channel_id=1, source_target_pairs={{0,4},{4,0},{8,12},{12,8},{1,5},{5,1},{9,13},{13,9},{2,6},{6,2},{1... | collective-permute-start | bytes 196616 | tf_op jit(solution)/shard_map/ppermute | solution.py:18
  64.9 4.6 %collective-permute-start.24 = (bf16[128,256]{1,0:T(8,128)(2,1)S(1)}, bf16[128,256]{1,0:T(8,128)(2,1)S(1)}, u32[]{:S(2)}, u32[]{:S(2)}) collective-permute-start(bf16[128,256]{1,0:T(8,128)(2,1)S(1)} %get-tuple-element.52), channel_id=1, source_target_pairs={{0,8},{4,12},{8,0},{12,4},{1,9},{5,13},{9,1},{13,5},{2,10},{6,14},... | collective-permute-start | bytes 196616 | tf_op jit(solution)/shard_map/ppermute | solution.py:18
  65.4 5.2 %collective-permute-start.25 = (bf16[128,256]{1,0:T(8,128)(2,1)S(1)}, bf16[128,256]{1,0:T(8,128)(2,1)S(1)}, u32[]{:S(2)}, u32[]{:S(2)}) collective-permute-start(bf16[128,256]{1,0:T(8,128)(2,1)S(1)} %get-tuple-element.53), channel_id=1, source_target_pairs={{0,12},{4,8},{8,4},{12,0},{1,13},{5,9},{9,5},{13,1},{2,14},{6,10},... | collective-permute-start | bytes 196616 | tf_op jit(solution)/shard_map/ppermute | solution.py:18
  (13 other events, 58.5 us)

commit v6 on v5

--- a/solution.py
+++ b/solution.py
@@ -14,6 +14,10 @@
     return n in (1, 2, 4)
 
 
+def steps_of(n):
+    return [0] + list(range(n - 1, 0, -1))
+
+
 def swap(values, axis, n, step):
     return lax.ppermute(values, axis, [(i, i ^ step) for i in range(n)])
 
@@ -25,13 +29,13 @@
 
 def gather(values, axis, n, step_to=swap):
     if is_direct(n):
-        return [values] + [step_to(values, axis, n, d) for d in range(1, n)]
+        return [values] + [step_to(values, axis, n, d) for d in steps_of(n)[1:]]
     return [lax.all_gather(values, axis, axis=0, tiled=True)]
 
 
 def scatter_sum(blocks, axis, n, step_to=swap):
     if is_direct(n):
-        return [blocks[0]] + [step_to(blocks[d], axis, n, d) for d in range(1, n)]
+        return [blocks[0]] + [step_to(block, axis, n, d) for block, d in zip(blocks[1:], steps_of(n)[1:])]
     return [lax.psum_scatter(blocks[0], axis, scatter_dimension=0, tiled=True)]
 
 
@@ -102,7 +106,7 @@
         return
     at = place(n, axis)
     size = pieces[0].shape[0]
-    for d, piece in enumerate(pieces):
+    for d, piece in zip(steps_of(n), pieces):
         buf[rows(at(d), size), :] = piece[...]
 
 
@@ -115,7 +119,7 @@
 def emit_blocks(term, outs, n, axis):
     at = place(n, axis)
     if is_direct(n):
-        for d, out_ref in zip(reversed(range(n)), reversed(outs)):
+        for d, out_ref in zip(reversed(steps_of(n)), reversed(outs)):
             out_ref[...] = term(at(d)).astype(out_ref.dtype)
     else:
         size = outs[0].shape[0] // n

time: 71.7 us -> 68.7 us (0.958)
  waiting for transfers between devices: 27 us -> 24 us
    ppermute x21, waiting for transfers between devices: 20.2 us -> 18.4 us  [swap(): return lax.ppermute(values, axis, [(i, i ^ step) for i in range(n)])]
    ppermute x6, waiting for transfers between devices: 6.8 us -> 5.66 us  [swap_cross(): return lax.ppermute(values, ('sec', axis), pairs)]
  transfers between devices with their start and end apart: 27 -> 27, of which waited for: 19 -> 21; matrix products, arithmetic and copies ran while one was open for 2% -> 2% of each run, Pallas kernels for 6% -> 6%
where the time goes in v6:
time: 68.7 us; the launch traced here: 68.4 us
  starting transfers between devices  32.3 us (47%)
  waiting for transfers between devices  24 us (35%)
  Pallas kernels  6.25 us (9%)
  local copies, waits for them, and re-layouts  3.21 us (5%)
  matrix products  1.73 us (3%)
  between operations  0.91 us (1%)
    ppermute x21, starting transfers between devices, swap(): return lax.ppermute(values, axis, [(i, i ^ step) for i in range(n)])  24.5 us
    ppermute x21, waiting for transfers between devices, swap(): return lax.ppermute(values, axis, [(i, i ^ step) for i in range(n)])  18.4 us
    ppermute x6, starting transfers between devices, swap_cross(): return lax.ppermute(values, ('sec', axis), pairs)  7.82 us
    pallas_call x21, Pallas kernels, call(): pl.pallas_call(kernel, out_shape=tuple((jax.ShapeDtypeStruct(s, t) for s,...  6.25 us
    ppermute x6, waiting for transfers between devices, swap_cross(): return lax.ppermute(values, ('sec', axis), pairs)  5.66 us
    unnamed x20, local copies, waits for them, and re-layouts  1.56 us
  transfers between devices with their start and end apart: 27, of which 21 were waited for; matrix products, arithmetic and copies ran while one was open for 2% of the time, Pallas kernels for 6%

profile of v6, /device:TPU:0, one launch (start us, length us, event | category | flops | bytes accessed | tf_op | source)
XLA Modules:
  0.0 68.4 jit_solution(7367460799654433591)
XLA Ops:
  1.8 4.0 %collective-permute-start = (bf16[128,256]{1,0:T(8,128)(2,1)S(1)}, bf16[128,256]{1,0:T(8,128)(2,1)S(1)}, u32[]{:S(2)}, u32[]{:S(2)}) collective-permute-start(bf16[128,256]{1,0:T(8,128)(2,1)S(1)} %get-tuple-element.55.refs_1_), channel_id=1, source_target_pairs={{0,12},{4,8},{8,4},{12,0},{1,13},{5,9},{9,5},{13,1},{2,14},{6,10},... | collective-permute-start | bytes 196616 | tf_op jit(solution)/shard_map/ppermute | solution.py:22
  6.4 1.3 %reshape.50.refs_1_ = bf16[4,128,512]{2,1,0:T(8,128)(2,1)S(1)} reshape(bf16[1,1,4,128,4,1,1,128]{7,4,6,5,3,2,1,0:T(4,128)(2,1)} %param.18) | data formatting | bytes 1048576 | tf_op jit(solution)/shard_map/reshape | solution.py:367
  8.0 2.0 %collective-permute-done.1.refs_3_ = bf16[128,256]{1,0:T(8,128)(2,1)S(1)} collective-permute-done((bf16[128,256]{1,0:T(8,128)(2,1)S(1)}, bf16[128,256]{1,0:T(8,128)(2,1)S(1)}, u32[]{:S(2)}, u32[]{:S(2)}) %collective-permute-start.1) | collective-permute-done | bytes 65568 | tf_op jit(solution)/shard_map/ppermute | solution.py:22
  10.8 3.7 %collective-permute-start.3 = (bf16[128,256]{1,0:T(8,128)(2,1)S(1)}, bf16[128,256]{1,0:T(8,128)(2,1)S(1)}, u32[]{:S(2)}, u32[]{:S(2)}) collective-permute-start(bf16[128,256]{1,0:T(8,128)(2,1)S(1)} %get-tuple-element.36), channel_id=1, source_target_pairs={{0,3},{1,2},{2,1},{3,0},{4,7},{5,6},{6,5},{7,4},{8,11},{9,10},{10,... | collective-permute-start | bytes 196616 | tf_op jit(solution)/shard_map/ppermute | solution.py:22
  18.0 1.7 %collective-permute-done.4 = bf16[128,256]{1,0:T(8,128)(2,1)S(1)} collective-permute-done((bf16[128,256]{1,0:T(8,128)(2,1)S(1)}, bf16[128,256]{1,0:T(8,128)(2,1)S(1)}, u32[]{:S(2)}, u32[]{:S(2)}) %collective-permute-start.4) | collective-permute-done | bytes 65568 | tf_op jit(solution)/shard_map/ppermute | solution.py:22
  20.0 1.7 %collective-permute-start.6 = (bf16[128,256]{1,0:T(8,128)(2,1)S(1)}, bf16[128,256]{1,0:T(8,128)(2,1)S(1)}, u32[]{:S(2)}, u32[]{:S(2)}) collective-permute-start(bf16[128,256]{1,0:T(8,128)(2,1)S(1)} %get-tuple-element.57.refs_1_), channel_id=1, source_target_pairs={{0,12},{4,8},{8,4},{12,0},{1,13},{5,9},{9,5},{13,1},{2,14},{6,10},... | collective-permute-start | bytes 196616 | tf_op jit(solution)/shard_map/ppermute | solution.py:22
  22.1 1.4 %collective-permute-start.8 = (bf16[128,256]{1,0:T(8,128)(2,1)S(1)}, bf16[128,256]{1,0:T(8,128)(2,1)S(1)}, u32[]{:S(2)}, u32[]{:S(2)}) collective-permute-start(bf16[128,256]{1,0:T(8,128)(2,1)S(1)} %get-tuple-element.57.refs_1_), channel_id=1, source_target_pairs={{0,4},{4,0},{8,12},{12,8},{1,5},{5,1},{9,13},{13,9},{2,6},{6,2},{1... | collective-permute-start | bytes 196616 | tf_op jit(solution)/shard_map/ppermute | solution.py:22
  23.5 1.7 %collective-permute-done.6.refs_2_ = bf16[128,256]{1,0:T(8,128)(2,1)S(1)} collective-permute-done((bf16[128,256]{1,0:T(8,128)(2,1)S(1)}, bf16[128,256]{1,0:T(8,128)(2,1)S(1)}, u32[]{:S(2)}, u32[]{:S(2)}) %collective-permute-start.6) | collective-permute-done | bytes 65568 | tf_op jit(solution)/shard_map/ppermute | solution.py:22
  28.4 2.2 %collective-permute-start.10 = (bf16[128,128]{1,0:T(8,128)(2,1)S(1)}, bf16[128,128]{1,0:T(8,128)(2,1)S(1)}, u32[]{:S(2)}, u32[]{:S(2)}) collective-permute-start(bf16[128,128]{1,0:T(8,128)(2,1)S(1)} %get-tuple-element.42), channel_id=1, source_target_pairs={{0,19},{1,18},{2,17},{3,16},{16,3},{17,2},{18,1},{19,0},{4,23},{5,... | collective-permute-start | bytes 98312 | tf_op jit(solution)/shard_map/ppermute | solution.py:27
  30.6 1.7 %collective-permute-start.12 = (bf16[128,128]{1,0:T(8,128)(2,1)S(1)}, bf16[128,128]{1,0:T(8,128)(2,1)S(1)}, u32[]{:S(2)}, u32[]{:S(2)}) collective-permute-start(bf16[128,128]{1,0:T(8,128)(2,1)S(1)} %get-tuple-element.44), channel_id=1, source_target_pairs={{0,17},{1,16},{2,19},{3,18},{16,1},{17,0},{18,3},{19,2},{4,21},{5,... | collective-permute-start | bytes 98312 | tf_op jit(solution)/shard_map/ppermute | solution.py:27
  33.6 1.8 %collective-permute-done.11.refs_2_ = bf16[128,128]{1,0:T(8,128)(2,1)S(1)} collective-permute-done((bf16[128,128]{1,0:T(8,128)(2,1)S(1)}, bf16[128,128]{1,0:T(8,128)(2,1)S(1)}, u32[]{:S(2)}, u32[]{:S(2)}) %collective-permute-start.11) | collective-permute-done | bytes 32800 | tf_op jit(solution)/shard_map/ppermute | solution.py:27
  35.8 2.1 %collective-permute-start.13 = (bf16[128,128]{1,0:T(8,128)(2,1)S(1)}, bf16[128,128]{1,0:T(8,128)(2,1)S(1)}, u32[]{:S(2)}, u32[]{:S(2)}) collective-permute-start(bf16[128,128]{1,0:T(8,128)(2,1)S(1)} %get-tuple-element.45.refs_0_), channel_id=1, source_target_pairs={{0,19},{1,18},{2,17},{3,16},{16,3},{17,2},{18,1},{19,0},{4,23},{5,... | collective-permute-start | bytes 98312 | tf_op jit(solution)/shard_map/ppermute | solution.py:27
  37.9 1.8 %collective-permute-start.15 = (bf16[128,128]{1,0:T(8,128)(2,1)S(1)}, bf16[128,128]{1,0:T(8,128)(2,1)S(1)}, u32[]{:S(2)}, u32[]{:S(2)}) collective-permute-start(bf16[128,128]{1,0:T(8,128)(2,1)S(1)} %get-tuple-element.45.refs_0_), channel_id=1, source_target_pairs={{0,17},{1,16},{2,19},{3,18},{16,1},{17,0},{18,3},{19,2},{4,21},{5,... | collective-permute-start | bytes 98312 | tf_op jit(solution)/shard_map/ppermute | solution.py:27
  39.7 1.4 %collective-permute-done.13.refs_1_ = bf16[128,128]{1,0:T(8,128)(2,1)S(1)} collective-permute-done((bf16[128,128]{1,0:T(8,128)(2,1)S(1)}, bf16[128,128]{1,0:T(8,128)(2,1)S(1)}, u32[]{:S(2)}, u32[]{:S(2)}) %collective-permute-start.13) | collective-permute-done | bytes 32800 | tf_op jit(solution)/shard_map/ppermute | solution.py:27
  41.0 1.4 %collective-permute-done.14.refs_2_ = bf16[128,128]{1,0:T(8,128)(2,1)S(1)} collective-permute-done((bf16[128,128]{1,0:T(8,128)(2,1)S(1)}, bf16[128,128]{1,0:T(8,128)(2,1)S(1)}, u32[]{:S(2)}, u32[]{:S(2)}) %collective-permute-start.14) | collective-permute-done | bytes 32800 | tf_op jit(solution)/shard_map/ppermute | solution.py:27
  44.2 2.4 %collective-permute-start.17 = (bf16[128,256]{1,0:T(8,128)(2,1)S(1)}, bf16[128,256]{1,0:T(8,128)(2,1)S(1)}, u32[]{:S(2)}, u32[]{:S(2)}) collective-permute-start(bf16[128,256]{1,0:T(8,128)(2,1)S(1)} %get-tuple-element.47), channel_id=1, source_target_pairs={{0,12},{4,8},{8,4},{12,0},{1,13},{5,9},{9,5},{13,1},{2,14},{6,10},... | collective-permute-start | bytes 196616 | tf_op jit(solution)/shard_map/ppermute | solution.py:22
  48.0 1.5 %collective-permute-done.17 = bf16[128,256]{1,0:T(8,128)(2,1)S(1)} collective-permute-done((bf16[128,256]{1,0:T(8,128)(2,1)S(1)}, bf16[128,256]{1,0:T(8,128)(2,1)S(1)}, u32[]{:S(2)}, u32[]{:S(2)}) %collective-permute-start.17) | collective-permute-done | bytes 65568 | tf_op jit(solution)/shard_map/ppermute | solution.py:22
  49.5 1.4 %collective-permute-done.18 = bf16[128,256]{1,0:T(8,128)(2,1)S(1)} collective-permute-done((bf16[128,256]{1,0:T(8,128)(2,1)S(1)}, bf16[128,256]{1,0:T(8,128)(2,1)S(1)}, u32[]{:S(2)}, u32[]{:S(2)}) %collective-permute-start.18) | collective-permute-done | bytes 65568 | tf_op jit(solution)/shard_map/ppermute | solution.py:22
  51.7 2.7 %collective-permute-start.20 = (bf16[128,256]{1,0:T(8,128)(2,1)S(1)}, bf16[128,256]{1,0:T(8,128)(2,1)S(1)}, u32[]{:S(2)}, u32[]{:S(2)}) collective-permute-start(bf16[128,256]{1,0:T(8,128)(2,1)S(1)} %get-tuple-element.59.refs_1_), channel_id=1, source_target_pairs={{0,3},{1,2},{2,1},{3,0},{4,7},{5,6},{6,5},{7,4},{8,11},{9,10},{10,... | collective-permute-start | bytes 196616 | tf_op jit(solution)/shard_map/ppermute | solution.py:22
  54.4 1.7 %collective-permute-start.22 = (bf16[128,256]{1,0:T(8,128)(2,1)S(1)}, bf16[128,256]{1,0:T(8,128)(2,1)S(1)}, u32[]{:S(2)}, u32[]{:S(2)}) collective-permute-start(bf16[128,256]{1,0:T(8,128)(2,1)S(1)} %get-tuple-element.59.refs_1_), channel_id=1, source_target_pairs={{0,1},{1,0},{2,3},{3,2},{4,5},{5,4},{6,7},{7,6},{8,9},{9,8},{10,11... | collective-permute-start | bytes 196616 | tf_op jit(solution)/shard_map/ppermute | solution.py:22
  56.5 1.8 %collective-permute-done.20.refs_2_ = bf16[128,256]{1,0:T(8,128)(2,1)S(1)} collective-permute-done((bf16[128,256]{1,0:T(8,128)(2,1)S(1)}, bf16[128,256]{1,0:T(8,128)(2,1)S(1)}, u32[]{:S(2)}, u32[]{:S(2)}) %collective-permute-start.20) | collective-permute-done | bytes 65568 | tf_op jit(solution)/shard_map/ppermute | solution.py:22
  58.3 1.6 %collective-permute-done.21.refs_3_ = bf16[128,256]{1,0:T(8,128)(2,1)S(1)} collective-permute-done((bf16[128,256]{1,0:T(8,128)(2,1)S(1)}, bf16[128,256]{1,0:T(8,128)(2,1)S(1)}, u32[]{:S(2)}, u32[]{:S(2)}) %collective-permute-start.21) | collective-permute-done | bytes 65568 | tf_op jit(solution)/shard_map/ppermute | solution.py:22
  60.3 1.5 %collective-permute-start.23 = (bf16[128,256]{1,0:T(8,128)(2,1)S(1)}, bf16[128,256]{1,0:T(8,128)(2,1)S(1)}, u32[]{:S(2)}, u32[]{:S(2)}) collective-permute-start(bf16[128,256]{1,0:T(8,128)(2,1)S(1)} %get-tuple-element.51), channel_id=1, source_target_pairs={{0,12},{4,8},{8,4},{12,0},{1,13},{5,9},{9,5},{13,1},{2,14},{6,10},... | collective-permute-start | bytes 196616 | tf_op jit(solution)/shard_map/ppermute | solution.py:22
  61.8 1.5 %collective-permute-start.24 = (bf16[128,256]{1,0:T(8,128)(2,1)S(1)}, bf16[128,256]{1,0:T(8,128)(2,1)S(1)}, u32[]{:S(2)}, u32[]{:S(2)}) collective-permute-start(bf16[128,256]{1,0:T(8,128)(2,1)S(1)} %get-tuple-element.52), channel_id=1, source_target_pairs={{0,8},{4,12},{8,0},{12,4},{1,9},{5,13},{9,1},{13,5},{2,10},{6,14},... | collective-permute-start | bytes 196616 | tf_op jit(solution)/shard_map/ppermute | solution.py:22
  (77 shorter events, 21.9 us)
Async XLA Ops:
  1.8 6.2 %collective-permute-start = (bf16[128,256]{1,0:T(8,128)(2,1)S(1)}, bf16[128,256]{1,0:T(8,128)(2,1)S(1)}, u32[]{:S(2)}, u32[]{:S(2)}) collective-permute-start(bf16[128,256]{1,0:T(8,128)(2,1)S(1)} %get-tuple-element.55.refs_1_), channel_id=1, source_target_pairs={{0,12},{4,8},{8,4},{12,0},{1,13},{5,9},{9,5},{13,1},{2,14},{6,10},... | collective-permute-start | bytes 196616 | tf_op jit(solution)/shard_map/ppermute | solution.py:22
  5.7 4.3 %collective-permute-start.1 = (bf16[128,256]{1,0:T(8,128)(2,1)S(1)}, bf16[128,256]{1,0:T(8,128)(2,1)S(1)}, u32[]{:S(2)}, u32[]{:S(2)}) collective-permute-start(bf16[128,256]{1,0:T(8,128)(2,1)S(1)} %get-tuple-element.55.refs_1_), channel_id=1, source_target_pairs={{0,8},{4,12},{8,0},{12,4},{1,9},{5,13},{9,1},{13,5},{2,10},{6,14},... | collective-permute-start | bytes 196616 | tf_op jit(solution)/shard_map/ppermute | solution.py:22
  6.2 4.3 %collective-permute-start.2 = (bf16[128,256]{1,0:T(8,128)(2,1)S(1)}, bf16[128,256]{1,0:T(8,128)(2,1)S(1)}, u32[]{:S(2)}, u32[]{:S(2)}) collective-permute-start(bf16[128,256]{1,0:T(8,128)(2,1)S(1)} %get-tuple-element.55.refs_1_), channel_id=1, source_target_pairs={{0,4},{4,0},{8,12},{12,8},{1,5},{5,1},{9,13},{13,9},{2,6},{6,2},{1... | collective-permute-start | bytes 196616 | tf_op jit(solution)/shard_map/ppermute | solution.py:22
  10.8 7.2 %collective-permute-start.3 = (bf16[128,256]{1,0:T(8,128)(2,1)S(1)}, bf16[128,256]{1,0:T(8,128)(2,1)S(1)}, u32[]{:S(2)}, u32[]{:S(2)}) collective-permute-start(bf16[128,256]{1,0:T(8,128)(2,1)S(1)} %get-tuple-element.36), channel_id=1, source_target_pairs={{0,3},{1,2},{2,1},{3,0},{4,7},{5,6},{6,5},{7,4},{8,11},{9,10},{10,... | collective-permute-start | bytes 196616 | tf_op jit(solution)/shard_map/ppermute | solution.py:22
  14.5 5.2 %collective-permute-start.4 = (bf16[128,256]{1,0:T(8,128)(2,1)S(1)}, bf16[128,256]{1,0:T(8,128)(2,1)S(1)}, u32[]{:S(2)}, u32[]{:S(2)}) collective-permute-start(bf16[128,256]{1,0:T(8,128)(2,1)S(1)} %get-tuple-element.37), channel_id=1, source_target_pairs={{0,2},{1,3},{2,0},{3,1},{4,6},{5,7},{6,4},{7,5},{8,10},{9,11},{10,... | collective-permute-start | bytes 196616 | tf_op jit(solution)/shard_map/ppermute | solution.py:22
  14.5 5.2 %collective-permute-start.5 = (bf16[128,256]{1,0:T(8,128)(2,1)S(1)}, bf16[128,256]{1,0:T(8,128)(2,1)S(1)}, u32[]{:S(2)}, u32[]{:S(2)}) collective-permute-start(bf16[128,256]{1,0:T(8,128)(2,1)S(1)} %get-tuple-element.38), channel_id=1, source_target_pairs={{0,1},{1,0},{2,3},{3,2},{4,5},{5,4},{6,7},{7,6},{8,9},{9,8},{10,11... | collective-permute-start | bytes 196616 | tf_op jit(solution)/shard_map/ppermute | solution.py:22
  20.0 5.2 %collective-permute-start.6 = (bf16[128,256]{1,0:T(8,128)(2,1)S(1)}, bf16[128,256]{1,0:T(8,128)(2,1)S(1)}, u32[]{:S(2)}, u32[]{:S(2)}) collective-permute-start(bf16[128,256]{1,0:T(8,128)(2,1)S(1)} %get-tuple-element.57.refs_1_), channel_id=1, source_target_pairs={{0,12},{4,8},{8,4},{12,0},{1,13},{5,9},{9,5},{13,1},{2,14},{6,10},... | collective-permute-start | bytes 196616 | tf_op jit(solution)/shard_map/ppermute | solution.py:22
  21.6 4.3 %collective-permute-start.7 = (bf16[128,256]{1,0:T(8,128)(2,1)S(1)}, bf16[128,256]{1,0:T(8,128)(2,1)S(1)}, u32[]{:S(2)}, u32[]{:S(2)}) collective-permute-start(bf16[128,256]{1,0:T(8,128)(2,1)S(1)} %get-tuple-element.57.refs_1_), channel_id=1, source_target_pairs={{0,8},{4,12},{8,0},{12,4},{1,9},{5,13},{9,1},{13,5},{2,10},{6,14},... | collective-permute-start | bytes 196616 | tf_op jit(solution)/shard_map/ppermute | solution.py:22
  22.1 4.3 %collective-permute-start.8 = (bf16[128,256]{1,0:T(8,128)(2,1)S(1)}, bf16[128,256]{1,0:T(8,128)(2,1)S(1)}, u32[]{:S(2)}, u32[]{:S(2)}) collective-permute-start(bf16[128,256]{1,0:T(8,128)(2,1)S(1)} %get-tuple-element.57.refs_1_), channel_id=1, source_target_pairs={{0,4},{4,0},{8,12},{12,8},{1,5},{5,1},{9,13},{13,9},{2,6},{6,2},{1... | collective-permute-start | bytes 196616 | tf_op jit(solution)/shard_map/ppermute | solution.py:22
  28.4 5.2 %collective-permute-start.10 = (bf16[128,128]{1,0:T(8,128)(2,1)S(1)}, bf16[128,128]{1,0:T(8,128)(2,1)S(1)}, u32[]{:S(2)}, u32[]{:S(2)}) collective-permute-start(bf16[128,128]{1,0:T(8,128)(2,1)S(1)} %get-tuple-element.42), channel_id=1, source_target_pairs={{0,19},{1,18},{2,17},{3,16},{16,3},{17,2},{18,1},{19,0},{4,23},{5,... | collective-permute-start | bytes 98312 | tf_op jit(solution)/shard_map/ppermute | solution.py:27
  30.6 4.8 %collective-permute-start.11 = (bf16[128,128]{1,0:T(8,128)(2,1)S(1)}, bf16[128,128]{1,0:T(8,128)(2,1)S(1)}, u32[]{:S(2)}, u32[]{:S(2)}) collective-permute-start(bf16[128,128]{1,0:T(8,128)(2,1)S(1)} %get-tuple-element.43), channel_id=1, source_target_pairs={{0,18},{1,19},{2,16},{3,17},{16,2},{17,3},{18,0},{19,1},{4,22},{5,... | collective-permute-start | bytes 98312 | tf_op jit(solution)/shard_map/ppermute | solution.py:27
  30.6 4.8 %collective-permute-start.12 = (bf16[128,128]{1,0:T(8,128)(2,1)S(1)}, bf16[128,128]{1,0:T(8,128)(2,1)S(1)}, u32[]{:S(2)}, u32[]{:S(2)}) collective-permute-start(bf16[128,128]{1,0:T(8,128)(2,1)S(1)} %get-tuple-element.44), channel_id=1, source_target_pairs={{0,17},{1,16},{2,19},{3,18},{16,1},{17,0},{18,3},{19,2},{4,21},{5,... | collective-permute-start | bytes 98312 | tf_op jit(solution)/shard_map/ppermute | solution.py:27
  35.8 5.3 %collective-permute-start.13 = (bf16[128,128]{1,0:T(8,128)(2,1)S(1)}, bf16[128,128]{1,0:T(8,128)(2,1)S(1)}, u32[]{:S(2)}, u32[]{:S(2)}) collective-permute-start(bf16[128,128]{1,0:T(8,128)(2,1)S(1)} %get-tuple-element.45.refs_0_), channel_id=1, source_target_pairs={{0,19},{1,18},{2,17},{3,16},{16,3},{17,2},{18,1},{19,0},{4,23},{5,... | collective-permute-start | bytes 98312 | tf_op jit(solution)/shard_map/ppermute | solution.py:27
  37.9 4.5 %collective-permute-start.14 = (bf16[128,128]{1,0:T(8,128)(2,1)S(1)}, bf16[128,128]{1,0:T(8,128)(2,1)S(1)}, u32[]{:S(2)}, u32[]{:S(2)}) collective-permute-start(bf16[128,128]{1,0:T(8,128)(2,1)S(1)} %get-tuple-element.45.refs_0_), channel_id=1, source_target_pairs={{0,18},{1,19},{2,16},{3,17},{16,2},{17,3},{18,0},{19,1},{4,22},{5,... | collective-permute-start | bytes 98312 | tf_op jit(solution)/shard_map/ppermute | solution.py:27
  37.9 4.5 %collective-permute-start.15 = (bf16[128,128]{1,0:T(8,128)(2,1)S(1)}, bf16[128,128]{1,0:T(8,128)(2,1)S(1)}, u32[]{:S(2)}, u32[]{:S(2)}) collective-permute-start(bf16[128,128]{1,0:T(8,128)(2,1)S(1)} %get-tuple-element.45.refs_0_), channel_id=1, source_target_pairs={{0,17},{1,16},{2,19},{3,18},{16,1},{17,0},{18,3},{19,2},{4,21},{5,... | collective-permute-start | bytes 98312 | tf_op jit(solution)/shard_map/ppermute | solution.py:27
  44.2 5.3 %collective-permute-start.17 = (bf16[128,256]{1,0:T(8,128)(2,1)S(1)}, bf16[128,256]{1,0:T(8,128)(2,1)S(1)}, u32[]{:S(2)}, u32[]{:S(2)}) collective-permute-start(bf16[128,256]{1,0:T(8,128)(2,1)S(1)} %get-tuple-element.47), channel_id=1, source_target_pairs={{0,12},{4,8},{8,4},{12,0},{1,13},{5,9},{9,5},{13,1},{2,14},{6,10},... | collective-permute-start | bytes 196616 | tf_op jit(solution)/shard_map/ppermute | solution.py:22
  46.6 4.3 %collective-permute-start.18 = (bf16[128,256]{1,0:T(8,128)(2,1)S(1)}, bf16[128,256]{1,0:T(8,128)(2,1)S(1)}, u32[]{:S(2)}, u32[]{:S(2)}) collective-permute-start(bf16[128,256]{1,0:T(8,128)(2,1)S(1)} %get-tuple-element.48), channel_id=1, source_target_pairs={{0,8},{4,12},{8,0},{12,4},{1,9},{5,13},{9,1},{13,5},{2,10},{6,14},... | collective-permute-start | bytes 196616 | tf_op jit(solution)/shard_map/ppermute | solution.py:22
  51.7 6.6 %collective-permute-start.20 = (bf16[128,256]{1,0:T(8,128)(2,1)S(1)}, bf16[128,256]{1,0:T(8,128)(2,1)S(1)}, u32[]{:S(2)}, u32[]{:S(2)}) collective-permute-start(bf16[128,256]{1,0:T(8,128)(2,1)S(1)} %get-tuple-element.59.refs_1_), channel_id=1, source_target_pairs={{0,3},{1,2},{2,1},{3,0},{4,7},{5,6},{6,5},{7,4},{8,11},{9,10},{10,... | collective-permute-start | bytes 196616 | tf_op jit(solution)/shard_map/ppermute | solution.py:22
  54.4 5.5 %collective-permute-start.21 = (bf16[128,256]{1,0:T(8,128)(2,1)S(1)}, bf16[128,256]{1,0:T(8,128)(2,1)S(1)}, u32[]{:S(2)}, u32[]{:S(2)}) collective-permute-start(bf16[128,256]{1,0:T(8,128)(2,1)S(1)} %get-tuple-element.59.refs_1_), channel_id=1, source_target_pairs={{0,2},{1,3},{2,0},{3,1},{4,6},{5,7},{6,4},{7,5},{8,10},{9,11},{10,... | collective-permute-start | bytes 196616 | tf_op jit(solution)/shard_map/ppermute | solution.py:22
  54.4 5.5 %collective-permute-start.22 = (bf16[128,256]{1,0:T(8,128)(2,1)S(1)}, bf16[128,256]{1,0:T(8,128)(2,1)S(1)}, u32[]{:S(2)}, u32[]{:S(2)}) collective-permute-start(bf16[128,256]{1,0:T(8,128)(2,1)S(1)} %get-tuple-element.59.refs_1_), channel_id=1, source_target_pairs={{0,1},{1,0},{2,3},{3,2},{4,5},{5,4},{6,7},{7,6},{8,9},{9,8},{10,11... | collective-permute-start | bytes 196616 | tf_op jit(solution)/shard_map/ppermute | solution.py:22
  56.1 7.8 %collective-permute-start.26 = (f32[128,128]{1,0:T(8,128)S(1)}, f32[128,128]{1,0:T(8,128)S(1)}, u32[]{:S(2)}, u32[]{:S(2)}) collective-permute-start(f32[128,128]{1,0:T(8,128)S(1)} %get-tuple-element.54.mine_ref), channel_id=1, source_target_pairs={{0,16},{16,0},{1,17},{17,1},{2,18},{18,2},{3,19},{19,3},{4,20},{20... | collective-permute-start | bytes 196616 | tf_op jit(solution)/shard_map/ppermute | solution.py:22
  60.3 5.7 %collective-permute-start.23 = (bf16[128,256]{1,0:T(8,128)(2,1)S(1)}, bf16[128,256]{1,0:T(8,128)(2,1)S(1)}, u32[]{:S(2)}, u32[]{:S(2)}) collective-permute-start(bf16[128,256]{1,0:T(8,128)(2,1)S(1)} %get-tuple-element.51), channel_id=1, source_target_pairs={{0,12},{4,8},{8,4},{12,0},{1,13},{5,9},{9,5},{13,1},{2,14},{6,10},... | collective-permute-start | bytes 196616 | tf_op jit(solution)/shard_map/ppermute | solution.py:22
  61.8 4.6 %collective-permute-start.24 = (bf16[128,256]{1,0:T(8,128)(2,1)S(1)}, bf16[128,256]{1,0:T(8,128)(2,1)S(1)}, u32[]{:S(2)}, u32[]{:S(2)}) collective-permute-start(bf16[128,256]{1,0:T(8,128)(2,1)S(1)} %get-tuple-element.52), channel_id=1, source_target_pairs={{0,8},{4,12},{8,0},{12,4},{1,9},{5,13},{9,1},{13,5},{2,10},{6,14},... | collective-permute-start | bytes 196616 | tf_op jit(solution)/shard_map/ppermute | solution.py:22
  63.3 4.3 %collective-permute-start.25 = (bf16[128,256]{1,0:T(8,128)(2,1)S(1)}, bf16[128,256]{1,0:T(8,128)(2,1)S(1)}, u32[]{:S(2)}, u32[]{:S(2)}) collective-permute-start(bf16[128,256]{1,0:T(8,128)(2,1)S(1)} %get-tuple-element.53), channel_id=1, source_target_pairs={{0,4},{4,0},{8,12},{12,8},{1,5},{5,1},{9,13},{13,9},{2,6},{6,2},{1... | collective-permute-start | bytes 196616 | tf_op jit(solution)/shard_map/ppermute | solution.py:22
  (13 other events, 54.9 us)

commit v7 on v5

--- a/solution.py
+++ b/solution.py
@@ -14,6 +14,13 @@
     return n in (1, 2, 4)
 
 
+ORDERS = {"row": (3, 1, 2), "col": (2, 3, 1), "cross": (2, 3, 1)}
+
+
+def steps_of(n, kind):
+    return [0] + [d for d in ORDERS[kind] if d < n]
+
+
 def swap(values, axis, n, step):
     return lax.ppermute(values, axis, [(i, i ^ step) for i in range(n)])
 
@@ -23,15 +30,19 @@
     return lax.ppermute(values, ("sec", axis), pairs)
 
 
+def kind_of(step_to, axis):
+    return "cross" if step_to is swap_cross else axis
+
+
 def gather(values, axis, n, step_to=swap):
     if is_direct(n):
-        return [values] + [step_to(values, axis, n, d) for d in range(1, n)]
+        return [values] + [step_to(values, axis, n, d) for d in steps_of(n, kind_of(step_to, axis))[1:]]
     return [lax.all_gather(values, axis, axis=0, tiled=True)]
 
 
 def scatter_sum(blocks, axis, n, step_to=swap):
     if is_direct(n):
-        return [blocks[0]] + [step_to(blocks[d], axis, n, d) for d in range(1, n)]
+        return [blocks[0]] + [step_to(block, axis, n, d) for block, d in zip(blocks[1:], steps_of(n, kind_of(step_to, axis))[1:])]
     return [lax.psum_scatter(blocks[0], axis, scatter_dimension=0, tiled=True)]
 
 
@@ -96,13 +107,13 @@
     return total
 
 
-def lay_out(pieces, buf, n, axis):
+def lay_out(pieces, buf, n, axis, kind=None):
     if not is_direct(n):
         buf[...] = pieces[0][...]
         return
     at = place(n, axis)
     size = pieces[0].shape[0]
-    for d, piece in enumerate(pieces):
+    for d, piece in zip(steps_of(n, kind or axis), pieces):
         buf[rows(at(d), size), :] = piece[...]
 
 
@@ -112,10 +123,10 @@
     return [((n * size, cols), F32)]
 
 
-def emit_blocks(term, outs, n, axis):
+def emit_blocks(term, outs, n, axis, kind=None):
     at = place(n, axis)
     if is_direct(n):
-        for d, out_ref in zip(reversed(range(n)), reversed(outs)):
+        for d, out_ref in zip(reversed(steps_of(n, kind or axis)), reversed(outs)):
             out_ref[...] = term(at(d)).astype(out_ref.dtype)
     else:
         size = outs[0].shape[0] // n
@@ -250,25 +261,37 @@
     half = mine.shape[1]
 
     def kernel(mine_ref, other_ref, *outs):
-        emit_blocks(lambda i: mine_ref[rows(i, width), :] + other_ref[rows(i, width), :], outs, n_col, "col")
+        emit_blocks(lambda i: mine_ref[rows(i, width), :] + other_ref[rows(i, width), :], outs, n_col, "col", "cross")
 
     return call(kernel, block_outs(n_col, width, half), [mine, other])
 
 
-def solve_top(sums, right_side, lower, upper, n_col):
+def square_inverse(inverse):
+    width = inverse.shape[1]
+
+    def kernel(inv_ref, out_ref):
+        value = inv_ref[0]
+        full = lax.dot_general(value, value, (((0,), (0,)), ((), ())), precision=lax.Precision.HIGHEST, preferred_element_type=F32)
+        high, low = split(full)
+        for k, part in enumerate((high, low, high)):
+            out_ref[:, pl.ds(k * width, width)] = part
+
+    return call(kernel, [((width, 3 * width), BF)], [inverse])[0]
+
+
+def solve_top(sums, right_side, square, n_col):
     count = len(sums)
     half = right_side.shape[1] // 2
 
     def kernel(*refs):
-        rhs_ref, low_ref, up_ref, x_ref, xb_ref = refs[count:]
+        rhs_ref, sq_ref, x_ref, xb_ref = refs[count:]
         mine = rhs_ref[:, rows(own_half(n_col), half)].astype(F32)
-        y = apply_split(low_ref[0], mine - total_of(refs[:count]))
-        x = apply_split(up_ref[0], y)
+        x = apply_split(sq_ref[...], mine - total_of(refs[:count]))
         x_ref[...] = x
         xb_ref[...] = x.astype(BF)
 
     shape = (right_side.shape[0], half)
-    return call(kernel, [(shape, F32), (shape, BF)], [*sums, right_side, lower, upper])
+    return call(kernel, [(shape, F32), (shape, BF)], [*sums, right_side, square])
 
 
 def stack_pieces(pieces, n, axis):
@@ -276,7 +299,7 @@
         return pieces[0]
 
     def kernel(*refs):
-        lay_out(refs[:-1], refs[-1], n, axis)
+        lay_out(refs[:-1], refs[-1], n, axis, "cross")
 
     shape = (n * pieces[0].shape[0], pieces[0].shape[1])
     return call(kernel, [(shape, BF)], list(pieces))[0]
@@ -376,8 +399,7 @@
         kept = top_half(ts, pieces, leaf_part, n_row, n_col, width, False)
         blocks = add_sections(kept, passed, n_col, width)
         sums = scatter_sum(blocks, "col", n_col, swap_cross)
-        lower, upper = split_inverse(top_inv[0], False), split_inverse(top_inv[0], True)
-        top_xh, top_xhb = solve_top(sums, top_rhs[0, 0], lower, upper, n_col)
+        top_xh, top_xhb = solve_top(sums, top_rhs[0, 0], square_inverse(top_inv[0]), n_col)
         top_stack = stack_pieces(gather(top_xhb, "col", n_col, swap_cross), n_col, "col")
         blocks, top_row = top_back_blocks(ts, top_stack, swap(top_stack, "sec", 2, 1), n_row, n_col, width)
         sums = scatter_sum(blocks, "row", n_row)

time: 71.7 us -> 67.5 us (0.941)
  starting transfers between devices: 32.3 us -> 29.9 us
  waiting for transfers between devices: 27 us -> 25.3 us
    ppermute x6, starting transfers between devices: 7.87 us -> 6.43 us  [swap_cross(): return lax.ppermute(values, ('sec', axis), pairs)]
    ppermute x21, waiting for transfers between devices: 20.2 us -> 19 us  [swap(): return lax.ppermute(values, axis, [(i, i ^ step) for i in range(n)])]
    ppermute x21, starting transfers between devices: 24.4 us -> 23.5 us  [swap(): return lax.ppermute(values, axis, [(i, i ^ step) for i in range(n)])]
    pallas_call x21 -> x20, Pallas kernels: 6.24 us -> 6.24 us  [call(): pl.pallas_call(kernel, out_shape=tuple((jax.ShapeDtypeStruct(s, t) for s,...]
  transfers between devices with their start and end apart: 27 -> 27, of which waited for: 19 -> 22; matrix products, arithmetic and copies ran while one was open for 2% -> 2% of each run, Pallas kernels for 6% -> 6%
where the time goes in v7:
time: 67.5 us; the launch traced here: 67.3 us
  starting transfers between devices  29.9 us (44%)
  waiting for transfers between devices  25.3 us (37%)
  Pallas kernels  6.24 us (9%)
  local copies, waits for them, and re-layouts  3.21 us (5%)
  matrix products  1.73 us (3%)
  between operations  0.9 us (1%)
    ppermute x21, starting transfers between devices, swap(): return lax.ppermute(values, axis, [(i, i ^ step) for i in range(n)])  23.5 us
    ppermute x21, waiting for transfers between devices, swap(): return lax.ppermute(values, axis, [(i, i ^ step) for i in range(n)])  19 us
    ppermute x6, starting transfers between devices, swap_cross(): return lax.ppermute(values, ('sec', axis), pairs)  6.43 us
    ppermute x6, waiting for transfers between devices, swap_cross(): return lax.ppermute(values, ('sec', axis), pairs)  6.26 us
    pallas_call x20, Pallas kernels, call(): pl.pallas_call(kernel, out_shape=tuple((jax.ShapeDtypeStruct(s, t) for s,...  6.24 us
    unnamed x20, local copies, waits for them, and re-layouts  1.56 us
  transfers between devices with their start and end apart: 27, of which 22 were waited for; matrix products, arithmetic and copies ran while one was open for 2% of the time, Pallas kernels for 6%

profile of v7, /device:TPU:0, one launch (start us, length us, event | category | flops | bytes accessed | tf_op | source)
XLA Modules:
  0.0 67.3 jit_solution(4487632042337863584)
XLA Ops:
  0.6 1.1 %fusion.19 = (bf16[128,256]{1,0:T(8,128)(2,1)S(1)}, f32[128,256]{1,0:T(8,128)S(1)}) fusion(bf16[1,1,1,1,128,256]{5,4,3,2,1,0:T(8,128)(2,1)} %param.12, f32[1,1,1,1,128,128]{5,4,3,2,1,0:T(8,128)} %param.15), kind=kOutput, calls=%fused_computation.22 | convolution fusion | flops 50364416 | bytes 327680 | tf_op jit(solution)/shard_map/mab,mbn->man/dot_general | solution.py:138
  1.8 4.0 %collective-permute-start = (bf16[128,256]{1,0:T(8,128)(2,1)S(1)}, bf16[128,256]{1,0:T(8,128)(2,1)S(1)}, u32[]{:S(2)}, u32[]{:S(2)}) collective-permute-start(bf16[128,256]{1,0:T(8,128)(2,1)S(1)} %get-tuple-element.55.refs_1_), channel_id=1, source_target_pairs={{0,12},{4,8},{8,4},{12,0},{1,13},{5,9},{9,5},{13,1},{2,14},{6,10},... | collective-permute-start | bytes 196616 | tf_op jit(solution)/shard_map/ppermute | solution.py:25
  6.4 1.3 %reshape.50.refs_1_ = bf16[4,128,512]{2,1,0:T(8,128)(2,1)S(1)} reshape(bf16[1,1,4,128,4,1,1,128]{7,4,6,5,3,2,1,0:T(4,128)(2,1)} %param.18) | data formatting | bytes 1048576 | tf_op jit(solution)/shard_map/reshape | solution.py:386
  8.2 1.8 %collective-permute-done.1.refs_3_ = bf16[128,256]{1,0:T(8,128)(2,1)S(1)} collective-permute-done((bf16[128,256]{1,0:T(8,128)(2,1)S(1)}, bf16[128,256]{1,0:T(8,128)(2,1)S(1)}, u32[]{:S(2)}, u32[]{:S(2)}) %collective-permute-start.1) | collective-permute-done | bytes 65568 | tf_op jit(solution)/shard_map/ppermute | solution.py:25
  10.8 2.7 %collective-permute-start.3 = (bf16[128,256]{1,0:T(8,128)(2,1)S(1)}, bf16[128,256]{1,0:T(8,128)(2,1)S(1)}, u32[]{:S(2)}, u32[]{:S(2)}) collective-permute-start(bf16[128,256]{1,0:T(8,128)(2,1)S(1)} %get-tuple-element.36), channel_id=1, source_target_pairs={{0,2},{1,3},{2,0},{3,1},{4,6},{5,7},{6,4},{7,5},{8,10},{9,11},{10,... | collective-permute-start | bytes 196616 | tf_op jit(solution)/shard_map/ppermute | solution.py:25
  13.5 1.3 %collective-permute-start.4 = (bf16[128,256]{1,0:T(8,128)(2,1)S(1)}, bf16[128,256]{1,0:T(8,128)(2,1)S(1)}, u32[]{:S(2)}, u32[]{:S(2)}) collective-permute-start(bf16[128,256]{1,0:T(8,128)(2,1)S(1)} %get-tuple-element.37), channel_id=1, source_target_pairs={{0,3},{1,2},{2,1},{3,0},{4,7},{5,6},{6,5},{7,4},{8,11},{9,10},{10,... | collective-permute-start | bytes 196616 | tf_op jit(solution)/shard_map/ppermute | solution.py:25
  17.8 1.9 %collective-permute-done.4 = bf16[128,256]{1,0:T(8,128)(2,1)S(1)} collective-permute-done((bf16[128,256]{1,0:T(8,128)(2,1)S(1)}, bf16[128,256]{1,0:T(8,128)(2,1)S(1)}, u32[]{:S(2)}, u32[]{:S(2)}) %collective-permute-start.4) | collective-permute-done | bytes 65568 | tf_op jit(solution)/shard_map/ppermute | solution.py:25
  20.1 1.5 %collective-permute-start.6 = (bf16[128,256]{1,0:T(8,128)(2,1)S(1)}, bf16[128,256]{1,0:T(8,128)(2,1)S(1)}, u32[]{:S(2)}, u32[]{:S(2)}) collective-permute-start(bf16[128,256]{1,0:T(8,128)(2,1)S(1)} %get-tuple-element.57.refs_1_), channel_id=1, source_target_pairs={{0,12},{4,8},{8,4},{12,0},{1,13},{5,9},{9,5},{13,1},{2,14},{6,10},... | collective-permute-start | bytes 196616 | tf_op jit(solution)/shard_map/ppermute | solution.py:25
  22.3 1.4 %collective-permute-start.8 = (bf16[128,256]{1,0:T(8,128)(2,1)S(1)}, bf16[128,256]{1,0:T(8,128)(2,1)S(1)}, u32[]{:S(2)}, u32[]{:S(2)}) collective-permute-start(bf16[128,256]{1,0:T(8,128)(2,1)S(1)} %get-tuple-element.57.refs_1_), channel_id=1, source_target_pairs={{0,8},{4,12},{8,0},{12,4},{1,9},{5,13},{9,1},{13,5},{2,10},{6,14},... | collective-permute-start | bytes 196616 | tf_op jit(solution)/shard_map/ppermute | solution.py:25
  23.7 1.7 %collective-permute-done.6.refs_2_ = bf16[128,256]{1,0:T(8,128)(2,1)S(1)} collective-permute-done((bf16[128,256]{1,0:T(8,128)(2,1)S(1)}, bf16[128,256]{1,0:T(8,128)(2,1)S(1)}, u32[]{:S(2)}, u32[]{:S(2)}) %collective-permute-start.6) | collective-permute-done | bytes 65568 | tf_op jit(solution)/shard_map/ppermute | solution.py:25
  27.4 1.1 %collective-permute-done.9.other_ref = f32[512,128]{1,0:T(8,128)S(1)} collective-permute-done((f32[512,128]{1,0:T(8,128)S(1)}, f32[512,128]{1,0:T(8,128)S(1)}, u32[]{:S(2)}, u32[]{:S(2)}) %collective-permute-start.9) | collective-permute-done | bytes 262176 | tf_op jit(solution)/shard_map/ppermute | solution.py:25
  28.6 1.4 %collective-permute-start.10 = (bf16[128,128]{1,0:T(8,128)(2,1)S(1)}, bf16[128,128]{1,0:T(8,128)(2,1)S(1)}, u32[]{:S(2)}, u32[]{:S(2)}) collective-permute-start(bf16[128,128]{1,0:T(8,128)(2,1)S(1)} %get-tuple-element.42), channel_id=1, source_target_pairs={{0,18},{1,19},{2,16},{3,17},{16,2},{17,3},{18,0},{19,1},{4,22},{5,... | collective-permute-start | bytes 98312 | tf_op jit(solution)/shard_map/ppermute | solution.py:30
  31.9 1.8 %collective-permute-done.10.refs_1_ = bf16[128,128]{1,0:T(8,128)(2,1)S(1)} collective-permute-done((bf16[128,128]{1,0:T(8,128)(2,1)S(1)}, bf16[128,128]{1,0:T(8,128)(2,1)S(1)}, u32[]{:S(2)}, u32[]{:S(2)}) %collective-permute-start.10) | collective-permute-done | bytes 32800 | tf_op jit(solution)/shard_map/ppermute | solution.py:30
  33.6 1.5 %collective-permute-done.11.refs_2_ = bf16[128,128]{1,0:T(8,128)(2,1)S(1)} collective-permute-done((bf16[128,128]{1,0:T(8,128)(2,1)S(1)}, bf16[128,128]{1,0:T(8,128)(2,1)S(1)}, u32[]{:S(2)}, u32[]{:S(2)}) %collective-permute-start.11) | collective-permute-done | bytes 32800 | tf_op jit(solution)/shard_map/ppermute | solution.py:30
  35.3 1.1 %collective-permute-start.13 = (bf16[128,128]{1,0:T(8,128)(2,1)S(1)}, bf16[128,128]{1,0:T(8,128)(2,1)S(1)}, u32[]{:S(2)}, u32[]{:S(2)}) collective-permute-start(bf16[128,128]{1,0:T(8,128)(2,1)S(1)} %get-tuple-element.45.refs_0_), channel_id=1, source_target_pairs={{0,18},{1,19},{2,16},{3,17},{16,2},{17,3},{18,0},{19,1},{4,22},{5,... | collective-permute-start | bytes 98312 | tf_op jit(solution)/shard_map/ppermute | solution.py:30
  36.4 1.3 %collective-permute-start.14 = (bf16[128,128]{1,0:T(8,128)(2,1)S(1)}, bf16[128,128]{1,0:T(8,128)(2,1)S(1)}, u32[]{:S(2)}, u32[]{:S(2)}) collective-permute-start(bf16[128,128]{1,0:T(8,128)(2,1)S(1)} %get-tuple-element.45.refs_0_), channel_id=1, source_target_pairs={{0,19},{1,18},{2,17},{3,16},{16,3},{17,2},{18,1},{19,0},{4,23},{5,... | collective-permute-start | bytes 98312 | tf_op jit(solution)/shard_map/ppermute | solution.py:30
  38.7 1.3 %collective-permute-done.13.refs_1_ = bf16[128,128]{1,0:T(8,128)(2,1)S(1)} collective-permute-done((bf16[128,128]{1,0:T(8,128)(2,1)S(1)}, bf16[128,128]{1,0:T(8,128)(2,1)S(1)}, u32[]{:S(2)}, u32[]{:S(2)}) %collective-permute-start.13) | collective-permute-done | bytes 32800 | tf_op jit(solution)/shard_map/ppermute | solution.py:30
  40.0 1.7 %collective-permute-done.14.refs_2_ = bf16[128,128]{1,0:T(8,128)(2,1)S(1)} collective-permute-done((bf16[128,128]{1,0:T(8,128)(2,1)S(1)}, bf16[128,128]{1,0:T(8,128)(2,1)S(1)}, u32[]{:S(2)}, u32[]{:S(2)}) %collective-permute-start.14) | collective-permute-done | bytes 32800 | tf_op jit(solution)/shard_map/ppermute | solution.py:30
  43.5 2.5 %collective-permute-start.17 = (bf16[128,256]{1,0:T(8,128)(2,1)S(1)}, bf16[128,256]{1,0:T(8,128)(2,1)S(1)}, u32[]{:S(2)}, u32[]{:S(2)}) collective-permute-start(bf16[128,256]{1,0:T(8,128)(2,1)S(1)} %get-tuple-element.47), channel_id=1, source_target_pairs={{0,12},{4,8},{8,4},{12,0},{1,13},{5,9},{9,5},{13,1},{2,14},{6,10},... | collective-permute-start | bytes 196616 | tf_op jit(solution)/shard_map/ppermute | solution.py:25
  47.3 1.9 %collective-permute-done.17 = bf16[128,256]{1,0:T(8,128)(2,1)S(1)} collective-permute-done((bf16[128,256]{1,0:T(8,128)(2,1)S(1)}, bf16[128,256]{1,0:T(8,128)(2,1)S(1)}, u32[]{:S(2)}, u32[]{:S(2)}) %collective-permute-start.17) | collective-permute-done | bytes 65568 | tf_op jit(solution)/shard_map/ppermute | solution.py:25
  51.1 1.5 %collective-permute-start.20 = (bf16[128,256]{1,0:T(8,128)(2,1)S(1)}, bf16[128,256]{1,0:T(8,128)(2,1)S(1)}, u32[]{:S(2)}, u32[]{:S(2)}) collective-permute-start(bf16[128,256]{1,0:T(8,128)(2,1)S(1)} %get-tuple-element.59.refs_1_), channel_id=1, source_target_pairs={{0,2},{1,3},{2,0},{3,1},{4,6},{5,7},{6,4},{7,5},{8,10},{9,11},{10,... | collective-permute-start | bytes 196616 | tf_op jit(solution)/shard_map/ppermute | solution.py:25
  52.6 1.3 %collective-permute-start.21 = (bf16[128,256]{1,0:T(8,128)(2,1)S(1)}, bf16[128,256]{1,0:T(8,128)(2,1)S(1)}, u32[]{:S(2)}, u32[]{:S(2)}) collective-permute-start(bf16[128,256]{1,0:T(8,128)(2,1)S(1)} %get-tuple-element.59.refs_1_), channel_id=1, source_target_pairs={{0,3},{1,2},{2,1},{3,0},{4,7},{5,6},{6,5},{7,4},{8,11},{9,10},{10,... | collective-permute-start | bytes 196616 | tf_op jit(solution)/shard_map/ppermute | solution.py:25
  55.0 2.9 %collective-permute-done.20.refs_2_ = bf16[128,256]{1,0:T(8,128)(2,1)S(1)} collective-permute-done((bf16[128,256]{1,0:T(8,128)(2,1)S(1)}, bf16[128,256]{1,0:T(8,128)(2,1)S(1)}, u32[]{:S(2)}, u32[]{:S(2)}) %collective-permute-start.20) | collective-permute-done | bytes 65568 | tf_op jit(solution)/shard_map/ppermute | solution.py:25
  59.6 2.0 %collective-permute-start.23 = (bf16[128,256]{1,0:T(8,128)(2,1)S(1)}, bf16[128,256]{1,0:T(8,128)(2,1)S(1)}, u32[]{:S(2)}, u32[]{:S(2)}) collective-permute-start(bf16[128,256]{1,0:T(8,128)(2,1)S(1)} %get-tuple-element.51), channel_id=1, source_target_pairs={{0,12},{4,8},{8,4},{12,0},{1,13},{5,9},{9,5},{13,1},{2,14},{6,10},... | collective-permute-start | bytes 196616 | tf_op jit(solution)/shard_map/ppermute | solution.py:25
  (76 shorter events, 24.5 us)
Async XLA Ops:
  1.8 6.4 %collective-permute-start = (bf16[128,256]{1,0:T(8,128)(2,1)S(1)}, bf16[128,256]{1,0:T(8,128)(2,1)S(1)}, u32[]{:S(2)}, u32[]{:S(2)}) collective-permute-start(bf16[128,256]{1,0:T(8,128)(2,1)S(1)} %get-tuple-element.55.refs_1_), channel_id=1, source_target_pairs={{0,12},{4,8},{8,4},{12,0},{1,13},{5,9},{9,5},{13,1},{2,14},{6,10},... | collective-permute-start | bytes 196616 | tf_op jit(solution)/shard_map/ppermute | solution.py:25
  5.7 4.3 %collective-permute-start.1 = (bf16[128,256]{1,0:T(8,128)(2,1)S(1)}, bf16[128,256]{1,0:T(8,128)(2,1)S(1)}, u32[]{:S(2)}, u32[]{:S(2)}) collective-permute-start(bf16[128,256]{1,0:T(8,128)(2,1)S(1)} %get-tuple-element.55.refs_1_), channel_id=1, source_target_pairs={{0,4},{4,0},{8,12},{12,8},{1,5},{5,1},{9,13},{13,9},{2,6},{6,2},{1... | collective-permute-start | bytes 196616 | tf_op jit(solution)/shard_map/ppermute | solution.py:25
  6.3 4.3 %collective-permute-start.2 = (bf16[128,256]{1,0:T(8,128)(2,1)S(1)}, bf16[128,256]{1,0:T(8,128)(2,1)S(1)}, u32[]{:S(2)}, u32[]{:S(2)}) collective-permute-start(bf16[128,256]{1,0:T(8,128)(2,1)S(1)} %get-tuple-element.55.refs_1_), channel_id=1, source_target_pairs={{0,8},{4,12},{8,0},{12,4},{1,9},{5,13},{9,1},{13,5},{2,10},{6,14},... | collective-permute-start | bytes 196616 | tf_op jit(solution)/shard_map/ppermute | solution.py:25
  10.8 6.9 %collective-permute-start.3 = (bf16[128,256]{1,0:T(8,128)(2,1)S(1)}, bf16[128,256]{1,0:T(8,128)(2,1)S(1)}, u32[]{:S(2)}, u32[]{:S(2)}) collective-permute-start(bf16[128,256]{1,0:T(8,128)(2,1)S(1)} %get-tuple-element.36), channel_id=1, source_target_pairs={{0,2},{1,3},{2,0},{3,1},{4,6},{5,7},{6,4},{7,5},{8,10},{9,11},{10,... | collective-permute-start | bytes 196616 | tf_op jit(solution)/shard_map/ppermute | solution.py:25
  13.5 6.2 %collective-permute-start.4 = (bf16[128,256]{1,0:T(8,128)(2,1)S(1)}, bf16[128,256]{1,0:T(8,128)(2,1)S(1)}, u32[]{:S(2)}, u32[]{:S(2)}) collective-permute-start(bf16[128,256]{1,0:T(8,128)(2,1)S(1)} %get-tuple-element.37), channel_id=1, source_target_pairs={{0,3},{1,2},{2,1},{3,0},{4,7},{5,6},{6,5},{7,4},{8,11},{9,10},{10,... | collective-permute-start | bytes 196616 | tf_op jit(solution)/shard_map/ppermute | solution.py:25
  14.8 5.0 %collective-permute-start.5 = (bf16[128,256]{1,0:T(8,128)(2,1)S(1)}, bf16[128,256]{1,0:T(8,128)(2,1)S(1)}, u32[]{:S(2)}, u32[]{:S(2)}) collective-permute-start(bf16[128,256]{1,0:T(8,128)(2,1)S(1)} %get-tuple-element.38), channel_id=1, source_target_pairs={{0,1},{1,0},{2,3},{3,2},{4,5},{5,4},{6,7},{7,6},{8,9},{9,8},{10,11... | collective-permute-start | bytes 196616 | tf_op jit(solution)/shard_map/ppermute | solution.py:25
  20.1 5.2 %collective-permute-start.6 = (bf16[128,256]{1,0:T(8,128)(2,1)S(1)}, bf16[128,256]{1,0:T(8,128)(2,1)S(1)}, u32[]{:S(2)}, u32[]{:S(2)}) collective-permute-start(bf16[128,256]{1,0:T(8,128)(2,1)S(1)} %get-tuple-element.57.refs_1_), channel_id=1, source_target_pairs={{0,12},{4,8},{8,4},{12,0},{1,13},{5,9},{9,5},{13,1},{2,14},{6,10},... | collective-permute-start | bytes 196616 | tf_op jit(solution)/shard_map/ppermute | solution.py:25
  21.6 4.3 %collective-permute-start.7 = (bf16[128,256]{1,0:T(8,128)(2,1)S(1)}, bf16[128,256]{1,0:T(8,128)(2,1)S(1)}, u32[]{:S(2)}, u32[]{:S(2)}) collective-permute-start(bf16[128,256]{1,0:T(8,128)(2,1)S(1)} %get-tuple-element.57.refs_1_), channel_id=1, source_target_pairs={{0,4},{4,0},{8,12},{12,8},{1,5},{5,1},{9,13},{13,9},{2,6},{6,2},{1... | collective-permute-start | bytes 196616 | tf_op jit(solution)/shard_map/ppermute | solution.py:25
  22.3 4.3 %collective-permute-start.8 = (bf16[128,256]{1,0:T(8,128)(2,1)S(1)}, bf16[128,256]{1,0:T(8,128)(2,1)S(1)}, u32[]{:S(2)}, u32[]{:S(2)}) collective-permute-start(bf16[128,256]{1,0:T(8,128)(2,1)S(1)} %get-tuple-element.57.refs_1_), channel_id=1, source_target_pairs={{0,8},{4,12},{8,0},{12,4},{1,9},{5,13},{9,1},{13,5},{2,10},{6,14},... | collective-permute-start | bytes 196616 | tf_op jit(solution)/shard_map/ppermute | solution.py:25
  28.6 5.1 %collective-permute-start.10 = (bf16[128,128]{1,0:T(8,128)(2,1)S(1)}, bf16[128,128]{1,0:T(8,128)(2,1)S(1)}, u32[]{:S(2)}, u32[]{:S(2)}) collective-permute-start(bf16[128,128]{1,0:T(8,128)(2,1)S(1)} %get-tuple-element.42), channel_id=1, source_target_pairs={{0,18},{1,19},{2,16},{3,17},{16,2},{17,3},{18,0},{19,1},{4,22},{5,... | collective-permute-start | bytes 98312 | tf_op jit(solution)/shard_map/ppermute | solution.py:30
  30.0 5.2 %collective-permute-start.11 = (bf16[128,128]{1,0:T(8,128)(2,1)S(1)}, bf16[128,128]{1,0:T(8,128)(2,1)S(1)}, u32[]{:S(2)}, u32[]{:S(2)}) collective-permute-start(bf16[128,128]{1,0:T(8,128)(2,1)S(1)} %get-tuple-element.43), channel_id=1, source_target_pairs={{0,19},{1,18},{2,17},{3,16},{16,3},{17,2},{18,1},{19,0},{4,23},{5,... | collective-permute-start | bytes 98312 | tf_op jit(solution)/shard_map/ppermute | solution.py:30
  31.0 4.1 %collective-permute-start.12 = (bf16[128,128]{1,0:T(8,128)(2,1)S(1)}, bf16[128,128]{1,0:T(8,128)(2,1)S(1)}, u32[]{:S(2)}, u32[]{:S(2)}) collective-permute-start(bf16[128,128]{1,0:T(8,128)(2,1)S(1)} %get-tuple-element.44), channel_id=1, source_target_pairs={{0,17},{1,16},{2,19},{3,18},{16,1},{17,0},{18,3},{19,2},{4,21},{5,... | collective-permute-start | bytes 98312 | tf_op jit(solution)/shard_map/ppermute | solution.py:30
  35.3 4.7 %collective-permute-start.13 = (bf16[128,128]{1,0:T(8,128)(2,1)S(1)}, bf16[128,128]{1,0:T(8,128)(2,1)S(1)}, u32[]{:S(2)}, u32[]{:S(2)}) collective-permute-start(bf16[128,128]{1,0:T(8,128)(2,1)S(1)} %get-tuple-element.45.refs_0_), channel_id=1, source_target_pairs={{0,18},{1,19},{2,16},{3,17},{16,2},{17,3},{18,0},{19,1},{4,22},{5,... | collective-permute-start | bytes 98312 | tf_op jit(solution)/shard_map/ppermute | solution.py:30
  36.4 5.3 %collective-permute-start.14 = (bf16[128,128]{1,0:T(8,128)(2,1)S(1)}, bf16[128,128]{1,0:T(8,128)(2,1)S(1)}, u32[]{:S(2)}, u32[]{:S(2)}) collective-permute-start(bf16[128,128]{1,0:T(8,128)(2,1)S(1)} %get-tuple-element.45.refs_0_), channel_id=1, source_target_pairs={{0,19},{1,18},{2,17},{3,16},{16,3},{17,2},{18,1},{19,0},{4,23},{5,... | collective-permute-start | bytes 98312 | tf_op jit(solution)/shard_map/ppermute | solution.py:30
  43.5 5.7 %collective-permute-start.17 = (bf16[128,256]{1,0:T(8,128)(2,1)S(1)}, bf16[128,256]{1,0:T(8,128)(2,1)S(1)}, u32[]{:S(2)}, u32[]{:S(2)}) collective-permute-start(bf16[128,256]{1,0:T(8,128)(2,1)S(1)} %get-tuple-element.47), channel_id=1, source_target_pairs={{0,12},{4,8},{8,4},{12,0},{1,13},{5,9},{9,5},{13,1},{2,14},{6,10},... | collective-permute-start | bytes 196616 | tf_op jit(solution)/shard_map/ppermute | solution.py:25
  46.0 4.3 %collective-permute-start.18 = (bf16[128,256]{1,0:T(8,128)(2,1)S(1)}, bf16[128,256]{1,0:T(8,128)(2,1)S(1)}, u32[]{:S(2)}, u32[]{:S(2)}) collective-permute-start(bf16[128,256]{1,0:T(8,128)(2,1)S(1)} %get-tuple-element.48), channel_id=1, source_target_pairs={{0,4},{4,0},{8,12},{12,8},{1,5},{5,1},{9,13},{13,9},{2,6},{6,2},{1... | collective-permute-start | bytes 196616 | tf_op jit(solution)/shard_map/ppermute | solution.py:25
  46.5 4.3 %collective-permute-start.19 = (bf16[128,256]{1,0:T(8,128)(2,1)S(1)}, bf16[128,256]{1,0:T(8,128)(2,1)S(1)}, u32[]{:S(2)}, u32[]{:S(2)}) collective-permute-start(bf16[128,256]{1,0:T(8,128)(2,1)S(1)} %get-tuple-element.49), channel_id=1, source_target_pairs={{0,8},{4,12},{8,0},{12,4},{1,9},{5,13},{9,1},{13,5},{2,10},{6,14},... | collective-permute-start | bytes 196616 | tf_op jit(solution)/shard_map/ppermute | solution.py:25
  51.1 6.8 %collective-permute-start.20 = (bf16[128,256]{1,0:T(8,128)(2,1)S(1)}, bf16[128,256]{1,0:T(8,128)(2,1)S(1)}, u32[]{:S(2)}, u32[]{:S(2)}) collective-permute-start(bf16[128,256]{1,0:T(8,128)(2,1)S(1)} %get-tuple-element.59.refs_1_), channel_id=1, source_target_pairs={{0,2},{1,3},{2,0},{3,1},{4,6},{5,7},{6,4},{7,5},{8,10},{9,11},{10,... | collective-permute-start | bytes 196616 | tf_op jit(solution)/shard_map/ppermute | solution.py:25
  52.6 6.2 %collective-permute-start.21 = (bf16[128,256]{1,0:T(8,128)(2,1)S(1)}, bf16[128,256]{1,0:T(8,128)(2,1)S(1)}, u32[]{:S(2)}, u32[]{:S(2)}) collective-permute-start(bf16[128,256]{1,0:T(8,128)(2,1)S(1)} %get-tuple-element.59.refs_1_), channel_id=1, source_target_pairs={{0,3},{1,2},{2,1},{3,0},{4,7},{5,6},{6,5},{7,4},{8,11},{9,10},{10,... | collective-permute-start | bytes 196616 | tf_op jit(solution)/shard_map/ppermute | solution.py:25
  53.9 5.3 %collective-permute-start.22 = (bf16[128,256]{1,0:T(8,128)(2,1)S(1)}, bf16[128,256]{1,0:T(8,128)(2,1)S(1)}, u32[]{:S(2)}, u32[]{:S(2)}) collective-permute-start(bf16[128,256]{1,0:T(8,128)(2,1)S(1)} %get-tuple-element.59.refs_1_), channel_id=1, source_target_pairs={{0,1},{1,0},{2,3},{3,2},{4,5},{5,4},{6,7},{7,6},{8,9},{9,8},{10,11... | collective-permute-start | bytes 196616 | tf_op jit(solution)/shard_map/ppermute | solution.py:25
  54.6 8.6 %collective-permute-start.26 = (f32[128,128]{1,0:T(8,128)S(1)}, f32[128,128]{1,0:T(8,128)S(1)}, u32[]{:S(2)}, u32[]{:S(2)}) collective-permute-start(f32[128,128]{1,0:T(8,128)S(1)} %get-tuple-element.54.mine_ref), channel_id=1, source_target_pairs={{0,16},{16,0},{1,17},{17,1},{2,18},{18,2},{3,19},{19,3},{4,20},{20... | collective-permute-start | bytes 196616 | tf_op jit(solution)/shard_map/ppermute | solution.py:25
  59.6 5.3 %collective-permute-start.23 = (bf16[128,256]{1,0:T(8,128)(2,1)S(1)}, bf16[128,256]{1,0:T(8,128)(2,1)S(1)}, u32[]{:S(2)}, u32[]{:S(2)}) collective-permute-start(bf16[128,256]{1,0:T(8,128)(2,1)S(1)} %get-tuple-element.51), channel_id=1, source_target_pairs={{0,12},{4,8},{8,4},{12,0},{1,13},{5,9},{9,5},{13,1},{2,14},{6,10},... | collective-permute-start | bytes 196616 | tf_op jit(solution)/shard_map/ppermute | solution.py:25
  61.6 4.3 %collective-permute-start.24 = (bf16[128,256]{1,0:T(8,128)(2,1)S(1)}, bf16[128,256]{1,0:T(8,128)(2,1)S(1)}, u32[]{:S(2)}, u32[]{:S(2)}) collective-permute-start(bf16[128,256]{1,0:T(8,128)(2,1)S(1)} %get-tuple-element.52), channel_id=1, source_target_pairs={{0,4},{4,0},{8,12},{12,8},{1,5},{5,1},{9,13},{13,9},{2,6},{6,2},{1... | collective-permute-start | bytes 196616 | tf_op jit(solution)/shard_map/ppermute | solution.py:25
  62.1 4.3 %collective-permute-start.25 = (bf16[128,256]{1,0:T(8,128)(2,1)S(1)}, bf16[128,256]{1,0:T(8,128)(2,1)S(1)}, u32[]{:S(2)}, u32[]{:S(2)}) collective-permute-start(bf16[128,256]{1,0:T(8,128)(2,1)S(1)} %get-tuple-element.53), channel_id=1, source_target_pairs={{0,8},{4,12},{8,0},{12,4},{1,9},{5,13},{9,1},{13,5},{2,10},{6,14},... | collective-permute-start | bytes 196616 | tf_op jit(solution)/shard_map/ppermute | solution.py:25
  (13 other events, 55.4 us)

commit v8 on v7

--- a/solution.py
+++ b/solution.py
@@ -14,11 +14,21 @@
     return n in (1, 2, 4)
 
 
-ORDERS = {"row": (3, 1, 2), "col": (2, 3, 1), "cross": (2, 3, 1)}
-
-
-def steps_of(n, kind):
-    return [0] + [d for d in ORDERS[kind] if d < n]
+ORDERS = {
+    "leaf_y": (3, 1, 2), "sep_sum": (2, 3, 1), "sep_y": (3, 1, 2), "top_sum": (2, 3, 1),
+    "top_x": (2, 3, 1), "sep_t": (3, 1, 2), "sep_x": (3, 1, 2), "leaf_t": (3, 1, 2),
+}
+CROSSED = ("top_sum", "top_x")
+
+
+class Exchange:
+    def __init__(self, name, axis, n):
+        self.axis, self.n, self.direct = axis, n, is_direct(n)
+        self.steps = [0] + [d for d in ORDERS[name] if d < n]
+        self.crossed = name in CROSSED
+
+    def to(self, values, step):
+        return (swap_cross if self.crossed else swap)(values, self.axis, self.n, step)
 
 
 def swap(values, axis, n, step):
@@ -30,20 +40,16 @@
     return lax.ppermute(values, ("sec", axis), pairs)
 
 
-def kind_of(step_to, axis):
-    return "cross" if step_to is swap_cross else axis
-
-
-def gather(values, axis, n, step_to=swap):
-    if is_direct(n):
-        return [values] + [step_to(values, axis, n, d) for d in steps_of(n, kind_of(step_to, axis))[1:]]
-    return [lax.all_gather(values, axis, axis=0, tiled=True)]
-
-
-def scatter_sum(blocks, axis, n, step_to=swap):
-    if is_direct(n):
-        return [blocks[0]] + [step_to(block, axis, n, d) for block, d in zip(blocks[1:], steps_of(n, kind_of(step_to, axis))[1:])]
-    return [lax.psum_scatter(blocks[0], axis, scatter_dimension=0, tiled=True)]
+def gather(values, ex):
+    if ex.direct:
+        return [values] + [ex.to(values, d) for d in ex.steps[1:]]
+    return [lax.all_gather(values, ex.axis, axis=0, tiled=True)]
+
+
+def scatter_sum(blocks, ex):
+    if ex.direct:
+        return [blocks[0]] + [ex.to(block, d) for block, d in zip(blocks[1:], ex.steps[1:])]
+    return [lax.psum_scatter(blocks[0], ex.axis, scatter_dimension=0, tiled=True)]
 
 
 def own_half(n_col):
@@ -71,10 +77,10 @@
     )(*args)
 
 
-def place(n, axis):
-    if not is_direct(n):
+def place(ex):
+    if not ex.direct:
         return lambda d: d
-    me = lax.axis_index(axis)
+    me = lax.axis_index(ex.axis)
     return lambda d: me ^ d
 
 
@@ -92,12 +98,24 @@
 
 def split(values):
     high = values.astype(BF)
-    return high, (values - high.astype(F32)).astype(BF)
+    rest = values - high.astype(F32)
+    mid = rest.astype(BF)
+    return high, mid, (rest - mid.astype(F32)).astype(BF)
+
+
+LEFT, RIGHT = (0, 1, 2, 0, 1, 0), (0, 0, 0, 1, 1, 2)
 
 
 def apply_split(parts, right_side):
-    high, low = split(right_side)
-    return dot(parts, jnp.concatenate([high, high, low], axis=0))
+    right = split(right_side)
+    return dot(parts, jnp.concatenate([right[k] for k in RIGHT], axis=0))
+
+
+def store_split(out_ref, values):
+    parts = split(values)
+    width = values.shape[1]
+    for place_of, k in enumerate(LEFT):
+        out_ref[:, place_of * width : (place_of + 1) * width] = parts[k]
 
 
 def total_of(refs):
@@ -107,30 +125,30 @@
     return total
 
 
-def lay_out(pieces, buf, n, axis, kind=None):
-    if not is_direct(n):
+def lay_out(pieces, buf, ex):
+    if not ex.direct:
         buf[...] = pieces[0][...]
         return
-    at = place(n, axis)
+    at = place(ex)
     size = pieces[0].shape[0]
-    for d, piece in zip(steps_of(n, kind or axis), pieces):
+    for d, piece in zip(ex.steps, pieces):
         buf[rows(at(d), size), :] = piece[...]
 
 
-def block_outs(n, size, cols, own=True):
-    if is_direct(n):
-        return [((size, cols), F32)] * own + [((size, cols), BF)] * (n - 1)
-    return [((n * size, cols), F32)]
-
-
-def emit_blocks(term, outs, n, axis, kind=None):
-    at = place(n, axis)
-    if is_direct(n):
-        for d, out_ref in zip(reversed(steps_of(n, kind or axis)), reversed(outs)):
+def block_outs(ex, size, cols, own=True):
+    if ex.direct:
+        return [((size, cols), F32)] * own + [((size, cols), BF)] * (ex.n - 1)
+    return [((ex.n * size, cols), F32)]
+
+
+def emit_blocks(term, outs, ex):
+    at = place(ex)
+    if ex.direct:
+        for d, out_ref in zip(reversed(ex.steps), reversed(outs)):
             out_ref[...] = term(at(d)).astype(out_ref.dtype)
     else:
-        size = outs[0].shape[0] // n
-        for d in range(n):
+        size = outs[0].shape[0] // ex.n
+        for d in range(ex.n):
             outs[0][pl.ds(d * size, size), :] = term(d)
 
 
@@ -155,16 +173,14 @@
     return call(kernel, [(t.shape, BF) for t in tile_sets], [*masks, *tile_sets])
 
 
-def split_inverse(inverse, transposed):
+def split_transposes(inverse):
     blocks, width = inverse.shape[:2]
 
     def kernel(inv_ref, out_ref):
         for m in range(blocks):
-            high, low = split(inv_ref[m].T if transposed else inv_ref[m])
-            for k, part in enumerate((high, low, high)):
-                out_ref[m, :, pl.ds(k * width, width)] = part
-
-    return call(kernel, [((blocks, width, 3 * width), BF)], [inverse])[0]
+            store_split(out_ref.at[m], inv_ref[m].T)
+
+    return call(kernel, [((blocks, width, len(LEFT) * width), BF)], [inverse])[0]
 
 
 def keep(values):
@@ -174,7 +190,7 @@
     return call(kernel, [(values.shape, values.dtype)], [values])[0]
 
 
-def forward_blocks(tiles, pieces, n_row, n_col, width):
+def forward_blocks(tiles, pieces, source, target, width):
     cols = pieces[0].shape[1]
     depth = tiles.shape[1]
     count = len(pieces)
@@ -182,16 +198,16 @@
     def kernel(*refs):
         tile_ref, piece_refs, outs = refs[0], refs[1 : 1 + count], refs[1 + count : -1]
         buf = refs[-1]
-        lay_out(piece_refs, buf, n_row, "row")
-        emit_blocks(lambda i: dot(tile_ref[rows(i, width), :], buf[...]), outs, n_col, "col")
-
-    outs = block_outs(n_col, width, cols, False) + [((depth, cols), BF)]
+        lay_out(piece_refs, buf, source)
+        emit_blocks(lambda i: dot(tile_ref[rows(i, width), :], buf[...]), outs, target)
+
+    outs = block_outs(target, width, cols, False) + [((depth, cols), BF)]
     got = call(kernel, outs, [tiles, *pieces], flops=2 * tiles.shape[0] * depth * cols)
-    return blocks_of(got, n_col)
-
-
-def blocks_of(got, n):
-    return ([None] if is_direct(n) else []) + list(got[:-1]), got[-1]
+    return blocks_of(got, target)
+
+
+def blocks_of(got, ex):
+    return ([None] if ex.direct else []) + list(got[:-1]), got[-1]
 
 
 def own_forward(tiles, values, width):
@@ -231,7 +247,7 @@
     return y, y.astype(BF)
 
 
-def top_half(tiles, pieces, leaf_part, n_row, n_col, width, passed):
+def top_half(tiles, pieces, leaf_part, source, n_col, width, passed):
     cols = pieces[0].shape[1]
     half = cols // 2
     count = len(pieces)
@@ -239,7 +255,7 @@
     def kernel(*refs):
         tile_ref, piece_refs = refs[0], refs[1 : 1 + count]
         part_ref, out_ref, buf = refs[1 + count :]
-        lay_out(piece_refs, buf, n_row, "row")
+        lay_out(piece_refs, buf, source)
         sec = lax.axis_index("sec")
         columns = rows(1 - sec if passed else sec, half)
         out_ref[...] = part_ref[:, columns] + dot(tile_ref[...], buf[:, columns])
@@ -257,26 +273,29 @@
     )[0]
 
 
-def add_sections(mine, other, n_col, width):
+def add_sections(mine, other, target, width):
     half = mine.shape[1]
 
     def kernel(mine_ref, other_ref, *outs):
-        emit_blocks(lambda i: mine_ref[rows(i, width), :] + other_ref[rows(i, width), :], outs, n_col, "col", "cross")
-
-    return call(kernel, block_outs(n_col, width, half), [mine, other])
+        emit_blocks(lambda i: mine_ref[rows(i, width), :] + other_ref[rows(i, width), :], outs, target)
+
+    return call(kernel, block_outs(target, width, half), [mine, other])
 
 
 def square_inverse(inverse):
-    width = inverse.shape[1]
+    width = inverse.shape[0]
 
     def kernel(inv_ref, out_ref):
-        value = inv_ref[0]
-        full = lax.dot_general(value, value, (((0,), (0,)), ((), ())), precision=lax.Precision.HIGHEST, preferred_element_type=F32)
-        high, low = split(full)
-        for k, part in enumerate((high, low, high)):
-            out_ref[:, pl.ds(k * width, width)] = part
-
-    return call(kernel, [((width, 3 * width), BF)], [inverse])[0]
+        value = inv_ref[...]
+        store_split(
+            out_ref,
+            lax.dot_general(
+                value, value, (((0,), (0,)), ((), ())),
+                precision=lax.Precision.HIGHEST, preferred_element_type=F32,
+            ),
+        )
+
+    return call(kernel, [((width, len(LEFT) * width), BF)], [inverse])[0]
 
 
 def solve_top(sums, right_side, square, n_col):
@@ -294,14 +313,14 @@
     return call(kernel, [(shape, F32), (shape, BF)], [*sums, right_side, square])
 
 
-def stack_pieces(pieces, n, axis):
-    if not is_direct(n):
+def stack_pieces(pieces, source):
+    if not source.direct:
         return pieces[0]
 
     def kernel(*refs):
-        lay_out(refs[:-1], refs[-1], n, axis, "cross")
-
-    shape = (n * pieces[0].shape[0], pieces[0].shape[1])
+        lay_out(refs[:-1], refs[-1], source)
+
+    shape = (source.n * pieces[0].shape[0], pieces[0].shape[1])
     return call(kernel, [(shape, BF)], list(pieces))[0]
 
 
@@ -316,7 +335,7 @@
     return call(kernel, [((mine.shape[0], 2 * half), mine.dtype)], [mine, other])[0]
 
 
-def top_back_blocks(tiles, mine, other, n_row, n_col, width):
+def top_back_blocks(tiles, mine, other, target, n_col, width):
     half = mine.shape[1]
 
     def kernel(tile_ref, mine_ref, other_ref, *outs):
@@ -328,29 +347,29 @@
             own = rows(lax.axis_index("col"), width)
             buf[own, rows(1 - sec, half)] = mine_ref[own, :]
             buf[own, rows(sec, half)] = other_ref[own, :]
-        emit_blocks(lambda i: dot_t(tile_ref[:, rows(i, width)], buf[...]), outs[:-1], n_row, "row")
-
-    outs = block_outs(n_row, width, 2 * half, False) + [((mine.shape[0], 2 * half), BF)]
+        emit_blocks(lambda i: dot_t(tile_ref[:, rows(i, width)], buf[...]), outs[:-1], target)
+
+    outs = block_outs(target, width, 2 * half, False) + [((mine.shape[0], 2 * half), BF)]
     got = call(kernel, outs, [tiles, mine, other], flops=4 * tiles.shape[0] * tiles.shape[1] * half)
-    return blocks_of(got, n_row)
-
-
-def back_blocks(tiles, pieces, top_part, n_row, n_col, span):
+    return blocks_of(got, target)
+
+
+def back_blocks(tiles, pieces, top_part, source, target, span):
     cols = pieces[0].shape[1]
     count = len(pieces)
 
     def kernel(*refs):
         tile_ref, piece_refs, part_ref = refs[0], refs[1 : 1 + count], refs[1 + count]
         outs, buf = refs[2 + count : -1], refs[-1]
-        lay_out(piece_refs, buf, n_col, "col")
+        lay_out(piece_refs, buf, source)
         emit_blocks(
             lambda i: part_ref[rows(i, span), :] + dot_t(tile_ref[:, rows(i, span)], buf[...]),
-            outs, n_row, "row",
+            outs, target,
         )
 
-    outs = block_outs(n_row, span, cols, False) + [((tiles.shape[0], cols), BF)]
+    outs = block_outs(target, span, cols, False) + [((tiles.shape[0], cols), BF)]
     got = call(kernel, outs, [tiles, *pieces, top_part], flops=2 * tiles.shape[0] * tiles.shape[1] * cols)
-    return blocks_of(got, n_row)
+    return blocks_of(got, target)
 
 
 def solve_back(sums, right_side, inverse):
@@ -380,13 +399,16 @@
         leaf_count, width, cols = leaf_rhs.shape[2], leaf_rhs.shape[4], leaf_rhs.shape[5]
         span = leaf_count * width
 
+        ex = {name: Exchange(name, "row", n_row) for name in ("leaf_y", "sep_y", "sep_t", "leaf_t")}
+        ex.update({name: Exchange(name, "col", n_col) for name in ("sep_sum", "top_sum", "top_x", "sep_x")})
+
         leaf_y, leaf_yb = leaf_first(leaf_inv[0, 0, :, 0], leaf_rhs[0, 0, :, 0])
-        leaf_pieces = gather(leaf_yb, "row", n_row)
+        pieces = gather(leaf_yb, ex["leaf_y"])
         shaped = [mask.reshape(n_col, 1, -1) for mask in masks]
         sl = mask_tiles([sep_leaf.reshape(n_col, width, -1)], shaped[:1], width)[0].reshape(n_col * width, -1)
-        blocks, leaf_col = forward_blocks(sl, leaf_pieces, n_row, n_col, width)
+        blocks, leaf_col = forward_blocks(sl, pieces, ex["leaf_y"], ex["sep_sum"], width)
         top_leaf, top_sep, leaf_col = lax.optimization_barrier((top_leaf, top_sep, leaf_col))
-        sums = scatter_sum(blocks, "col", n_col)
+        sums = scatter_sum(blocks, ex["sep_sum"])
         tops = [values.reshape(n_col, width, -1) for values in (top_leaf, top_sep)]
         tl, ts = [values.reshape(n_col * width, -1) for values in mask_tiles(tops, shaped[1:], width)]
         if is_direct(n_col):
@@ -394,26 +416,28 @@
         leaf_part = plain_product(tl, leaf_col, False)
         sums[0], ts, leaf_part = lax.optimization_barrier((sums[0], ts, leaf_part))
         sep_y, sep_yb = solve_forward(sums, sep_rhs[0, 0, 0], sep_inv[0, 0, 0])
-        pieces = gather(sep_yb, "row", n_row)
-        passed = swap(top_half(ts, pieces, leaf_part, n_row, n_col, width, True), "sec", 2, 1)
-        kept = top_half(ts, pieces, leaf_part, n_row, n_col, width, False)
-        blocks = add_sections(kept, passed, n_col, width)
-        sums = scatter_sum(blocks, "col", n_col, swap_cross)
-        top_xh, top_xhb = solve_top(sums, top_rhs[0, 0], square_inverse(top_inv[0]), n_col)
-        top_stack = stack_pieces(gather(top_xhb, "col", n_col, swap_cross), n_col, "col")
-        blocks, top_row = top_back_blocks(ts, top_stack, swap(top_stack, "sec", 2, 1), n_row, n_col, width)
-        sums = scatter_sum(blocks, "row", n_row)
+
+        pieces = gather(sep_yb, ex["sep_y"])
+        passed = swap(top_half(ts, pieces, leaf_part, ex["sep_y"], n_col, width, True), "sec", 2, 1)
+        kept = top_half(ts, pieces, leaf_part, ex["sep_y"], n_col, width, False)
+        sums = scatter_sum(add_sections(kept, passed, ex["top_sum"], width), ex["top_sum"])
+        top_xh, top_xhb = solve_top(sums, top_rhs[0, 0], square_inverse(top_inv[0, 0]), n_col)
+        top_stack = stack_pieces(gather(top_xhb, ex["top_x"]), ex["top_x"])
+
+        blocks, top_row = top_back_blocks(ts, top_stack, swap(top_stack, "sec", 2, 1), ex["sep_t"], n_col, width)
+        sums = scatter_sum(blocks, ex["sep_t"])
         if is_direct(n_row):
             sums[0] = own_back(ts, top_row, width)
         top_part = plain_product(tl, top_row, True)
         top_x = join_halves(top_xh, swap(top_xh, "sec", 2, 1), n_col)
         sep_x, sep_xb = solve_back(sums, sep_y, sep_inv[0, 0, 0])
-        pieces = gather(sep_xb, "col", n_col)
-        blocks, sep_row = back_blocks(sl, pieces, top_part, n_row, n_col, span)
-        sums = scatter_sum(blocks, "row", n_row)
+
+        pieces = gather(sep_xb, ex["sep_x"])
+        blocks, sep_row = back_blocks(sl, pieces, top_part, ex["sep_x"], ex["leaf_t"], span)
+        sums = scatter_sum(blocks, ex["leaf_t"])
         if is_direct(n_row):
             sums[0] = own_back(sl, sep_row, span, top_part)
-        leaf_x = solve_last(sums, leaf_y, split_inverse(leaf_inv[0, 0, :, 0], True))
+        leaf_x = solve_last(sums, leaf_y, split_transposes(leaf_inv[0, 0, :, 0]))
         return (
             leaf_x.reshape(1, 1, leaf_count, 1, width, cols),
             keep(sep_x)[None, None, None],

time: 67.5 us -> 67.6 us (level)
  starting transfers between devices: 29.9 us -> 30.8 us
  waiting for transfers between devices: 25.3 us -> 24.4 us
    ppermute x21, waiting for transfers between devices: 19 us -> 18.1 us  [swap(): return lax.ppermute(values, axis, [(i, i ^ step) for i in range(n)])]
    ppermute x21, starting transfers between devices: 23.5 us -> 24.4 us  [swap(): return lax.ppermute(values, axis, [(i, i ^ step) for i in range(n)])]
where the time goes in v8:
time: 67.6 us; the launch traced here: 67.3 us
  starting transfers between devices  30.8 us (46%)
  waiting for transfers between devices  24.4 us (36%)
  Pallas kernels  6.3 us (9%)
  local copies, waits for them, and re-layouts  3.21 us (5%)
  matrix products  1.73 us (3%)
  between operations  0.89 us (1%)
    ppermute x21, starting transfers between devices, swap(): return lax.ppermute(values, axis, [(i, i ^ step) for i in range(n)])  24.4 us
    ppermute x21, waiting for transfers between devices, swap(): return lax.ppermute(values, axis, [(i, i ^ step) for i in range(n)])  18.1 us
    ppermute x6, starting transfers between devices, swap_cross(): return lax.ppermute(values, ('sec', axis), pairs)  6.43 us
    pallas_call x20, Pallas kernels, call(): pl.pallas_call(kernel, out_shape=tuple((jax.ShapeDtypeStruct(s, t) for s,...  6.3 us
    ppermute x6, waiting for transfers between devices, swap_cross(): return lax.ppermute(values, ('sec', axis), pairs)  6.25 us
    unnamed x20, local copies, waits for them, and re-layouts  1.56 us
  transfers between devices with their start and end apart: 27, of which 22 were waited for; matrix products, arithmetic and copies ran while one was open for 2% of the time, Pallas kernels for 6%

profile of v8, /device:TPU:0, one launch (start us, length us, event | category | flops | bytes accessed | tf_op | source)
XLA Modules:
  0.0 67.3 jit_solution(3102936794286784041)
XLA Ops:
  0.6 1.1 %fusion.19 = (bf16[128,256]{1,0:T(8,128)(2,1)S(1)}, f32[128,256]{1,0:T(8,128)S(1)}) fusion(bf16[1,1,1,1,128,256]{5,4,3,2,1,0:T(8,128)(2,1)} %param.12, f32[1,1,1,1,128,128]{5,4,3,2,1,0:T(8,128)} %param.15), kind=kOutput, calls=%fused_computation.22 | convolution fusion | flops 50364416 | bytes 327680 | tf_op jit(solution)/shard_map/mab,mbn->man/dot_general | solution.py:156
  1.8 4.0 %collective-permute-start = (bf16[128,256]{1,0:T(8,128)(2,1)S(1)}, bf16[128,256]{1,0:T(8,128)(2,1)S(1)}, u32[]{:S(2)}, u32[]{:S(2)}) collective-permute-start(bf16[128,256]{1,0:T(8,128)(2,1)S(1)} %get-tuple-element.55.refs_1_), channel_id=1, source_target_pairs={{0,12},{4,8},{8,4},{12,0},{1,13},{5,9},{9,5},{13,1},{2,14},{6,10},... | collective-permute-start | bytes 196616 | tf_op jit(solution)/shard_map/ppermute | solution.py:35
  6.4 1.3 %reshape.50.refs_1_ = bf16[4,128,512]{2,1,0:T(8,128)(2,1)S(1)} reshape(bf16[1,1,4,128,4,1,1,128]{7,4,6,5,3,2,1,0:T(4,128)(2,1)} %param.18) | data formatting | bytes 1048576 | tf_op jit(solution)/shard_map/reshape | solution.py:408
  8.2 1.8 %collective-permute-done.1.refs_3_ = bf16[128,256]{1,0:T(8,128)(2,1)S(1)} collective-permute-done((bf16[128,256]{1,0:T(8,128)(2,1)S(1)}, bf16[128,256]{1,0:T(8,128)(2,1)S(1)}, u32[]{:S(2)}, u32[]{:S(2)}) %collective-permute-start.1) | collective-permute-done | bytes 65568 | tf_op jit(solution)/shard_map/ppermute | solution.py:35
  10.8 2.7 %collective-permute-start.3 = (bf16[128,256]{1,0:T(8,128)(2,1)S(1)}, bf16[128,256]{1,0:T(8,128)(2,1)S(1)}, u32[]{:S(2)}, u32[]{:S(2)}) collective-permute-start(bf16[128,256]{1,0:T(8,128)(2,1)S(1)} %get-tuple-element.36), channel_id=1, source_target_pairs={{0,2},{1,3},{2,0},{3,1},{4,6},{5,7},{6,4},{7,5},{8,10},{9,11},{10,... | collective-permute-start | bytes 196616 | tf_op jit(solution)/shard_map/ppermute | solution.py:35
  13.5 1.3 %collective-permute-start.4 = (bf16[128,256]{1,0:T(8,128)(2,1)S(1)}, bf16[128,256]{1,0:T(8,128)(2,1)S(1)}, u32[]{:S(2)}, u32[]{:S(2)}) collective-permute-start(bf16[128,256]{1,0:T(8,128)(2,1)S(1)} %get-tuple-element.37), channel_id=1, source_target_pairs={{0,3},{1,2},{2,1},{3,0},{4,7},{5,6},{6,5},{7,4},{8,11},{9,10},{10,... | collective-permute-start | bytes 196616 | tf_op jit(solution)/shard_map/ppermute | solution.py:35
  17.8 1.9 %collective-permute-done.4 = bf16[128,256]{1,0:T(8,128)(2,1)S(1)} collective-permute-done((bf16[128,256]{1,0:T(8,128)(2,1)S(1)}, bf16[128,256]{1,0:T(8,128)(2,1)S(1)}, u32[]{:S(2)}, u32[]{:S(2)}) %collective-permute-start.4) | collective-permute-done | bytes 65568 | tf_op jit(solution)/shard_map/ppermute | solution.py:35
  20.1 1.5 %collective-permute-start.6 = (bf16[128,256]{1,0:T(8,128)(2,1)S(1)}, bf16[128,256]{1,0:T(8,128)(2,1)S(1)}, u32[]{:S(2)}, u32[]{:S(2)}) collective-permute-start(bf16[128,256]{1,0:T(8,128)(2,1)S(1)} %get-tuple-element.57.refs_1_), channel_id=1, source_target_pairs={{0,12},{4,8},{8,4},{12,0},{1,13},{5,9},{9,5},{13,1},{2,14},{6,10},... | collective-permute-start | bytes 196616 | tf_op jit(solution)/shard_map/ppermute | solution.py:35
  22.3 1.4 %collective-permute-start.8 = (bf16[128,256]{1,0:T(8,128)(2,1)S(1)}, bf16[128,256]{1,0:T(8,128)(2,1)S(1)}, u32[]{:S(2)}, u32[]{:S(2)}) collective-permute-start(bf16[128,256]{1,0:T(8,128)(2,1)S(1)} %get-tuple-element.57.refs_1_), channel_id=1, source_target_pairs={{0,8},{4,12},{8,0},{12,4},{1,9},{5,13},{9,1},{13,5},{2,10},{6,14},... | collective-permute-start | bytes 196616 | tf_op jit(solution)/shard_map/ppermute | solution.py:35
  23.7 1.7 %collective-permute-done.6.refs_2_ = bf16[128,256]{1,0:T(8,128)(2,1)S(1)} collective-permute-done((bf16[128,256]{1,0:T(8,128)(2,1)S(1)}, bf16[128,256]{1,0:T(8,128)(2,1)S(1)}, u32[]{:S(2)}, u32[]{:S(2)}) %collective-permute-start.6) | collective-permute-done | bytes 65568 | tf_op jit(solution)/shard_map/ppermute | solution.py:35
  27.4 1.1 %collective-permute-done.9.other_ref = f32[512,128]{1,0:T(8,128)S(1)} collective-permute-done((f32[512,128]{1,0:T(8,128)S(1)}, f32[512,128]{1,0:T(8,128)S(1)}, u32[]{:S(2)}, u32[]{:S(2)}) %collective-permute-start.9) | collective-permute-done | bytes 262176 | tf_op jit(solution)/shard_map/ppermute | solution.py:35
  28.6 1.4 %collective-permute-start.10 = (bf16[128,128]{1,0:T(8,128)(2,1)S(1)}, bf16[128,128]{1,0:T(8,128)(2,1)S(1)}, u32[]{:S(2)}, u32[]{:S(2)}) collective-permute-start(bf16[128,128]{1,0:T(8,128)(2,1)S(1)} %get-tuple-element.42), channel_id=1, source_target_pairs={{0,18},{1,19},{2,16},{3,17},{16,2},{17,3},{18,0},{19,1},{4,22},{5,... | collective-permute-start | bytes 98312 | tf_op jit(solution)/shard_map/ppermute | solution.py:40
  31.9 1.7 %collective-permute-done.10.refs_1_ = bf16[128,128]{1,0:T(8,128)(2,1)S(1)} collective-permute-done((bf16[128,128]{1,0:T(8,128)(2,1)S(1)}, bf16[128,128]{1,0:T(8,128)(2,1)S(1)}, u32[]{:S(2)}, u32[]{:S(2)}) %collective-permute-start.10) | collective-permute-done | bytes 32800 | tf_op jit(solution)/shard_map/ppermute | solution.py:40
  33.6 1.5 %collective-permute-done.11.refs_2_ = bf16[128,128]{1,0:T(8,128)(2,1)S(1)} collective-permute-done((bf16[128,128]{1,0:T(8,128)(2,1)S(1)}, bf16[128,128]{1,0:T(8,128)(2,1)S(1)}, u32[]{:S(2)}, u32[]{:S(2)}) %collective-permute-start.11) | collective-permute-done | bytes 32800 | tf_op jit(solution)/shard_map/ppermute | solution.py:40
  36.5 1.3 %collective-permute-start.14 = (bf16[128,128]{1,0:T(8,128)(2,1)S(1)}, bf16[128,128]{1,0:T(8,128)(2,1)S(1)}, u32[]{:S(2)}, u32[]{:S(2)}) collective-permute-start(bf16[128,128]{1,0:T(8,128)(2,1)S(1)} %get-tuple-element.45.refs_0_), channel_id=1, source_target_pairs={{0,19},{1,18},{2,17},{3,16},{16,3},{17,2},{18,1},{19,0},{4,23},{5,... | collective-permute-start | bytes 98312 | tf_op jit(solution)/shard_map/ppermute | solution.py:40
  38.8 1.3 %collective-permute-done.13.refs_1_ = bf16[128,128]{1,0:T(8,128)(2,1)S(1)} collective-permute-done((bf16[128,128]{1,0:T(8,128)(2,1)S(1)}, bf16[128,128]{1,0:T(8,128)(2,1)S(1)}, u32[]{:S(2)}, u32[]{:S(2)}) %collective-permute-start.13) | collective-permute-done | bytes 32800 | tf_op jit(solution)/shard_map/ppermute | solution.py:40
  40.0 1.7 %collective-permute-done.14.refs_2_ = bf16[128,128]{1,0:T(8,128)(2,1)S(1)} collective-permute-done((bf16[128,128]{1,0:T(8,128)(2,1)S(1)}, bf16[128,128]{1,0:T(8,128)(2,1)S(1)}, u32[]{:S(2)}, u32[]{:S(2)}) %collective-permute-start.14) | collective-permute-done | bytes 32800 | tf_op jit(solution)/shard_map/ppermute | solution.py:40
  43.5 2.5 %collective-permute-start.17 = (bf16[128,256]{1,0:T(8,128)(2,1)S(1)}, bf16[128,256]{1,0:T(8,128)(2,1)S(1)}, u32[]{:S(2)}, u32[]{:S(2)}) collective-permute-start(bf16[128,256]{1,0:T(8,128)(2,1)S(1)} %get-tuple-element.47), channel_id=1, source_target_pairs={{0,12},{4,8},{8,4},{12,0},{1,13},{5,9},{9,5},{13,1},{2,14},{6,10},... | collective-permute-start | bytes 196616 | tf_op jit(solution)/shard_map/ppermute | solution.py:35
  47.3 1.9 %collective-permute-done.17 = bf16[128,256]{1,0:T(8,128)(2,1)S(1)} collective-permute-done((bf16[128,256]{1,0:T(8,128)(2,1)S(1)}, bf16[128,256]{1,0:T(8,128)(2,1)S(1)}, u32[]{:S(2)}, u32[]{:S(2)}) %collective-permute-start.17) | collective-permute-done | bytes 65568 | tf_op jit(solution)/shard_map/ppermute | solution.py:35
  51.1 2.4 %collective-permute-start.20 = (bf16[128,256]{1,0:T(8,128)(2,1)S(1)}, bf16[128,256]{1,0:T(8,128)(2,1)S(1)}, u32[]{:S(2)}, u32[]{:S(2)}) collective-permute-start(bf16[128,256]{1,0:T(8,128)(2,1)S(1)} %get-tuple-element.59.refs_1_), channel_id=1, source_target_pairs={{0,3},{1,2},{2,1},{3,0},{4,7},{5,6},{6,5},{7,4},{8,11},{9,10},{10,... | collective-permute-start | bytes 196616 | tf_op jit(solution)/shard_map/ppermute | solution.py:35
  53.6 2.0 %collective-permute-start.22 = (bf16[128,256]{1,0:T(8,128)(2,1)S(1)}, bf16[128,256]{1,0:T(8,128)(2,1)S(1)}, u32[]{:S(2)}, u32[]{:S(2)}) collective-permute-start(bf16[128,256]{1,0:T(8,128)(2,1)S(1)} %get-tuple-element.59.refs_1_), channel_id=1, source_target_pairs={{0,2},{1,3},{2,0},{3,1},{4,6},{5,7},{6,4},{7,5},{8,10},{9,11},{10,... | collective-permute-start | bytes 196616 | tf_op jit(solution)/shard_map/ppermute | solution.py:35
  55.9 1.8 %collective-permute-done.20.refs_2_ = bf16[128,256]{1,0:T(8,128)(2,1)S(1)} collective-permute-done((bf16[128,256]{1,0:T(8,128)(2,1)S(1)}, bf16[128,256]{1,0:T(8,128)(2,1)S(1)}, u32[]{:S(2)}, u32[]{:S(2)}) %collective-permute-start.20) | collective-permute-done | bytes 65568 | tf_op jit(solution)/shard_map/ppermute | solution.py:35
  59.3 2.1 %collective-permute-start.23 = (bf16[128,256]{1,0:T(8,128)(2,1)S(1)}, bf16[128,256]{1,0:T(8,128)(2,1)S(1)}, u32[]{:S(2)}, u32[]{:S(2)}) collective-permute-start(bf16[128,256]{1,0:T(8,128)(2,1)S(1)} %get-tuple-element.51), channel_id=1, source_target_pairs={{0,12},{4,8},{8,4},{12,0},{1,13},{5,9},{9,5},{13,1},{2,14},{6,10},... | collective-permute-start | bytes 196616 | tf_op jit(solution)/shard_map/ppermute | solution.py:35
  64.6 1.1 %collective-permute-done.24.refs_2_ = bf16[128,256]{1,0:T(8,128)(2,1)S(1)} collective-permute-done((bf16[128,256]{1,0:T(8,128)(2,1)S(1)}, bf16[128,256]{1,0:T(8,128)(2,1)S(1)}, u32[]{:S(2)}, u32[]{:S(2)}) %collective-permute-start.24) | collective-permute-done | bytes 65568 | tf_op jit(solution)/shard_map/ppermute | solution.py:35
  (76 shorter events, 23.9 us)
Async XLA Ops:
  1.8 6.4 %collective-permute-start = (bf16[128,256]{1,0:T(8,128)(2,1)S(1)}, bf16[128,256]{1,0:T(8,128)(2,1)S(1)}, u32[]{:S(2)}, u32[]{:S(2)}) collective-permute-start(bf16[128,256]{1,0:T(8,128)(2,1)S(1)} %get-tuple-element.55.refs_1_), channel_id=1, source_target_pairs={{0,12},{4,8},{8,4},{12,0},{1,13},{5,9},{9,5},{13,1},{2,14},{6,10},... | collective-permute-start | bytes 196616 | tf_op jit(solution)/shard_map/ppermute | solution.py:35
  5.7 4.3 %collective-permute-start.1 = (bf16[128,256]{1,0:T(8,128)(2,1)S(1)}, bf16[128,256]{1,0:T(8,128)(2,1)S(1)}, u32[]{:S(2)}, u32[]{:S(2)}) collective-permute-start(bf16[128,256]{1,0:T(8,128)(2,1)S(1)} %get-tuple-element.55.refs_1_), channel_id=1, source_target_pairs={{0,4},{4,0},{8,12},{12,8},{1,5},{5,1},{9,13},{13,9},{2,6},{6,2},{1... | collective-permute-start | bytes 196616 | tf_op jit(solution)/shard_map/ppermute | solution.py:35
  6.3 4.3 %collective-permute-start.2 = (bf16[128,256]{1,0:T(8,128)(2,1)S(1)}, bf16[128,256]{1,0:T(8,128)(2,1)S(1)}, u32[]{:S(2)}, u32[]{:S(2)}) collective-permute-start(bf16[128,256]{1,0:T(8,128)(2,1)S(1)} %get-tuple-element.55.refs_1_), channel_id=1, source_target_pairs={{0,8},{4,12},{8,0},{12,4},{1,9},{5,13},{9,1},{13,5},{2,10},{6,14},... | collective-permute-start | bytes 196616 | tf_op jit(solution)/shard_map/ppermute | solution.py:35
  10.8 6.9 %collective-permute-start.3 = (bf16[128,256]{1,0:T(8,128)(2,1)S(1)}, bf16[128,256]{1,0:T(8,128)(2,1)S(1)}, u32[]{:S(2)}, u32[]{:S(2)}) collective-permute-start(bf16[128,256]{1,0:T(8,128)(2,1)S(1)} %get-tuple-element.36), channel_id=1, source_target_pairs={{0,2},{1,3},{2,0},{3,1},{4,6},{5,7},{6,4},{7,5},{8,10},{9,11},{10,... | collective-permute-start | bytes 196616 | tf_op jit(solution)/shard_map/ppermute | solution.py:35
  13.5 6.2 %collective-permute-start.4 = (bf16[128,256]{1,0:T(8,128)(2,1)S(1)}, bf16[128,256]{1,0:T(8,128)(2,1)S(1)}, u32[]{:S(2)}, u32[]{:S(2)}) collective-permute-start(bf16[128,256]{1,0:T(8,128)(2,1)S(1)} %get-tuple-element.37), channel_id=1, source_target_pairs={{0,3},{1,2},{2,1},{3,0},{4,7},{5,6},{6,5},{7,4},{8,11},{9,10},{10,... | collective-permute-start | bytes 196616 | tf_op jit(solution)/shard_map/ppermute | solution.py:35
  14.8 5.0 %collective-permute-start.5 = (bf16[128,256]{1,0:T(8,128)(2,1)S(1)}, bf16[128,256]{1,0:T(8,128)(2,1)S(1)}, u32[]{:S(2)}, u32[]{:S(2)}) collective-permute-start(bf16[128,256]{1,0:T(8,128)(2,1)S(1)} %get-tuple-element.38), channel_id=1, source_target_pairs={{0,1},{1,0},{2,3},{3,2},{4,5},{5,4},{6,7},{7,6},{8,9},{9,8},{10,11... | collective-permute-start | bytes 196616 | tf_op jit(solution)/shard_map/ppermute | solution.py:35
  20.1 5.2 %collective-permute-start.6 = (bf16[128,256]{1,0:T(8,128)(2,1)S(1)}, bf16[128,256]{1,0:T(8,128)(2,1)S(1)}, u32[]{:S(2)}, u32[]{:S(2)}) collective-permute-start(bf16[128,256]{1,0:T(8,128)(2,1)S(1)} %get-tuple-element.57.refs_1_), channel_id=1, source_target_pairs={{0,12},{4,8},{8,4},{12,0},{1,13},{5,9},{9,5},{13,1},{2,14},{6,10},... | collective-permute-start | bytes 196616 | tf_op jit(solution)/shard_map/ppermute | solution.py:35
  21.6 4.3 %collective-permute-start.7 = (bf16[128,256]{1,0:T(8,128)(2,1)S(1)}, bf16[128,256]{1,0:T(8,128)(2,1)S(1)}, u32[]{:S(2)}, u32[]{:S(2)}) collective-permute-start(bf16[128,256]{1,0:T(8,128)(2,1)S(1)} %get-tuple-element.57.refs_1_), channel_id=1, source_target_pairs={{0,4},{4,0},{8,12},{12,8},{1,5},{5,1},{9,13},{13,9},{2,6},{6,2},{1... | collective-permute-start | bytes 196616 | tf_op jit(solution)/shard_map/ppermute | solution.py:35
  22.3 4.3 %collective-permute-start.8 = (bf16[128,256]{1,0:T(8,128)(2,1)S(1)}, bf16[128,256]{1,0:T(8,128)(2,1)S(1)}, u32[]{:S(2)}, u32[]{:S(2)}) collective-permute-start(bf16[128,256]{1,0:T(8,128)(2,1)S(1)} %get-tuple-element.57.refs_1_), channel_id=1, source_target_pairs={{0,8},{4,12},{8,0},{12,4},{1,9},{5,13},{9,1},{13,5},{2,10},{6,14},... | collective-permute-start | bytes 196616 | tf_op jit(solution)/shard_map/ppermute | solution.py:35
  28.6 5.1 %collective-permute-start.10 = (bf16[128,128]{1,0:T(8,128)(2,1)S(1)}, bf16[128,128]{1,0:T(8,128)(2,1)S(1)}, u32[]{:S(2)}, u32[]{:S(2)}) collective-permute-start(bf16[128,128]{1,0:T(8,128)(2,1)S(1)} %get-tuple-element.42), channel_id=1, source_target_pairs={{0,18},{1,19},{2,16},{3,17},{16,2},{17,3},{18,0},{19,1},{4,22},{5,... | collective-permute-start | bytes 98312 | tf_op jit(solution)/shard_map/ppermute | solution.py:40
  30.0 5.2 %collective-permute-start.11 = (bf16[128,128]{1,0:T(8,128)(2,1)S(1)}, bf16[128,128]{1,0:T(8,128)(2,1)S(1)}, u32[]{:S(2)}, u32[]{:S(2)}) collective-permute-start(bf16[128,128]{1,0:T(8,128)(2,1)S(1)} %get-tuple-element.43), channel_id=1, source_target_pairs={{0,19},{1,18},{2,17},{3,16},{16,3},{17,2},{18,1},{19,0},{4,23},{5,... | collective-permute-start | bytes 98312 | tf_op jit(solution)/shard_map/ppermute | solution.py:40
  31.0 4.1 %collective-permute-start.12 = (bf16[128,128]{1,0:T(8,128)(2,1)S(1)}, bf16[128,128]{1,0:T(8,128)(2,1)S(1)}, u32[]{:S(2)}, u32[]{:S(2)}) collective-permute-start(bf16[128,128]{1,0:T(8,128)(2,1)S(1)} %get-tuple-element.44), channel_id=1, source_target_pairs={{0,17},{1,16},{2,19},{3,18},{16,1},{17,0},{18,3},{19,2},{4,21},{5,... | collective-permute-start | bytes 98312 | tf_op jit(solution)/shard_map/ppermute | solution.py:40
  35.4 4.7 %collective-permute-start.13 = (bf16[128,128]{1,0:T(8,128)(2,1)S(1)}, bf16[128,128]{1,0:T(8,128)(2,1)S(1)}, u32[]{:S(2)}, u32[]{:S(2)}) collective-permute-start(bf16[128,128]{1,0:T(8,128)(2,1)S(1)} %get-tuple-element.45.refs_0_), channel_id=1, source_target_pairs={{0,18},{1,19},{2,16},{3,17},{16,2},{17,3},{18,0},{19,1},{4,22},{5,... | collective-permute-start | bytes 98312 | tf_op jit(solution)/shard_map/ppermute | solution.py:40
  36.5 5.3 %collective-permute-start.14 = (bf16[128,128]{1,0:T(8,128)(2,1)S(1)}, bf16[128,128]{1,0:T(8,128)(2,1)S(1)}, u32[]{:S(2)}, u32[]{:S(2)}) collective-permute-start(bf16[128,128]{1,0:T(8,128)(2,1)S(1)} %get-tuple-element.45.refs_0_), channel_id=1, source_target_pairs={{0,19},{1,18},{2,17},{3,16},{16,3},{17,2},{18,1},{19,0},{4,23},{5,... | collective-permute-start | bytes 98312 | tf_op jit(solution)/shard_map/ppermute | solution.py:40
  43.5 5.7 %collective-permute-start.17 = (bf16[128,256]{1,0:T(8,128)(2,1)S(1)}, bf16[128,256]{1,0:T(8,128)(2,1)S(1)}, u32[]{:S(2)}, u32[]{:S(2)}) collective-permute-start(bf16[128,256]{1,0:T(8,128)(2,1)S(1)} %get-tuple-element.47), channel_id=1, source_target_pairs={{0,12},{4,8},{8,4},{12,0},{1,13},{5,9},{9,5},{13,1},{2,14},{6,10},... | collective-permute-start | bytes 196616 | tf_op jit(solution)/shard_map/ppermute | solution.py:35
  46.0 4.3 %collective-permute-start.18 = (bf16[128,256]{1,0:T(8,128)(2,1)S(1)}, bf16[128,256]{1,0:T(8,128)(2,1)S(1)}, u32[]{:S(2)}, u32[]{:S(2)}) collective-permute-start(bf16[128,256]{1,0:T(8,128)(2,1)S(1)} %get-tuple-element.48), channel_id=1, source_target_pairs={{0,4},{4,0},{8,12},{12,8},{1,5},{5,1},{9,13},{13,9},{2,6},{6,2},{1... | collective-permute-start | bytes 196616 | tf_op jit(solution)/shard_map/ppermute | solution.py:35
  46.5 4.3 %collective-permute-start.19 = (bf16[128,256]{1,0:T(8,128)(2,1)S(1)}, bf16[128,256]{1,0:T(8,128)(2,1)S(1)}, u32[]{:S(2)}, u32[]{:S(2)}) collective-permute-start(bf16[128,256]{1,0:T(8,128)(2,1)S(1)} %get-tuple-element.49), channel_id=1, source_target_pairs={{0,8},{4,12},{8,0},{12,4},{1,9},{5,13},{9,1},{13,5},{2,10},{6,14},... | collective-permute-start | bytes 196616 | tf_op jit(solution)/shard_map/ppermute | solution.py:35
  51.1 6.6 %collective-permute-start.20 = (bf16[128,256]{1,0:T(8,128)(2,1)S(1)}, bf16[128,256]{1,0:T(8,128)(2,1)S(1)}, u32[]{:S(2)}, u32[]{:S(2)}) collective-permute-start(bf16[128,256]{1,0:T(8,128)(2,1)S(1)} %get-tuple-element.59.refs_1_), channel_id=1, source_target_pairs={{0,3},{1,2},{2,1},{3,0},{4,7},{5,6},{6,5},{7,4},{8,11},{9,10},{10,... | collective-permute-start | bytes 196616 | tf_op jit(solution)/shard_map/ppermute | solution.py:35
  53.6 5.2 %collective-permute-start.21 = (bf16[128,256]{1,0:T(8,128)(2,1)S(1)}, bf16[128,256]{1,0:T(8,128)(2,1)S(1)}, u32[]{:S(2)}, u32[]{:S(2)}) collective-permute-start(bf16[128,256]{1,0:T(8,128)(2,1)S(1)} %get-tuple-element.59.refs_1_), channel_id=1, source_target_pairs={{0,1},{1,0},{2,3},{3,2},{4,5},{5,4},{6,7},{7,6},{8,9},{9,8},{10,11... | collective-permute-start | bytes 196616 | tf_op jit(solution)/shard_map/ppermute | solution.py:35
  53.6 5.4 %collective-permute-start.22 = (bf16[128,256]{1,0:T(8,128)(2,1)S(1)}, bf16[128,256]{1,0:T(8,128)(2,1)S(1)}, u32[]{:S(2)}, u32[]{:S(2)}) collective-permute-start(bf16[128,256]{1,0:T(8,128)(2,1)S(1)} %get-tuple-element.59.refs_1_), channel_id=1, source_target_pairs={{0,2},{1,3},{2,0},{3,1},{4,6},{5,7},{6,4},{7,5},{8,10},{9,11},{10,... | collective-permute-start | bytes 196616 | tf_op jit(solution)/shard_map/ppermute | solution.py:35
  55.6 7.4 %collective-permute-start.26 = (f32[128,128]{1,0:T(8,128)S(1)}, f32[128,128]{1,0:T(8,128)S(1)}, u32[]{:S(2)}, u32[]{:S(2)}) collective-permute-start(f32[128,128]{1,0:T(8,128)S(1)} %get-tuple-element.54.mine_ref), channel_id=1, source_target_pairs={{0,16},{16,0},{1,17},{17,1},{2,18},{18,2},{3,19},{19,3},{4,20},{20... | collective-permute-start | bytes 196616 | tf_op jit(solution)/shard_map/ppermute | solution.py:35
  59.3 5.3 %collective-permute-start.23 = (bf16[128,256]{1,0:T(8,128)(2,1)S(1)}, bf16[128,256]{1,0:T(8,128)(2,1)S(1)}, u32[]{:S(2)}, u32[]{:S(2)}) collective-permute-start(bf16[128,256]{1,0:T(8,128)(2,1)S(1)} %get-tuple-element.51), channel_id=1, source_target_pairs={{0,12},{4,8},{8,4},{12,0},{1,13},{5,9},{9,5},{13,1},{2,14},{6,10},... | collective-permute-start | bytes 196616 | tf_op jit(solution)/shard_map/ppermute | solution.py:35
  61.4 4.3 %collective-permute-start.24 = (bf16[128,256]{1,0:T(8,128)(2,1)S(1)}, bf16[128,256]{1,0:T(8,128)(2,1)S(1)}, u32[]{:S(2)}, u32[]{:S(2)}) collective-permute-start(bf16[128,256]{1,0:T(8,128)(2,1)S(1)} %get-tuple-element.52), channel_id=1, source_target_pairs={{0,4},{4,0},{8,12},{12,8},{1,5},{5,1},{9,13},{13,9},{2,6},{6,2},{1... | collective-permute-start | bytes 196616 | tf_op jit(solution)/shard_map/ppermute | solution.py:35
  62.1 4.3 %collective-permute-start.25 = (bf16[128,256]{1,0:T(8,128)(2,1)S(1)}, bf16[128,256]{1,0:T(8,128)(2,1)S(1)}, u32[]{:S(2)}, u32[]{:S(2)}) collective-permute-start(bf16[128,256]{1,0:T(8,128)(2,1)S(1)} %get-tuple-element.53), channel_id=1, source_target_pairs={{0,8},{4,12},{8,0},{12,4},{1,9},{5,13},{9,1},{13,5},{2,10},{6,14},... | collective-permute-start | bytes 196616 | tf_op jit(solution)/shard_map/ppermute | solution.py:35
  (13 other events, 54.1 us)

commit v9 on v8

--- a/solution.py
+++ b/solution.py
@@ -158,19 +158,23 @@
     return y, y.astype(BF)
 
 
-def mask_tiles(tile_sets, masks, width):
+def mask_tiles(tile_sets, masks, width, carried=()):
     count = len(masks)
     n_col = masks[0].shape[0]
 
     def kernel(*refs):
-        mask_refs, tile_refs, outs = refs[:count], refs[count : 2 * count], refs[2 * count :]
+        mask_refs, tile_refs = refs[:count], refs[count : 2 * count]
+        later, outs = refs[2 * count : 2 * count + len(carried)], refs[2 * count + len(carried) :]
+        for in_ref, out_ref in zip(later, outs[count:]):
+            out_ref[...] = in_ref[...]
         for i in range(count):
             for k in range(masks[i].shape[2]):
                 weight = jnp.broadcast_to(mask_refs[i][:, :, k : k + 1].astype(F32), (n_col, 1, width)).astype(BF)
                 lanes = pl.ds(k * width, width)
                 outs[i][:, :, lanes] = tile_refs[i][:, :, lanes] * weight
 
-    return call(kernel, [(t.shape, BF) for t in tile_sets], [*masks, *tile_sets])
+    outs = [(t.shape, BF) for t in tile_sets] + [(m.shape, m.dtype) for m in carried]
+    return call(kernel, outs, [*masks, *tile_sets, *carried])
 
 
 def split_transposes(inverse):
@@ -405,7 +409,8 @@
         leaf_y, leaf_yb = leaf_first(leaf_inv[0, 0, :, 0], leaf_rhs[0, 0, :, 0])
         pieces = gather(leaf_yb, ex["leaf_y"])
         shaped = [mask.reshape(n_col, 1, -1) for mask in masks]
-        sl = mask_tiles([sep_leaf.reshape(n_col, width, -1)], shaped[:1], width)[0].reshape(n_col * width, -1)
+        sl, *shaped[1:] = mask_tiles([sep_leaf.reshape(n_col, width, -1)], shaped[:1], width, shaped[1:])
+        sl = sl.reshape(n_col * width, -1)
         blocks, leaf_col = forward_blocks(sl, pieces, ex["leaf_y"], ex["sep_sum"], width)
         top_leaf, top_sep, leaf_col = lax.optimization_barrier((top_leaf, top_sep, leaf_col))
         sums = scatter_sum(blocks, ex["sep_sum"])

time: 67.6 us -> 67.5 us (level)
  transfers between devices with their start and end apart: 27 -> 27, of which waited for: 22 -> 21; matrix products, arithmetic and copies ran while one was open for 2% -> 2% of each run, Pallas kernels for 6% -> 6%
where the time goes in v9:
time: 67.5 us; the launch traced here: 67.2 us
  starting transfers between devices  30.8 us (46%)
  waiting for transfers between devices  24.3 us (36%)
  Pallas kernels  6.31 us (9%)
  local copies, waits for them, and re-layouts  3.2 us (5%)
  matrix products  1.73 us (3%)
  between operations  0.91 us (1%)
    ppermute x21, starting transfers between devices, swap(): return lax.ppermute(values, axis, [(i, i ^ step) for i in range(n)])  24.4 us
    ppermute x21, waiting for transfers between devices, swap(): return lax.ppermute(values, axis, [(i, i ^ step) for i in range(n)])  18 us
    ppermute x6, starting transfers between devices, swap_cross(): return lax.ppermute(values, ('sec', axis), pairs)  6.43 us
    pallas_call x20, Pallas kernels, call(): pl.pallas_call(kernel, out_shape=tuple((jax.ShapeDtypeStruct(s, t) for s,...  6.31 us
    ppermute x6, waiting for transfers between devices, swap_cross(): return lax.ppermute(values, ('sec', axis), pairs)  6.24 us
    unnamed x20, local copies, waits for them, and re-layouts  1.56 us
  transfers between devices with their start and end apart: 27, of which 21 were waited for; matrix products, arithmetic and copies ran while one was open for 2% of the time, Pallas kernels for 6%

profile of v9, /device:TPU:0, one launch (start us, length us, event | category | flops | bytes accessed | tf_op | source)
XLA Modules:
  0.0 67.2 jit_solution(15762891248567631009)
XLA Ops:
  1.8 4.0 %collective-permute-start = (bf16[128,256]{1,0:T(8,128)(2,1)S(1)}, bf16[128,256]{1,0:T(8,128)(2,1)S(1)}, u32[]{:S(2)}, u32[]{:S(2)}) collective-permute-start(bf16[128,256]{1,0:T(8,128)(2,1)S(1)} %get-tuple-element.61.refs_1_), channel_id=1, source_target_pairs={{0,12},{4,8},{8,4},{12,0},{1,13},{5,9},{9,5},{13,1},{2,14},{6,10},... | collective-permute-start | bytes 196616 | tf_op jit(solution)/shard_map/ppermute | solution.py:35
  6.4 1.3 %reshape.50.refs_1_ = bf16[4,128,512]{2,1,0:T(8,128)(2,1)S(1)} reshape(bf16[1,1,4,128,4,1,1,128]{7,4,6,5,3,2,1,0:T(4,128)(2,1)} %param.18) | data formatting | bytes 1048576 | tf_op jit(solution)/shard_map/reshape | solution.py:412
  8.5 1.5 %collective-permute-done.1.refs_3_ = bf16[128,256]{1,0:T(8,128)(2,1)S(1)} collective-permute-done((bf16[128,256]{1,0:T(8,128)(2,1)S(1)}, bf16[128,256]{1,0:T(8,128)(2,1)S(1)}, u32[]{:S(2)}, u32[]{:S(2)}) %collective-permute-start.1) | collective-permute-done | bytes 65568 | tf_op jit(solution)/shard_map/ppermute | solution.py:35
  10.8 2.7 %collective-permute-start.3 = (bf16[128,256]{1,0:T(8,128)(2,1)S(1)}, bf16[128,256]{1,0:T(8,128)(2,1)S(1)}, u32[]{:S(2)}, u32[]{:S(2)}) collective-permute-start(bf16[128,256]{1,0:T(8,128)(2,1)S(1)} %get-tuple-element.42), channel_id=1, source_target_pairs={{0,2},{1,3},{2,0},{3,1},{4,6},{5,7},{6,4},{7,5},{8,10},{9,11},{10,... | collective-permute-start | bytes 196616 | tf_op jit(solution)/shard_map/ppermute | solution.py:35
  13.5 1.3 %collective-permute-start.4 = (bf16[128,256]{1,0:T(8,128)(2,1)S(1)}, bf16[128,256]{1,0:T(8,128)(2,1)S(1)}, u32[]{:S(2)}, u32[]{:S(2)}) collective-permute-start(bf16[128,256]{1,0:T(8,128)(2,1)S(1)} %get-tuple-element.43), channel_id=1, source_target_pairs={{0,3},{1,2},{2,1},{3,0},{4,7},{5,6},{6,5},{7,4},{8,11},{9,10},{10,... | collective-permute-start | bytes 196616 | tf_op jit(solution)/shard_map/ppermute | solution.py:35
  17.1 2.6 %collective-permute-done.4 = bf16[128,256]{1,0:T(8,128)(2,1)S(1)} collective-permute-done((bf16[128,256]{1,0:T(8,128)(2,1)S(1)}, bf16[128,256]{1,0:T(8,128)(2,1)S(1)}, u32[]{:S(2)}, u32[]{:S(2)}) %collective-permute-start.4) | collective-permute-done | bytes 65568 | tf_op jit(solution)/shard_map/ppermute | solution.py:35
  20.1 1.5 %collective-permute-start.6 = (bf16[128,256]{1,0:T(8,128)(2,1)S(1)}, bf16[128,256]{1,0:T(8,128)(2,1)S(1)}, u32[]{:S(2)}, u32[]{:S(2)}) collective-permute-start(bf16[128,256]{1,0:T(8,128)(2,1)S(1)} %get-tuple-element.63.refs_1_), channel_id=1, source_target_pairs={{0,12},{4,8},{8,4},{12,0},{1,13},{5,9},{9,5},{13,1},{2,14},{6,10},... | collective-permute-start | bytes 196616 | tf_op jit(solution)/shard_map/ppermute | solution.py:35
  22.3 1.4 %collective-permute-start.8 = (bf16[128,256]{1,0:T(8,128)(2,1)S(1)}, bf16[128,256]{1,0:T(8,128)(2,1)S(1)}, u32[]{:S(2)}, u32[]{:S(2)}) collective-permute-start(bf16[128,256]{1,0:T(8,128)(2,1)S(1)} %get-tuple-element.63.refs_1_), channel_id=1, source_target_pairs={{0,8},{4,12},{8,0},{12,4},{1,9},{5,13},{9,1},{13,5},{2,10},{6,14},... | collective-permute-start | bytes 196616 | tf_op jit(solution)/shard_map/ppermute | solution.py:35
  23.7 1.7 %collective-permute-done.6.refs_2_ = bf16[128,256]{1,0:T(8,128)(2,1)S(1)} collective-permute-done((bf16[128,256]{1,0:T(8,128)(2,1)S(1)}, bf16[128,256]{1,0:T(8,128)(2,1)S(1)}, u32[]{:S(2)}, u32[]{:S(2)}) %collective-permute-start.6) | collective-permute-done | bytes 65568 | tf_op jit(solution)/shard_map/ppermute | solution.py:35
  27.4 1.1 %collective-permute-done.9.other_ref = f32[512,128]{1,0:T(8,128)S(1)} collective-permute-done((f32[512,128]{1,0:T(8,128)S(1)}, f32[512,128]{1,0:T(8,128)S(1)}, u32[]{:S(2)}, u32[]{:S(2)}) %collective-permute-start.9) | collective-permute-done | bytes 262176 | tf_op jit(solution)/shard_map/ppermute | solution.py:35
  28.6 1.4 %collective-permute-start.10 = (bf16[128,128]{1,0:T(8,128)(2,1)S(1)}, bf16[128,128]{1,0:T(8,128)(2,1)S(1)}, u32[]{:S(2)}, u32[]{:S(2)}) collective-permute-start(bf16[128,128]{1,0:T(8,128)(2,1)S(1)} %get-tuple-element.48), channel_id=1, source_target_pairs={{0,18},{1,19},{2,16},{3,17},{16,2},{17,3},{18,0},{19,1},{4,22},{5,... | collective-permute-start | bytes 98312 | tf_op jit(solution)/shard_map/ppermute | solution.py:40
  31.9 1.5 %collective-permute-done.10.refs_1_ = bf16[128,128]{1,0:T(8,128)(2,1)S(1)} collective-permute-done((bf16[128,128]{1,0:T(8,128)(2,1)S(1)}, bf16[128,128]{1,0:T(8,128)(2,1)S(1)}, u32[]{:S(2)}, u32[]{:S(2)}) %collective-permute-start.10) | collective-permute-done | bytes 32800 | tf_op jit(solution)/shard_map/ppermute | solution.py:40
  33.4 1.7 %collective-permute-done.11.refs_2_ = bf16[128,128]{1,0:T(8,128)(2,1)S(1)} collective-permute-done((bf16[128,128]{1,0:T(8,128)(2,1)S(1)}, bf16[128,128]{1,0:T(8,128)(2,1)S(1)}, u32[]{:S(2)}, u32[]{:S(2)}) %collective-permute-start.11) | collective-permute-done | bytes 32800 | tf_op jit(solution)/shard_map/ppermute | solution.py:40
  36.5 1.1 %collective-permute-start.14 = (bf16[128,128]{1,0:T(8,128)(2,1)S(1)}, bf16[128,128]{1,0:T(8,128)(2,1)S(1)}, u32[]{:S(2)}, u32[]{:S(2)}) collective-permute-start(bf16[128,128]{1,0:T(8,128)(2,1)S(1)} %get-tuple-element.51.refs_0_), channel_id=1, source_target_pairs={{0,19},{1,18},{2,17},{3,16},{16,3},{17,2},{18,1},{19,0},{4,23},{5,... | collective-permute-start | bytes 98312 | tf_op jit(solution)/shard_map/ppermute | solution.py:40
  37.6 1.2 %collective-permute-start.15 = (bf16[128,128]{1,0:T(8,128)(2,1)S(1)}, bf16[128,128]{1,0:T(8,128)(2,1)S(1)}, u32[]{:S(2)}, u32[]{:S(2)}) collective-permute-start(bf16[128,128]{1,0:T(8,128)(2,1)S(1)} %get-tuple-element.51.refs_0_), channel_id=1, source_target_pairs={{0,17},{1,16},{2,19},{3,18},{16,1},{17,0},{18,3},{19,2},{4,21},{5,... | collective-permute-start | bytes 98312 | tf_op jit(solution)/shard_map/ppermute | solution.py:40
  38.8 1.3 %collective-permute-done.13.refs_1_ = bf16[128,128]{1,0:T(8,128)(2,1)S(1)} collective-permute-done((bf16[128,128]{1,0:T(8,128)(2,1)S(1)}, bf16[128,128]{1,0:T(8,128)(2,1)S(1)}, u32[]{:S(2)}, u32[]{:S(2)}) %collective-permute-start.13) | collective-permute-done | bytes 32800 | tf_op jit(solution)/shard_map/ppermute | solution.py:40
  40.0 1.7 %collective-permute-done.14.refs_2_ = bf16[128,128]{1,0:T(8,128)(2,1)S(1)} collective-permute-done((bf16[128,128]{1,0:T(8,128)(2,1)S(1)}, bf16[128,128]{1,0:T(8,128)(2,1)S(1)}, u32[]{:S(2)}, u32[]{:S(2)}) %collective-permute-start.14) | collective-permute-done | bytes 32800 | tf_op jit(solution)/shard_map/ppermute | solution.py:40
  43.5 2.5 %collective-permute-start.17 = (bf16[128,256]{1,0:T(8,128)(2,1)S(1)}, bf16[128,256]{1,0:T(8,128)(2,1)S(1)}, u32[]{:S(2)}, u32[]{:S(2)}) collective-permute-start(bf16[128,256]{1,0:T(8,128)(2,1)S(1)} %get-tuple-element.53), channel_id=1, source_target_pairs={{0,12},{4,8},{8,4},{12,0},{1,13},{5,9},{9,5},{13,1},{2,14},{6,10},... | collective-permute-start | bytes 196616 | tf_op jit(solution)/shard_map/ppermute | solution.py:35
  47.3 1.9 %collective-permute-done.17 = bf16[128,256]{1,0:T(8,128)(2,1)S(1)} collective-permute-done((bf16[128,256]{1,0:T(8,128)(2,1)S(1)}, bf16[128,256]{1,0:T(8,128)(2,1)S(1)}, u32[]{:S(2)}, u32[]{:S(2)}) %collective-permute-start.17) | collective-permute-done | bytes 65568 | tf_op jit(solution)/shard_map/ppermute | solution.py:35
  51.1 2.4 %collective-permute-start.20 = (bf16[128,256]{1,0:T(8,128)(2,1)S(1)}, bf16[128,256]{1,0:T(8,128)(2,1)S(1)}, u32[]{:S(2)}, u32[]{:S(2)}) collective-permute-start(bf16[128,256]{1,0:T(8,128)(2,1)S(1)} %get-tuple-element.65.refs_1_), channel_id=1, source_target_pairs={{0,3},{1,2},{2,1},{3,0},{4,7},{5,6},{6,5},{7,4},{8,11},{9,10},{10,... | collective-permute-start | bytes 196616 | tf_op jit(solution)/shard_map/ppermute | solution.py:35
  53.6 2.0 %collective-permute-start.22 = (bf16[128,256]{1,0:T(8,128)(2,1)S(1)}, bf16[128,256]{1,0:T(8,128)(2,1)S(1)}, u32[]{:S(2)}, u32[]{:S(2)}) collective-permute-start(bf16[128,256]{1,0:T(8,128)(2,1)S(1)} %get-tuple-element.65.refs_1_), channel_id=1, source_target_pairs={{0,2},{1,3},{2,0},{3,1},{4,6},{5,7},{6,4},{7,5},{8,10},{9,11},{10,... | collective-permute-start | bytes 196616 | tf_op jit(solution)/shard_map/ppermute | solution.py:35
  55.9 1.8 %collective-permute-done.20.refs_2_ = bf16[128,256]{1,0:T(8,128)(2,1)S(1)} collective-permute-done((bf16[128,256]{1,0:T(8,128)(2,1)S(1)}, bf16[128,256]{1,0:T(8,128)(2,1)S(1)}, u32[]{:S(2)}, u32[]{:S(2)}) %collective-permute-start.20) | collective-permute-done | bytes 65568 | tf_op jit(solution)/shard_map/ppermute | solution.py:35
  59.3 2.1 %collective-permute-start.23 = (bf16[128,256]{1,0:T(8,128)(2,1)S(1)}, bf16[128,256]{1,0:T(8,128)(2,1)S(1)}, u32[]{:S(2)}, u32[]{:S(2)}) collective-permute-start(bf16[128,256]{1,0:T(8,128)(2,1)S(1)} %get-tuple-element.57), channel_id=1, source_target_pairs={{0,12},{4,8},{8,4},{12,0},{1,13},{5,9},{9,5},{13,1},{2,14},{6,10},... | collective-permute-start | bytes 196616 | tf_op jit(solution)/shard_map/ppermute | solution.py:35
  64.5 1.1 %collective-permute-done.24.refs_2_ = bf16[128,256]{1,0:T(8,128)(2,1)S(1)} collective-permute-done((bf16[128,256]{1,0:T(8,128)(2,1)S(1)}, bf16[128,256]{1,0:T(8,128)(2,1)S(1)}, u32[]{:S(2)}, u32[]{:S(2)}) %collective-permute-start.24) | collective-permute-done | bytes 65568 | tf_op jit(solution)/shard_map/ppermute | solution.py:35
  (76 shorter events, 23.6 us)
Async XLA Ops:
  1.8 6.7 %collective-permute-start = (bf16[128,256]{1,0:T(8,128)(2,1)S(1)}, bf16[128,256]{1,0:T(8,128)(2,1)S(1)}, u32[]{:S(2)}, u32[]{:S(2)}) collective-permute-start(bf16[128,256]{1,0:T(8,128)(2,1)S(1)} %get-tuple-element.61.refs_1_), channel_id=1, source_target_pairs={{0,12},{4,8},{8,4},{12,0},{1,13},{5,9},{9,5},{13,1},{2,14},{6,10},... | collective-permute-start | bytes 196616 | tf_op jit(solution)/shard_map/ppermute | solution.py:35
  5.7 4.3 %collective-permute-start.1 = (bf16[128,256]{1,0:T(8,128)(2,1)S(1)}, bf16[128,256]{1,0:T(8,128)(2,1)S(1)}, u32[]{:S(2)}, u32[]{:S(2)}) collective-permute-start(bf16[128,256]{1,0:T(8,128)(2,1)S(1)} %get-tuple-element.61.refs_1_), channel_id=1, source_target_pairs={{0,4},{4,0},{8,12},{12,8},{1,5},{5,1},{9,13},{13,9},{2,6},{6,2},{1... | collective-permute-start | bytes 196616 | tf_op jit(solution)/shard_map/ppermute | solution.py:35
  6.3 4.3 %collective-permute-start.2 = (bf16[128,256]{1,0:T(8,128)(2,1)S(1)}, bf16[128,256]{1,0:T(8,128)(2,1)S(1)}, u32[]{:S(2)}, u32[]{:S(2)}) collective-permute-start(bf16[128,256]{1,0:T(8,128)(2,1)S(1)} %get-tuple-element.61.refs_1_), channel_id=1, source_target_pairs={{0,8},{4,12},{8,0},{12,4},{1,9},{5,13},{9,1},{13,5},{2,10},{6,14},... | collective-permute-start | bytes 196616 | tf_op jit(solution)/shard_map/ppermute | solution.py:35
  10.8 6.3 %collective-permute-start.3 = (bf16[128,256]{1,0:T(8,128)(2,1)S(1)}, bf16[128,256]{1,0:T(8,128)(2,1)S(1)}, u32[]{:S(2)}, u32[]{:S(2)}) collective-permute-start(bf16[128,256]{1,0:T(8,128)(2,1)S(1)} %get-tuple-element.42), channel_id=1, source_target_pairs={{0,2},{1,3},{2,0},{3,1},{4,6},{5,7},{6,4},{7,5},{8,10},{9,11},{10,... | collective-permute-start | bytes 196616 | tf_op jit(solution)/shard_map/ppermute | solution.py:35
  13.5 6.2 %collective-permute-start.4 = (bf16[128,256]{1,0:T(8,128)(2,1)S(1)}, bf16[128,256]{1,0:T(8,128)(2,1)S(1)}, u32[]{:S(2)}, u32[]{:S(2)}) collective-permute-start(bf16[128,256]{1,0:T(8,128)(2,1)S(1)} %get-tuple-element.43), channel_id=1, source_target_pairs={{0,3},{1,2},{2,1},{3,0},{4,7},{5,6},{6,5},{7,4},{8,11},{9,10},{10,... | collective-permute-start | bytes 196616 | tf_op jit(solution)/shard_map/ppermute | solution.py:35
  14.8 5.0 %collective-permute-start.5 = (bf16[128,256]{1,0:T(8,128)(2,1)S(1)}, bf16[128,256]{1,0:T(8,128)(2,1)S(1)}, u32[]{:S(2)}, u32[]{:S(2)}) collective-permute-start(bf16[128,256]{1,0:T(8,128)(2,1)S(1)} %get-tuple-element.44), channel_id=1, source_target_pairs={{0,1},{1,0},{2,3},{3,2},{4,5},{5,4},{6,7},{7,6},{8,9},{9,8},{10,11... | collective-permute-start | bytes 196616 | tf_op jit(solution)/shard_map/ppermute | solution.py:35
  20.1 5.2 %collective-permute-start.6 = (bf16[128,256]{1,0:T(8,128)(2,1)S(1)}, bf16[128,256]{1,0:T(8,128)(2,1)S(1)}, u32[]{:S(2)}, u32[]{:S(2)}) collective-permute-start(bf16[128,256]{1,0:T(8,128)(2,1)S(1)} %get-tuple-element.63.refs_1_), channel_id=1, source_target_pairs={{0,12},{4,8},{8,4},{12,0},{1,13},{5,9},{9,5},{13,1},{2,14},{6,10},... | collective-permute-start | bytes 196616 | tf_op jit(solution)/shard_map/ppermute | solution.py:35
  21.6 4.3 %collective-permute-start.7 = (bf16[128,256]{1,0:T(8,128)(2,1)S(1)}, bf16[128,256]{1,0:T(8,128)(2,1)S(1)}, u32[]{:S(2)}, u32[]{:S(2)}) collective-permute-start(bf16[128,256]{1,0:T(8,128)(2,1)S(1)} %get-tuple-element.63.refs_1_), channel_id=1, source_target_pairs={{0,4},{4,0},{8,12},{12,8},{1,5},{5,1},{9,13},{13,9},{2,6},{6,2},{1... | collective-permute-start | bytes 196616 | tf_op jit(solution)/shard_map/ppermute | solution.py:35
  22.3 4.3 %collective-permute-start.8 = (bf16[128,256]{1,0:T(8,128)(2,1)S(1)}, bf16[128,256]{1,0:T(8,128)(2,1)S(1)}, u32[]{:S(2)}, u32[]{:S(2)}) collective-permute-start(bf16[128,256]{1,0:T(8,128)(2,1)S(1)} %get-tuple-element.63.refs_1_), channel_id=1, source_target_pairs={{0,8},{4,12},{8,0},{12,4},{1,9},{5,13},{9,1},{13,5},{2,10},{6,14},... | collective-permute-start | bytes 196616 | tf_op jit(solution)/shard_map/ppermute | solution.py:35
  28.6 4.8 %collective-permute-start.10 = (bf16[128,128]{1,0:T(8,128)(2,1)S(1)}, bf16[128,128]{1,0:T(8,128)(2,1)S(1)}, u32[]{:S(2)}, u32[]{:S(2)}) collective-permute-start(bf16[128,128]{1,0:T(8,128)(2,1)S(1)} %get-tuple-element.48), channel_id=1, source_target_pairs={{0,18},{1,19},{2,16},{3,17},{16,2},{17,3},{18,0},{19,1},{4,22},{5,... | collective-permute-start | bytes 98312 | tf_op jit(solution)/shard_map/ppermute | solution.py:40
  30.0 5.2 %collective-permute-start.11 = (bf16[128,128]{1,0:T(8,128)(2,1)S(1)}, bf16[128,128]{1,0:T(8,128)(2,1)S(1)}, u32[]{:S(2)}, u32[]{:S(2)}) collective-permute-start(bf16[128,128]{1,0:T(8,128)(2,1)S(1)} %get-tuple-element.49), channel_id=1, source_target_pairs={{0,19},{1,18},{2,17},{3,16},{16,3},{17,2},{18,1},{19,0},{4,23},{5,... | collective-permute-start | bytes 98312 | tf_op jit(solution)/shard_map/ppermute | solution.py:40
  30.7 4.4 %collective-permute-start.12 = (bf16[128,128]{1,0:T(8,128)(2,1)S(1)}, bf16[128,128]{1,0:T(8,128)(2,1)S(1)}, u32[]{:S(2)}, u32[]{:S(2)}) collective-permute-start(bf16[128,128]{1,0:T(8,128)(2,1)S(1)} %get-tuple-element.50), channel_id=1, source_target_pairs={{0,17},{1,16},{2,19},{3,18},{16,1},{17,0},{18,3},{19,2},{4,21},{5,... | collective-permute-start | bytes 98312 | tf_op jit(solution)/shard_map/ppermute | solution.py:40
  35.4 4.7 %collective-permute-start.13 = (bf16[128,128]{1,0:T(8,128)(2,1)S(1)}, bf16[128,128]{1,0:T(8,128)(2,1)S(1)}, u32[]{:S(2)}, u32[]{:S(2)}) collective-permute-start(bf16[128,128]{1,0:T(8,128)(2,1)S(1)} %get-tuple-element.51.refs_0_), channel_id=1, source_target_pairs={{0,18},{1,19},{2,16},{3,17},{16,2},{17,3},{18,0},{19,1},{4,22},{5,... | collective-permute-start | bytes 98312 | tf_op jit(solution)/shard_map/ppermute | solution.py:40
  36.5 5.3 %collective-permute-start.14 = (bf16[128,128]{1,0:T(8,128)(2,1)S(1)}, bf16[128,128]{1,0:T(8,128)(2,1)S(1)}, u32[]{:S(2)}, u32[]{:S(2)}) collective-permute-start(bf16[128,128]{1,0:T(8,128)(2,1)S(1)} %get-tuple-element.51.refs_0_), channel_id=1, source_target_pairs={{0,19},{1,18},{2,17},{3,16},{16,3},{17,2},{18,1},{19,0},{4,23},{5,... | collective-permute-start | bytes 98312 | tf_op jit(solution)/shard_map/ppermute | solution.py:40
  43.5 5.7 %collective-permute-start.17 = (bf16[128,256]{1,0:T(8,128)(2,1)S(1)}, bf16[128,256]{1,0:T(8,128)(2,1)S(1)}, u32[]{:S(2)}, u32[]{:S(2)}) collective-permute-start(bf16[128,256]{1,0:T(8,128)(2,1)S(1)} %get-tuple-element.53), channel_id=1, source_target_pairs={{0,12},{4,8},{8,4},{12,0},{1,13},{5,9},{9,5},{13,1},{2,14},{6,10},... | collective-permute-start | bytes 196616 | tf_op jit(solution)/shard_map/ppermute | solution.py:35
  46.0 4.3 %collective-permute-start.18 = (bf16[128,256]{1,0:T(8,128)(2,1)S(1)}, bf16[128,256]{1,0:T(8,128)(2,1)S(1)}, u32[]{:S(2)}, u32[]{:S(2)}) collective-permute-start(bf16[128,256]{1,0:T(8,128)(2,1)S(1)} %get-tuple-element.54), channel_id=1, source_target_pairs={{0,4},{4,0},{8,12},{12,8},{1,5},{5,1},{9,13},{13,9},{2,6},{6,2},{1... | collective-permute-start | bytes 196616 | tf_op jit(solution)/shard_map/ppermute | solution.py:35
  46.5 4.3 %collective-permute-start.19 = (bf16[128,256]{1,0:T(8,128)(2,1)S(1)}, bf16[128,256]{1,0:T(8,128)(2,1)S(1)}, u32[]{:S(2)}, u32[]{:S(2)}) collective-permute-start(bf16[128,256]{1,0:T(8,128)(2,1)S(1)} %get-tuple-element.55), channel_id=1, source_target_pairs={{0,8},{4,12},{8,0},{12,4},{1,9},{5,13},{9,1},{13,5},{2,10},{6,14},... | collective-permute-start | bytes 196616 | tf_op jit(solution)/shard_map/ppermute | solution.py:35
  51.1 6.6 %collective-permute-start.20 = (bf16[128,256]{1,0:T(8,128)(2,1)S(1)}, bf16[128,256]{1,0:T(8,128)(2,1)S(1)}, u32[]{:S(2)}, u32[]{:S(2)}) collective-permute-start(bf16[128,256]{1,0:T(8,128)(2,1)S(1)} %get-tuple-element.65.refs_1_), channel_id=1, source_target_pairs={{0,3},{1,2},{2,1},{3,0},{4,7},{5,6},{6,5},{7,4},{8,11},{9,10},{10,... | collective-permute-start | bytes 196616 | tf_op jit(solution)/shard_map/ppermute | solution.py:35
  53.5 5.1 %collective-permute-start.21 = (bf16[128,256]{1,0:T(8,128)(2,1)S(1)}, bf16[128,256]{1,0:T(8,128)(2,1)S(1)}, u32[]{:S(2)}, u32[]{:S(2)}) collective-permute-start(bf16[128,256]{1,0:T(8,128)(2,1)S(1)} %get-tuple-element.65.refs_1_), channel_id=1, source_target_pairs={{0,1},{1,0},{2,3},{3,2},{4,5},{5,4},{6,7},{7,6},{8,9},{9,8},{10,11... | collective-permute-start | bytes 196616 | tf_op jit(solution)/shard_map/ppermute | solution.py:35
  53.6 5.4 %collective-permute-start.22 = (bf16[128,256]{1,0:T(8,128)(2,1)S(1)}, bf16[128,256]{1,0:T(8,128)(2,1)S(1)}, u32[]{:S(2)}, u32[]{:S(2)}) collective-permute-start(bf16[128,256]{1,0:T(8,128)(2,1)S(1)} %get-tuple-element.65.refs_1_), channel_id=1, source_target_pairs={{0,2},{1,3},{2,0},{3,1},{4,6},{5,7},{6,4},{7,5},{8,10},{9,11},{10,... | collective-permute-start | bytes 196616 | tf_op jit(solution)/shard_map/ppermute | solution.py:35
  55.6 7.4 %collective-permute-start.26 = (f32[128,128]{1,0:T(8,128)S(1)}, f32[128,128]{1,0:T(8,128)S(1)}, u32[]{:S(2)}, u32[]{:S(2)}) collective-permute-start(f32[128,128]{1,0:T(8,128)S(1)} %get-tuple-element.60.mine_ref), channel_id=1, source_target_pairs={{0,16},{16,0},{1,17},{17,1},{2,18},{18,2},{3,19},{19,3},{4,20},{20... | collective-permute-start | bytes 196616 | tf_op jit(solution)/shard_map/ppermute | solution.py:35
  59.3 5.3 %collective-permute-start.23 = (bf16[128,256]{1,0:T(8,128)(2,1)S(1)}, bf16[128,256]{1,0:T(8,128)(2,1)S(1)}, u32[]{:S(2)}, u32[]{:S(2)}) collective-permute-start(bf16[128,256]{1,0:T(8,128)(2,1)S(1)} %get-tuple-element.57), channel_id=1, source_target_pairs={{0,12},{4,8},{8,4},{12,0},{1,13},{5,9},{9,5},{13,1},{2,14},{6,10},... | collective-permute-start | bytes 196616 | tf_op jit(solution)/shard_map/ppermute | solution.py:35
  61.4 4.3 %collective-permute-start.24 = (bf16[128,256]{1,0:T(8,128)(2,1)S(1)}, bf16[128,256]{1,0:T(8,128)(2,1)S(1)}, u32[]{:S(2)}, u32[]{:S(2)}) collective-permute-start(bf16[128,256]{1,0:T(8,128)(2,1)S(1)} %get-tuple-element.58), channel_id=1, source_target_pairs={{0,4},{4,0},{8,12},{12,8},{1,5},{5,1},{9,13},{13,9},{2,6},{6,2},{1... | collective-permute-start | bytes 196616 | tf_op jit(solution)/shard_map/ppermute | solution.py:35
  62.1 4.3 %collective-permute-start.25 = (bf16[128,256]{1,0:T(8,128)(2,1)S(1)}, bf16[128,256]{1,0:T(8,128)(2,1)S(1)}, u32[]{:S(2)}, u32[]{:S(2)}) collective-permute-start(bf16[128,256]{1,0:T(8,128)(2,1)S(1)} %get-tuple-element.59), channel_id=1, source_target_pairs={{0,8},{4,12},{8,0},{12,4},{1,9},{5,13},{9,1},{13,5},{2,10},{6,14},... | collective-permute-start | bytes 196616 | tf_op jit(solution)/shard_map/ppermute | solution.py:35
  (13 other events, 54.3 us)

commit v10 on v8

--- a/solution.py
+++ b/solution.py
@@ -72,7 +72,7 @@
         in_specs=[VMEM] * len(args),
         out_specs=(VMEM,) * len(outs),
         scratch_shapes=[pltpu.VMEM(s, t) for s, t in scratch],
-        compiler_params=pltpu.CompilerParams(vmem_limit_bytes=total + (6 << 20)),
+        compiler_params=pltpu.CompilerParams(vmem_limit_bytes=total + (2 << 20)),
         cost_estimate=pl.CostEstimate(flops=flops, bytes_accessed=total, transcendentals=0),
     )(*args)
 

time: 67.6 us -> 67.6 us (level)
  no operation moved by 1% of the time
where the time goes in v10:
time: 67.6 us; the launch traced here: 67.3 us
  starting transfers between devices  30.8 us (46%)
  waiting for transfers between devices  24.4 us (36%)
  Pallas kernels  6.3 us (9%)
  local copies, waits for them, and re-layouts  3.21 us (5%)
  matrix products  1.73 us (3%)
  between operations  0.89 us (1%)
    ppermute x21, starting transfers between devices, swap(): return lax.ppermute(values, axis, [(i, i ^ step) for i in range(n)])  24.4 us
    ppermute x21, waiting for transfers between devices, swap(): return lax.ppermute(values, axis, [(i, i ^ step) for i in range(n)])  18.1 us
    ppermute x6, starting transfers between devices, swap_cross(): return lax.ppermute(values, ('sec', axis), pairs)  6.43 us
    pallas_call x20, Pallas kernels, call(): pl.pallas_call(kernel, out_shape=tuple((jax.ShapeDtypeStruct(s, t) for s,...  6.3 us
    ppermute x6, waiting for transfers between devices, swap_cross(): return lax.ppermute(values, ('sec', axis), pairs)  6.25 us
    unnamed x20, local copies, waits for them, and re-layouts  1.56 us
  transfers between devices with their start and end apart: 27, of which 22 were waited for; matrix products, arithmetic and copies ran while one was open for 2% of the time, Pallas kernels for 6%

profile of v10, /device:TPU:0, one launch (start us, length us, event | category | flops | bytes accessed | tf_op | source)
XLA Modules:
  0.0 67.3 jit_solution(1225786400078675719)
XLA Ops:
  0.6 1.1 %fusion.19 = (bf16[128,256]{1,0:T(8,128)(2,1)S(1)}, f32[128,256]{1,0:T(8,128)S(1)}) fusion(bf16[1,1,1,1,128,256]{5,4,3,2,1,0:T(8,128)(2,1)} %param.12, f32[1,1,1,1,128,128]{5,4,3,2,1,0:T(8,128)} %param.15), kind=kOutput, calls=%fused_computation.22 | convolution fusion | flops 50364416 | bytes 327680 | tf_op jit(solution)/shard_map/mab,mbn->man/dot_general | solution.py:156
  1.8 4.0 %collective-permute-start = (bf16[128,256]{1,0:T(8,128)(2,1)S(1)}, bf16[128,256]{1,0:T(8,128)(2,1)S(1)}, u32[]{:S(2)}, u32[]{:S(2)}) collective-permute-start(bf16[128,256]{1,0:T(8,128)(2,1)S(1)} %get-tuple-element.55.refs_1_), channel_id=1, source_target_pairs={{0,12},{4,8},{8,4},{12,0},{1,13},{5,9},{9,5},{13,1},{2,14},{6,10},... | collective-permute-start | bytes 196616 | tf_op jit(solution)/shard_map/ppermute | solution.py:35
  6.4 1.3 %reshape.50.refs_1_ = bf16[4,128,512]{2,1,0:T(8,128)(2,1)S(1)} reshape(bf16[1,1,4,128,4,1,1,128]{7,4,6,5,3,2,1,0:T(4,128)(2,1)} %param.18) | data formatting | bytes 1048576 | tf_op jit(solution)/shard_map/reshape | solution.py:408
  8.2 1.8 %collective-permute-done.1.refs_3_ = bf16[128,256]{1,0:T(8,128)(2,1)S(1)} collective-permute-done((bf16[128,256]{1,0:T(8,128)(2,1)S(1)}, bf16[128,256]{1,0:T(8,128)(2,1)S(1)}, u32[]{:S(2)}, u32[]{:S(2)}) %collective-permute-start.1) | collective-permute-done | bytes 65568 | tf_op jit(solution)/shard_map/ppermute | solution.py:35
  10.8 2.7 %collective-permute-start.3 = (bf16[128,256]{1,0:T(8,128)(2,1)S(1)}, bf16[128,256]{1,0:T(8,128)(2,1)S(1)}, u32[]{:S(2)}, u32[]{:S(2)}) collective-permute-start(bf16[128,256]{1,0:T(8,128)(2,1)S(1)} %get-tuple-element.36), channel_id=1, source_target_pairs={{0,2},{1,3},{2,0},{3,1},{4,6},{5,7},{6,4},{7,5},{8,10},{9,11},{10,... | collective-permute-start | bytes 196616 | tf_op jit(solution)/shard_map/ppermute | solution.py:35
  13.5 1.3 %collective-permute-start.4 = (bf16[128,256]{1,0:T(8,128)(2,1)S(1)}, bf16[128,256]{1,0:T(8,128)(2,1)S(1)}, u32[]{:S(2)}, u32[]{:S(2)}) collective-permute-start(bf16[128,256]{1,0:T(8,128)(2,1)S(1)} %get-tuple-element.37), channel_id=1, source_target_pairs={{0,3},{1,2},{2,1},{3,0},{4,7},{5,6},{6,5},{7,4},{8,11},{9,10},{10,... | collective-permute-start | bytes 196616 | tf_op jit(solution)/shard_map/ppermute | solution.py:35
  17.8 1.9 %collective-permute-done.4 = bf16[128,256]{1,0:T(8,128)(2,1)S(1)} collective-permute-done((bf16[128,256]{1,0:T(8,128)(2,1)S(1)}, bf16[128,256]{1,0:T(8,128)(2,1)S(1)}, u32[]{:S(2)}, u32[]{:S(2)}) %collective-permute-start.4) | collective-permute-done | bytes 65568 | tf_op jit(solution)/shard_map/ppermute | solution.py:35
  20.1 1.5 %collective-permute-start.6 = (bf16[128,256]{1,0:T(8,128)(2,1)S(1)}, bf16[128,256]{1,0:T(8,128)(2,1)S(1)}, u32[]{:S(2)}, u32[]{:S(2)}) collective-permute-start(bf16[128,256]{1,0:T(8,128)(2,1)S(1)} %get-tuple-element.57.refs_1_), channel_id=1, source_target_pairs={{0,12},{4,8},{8,4},{12,0},{1,13},{5,9},{9,5},{13,1},{2,14},{6,10},... | collective-permute-start | bytes 196616 | tf_op jit(solution)/shard_map/ppermute | solution.py:35
  22.3 1.4 %collective-permute-start.8 = (bf16[128,256]{1,0:T(8,128)(2,1)S(1)}, bf16[128,256]{1,0:T(8,128)(2,1)S(1)}, u32[]{:S(2)}, u32[]{:S(2)}) collective-permute-start(bf16[128,256]{1,0:T(8,128)(2,1)S(1)} %get-tuple-element.57.refs_1_), channel_id=1, source_target_pairs={{0,8},{4,12},{8,0},{12,4},{1,9},{5,13},{9,1},{13,5},{2,10},{6,14},... | collective-permute-start | bytes 196616 | tf_op jit(solution)/shard_map/ppermute | solution.py:35
  23.7 1.7 %collective-permute-done.6.refs_2_ = bf16[128,256]{1,0:T(8,128)(2,1)S(1)} collective-permute-done((bf16[128,256]{1,0:T(8,128)(2,1)S(1)}, bf16[128,256]{1,0:T(8,128)(2,1)S(1)}, u32[]{:S(2)}, u32[]{:S(2)}) %collective-permute-start.6) | collective-permute-done | bytes 65568 | tf_op jit(solution)/shard_map/ppermute | solution.py:35
  27.4 1.1 %collective-permute-done.9.other_ref = f32[512,128]{1,0:T(8,128)S(1)} collective-permute-done((f32[512,128]{1,0:T(8,128)S(1)}, f32[512,128]{1,0:T(8,128)S(1)}, u32[]{:S(2)}, u32[]{:S(2)}) %collective-permute-start.9) | collective-permute-done | bytes 262176 | tf_op jit(solution)/shard_map/ppermute | solution.py:35
  28.6 1.4 %collective-permute-start.10 = (bf16[128,128]{1,0:T(8,128)(2,1)S(1)}, bf16[128,128]{1,0:T(8,128)(2,1)S(1)}, u32[]{:S(2)}, u32[]{:S(2)}) collective-permute-start(bf16[128,128]{1,0:T(8,128)(2,1)S(1)} %get-tuple-element.42), channel_id=1, source_target_pairs={{0,18},{1,19},{2,16},{3,17},{16,2},{17,3},{18,0},{19,1},{4,22},{5,... | collective-permute-start | bytes 98312 | tf_op jit(solution)/shard_map/ppermute | solution.py:40
  31.9 1.7 %collective-permute-done.10.refs_1_ = bf16[128,128]{1,0:T(8,128)(2,1)S(1)} collective-permute-done((bf16[128,128]{1,0:T(8,128)(2,1)S(1)}, bf16[128,128]{1,0:T(8,128)(2,1)S(1)}, u32[]{:S(2)}, u32[]{:S(2)}) %collective-permute-start.10) | collective-permute-done | bytes 32800 | tf_op jit(solution)/shard_map/ppermute | solution.py:40
  33.6 1.5 %collective-permute-done.11.refs_2_ = bf16[128,128]{1,0:T(8,128)(2,1)S(1)} collective-permute-done((bf16[128,128]{1,0:T(8,128)(2,1)S(1)}, bf16[128,128]{1,0:T(8,128)(2,1)S(1)}, u32[]{:S(2)}, u32[]{:S(2)}) %collective-permute-start.11) | collective-permute-done | bytes 32800 | tf_op jit(solution)/shard_map/ppermute | solution.py:40
  36.5 1.3 %collective-permute-start.14 = (bf16[128,128]{1,0:T(8,128)(2,1)S(1)}, bf16[128,128]{1,0:T(8,128)(2,1)S(1)}, u32[]{:S(2)}, u32[]{:S(2)}) collective-permute-start(bf16[128,128]{1,0:T(8,128)(2,1)S(1)} %get-tuple-element.45.refs_0_), channel_id=1, source_target_pairs={{0,19},{1,18},{2,17},{3,16},{16,3},{17,2},{18,1},{19,0},{4,23},{5,... | collective-permute-start | bytes 98312 | tf_op jit(solution)/shard_map/ppermute | solution.py:40
  38.8 1.3 %collective-permute-done.13.refs_1_ = bf16[128,128]{1,0:T(8,128)(2,1)S(1)} collective-permute-done((bf16[128,128]{1,0:T(8,128)(2,1)S(1)}, bf16[128,128]{1,0:T(8,128)(2,1)S(1)}, u32[]{:S(2)}, u32[]{:S(2)}) %collective-permute-start.13) | collective-permute-done | bytes 32800 | tf_op jit(solution)/shard_map/ppermute | solution.py:40
  40.0 1.7 %collective-permute-done.14.refs_2_ = bf16[128,128]{1,0:T(8,128)(2,1)S(1)} collective-permute-done((bf16[128,128]{1,0:T(8,128)(2,1)S(1)}, bf16[128,128]{1,0:T(8,128)(2,1)S(1)}, u32[]{:S(2)}, u32[]{:S(2)}) %collective-permute-start.14) | collective-permute-done | bytes 32800 | tf_op jit(solution)/shard_map/ppermute | solution.py:40
  43.5 2.5 %collective-permute-start.17 = (bf16[128,256]{1,0:T(8,128)(2,1)S(1)}, bf16[128,256]{1,0:T(8,128)(2,1)S(1)}, u32[]{:S(2)}, u32[]{:S(2)}) collective-permute-start(bf16[128,256]{1,0:T(8,128)(2,1)S(1)} %get-tuple-element.47), channel_id=1, source_target_pairs={{0,12},{4,8},{8,4},{12,0},{1,13},{5,9},{9,5},{13,1},{2,14},{6,10},... | collective-permute-start | bytes 196616 | tf_op jit(solution)/shard_map/ppermute | solution.py:35
  47.3 1.9 %collective-permute-done.17 = bf16[128,256]{1,0:T(8,128)(2,1)S(1)} collective-permute-done((bf16[128,256]{1,0:T(8,128)(2,1)S(1)}, bf16[128,256]{1,0:T(8,128)(2,1)S(1)}, u32[]{:S(2)}, u32[]{:S(2)}) %collective-permute-start.17) | collective-permute-done | bytes 65568 | tf_op jit(solution)/shard_map/ppermute | solution.py:35
  51.1 2.4 %collective-permute-start.20 = (bf16[128,256]{1,0:T(8,128)(2,1)S(1)}, bf16[128,256]{1,0:T(8,128)(2,1)S(1)}, u32[]{:S(2)}, u32[]{:S(2)}) collective-permute-start(bf16[128,256]{1,0:T(8,128)(2,1)S(1)} %get-tuple-element.59.refs_1_), channel_id=1, source_target_pairs={{0,3},{1,2},{2,1},{3,0},{4,7},{5,6},{6,5},{7,4},{8,11},{9,10},{10,... | collective-permute-start | bytes 196616 | tf_op jit(solution)/shard_map/ppermute | solution.py:35
  53.6 2.0 %collective-permute-start.22 = (bf16[128,256]{1,0:T(8,128)(2,1)S(1)}, bf16[128,256]{1,0:T(8,128)(2,1)S(1)}, u32[]{:S(2)}, u32[]{:S(2)}) collective-permute-start(bf16[128,256]{1,0:T(8,128)(2,1)S(1)} %get-tuple-element.59.refs_1_), channel_id=1, source_target_pairs={{0,2},{1,3},{2,0},{3,1},{4,6},{5,7},{6,4},{7,5},{8,10},{9,11},{10,... | collective-permute-start | bytes 196616 | tf_op jit(solution)/shard_map/ppermute | solution.py:35
  55.9 1.8 %collective-permute-done.20.refs_2_ = bf16[128,256]{1,0:T(8,128)(2,1)S(1)} collective-permute-done((bf16[128,256]{1,0:T(8,128)(2,1)S(1)}, bf16[128,256]{1,0:T(8,128)(2,1)S(1)}, u32[]{:S(2)}, u32[]{:S(2)}) %collective-permute-start.20) | collective-permute-done | bytes 65568 | tf_op jit(solution)/shard_map/ppermute | solution.py:35
  59.3 2.1 %collective-permute-start.23 = (bf16[128,256]{1,0:T(8,128)(2,1)S(1)}, bf16[128,256]{1,0:T(8,128)(2,1)S(1)}, u32[]{:S(2)}, u32[]{:S(2)}) collective-permute-start(bf16[128,256]{1,0:T(8,128)(2,1)S(1)} %get-tuple-element.51), channel_id=1, source_target_pairs={{0,12},{4,8},{8,4},{12,0},{1,13},{5,9},{9,5},{13,1},{2,14},{6,10},... | collective-permute-start | bytes 196616 | tf_op jit(solution)/shard_map/ppermute | solution.py:35
  64.6 1.1 %collective-permute-done.24.refs_2_ = bf16[128,256]{1,0:T(8,128)(2,1)S(1)} collective-permute-done((bf16[128,256]{1,0:T(8,128)(2,1)S(1)}, bf16[128,256]{1,0:T(8,128)(2,1)S(1)}, u32[]{:S(2)}, u32[]{:S(2)}) %collective-permute-start.24) | collective-permute-done | bytes 65568 | tf_op jit(solution)/shard_map/ppermute | solution.py:35
  (76 shorter events, 23.9 us)
Async XLA Ops:
  1.8 6.4 %collective-permute-start = (bf16[128,256]{1,0:T(8,128)(2,1)S(1)}, bf16[128,256]{1,0:T(8,128)(2,1)S(1)}, u32[]{:S(2)}, u32[]{:S(2)}) collective-permute-start(bf16[128,256]{1,0:T(8,128)(2,1)S(1)} %get-tuple-element.55.refs_1_), channel_id=1, source_target_pairs={{0,12},{4,8},{8,4},{12,0},{1,13},{5,9},{9,5},{13,1},{2,14},{6,10},... | collective-permute-start | bytes 196616 | tf_op jit(solution)/shard_map/ppermute | solution.py:35
  5.7 4.3 %collective-permute-start.1 = (bf16[128,256]{1,0:T(8,128)(2,1)S(1)}, bf16[128,256]{1,0:T(8,128)(2,1)S(1)}, u32[]{:S(2)}, u32[]{:S(2)}) collective-permute-start(bf16[128,256]{1,0:T(8,128)(2,1)S(1)} %get-tuple-element.55.refs_1_), channel_id=1, source_target_pairs={{0,4},{4,0},{8,12},{12,8},{1,5},{5,1},{9,13},{13,9},{2,6},{6,2},{1... | collective-permute-start | bytes 196616 | tf_op jit(solution)/shard_map/ppermute | solution.py:35
  6.3 4.3 %collective-permute-start.2 = (bf16[128,256]{1,0:T(8,128)(2,1)S(1)}, bf16[128,256]{1,0:T(8,128)(2,1)S(1)}, u32[]{:S(2)}, u32[]{:S(2)}) collective-permute-start(bf16[128,256]{1,0:T(8,128)(2,1)S(1)} %get-tuple-element.55.refs_1_), channel_id=1, source_target_pairs={{0,8},{4,12},{8,0},{12,4},{1,9},{5,13},{9,1},{13,5},{2,10},{6,14},... | collective-permute-start | bytes 196616 | tf_op jit(solution)/shard_map/ppermute | solution.py:35
  10.8 6.9 %collective-permute-start.3 = (bf16[128,256]{1,0:T(8,128)(2,1)S(1)}, bf16[128,256]{1,0:T(8,128)(2,1)S(1)}, u32[]{:S(2)}, u32[]{:S(2)}) collective-permute-start(bf16[128,256]{1,0:T(8,128)(2,1)S(1)} %get-tuple-element.36), channel_id=1, source_target_pairs={{0,2},{1,3},{2,0},{3,1},{4,6},{5,7},{6,4},{7,5},{8,10},{9,11},{10,... | collective-permute-start | bytes 196616 | tf_op jit(solution)/shard_map/ppermute | solution.py:35
  13.5 6.2 %collective-permute-start.4 = (bf16[128,256]{1,0:T(8,128)(2,1)S(1)}, bf16[128,256]{1,0:T(8,128)(2,1)S(1)}, u32[]{:S(2)}, u32[]{:S(2)}) collective-permute-start(bf16[128,256]{1,0:T(8,128)(2,1)S(1)} %get-tuple-element.37), channel_id=1, source_target_pairs={{0,3},{1,2},{2,1},{3,0},{4,7},{5,6},{6,5},{7,4},{8,11},{9,10},{10,... | collective-permute-start | bytes 196616 | tf_op jit(solution)/shard_map/ppermute | solution.py:35
  14.8 5.0 %collective-permute-start.5 = (bf16[128,256]{1,0:T(8,128)(2,1)S(1)}, bf16[128,256]{1,0:T(8,128)(2,1)S(1)}, u32[]{:S(2)}, u32[]{:S(2)}) collective-permute-start(bf16[128,256]{1,0:T(8,128)(2,1)S(1)} %get-tuple-element.38), channel_id=1, source_target_pairs={{0,1},{1,0},{2,3},{3,2},{4,5},{5,4},{6,7},{7,6},{8,9},{9,8},{10,11... | collective-permute-start | bytes 196616 | tf_op jit(solution)/shard_map/ppermute | solution.py:35
  20.1 5.2 %collective-permute-start.6 = (bf16[128,256]{1,0:T(8,128)(2,1)S(1)}, bf16[128,256]{1,0:T(8,128)(2,1)S(1)}, u32[]{:S(2)}, u32[]{:S(2)}) collective-permute-start(bf16[128,256]{1,0:T(8,128)(2,1)S(1)} %get-tuple-element.57.refs_1_), channel_id=1, source_target_pairs={{0,12},{4,8},{8,4},{12,0},{1,13},{5,9},{9,5},{13,1},{2,14},{6,10},... | collective-permute-start | bytes 196616 | tf_op jit(solution)/shard_map/ppermute | solution.py:35
  21.6 4.3 %collective-permute-start.7 = (bf16[128,256]{1,0:T(8,128)(2,1)S(1)}, bf16[128,256]{1,0:T(8,128)(2,1)S(1)}, u32[]{:S(2)}, u32[]{:S(2)}) collective-permute-start(bf16[128,256]{1,0:T(8,128)(2,1)S(1)} %get-tuple-element.57.refs_1_), channel_id=1, source_target_pairs={{0,4},{4,0},{8,12},{12,8},{1,5},{5,1},{9,13},{13,9},{2,6},{6,2},{1... | collective-permute-start | bytes 196616 | tf_op jit(solution)/shard_map/ppermute | solution.py:35
  22.3 4.3 %collective-permute-start.8 = (bf16[128,256]{1,0:T(8,128)(2,1)S(1)}, bf16[128,256]{1,0:T(8,128)(2,1)S(1)}, u32[]{:S(2)}, u32[]{:S(2)}) collective-permute-start(bf16[128,256]{1,0:T(8,128)(2,1)S(1)} %get-tuple-element.57.refs_1_), channel_id=1, source_target_pairs={{0,8},{4,12},{8,0},{12,4},{1,9},{5,13},{9,1},{13,5},{2,10},{6,14},... | collective-permute-start | bytes 196616 | tf_op jit(solution)/shard_map/ppermute | solution.py:35
  28.6 5.1 %collective-permute-start.10 = (bf16[128,128]{1,0:T(8,128)(2,1)S(1)}, bf16[128,128]{1,0:T(8,128)(2,1)S(1)}, u32[]{:S(2)}, u32[]{:S(2)}) collective-permute-start(bf16[128,128]{1,0:T(8,128)(2,1)S(1)} %get-tuple-element.42), channel_id=1, source_target_pairs={{0,18},{1,19},{2,16},{3,17},{16,2},{17,3},{18,0},{19,1},{4,22},{5,... | collective-permute-start | bytes 98312 | tf_op jit(solution)/shard_map/ppermute | solution.py:40
  30.0 5.2 %collective-permute-start.11 = (bf16[128,128]{1,0:T(8,128)(2,1)S(1)}, bf16[128,128]{1,0:T(8,128)(2,1)S(1)}, u32[]{:S(2)}, u32[]{:S(2)}) collective-permute-start(bf16[128,128]{1,0:T(8,128)(2,1)S(1)} %get-tuple-element.43), channel_id=1, source_target_pairs={{0,19},{1,18},{2,17},{3,16},{16,3},{17,2},{18,1},{19,0},{4,23},{5,... | collective-permute-start | bytes 98312 | tf_op jit(solution)/shard_map/ppermute | solution.py:40
  31.0 4.1 %collective-permute-start.12 = (bf16[128,128]{1,0:T(8,128)(2,1)S(1)}, bf16[128,128]{1,0:T(8,128)(2,1)S(1)}, u32[]{:S(2)}, u32[]{:S(2)}) collective-permute-start(bf16[128,128]{1,0:T(8,128)(2,1)S(1)} %get-tuple-element.44), channel_id=1, source_target_pairs={{0,17},{1,16},{2,19},{3,18},{16,1},{17,0},{18,3},{19,2},{4,21},{5,... | collective-permute-start | bytes 98312 | tf_op jit(solution)/shard_map/ppermute | solution.py:40
  35.4 4.7 %collective-permute-start.13 = (bf16[128,128]{1,0:T(8,128)(2,1)S(1)}, bf16[128,128]{1,0:T(8,128)(2,1)S(1)}, u32[]{:S(2)}, u32[]{:S(2)}) collective-permute-start(bf16[128,128]{1,0:T(8,128)(2,1)S(1)} %get-tuple-element.45.refs_0_), channel_id=1, source_target_pairs={{0,18},{1,19},{2,16},{3,17},{16,2},{17,3},{18,0},{19,1},{4,22},{5,... | collective-permute-start | bytes 98312 | tf_op jit(solution)/shard_map/ppermute | solution.py:40
  36.5 5.3 %collective-permute-start.14 = (bf16[128,128]{1,0:T(8,128)(2,1)S(1)}, bf16[128,128]{1,0:T(8,128)(2,1)S(1)}, u32[]{:S(2)}, u32[]{:S(2)}) collective-permute-start(bf16[128,128]{1,0:T(8,128)(2,1)S(1)} %get-tuple-element.45.refs_0_), channel_id=1, source_target_pairs={{0,19},{1,18},{2,17},{3,16},{16,3},{17,2},{18,1},{19,0},{4,23},{5,... | collective-permute-start | bytes 98312 | tf_op jit(solution)/shard_map/ppermute | solution.py:40
  43.5 5.7 %collective-permute-start.17 = (bf16[128,256]{1,0:T(8,128)(2,1)S(1)}, bf16[128,256]{1,0:T(8,128)(2,1)S(1)}, u32[]{:S(2)}, u32[]{:S(2)}) collective-permute-start(bf16[128,256]{1,0:T(8,128)(2,1)S(1)} %get-tuple-element.47), channel_id=1, source_target_pairs={{0,12},{4,8},{8,4},{12,0},{1,13},{5,9},{9,5},{13,1},{2,14},{6,10},... | collective-permute-start | bytes 196616 | tf_op jit(solution)/shard_map/ppermute | solution.py:35
  46.0 4.3 %collective-permute-start.18 = (bf16[128,256]{1,0:T(8,128)(2,1)S(1)}, bf16[128,256]{1,0:T(8,128)(2,1)S(1)}, u32[]{:S(2)}, u32[]{:S(2)}) collective-permute-start(bf16[128,256]{1,0:T(8,128)(2,1)S(1)} %get-tuple-element.48), channel_id=1, source_target_pairs={{0,4},{4,0},{8,12},{12,8},{1,5},{5,1},{9,13},{13,9},{2,6},{6,2},{1... | collective-permute-start | bytes 196616 | tf_op jit(solution)/shard_map/ppermute | solution.py:35
  46.5 4.3 %collective-permute-start.19 = (bf16[128,256]{1,0:T(8,128)(2,1)S(1)}, bf16[128,256]{1,0:T(8,128)(2,1)S(1)}, u32[]{:S(2)}, u32[]{:S(2)}) collective-permute-start(bf16[128,256]{1,0:T(8,128)(2,1)S(1)} %get-tuple-element.49), channel_id=1, source_target_pairs={{0,8},{4,12},{8,0},{12,4},{1,9},{5,13},{9,1},{13,5},{2,10},{6,14},... | collective-permute-start | bytes 196616 | tf_op jit(solution)/shard_map/ppermute | solution.py:35
  51.1 6.6 %collective-permute-start.20 = (bf16[128,256]{1,0:T(8,128)(2,1)S(1)}, bf16[128,256]{1,0:T(8,128)(2,1)S(1)}, u32[]{:S(2)}, u32[]{:S(2)}) collective-permute-start(bf16[128,256]{1,0:T(8,128)(2,1)S(1)} %get-tuple-element.59.refs_1_), channel_id=1, source_target_pairs={{0,3},{1,2},{2,1},{3,0},{4,7},{5,6},{6,5},{7,4},{8,11},{9,10},{10,... | collective-permute-start | bytes 196616 | tf_op jit(solution)/shard_map/ppermute | solution.py:35
  53.6 5.2 %collective-permute-start.21 = (bf16[128,256]{1,0:T(8,128)(2,1)S(1)}, bf16[128,256]{1,0:T(8,128)(2,1)S(1)}, u32[]{:S(2)}, u32[]{:S(2)}) collective-permute-start(bf16[128,256]{1,0:T(8,128)(2,1)S(1)} %get-tuple-element.59.refs_1_), channel_id=1, source_target_pairs={{0,1},{1,0},{2,3},{3,2},{4,5},{5,4},{6,7},{7,6},{8,9},{9,8},{10,11... | collective-permute-start | bytes 196616 | tf_op jit(solution)/shard_map/ppermute | solution.py:35
  53.6 5.4 %collective-permute-start.22 = (bf16[128,256]{1,0:T(8,128)(2,1)S(1)}, bf16[128,256]{1,0:T(8,128)(2,1)S(1)}, u32[]{:S(2)}, u32[]{:S(2)}) collective-permute-start(bf16[128,256]{1,0:T(8,128)(2,1)S(1)} %get-tuple-element.59.refs_1_), channel_id=1, source_target_pairs={{0,2},{1,3},{2,0},{3,1},{4,6},{5,7},{6,4},{7,5},{8,10},{9,11},{10,... | collective-permute-start | bytes 196616 | tf_op jit(solution)/shard_map/ppermute | solution.py:35
  55.6 7.4 %collective-permute-start.26 = (f32[128,128]{1,0:T(8,128)S(1)}, f32[128,128]{1,0:T(8,128)S(1)}, u32[]{:S(2)}, u32[]{:S(2)}) collective-permute-start(f32[128,128]{1,0:T(8,128)S(1)} %get-tuple-element.54.mine_ref), channel_id=1, source_target_pairs={{0,16},{16,0},{1,17},{17,1},{2,18},{18,2},{3,19},{19,3},{4,20},{20... | collective-permute-start | bytes 196616 | tf_op jit(solution)/shard_map/ppermute | solution.py:35
  59.3 5.3 %collective-permute-start.23 = (bf16[128,256]{1,0:T(8,128)(2,1)S(1)}, bf16[128,256]{1,0:T(8,128)(2,1)S(1)}, u32[]{:S(2)}, u32[]{:S(2)}) collective-permute-start(bf16[128,256]{1,0:T(8,128)(2,1)S(1)} %get-tuple-element.51), channel_id=1, source_target_pairs={{0,12},{4,8},{8,4},{12,0},{1,13},{5,9},{9,5},{13,1},{2,14},{6,10},... | collective-permute-start | bytes 196616 | tf_op jit(solution)/shard_map/ppermute | solution.py:35
  61.4 4.3 %collective-permute-start.24 = (bf16[128,256]{1,0:T(8,128)(2,1)S(1)}, bf16[128,256]{1,0:T(8,128)(2,1)S(1)}, u32[]{:S(2)}, u32[]{:S(2)}) collective-permute-start(bf16[128,256]{1,0:T(8,128)(2,1)S(1)} %get-tuple-element.52), channel_id=1, source_target_pairs={{0,4},{4,0},{8,12},{12,8},{1,5},{5,1},{9,13},{13,9},{2,6},{6,2},{1... | collective-permute-start | bytes 196616 | tf_op jit(solution)/shard_map/ppermute | solution.py:35
  62.1 4.3 %collective-permute-start.25 = (bf16[128,256]{1,0:T(8,128)(2,1)S(1)}, bf16[128,256]{1,0:T(8,128)(2,1)S(1)}, u32[]{:S(2)}, u32[]{:S(2)}) collective-permute-start(bf16[128,256]{1,0:T(8,128)(2,1)S(1)} %get-tuple-element.53), channel_id=1, source_target_pairs={{0,8},{4,12},{8,0},{12,4},{1,9},{5,13},{9,1},{13,5},{2,10},{6,14},... | collective-permute-start | bytes 196616 | tf_op jit(solution)/shard_map/ppermute | solution.py:35
  (13 other events, 54.1 us)
